TPU v7x, 32 devices: a whole 2x2x4 slice. The times are simulated.
32 devices in a mesh: grp: 2 (over y), col: 16 (over z, x, core).
Axes of the slice: x: 2, y: 2, z: 4, core: 2. Of those that a mesh axis runs over, the one named last changes fastest.
Arguments:
- tokens: bfloat16 [256, 14336], P(('grp', 'col')), parts along dimension 0, may hold values from -6 to 6
- slab_lengths: int32 [32], P('grp'), parts along dimension 0, may hold values from 1 to 8, 96 in all
- tile_owner: int32 [136], replicated, may hold values from 0 to 15, as said below
Outputs:
- factor_tiles: float32 [352, 896, 896], P(('grp', 'col')), parts along dimension 0
There are 2 independent parts, one for each index of `grp`. A program takes and returns all parts, laid end to end along the dimension named above; an argument that names none is the same for every part. Nothing has to cross between parts.
Inputs may be any that keep to these rules, and one draw needn't show every extreme that they name: tile_owner[t] is one of the two blocks i, j of tile t, and the other block lies at most 10 indices before the owner, counted cyclically over 16; no device owns more than 11 tiles and some device owns exactly 11.
All inputs are finite; a program needn't handle non-finite values.
Results may differ from a plain program's by a relative error of at most 0.0003.
Values may be sent and summed in bfloat16 or wider, within the bound.
No kernel may reach another device: no remote copies, remote signals or barrier semaphores. Data moves between devices by JAX's collectives and lax.ppermute only.
A program may use at most 128 MiB of HBM per device.

v0:
```python
import functools

import jax
import jax.numpy as jnp
from jax import lax
from jax.experimental import pallas as pl
from jax.experimental.pallas import tpu as pltpu
from jax.sharding import PartitionSpec as P

BUFFERS = 4


def tile_kernel(
    devices, reach, slots, aligned, owner_ref, device_ref, scale_ref, x_ref, mask_ref,
    out_ref, blocks, mask, tiles, zeros, in_sems, mask_sem, out_sems, zero_sems,
):
    device = device_ref[0]
    width = blocks.shape[2]

    def owned(partner):
        low = jnp.minimum(device, partner)
        high = jnp.maximum(device, partner)
        index = low * devices - low * (low - 1) // 2 + (high - low)
        return owner_ref[index] == device

    def fetch(partner):
        if aligned:
            source = x_ref.at[:, pl.ds(pl.multiple_of(partner * width, 128), width)]
        else:
            source = x_ref.at[partner]
        return pltpu.make_async_copy(source, blocks.at[partner], in_sems.at[partner])

    def put(buffer, slot):
        return pltpu.make_async_copy(tiles.at[buffer], out_ref.at[slot], out_sems.at[buffer])

    def clear(slot):
        return pltpu.make_async_copy(zeros, out_ref.at[slot], zero_sems.at[slot])

    mask_copy = pltpu.make_async_copy(mask_ref, mask, mask_sem)
    mask_copy.start()
    fetch(device).start()

    def start_fetch(partner, count):
        mine = owned(partner)

        @pl.when(mine & (partner != device))
        def _():
            fetch(partner).start()

        return count + mine.astype(jnp.int32)

    count = lax.fori_loop(0, devices, start_fetch, jnp.int32(0))

    zeros[...] = jnp.zeros_like(zeros)

    def start_clear(slot, carry):
        clear(slot).start()
        return carry

    lax.fori_loop(count, slots, start_clear, 0)

    mask_copy.wait()
    fetch(device).wait()
    blocks[devices] = blocks[device] * mask[...]
    scale = scale_ref[0]

    def visit(partner, slot):
        mine = owned(partner)

        @pl.when(mine)
        def _():
            @pl.when(partner != device)
            def _():
                fetch(partner).wait()

            buffer = lax.rem(slot, BUFFERS)

            @pl.when(slot >= BUFFERS)
            def _():
                put(buffer, slot - BUFFERS).wait()

            left = jnp.where(partner <= device, partner, devices)
            right = jnp.where(partner <= device, devices, partner)
            step = 128 if aligned else width
            for row in range(0, width, step):
                product = lax.dot_general(
                    blocks[left, :, row:row + step],
                    blocks[right],
                    (((0,), (0,)), ((), ())),
                    preferred_element_type=jnp.float32,
                )
                tiles[buffer, row:row + step, :] = product * scale
            put(buffer, slot).start()

        return slot + mine.astype(jnp.int32)

    lax.fori_loop(0, devices, visit, jnp.int32(0))

    def drain(slot, carry):
        put(lax.rem(slot, BUFFERS), slot).wait()
        return carry

    lax.fori_loop(jnp.maximum(count - BUFFERS, 0), count, drain, 0)

    def end_clear(slot, carry):
        clear(slot).wait()
        return carry

    lax.fori_loop(count, slots, end_clear, 0)


def per_device(tokens, slab_lengths, tile_owner):
    devices = lax.axis_size("col")
    device = lax.axis_index("col")
    reach = devices // 2 + devices // 8
    slots = reach + 1
    slab, units = tokens.shape
    rows = slab * devices
    width = units // devices
    aligned = width % 128 == 0

    x = lax.all_gather(tokens, "col", axis=0, tiled=True)
    if not aligned:
        x = x.reshape(rows, devices, width).transpose(1, 0, 2)

    valid = jnp.arange(slab, dtype=jnp.int32)[None, :] < slab_lengths[:, None]
    mask = jnp.broadcast_to(valid.reshape(rows, 1), (rows, width)).astype(jnp.bfloat16)
    scale = 1.0 / jnp.sum(slab_lengths).astype(jnp.float32)

    return pl.pallas_call(
        functools.partial(tile_kernel, devices, reach, slots, aligned),
        out_shape=jax.ShapeDtypeStruct((slots, width, width), jnp.float32),
        in_specs=[
            pl.BlockSpec(memory_space=pltpu.SMEM),
            pl.BlockSpec(memory_space=pltpu.SMEM),
            pl.BlockSpec(memory_space=pltpu.SMEM),
            pl.BlockSpec(memory_space=pl.ANY),
            pl.BlockSpec(memory_space=pl.ANY),
        ],
        out_specs=pl.BlockSpec(memory_space=pl.ANY),
        scratch_shapes=[
            pltpu.VMEM((devices + 1, rows, width), jnp.bfloat16),
            pltpu.VMEM((rows, width), jnp.bfloat16),
            pltpu.VMEM((BUFFERS, width, width), jnp.float32),
            pltpu.VMEM((width, width), jnp.float32),
            pltpu.SemaphoreType.DMA((devices,)),
            pltpu.SemaphoreType.DMA,
            pltpu.SemaphoreType.DMA((BUFFERS,)),
            pltpu.SemaphoreType.DMA((slots,)),
        ],
        compiler_params=pltpu.CompilerParams(vmem_limit_bytes=50 * 1024 * 1024),
        cost_estimate=pl.CostEstimate(
            flops=2 * slots * rows * width * width,
            bytes_accessed=4 * slots * width * width + 2 * slots * rows * width,
            transcendentals=0,
        ),
    )(tile_owner, device.reshape(1).astype(jnp.int32), scale.reshape(1), x, mask)


def solution(mesh):
    return jax.shard_map(
        per_device,
        mesh=mesh,
        in_specs=(P(("grp", "col"), None), P("grp"), P()),
        out_specs=P(("grp", "col"), None, None),
        check_vma=False,
    )
```

profile of v0, /device:TPU:0, one launch (start us, length us, event | category | flops | bytes accessed | tf_op | source)
XLA Modules:
  0.0 83.1 jit_solution(18168217369659985964)
XLA Ops:
  6.5 0.0 all-gather.2.cloned.1.call-start
  6.5 0.7 all-gather.2.cloned.1.call-update
  7.3 1.3 %reduce_sum.9 = s32[]{:T(128)} reduce(s32[16]{0:T(128)} %param.4, s32[]{:T(128)} %constant.2.clone.1), dimensions={0}, to_apply=%region_0.0 | reduce | flops 15 | bytes 72 | tf_op jit(solution)/shard_map/reduce_sum | solution.py:128
  9.2 0.7 fusion
  9.9 0.1 reshape.26
  10.1 49.8 %all-gather.2.cloned.1.call-done.x_ref = bf16[128,14336]{1,0:T(8,128)(2,1)} async-done(((bf16[8,14336]{1,0:T(8,128)(2,1)}), bf16[128,14336]{1,0:T(8,128)(2,1)}) %all-gather.2.cloned.1.call-update) | async-done | bytes 3670032 | tf_op jit(solution)/shard_map/all_gather | solution.py:122
  59.9 0.1 broadcast_in_dim.2.mask_ref
  60.0 0.0 copy-start
  60.0 2.0 %copy-done = bf16[128,14336]{1,0:T(8,128)(2,1)S(1)} copy-done((bf16[128,14336]{1,0:T(8,128)(2,1)S(1)}, bf16[128,14336]{1,0:T(8,128)(2,1)}, u32[]{:S(2)}) %copy-start) | copy-done | bytes 3670040
  62.0 0.0 copy-start.1
  62.0 0.7 copy-done.1
  62.7 13.5 %shard_map.37 = f32[11,896,896]{2,1,0:T(8,128)} custom-call(s32[136]{0:T(256)S(1)} %copy-done.1, s32[1]{0:T(128)} %bitcast.device_ref, f32[1]{0:T(128)} %bitcast.1.scale_ref, bf16[128,14336]{1,0:T(8,128)(2,1)S(1)} %copy-done, bf16[128,896]{1,0:T(8,128)(2,1)S(1)} %broadcast_in_dim.2.mask_ref), custom_call_target="tpu_custom_call" | custom-call | flops 2260729856 | bytes 37847040 | tf_op jit(solution)/shard_map/pallas_call | solution.py:130
Async XLA Ops:
  6.5 53.3 %all-gather.2.cloned.1.call-start = ((), (), s32[]{:S(2)}) async-start(), calls=%async_computation | async-start | bytes 3899392 | tf_op jit(solution)/shard_map/all_gather | solution.py:122
  60.0 2.0 %copy-start = (bf16[128,14336]{1,0:T(8,128)(2,1)S(1)}, bf16[128,14336]{1,0:T(8,128)(2,1)}, u32[]{:S(2)}) copy-start(bf16[128,14336]{1,0:T(8,128)(2,1)} %all-gather.2.cloned.1.call-done.x_ref) | copy-start | bytes 11010052
  62.0 0.7 copy-start.1
Sparse Core Ops, SparseCore 0:
  9.6 50.1 all-gather.1
where the time goes:
time: 83.2 us; the launch traced here: 83.1 us
  waiting for transfers between devices  50.5 us (61%)
  between operations  14.1 us (17%)
  Pallas kernels  13.5 us (16%)
  local copies, waits for them, and re-layouts  2.89 us (3%)
  other arithmetic  2.02 us (2%)
    all_gather x1, waiting for transfers between devices, per_device(): x = lax.all_gather(tokens, 'col', axis=0, tiled=True)  49.8 us
    pallas_call x1, Pallas kernels, per_device(): pl.pallas_call(functools.partial(tile_kernel, devices, reach, slots, alig...  13.5 us
    unnamed x4, local copies, waits for them, and re-layouts  2.71 us
  transfers between devices with their start and end apart: 1, of which 1 were waited for; matrix products, arithmetic and copies ran while one was open for 3% of the time, Pallas kernels for 0%

commit v1 on v0

v1 whole, which is shorter than its diff:
```python
import functools

import jax
import jax.numpy as jnp
import numpy as np
from jax import lax
from jax.experimental import pallas as pl
from jax.experimental.pallas import tpu as pltpu
from jax.sharding import PartitionSpec as P

BUFFERS = 4
RING_LIMIT = 16


def tile_number(devices, device, partner):
    low = jnp.minimum(device, partner)
    high = jnp.maximum(device, partner)
    return low * devices - low * (low - 1) // 2 + (high - low)


def gathered_kernel(
    devices, slots, owner_ref, device_ref, scale_ref, x_ref, mask_ref,
    out_ref, blocks, mask, tiles, zeros, in_sems, mask_sem, out_sems, zero_sems,
):
    device = device_ref[0]
    width = blocks.shape[2]

    def owned(partner):
        return owner_ref[tile_number(devices, device, partner)] == device

    def fetch(partner):
        return pltpu.make_async_copy(x_ref.at[partner], blocks.at[partner], in_sems.at[partner])

    def put(buffer, slot):
        return pltpu.make_async_copy(tiles.at[buffer], out_ref.at[slot], out_sems.at[buffer])

    def clear(slot):
        return pltpu.make_async_copy(zeros, out_ref.at[slot], zero_sems.at[slot])

    mask_copy = pltpu.make_async_copy(mask_ref, mask, mask_sem)
    mask_copy.start()
    fetch(device).start()

    def start_fetch(partner, count):
        mine = owned(partner)

        @pl.when(mine & (partner != device))
        def _():
            fetch(partner).start()

        return count + mine.astype(jnp.int32)

    count = lax.fori_loop(0, devices, start_fetch, jnp.int32(0))

    zeros[...] = jnp.zeros_like(zeros)

    def start_clear(slot, carry):
        clear(slot).start()
        return carry

    lax.fori_loop(count, slots, start_clear, 0)

    mask_copy.wait()
    fetch(device).wait()
    blocks[devices] = blocks[device] * mask[...]
    scale = scale_ref[0]

    def visit(partner, slot):
        mine = owned(partner)

        @pl.when(mine)
        def _():
            @pl.when(partner != device)
            def _():
                fetch(partner).wait()

            buffer = lax.rem(slot, BUFFERS)

            @pl.when(slot >= BUFFERS)
            def _():
                put(buffer, slot - BUFFERS).wait()

            left = jnp.where(partner <= device, partner, devices)
            right = jnp.where(partner <= device, devices, partner)
            product = lax.dot_general(
                blocks[left], blocks[right], (((0,), (0,)), ((), ())),
                preferred_element_type=jnp.float32,
            )
            tiles[buffer] = product * scale
            put(buffer, slot).start()

        return slot + mine.astype(jnp.int32)

    lax.fori_loop(0, devices, visit, jnp.int32(0))

    def drain(slot, carry):
        put(lax.rem(slot, BUFFERS), slot).wait()
        return carry

    lax.fori_loop(jnp.maximum(count - BUFFERS, 0), count, drain, 0)

    def end_clear(slot, carry):
        clear(slot).wait()
        return carry

    lax.fori_loop(count, slots, end_clear, 0)


def gathered_form(tokens, slab_lengths, tile_owner, devices, device, slots, scale):
    slab, units = tokens.shape
    rows = slab * devices
    width = units // devices
    x = lax.all_gather(tokens, "col", axis=0, tiled=True)
    x = x.reshape(rows, devices, width).transpose(1, 0, 2)
    valid = jnp.arange(slab, dtype=jnp.int32)[None, :] < slab_lengths[:, None]
    mask = jnp.broadcast_to(valid.reshape(rows, 1), (rows, width)).astype(jnp.bfloat16)
    return pl.pallas_call(
        functools.partial(gathered_kernel, devices, slots),
        out_shape=jax.ShapeDtypeStruct((slots, width, width), jnp.float32),
        in_specs=[pl.BlockSpec(memory_space=pltpu.SMEM)] * 3 + [pl.BlockSpec(memory_space=pl.ANY)] * 2,
        out_specs=pl.BlockSpec(memory_space=pl.ANY),
        scratch_shapes=[
            pltpu.VMEM((devices + 1, rows, width), jnp.bfloat16),
            pltpu.VMEM((rows, width), jnp.bfloat16),
            pltpu.VMEM((BUFFERS, width, width), jnp.float32),
            pltpu.VMEM((width, width), jnp.float32),
            pltpu.SemaphoreType.DMA((devices,)),
            pltpu.SemaphoreType.DMA,
            pltpu.SemaphoreType.DMA((BUFFERS,)),
            pltpu.SemaphoreType.DMA((slots,)),
        ],
        compiler_params=pltpu.CompilerParams(vmem_limit_bytes=50 * 1024 * 1024),
    )(tile_owner, device.reshape(1), scale.reshape(1), x, mask)


def ring_plan(devices):
    chips = devices // 2
    order = list(range(0, chips, 2)) + list(range(1, chips, 2))[::-1]
    place = {chip: at for at, chip in enumerate(order)}
    onward = []
    for device in range(devices):
        chip, core = divmod(device, 2)
        step = 1 if core == 0 else -1
        onward.append(order[(place[chip] + step) % chips] * 2 + core)
    backward = [onward.index(device) for device in range(devices)]
    return onward, backward


def ring_gather(tokens, devices):
    onward, backward = ring_plan(devices)
    sibling = [device ^ 1 for device in range(devices)]
    here = list(range(devices))

    def send(value, target):
        return lax.ppermute(value, "col", list(enumerate(target)))

    def received(source, target):
        return [source[target.index(device)] for device in range(devices)]

    chips = devices // 2
    ahead, back = tokens, tokens
    ahead_from, back_from = here, here
    slabs, sources = [tokens], [here]
    for step in range(1, chips // 2 + 1):
        ahead = send(ahead, onward)
        ahead_from = received(ahead_from, onward)
        slabs.append(ahead)
        sources.append(ahead_from)
        if 2 * step < chips:
            back = send(back, backward)
            back_from = received(back_from, backward)
            slabs.append(back)
            sources.append(back_from)
    for value, source in list(zip(slabs, sources)):
        slabs.append(send(value, sibling))
        sources.append(received(source, sibling))
    return slabs, np.array(sources, np.int32).T


def ring_kernel(devices, slots, count_in, owner_ref, device_ref, kept_ref, scale_ref, *refs):
    slabs = refs[:count_in]
    out_ref, pair, tiles, zeros, out_sems, zero_sems = refs[count_in:]
    device = device_ref[0]
    slab, width = slabs[0].shape[0], pair.shape[2]

    def owned(partner):
        return owner_ref[tile_number(devices, device, partner)] == device

    def put(buffer, slot):
        return pltpu.make_async_copy(tiles.at[buffer], out_ref.at[slot], out_sems.at[buffer])

    def clear(slot):
        return pltpu.make_async_copy(zeros, out_ref.at[slot], zero_sems.at[slot])

    def column_block(partner, masked):
        columns = pl.ds(pl.multiple_of(partner * width, 128), width)
        parts = []
        for at, ref in enumerate(slabs):
            part = ref[:, columns].astype(jnp.float32)
            if masked:
                row = lax.broadcasted_iota(jnp.int32, (slab, width), 0)
                part = jnp.where(row < kept_ref[at], part, 0.0)
            parts.append(part)
        return jnp.concatenate(parts, axis=0).astype(jnp.bfloat16)

    count = lax.fori_loop(
        0, devices, lambda partner, total: total + owned(partner).astype(jnp.int32), jnp.int32(0)
    )

    @pl.when(count < slots)
    def _():
        zeros[...] = jnp.zeros_like(zeros)

    def start_clear(slot, carry):
        clear(slot).start()
        return carry

    lax.fori_loop(count, slots, start_clear, 0)

    pair[0] = column_block(device, True)
    scale = scale_ref[0]

    def visit(partner, slot):
        mine = owned(partner)

        @pl.when(mine)
        def _():
            buffer = lax.rem(slot, BUFFERS)
            pair[1] = column_block(partner, False)

            @pl.when(slot >= BUFFERS)
            def _():
                put(buffer, slot - BUFFERS).wait()

            left = (partner <= device).astype(jnp.int32)
            for row in range(0, width, 128):
                product = lax.dot_general(
                    pair[left, :, row:row + 128], pair[1 - left], (((0,), (0,)), ((), ())),
                    preferred_element_type=jnp.float32,
                )
                tiles[buffer, row:row + 128, :] = product * scale
            put(buffer, slot).start()

        return slot + mine.astype(jnp.int32)

    lax.fori_loop(0, devices, visit, jnp.int32(0))

    def drain(slot, carry):
        put(lax.rem(slot, BUFFERS), slot).wait()
        return carry

    lax.fori_loop(jnp.maximum(count - BUFFERS, 0), count, drain, 0)

    def end_clear(slot, carry):
        clear(slot).wait()
        return carry

    lax.fori_loop(count, slots, end_clear, 0)


def ring_form(tokens, slab_lengths, tile_owner, devices, device, slots, scale):
    slab, units = tokens.shape
    width = units // devices
    slabs, sources = ring_gather(tokens, devices)
    kept = slab_lengths[jnp.asarray(sources)[device]]
    return pl.pallas_call(
        functools.partial(ring_kernel, devices, slots, len(slabs)),
        out_shape=jax.ShapeDtypeStruct((slots, width, width), jnp.float32),
        in_specs=[pl.BlockSpec(memory_space=pltpu.SMEM)] * 4
        + [pl.BlockSpec(memory_space=pltpu.VMEM)] * len(slabs),
        out_specs=pl.BlockSpec(memory_space=pl.ANY),
        scratch_shapes=[
            pltpu.VMEM((2, slab * devices, width), jnp.bfloat16),
            pltpu.VMEM((BUFFERS, width, width), jnp.float32),
            pltpu.VMEM((width, width), jnp.float32),
            pltpu.SemaphoreType.DMA((BUFFERS,)),
            pltpu.SemaphoreType.DMA((slots,)),
        ],
        compiler_params=pltpu.CompilerParams(vmem_limit_bytes=32 * 1024 * 1024),
        cost_estimate=pl.CostEstimate(
            flops=2 * slots * slab * devices * width * width,
            bytes_accessed=4 * slots * width * width,
            transcendentals=0,
        ),
    )(tile_owner, device.reshape(1), kept, scale.reshape(1), *slabs)


def per_device(tokens, slab_lengths, tile_owner):
    devices = lax.axis_size("col")
    device = lax.axis_index("col").astype(jnp.int32)
    slots = devices // 2 + devices // 8 + 1
    width = tokens.shape[1] // devices
    scale = 1.0 / jnp.sum(slab_lengths).astype(jnp.float32)
    form = ring_form if devices <= RING_LIMIT and width % 128 == 0 else gathered_form
    return form(tokens, slab_lengths, tile_owner, devices, device, slots, scale)


def solution(mesh):
    return jax.shard_map(
        per_device,
        mesh=mesh,
        in_specs=(P(("grp", "col"), None), P("grp"), P()),
        out_specs=P(("grp", "col"), None, None),
        check_vma=False,
    )
```

time: 83.2 us -> 50.5 us (0.61)
  waiting for transfers between devices: 50.5 us -> 23.8 us
  between operations: 14.1 us -> 0.78 us
  starting transfers between devices: 0.01 us -> 7.74 us
    all_gather x1 -> x0, waiting for transfers between devices: 49.8 us -> none  [per_device(): x = lax.all_gather(tokens, 'col', axis=0, tiled=True)]
    ppermute x0 -> x15, waiting for transfers between devices: none -> 23.8 us  [send(): return lax.ppermute(value, 'col', list(enumerate(target)))]
    ppermute x0 -> x15, starting transfers between devices: none -> 7.74 us  [send(): return lax.ppermute(value, 'col', list(enumerate(target)))]
    gather x0 -> x1, local copies, waits for them, and re-layouts: none -> 1.31 us  [ring_form(): kept = slab_lengths[jnp.asarray(sources)[device]]]
    unnamed x4, local copies, waits for them, and re-layouts: 2.71 us -> 1.61 us
  transfers between devices with their start and end apart: 1 -> 15, of which waited for: 1 -> 6; matrix products, arithmetic and copies ran while one was open for 3% -> 7% of each run, Pallas kernels for 0% -> 0%
where the time goes in v1:
time: 50.5 us; the launch traced here: 50 us
  waiting for transfers between devices  23.8 us (47%)
  Pallas kernels  12.8 us (25%)
  starting transfers between devices  7.74 us (15%)
  local copies, waits for them, and re-layouts  2.93 us (6%)
  other arithmetic  2 us (4%)
  between operations  0.78 us (2%)
    ppermute x15, waiting for transfers between devices, send(): return lax.ppermute(value, 'col', list(enumerate(target)))  23.8 us
    pallas_call x1, Pallas kernels, ring_form(): pl.pallas_call(functools.partial(ring_kernel, devices, slots, len(slabs))...  12.8 us
    ppermute x15, starting transfers between devices, send(): return lax.ppermute(value, 'col', list(enumerate(target)))  7.74 us
    unnamed x4, local copies, waits for them, and re-layouts  1.61 us
    gather x1, local copies, waits for them, and re-layouts, ring_form(): kept = slab_lengths[jnp.asarray(sources)[device]]  1.31 us
    reduce_sum x1, other arithmetic, per_device(): scale = 1.0 / jnp.sum(slab_lengths).astype(jnp.float32)  1.29 us
  transfers between devices with their start and end apart: 15, of which 6 were waited for; matrix products, arithmetic and copies ran while one was open for 7% of the time, Pallas kernels for 0%

profile of v1, /device:TPU:0, one launch (start us, length us, event | category | flops | bytes accessed | tf_op | source)
XLA Modules:
  0.0 50.0 jit_solution(2226215606585307915)
XLA Ops:
  0.0 3.0 %collective-permute-start = (bf16[8,14336]{1,0:T(8,128)(2,1)}, bf16[8,14336]{1,0:T(8,128)(2,1)S(1)}, u32[]{:S(2)}, u32[]{:S(2)}) collective-permute-start(bf16[8,14336]{1,0:T(8,128)(2,1)} %refs_0_.1), channel_id=1, source_target_pairs={{0,4},{1,3},{2,0},{3,7},{4,8},{5,1},{6,2},{7,11},{8,12},{9,5},{10,... | collective-permute-start | bytes 688136 | tf_op jit(solution)/shard_map/ppermute | solution.py:155
  3.0 0.0 collective-permute-start.1
  3.0 6.0 %collective-permute-done.refs_1_ = bf16[8,14336]{1,0:T(8,128)(2,1)S(1)} collective-permute-done((bf16[8,14336]{1,0:T(8,128)(2,1)}, bf16[8,14336]{1,0:T(8,128)(2,1)S(1)}, u32[]{:S(2)}, u32[]{:S(2)}) %collective-permute-start) | collective-permute-done | bytes 229408 | tf_op jit(solution)/shard_map/ppermute | solution.py:155
  9.1 1.5 %collective-permute-start.2 = (bf16[8,14336]{1,0:T(8,128)(2,1)S(1)}, bf16[8,14336]{1,0:T(8,128)(2,1)S(1)}, u32[]{:S(2)}, u32[]{:S(2)}) collective-permute-start(bf16[8,14336]{1,0:T(8,128)(2,1)S(1)} %collective-permute-done.refs_1_), channel_id=1, source_target_pairs={{0,4},{1,3},{2,0},{3,7},{4,8},{5,1},{6,2},{7,11},{8,12},{9,5},{10,... | collective-permute-start | bytes 688136 | tf_op jit(solution)/shard_map/ppermute | solution.py:155
  10.6 0.0 collective-permute-done.1.refs_2_
  10.6 0.9 %collective-permute-start.3 = (bf16[8,14336]{1,0:T(8,128)(2,1)S(1)}, bf16[8,14336]{1,0:T(8,128)(2,1)S(1)}, u32[]{:S(2)}, u32[]{:S(2)}) collective-permute-start(bf16[8,14336]{1,0:T(8,128)(2,1)S(1)} %collective-permute-done.1.refs_2_), channel_id=1, source_target_pairs={{0,2},{1,5},{2,6},{3,1},{4,0},{5,9},{6,10},{7,3},{8,4},{9,13},{10,... | collective-permute-start | bytes 688136 | tf_op jit(solution)/shard_map/ppermute | solution.py:155
  11.5 5.9 %collective-permute-done.2.refs_3_ = bf16[8,14336]{1,0:T(8,128)(2,1)S(1)} collective-permute-done((bf16[8,14336]{1,0:T(8,128)(2,1)S(1)}, bf16[8,14336]{1,0:T(8,128)(2,1)S(1)}, u32[]{:S(2)}, u32[]{:S(2)}) %collective-permute-start.2) | collective-permute-done | bytes 229408 | tf_op jit(solution)/shard_map/ppermute | solution.py:155
  17.3 0.0 collective-permute-start.4
  17.3 0.0 collective-permute-start.7
  17.4 0.5 %collective-permute-start.9 = (bf16[8,14336]{1,0:T(8,128)(2,1)S(1)}, bf16[8,14336]{1,0:T(8,128)(2,1)S(1)}, u32[]{:S(2)}, u32[]{:S(2)}) collective-permute-start(bf16[8,14336]{1,0:T(8,128)(2,1)S(1)} %collective-permute-done.1.refs_2_), channel_id=1, source_target_pairs={{0,1},{1,0},{2,3},{3,2},{4,5},{5,4},{6,7},{7,6},{8,9},{9,8},{10,11... | collective-permute-start | bytes 688136 | tf_op jit(solution)/shard_map/ppermute | solution.py:155
  17.9 0.0 collective-permute-start.8
  17.9 0.8 %collective-permute-done.3.refs_4_ = bf16[8,14336]{1,0:T(8,128)(2,1)S(1)} collective-permute-done((bf16[8,14336]{1,0:T(8,128)(2,1)S(1)}, bf16[8,14336]{1,0:T(8,128)(2,1)S(1)}, u32[]{:S(2)}, u32[]{:S(2)}) %collective-permute-start.3) | collective-permute-done | bytes 229408 | tf_op jit(solution)/shard_map/ppermute | solution.py:155
  18.7 1.2 %collective-permute-start.5 = (bf16[8,14336]{1,0:T(8,128)(2,1)S(1)}, bf16[8,14336]{1,0:T(8,128)(2,1)S(1)}, u32[]{:S(2)}, u32[]{:S(2)}) collective-permute-start(bf16[8,14336]{1,0:T(8,128)(2,1)S(1)} %collective-permute-done.3.refs_4_), channel_id=1, source_target_pairs={{0,2},{1,5},{2,6},{3,1},{4,0},{5,9},{6,10},{7,3},{8,4},{9,13},{10,... | collective-permute-start | bytes 688136 | tf_op jit(solution)/shard_map/ppermute | solution.py:155
  19.9 5.6 %collective-permute-done.4.refs_5_ = bf16[8,14336]{1,0:T(8,128)(2,1)S(1)} collective-permute-done((bf16[8,14336]{1,0:T(8,128)(2,1)S(1)}, bf16[8,14336]{1,0:T(8,128)(2,1)S(1)}, u32[]{:S(2)}, u32[]{:S(2)}) %collective-permute-start.4) | collective-permute-done | bytes 229408 | tf_op jit(solution)/shard_map/ppermute | solution.py:155
  25.5 0.0 collective-permute-start.6
  25.5 0.0 collective-permute-done.7.refs_8_
  25.5 0.0 collective-permute-start.11
  25.5 0.0 collective-permute-done.9.refs_10_
  25.5 0.5 collective-permute-start.10
  26.0 0.0 collective-permute-done.8.refs_9_
  26.0 0.1 collective-permute-start.12
  26.1 1.0 %collective-permute-done.5.refs_6_ = bf16[8,14336]{1,0:T(8,128)(2,1)S(1)} collective-permute-done((bf16[8,14336]{1,0:T(8,128)(2,1)S(1)}, bf16[8,14336]{1,0:T(8,128)(2,1)S(1)}, u32[]{:S(2)}, u32[]{:S(2)}) %collective-permute-start.5) | collective-permute-done | bytes 229408 | tf_op jit(solution)/shard_map/ppermute | solution.py:155
  27.1 0.0 collective-permute-start.13
  27.1 4.4 %collective-permute-done.6.refs_7_ = bf16[8,14336]{1,0:T(8,128)(2,1)S(1)} collective-permute-done((bf16[8,14336]{1,0:T(8,128)(2,1)S(1)}, bf16[8,14336]{1,0:T(8,128)(2,1)S(1)}, u32[]{:S(2)}, u32[]{:S(2)}) %collective-permute-start.6) | collective-permute-done | bytes 229408 | tf_op jit(solution)/shard_map/ppermute | solution.py:155
  31.5 0.0 collective-permute-start.14
  31.5 1.3 %reduce_sum.9 = s32[]{:T(128)} reduce(s32[16]{0:T(128)} %param.5, s32[]{:T(128)} %constant.6.clone.1), dimensions={0}, to_apply=%region_0.0 | reduce | flops 15 | bytes 72 | tf_op jit(solution)/shard_map/reduce_sum | solution.py:293
  33.5 0.7 %fusion = s32[16]{0:T(128)S(1)} fusion(s32[16,16]{1,0:T(8,128)} %constant.3.clone, s32[]{:T(128)S(6)} %select_n.13), kind=kLoop, calls=%fused_computation.3 | loop fusion | flops 48 | bytes 132 | tf_op jit(solution)/shard_map/select_n | solution.py:265
  34.2 1.3 %gather_fusion = s32[16]{0:T(128)S(1)} fusion(s32[16]{0:T(128)} %param.5, s32[1024]{0:T(1024)S(1)} %pad_clamp_fusion), kind=kCustom, calls=%fused_computation | custom fusion | bytes 192 | tf_op jit(solution)/shard_map/gather | solution.py:265
  35.5 0.0 collective-permute-done.11.refs_12_
  35.5 0.0 collective-permute-done.10.refs_11_
  35.6 0.0 collective-permute-done.13.refs_14_
  35.6 0.0 collective-permute-done.12.refs_13_
  35.6 0.0 collective-permute-done.14.refs_15_
  35.6 0.0 copy-start
  35.6 0.9 %copy-done = bf16[8,14336]{1,0:T(8,128)(2,1)S(1)} copy-done((bf16[8,14336]{1,0:T(8,128)(2,1)S(1)}, bf16[8,14336]{1,0:T(8,128)(2,1)}, u32[]{:S(2)}) %copy-start) | copy-done | bytes 229400
  36.5 0.0 copy-start.1
  36.5 0.7 %copy-done.1 = s32[136]{0:T(256)S(1)} copy-done((s32[136]{0:T(256)S(1)}, s32[136]{0:T(256)}, u32[]{:S(2)}) %copy-start.1) | copy-done | bytes 568
  37.2 12.8 %shard_map.46 = f32[11,896,896]{2,1,0:T(8,128)} custom-call(s32[136]{0:T(256)S(1)} %copy-done.1, s32[1]{0:T(128)} %bitcast.device_ref, s32[16]{0:T(128)S(1)} %gather_fusion, f32[1]{0:T(128)} %bitcast.3.scale_ref, bf16[8,14336]{1,0:T(8,128)(2,1)S(1)} %copy-done, bf16[8,14336]{1,0:T(8,128)(2,1)S(1)} %collective-permute-done.refs_1_, ...), custom_call_target="tpu_custom_call" | custom-call | flops 2260729856 | bytes 35323904 | tf_op jit(solution)/shard_map/pallas_call | solution.py:266
  (1 shorter events, 0.0 us)
Async XLA Ops:
  0.0 9.1 %collective-permute-start = (bf16[8,14336]{1,0:T(8,128)(2,1)}, bf16[8,14336]{1,0:T(8,128)(2,1)S(1)}, u32[]{:S(2)}, u32[]{:S(2)}) collective-permute-start(bf16[8,14336]{1,0:T(8,128)(2,1)} %refs_0_.1), channel_id=1, source_target_pairs={{0,4},{1,3},{2,0},{3,7},{4,8},{5,1},{6,2},{7,11},{8,12},{9,5},{10,... | collective-permute-start | bytes 688136 | tf_op jit(solution)/shard_map/ppermute | solution.py:155
  3.0 7.6 %collective-permute-start.1 = (bf16[8,14336]{1,0:T(8,128)(2,1)}, bf16[8,14336]{1,0:T(8,128)(2,1)S(1)}, u32[]{:S(2)}, u32[]{:S(2)}) collective-permute-start(bf16[8,14336]{1,0:T(8,128)(2,1)} %refs_0_.1), channel_id=1, source_target_pairs={{0,2},{1,5},{2,6},{3,1},{4,0},{5,9},{6,10},{7,3},{8,4},{9,13},{10,... | collective-permute-start | bytes 688136 | tf_op jit(solution)/shard_map/ppermute | solution.py:155
  9.1 8.3 %collective-permute-start.2 = (bf16[8,14336]{1,0:T(8,128)(2,1)S(1)}, bf16[8,14336]{1,0:T(8,128)(2,1)S(1)}, u32[]{:S(2)}, u32[]{:S(2)}) collective-permute-start(bf16[8,14336]{1,0:T(8,128)(2,1)S(1)} %collective-permute-done.refs_1_), channel_id=1, source_target_pairs={{0,4},{1,3},{2,0},{3,7},{4,8},{5,1},{6,2},{7,11},{8,12},{9,5},{10,... | collective-permute-start | bytes 688136 | tf_op jit(solution)/shard_map/ppermute | solution.py:155
  10.6 8.1 %collective-permute-start.3 = (bf16[8,14336]{1,0:T(8,128)(2,1)S(1)}, bf16[8,14336]{1,0:T(8,128)(2,1)S(1)}, u32[]{:S(2)}, u32[]{:S(2)}) collective-permute-start(bf16[8,14336]{1,0:T(8,128)(2,1)S(1)} %collective-permute-done.1.refs_2_), channel_id=1, source_target_pairs={{0,2},{1,5},{2,6},{3,1},{4,0},{5,9},{6,10},{7,3},{8,4},{9,13},{10,... | collective-permute-start | bytes 688136 | tf_op jit(solution)/shard_map/ppermute | solution.py:155
  17.3 8.1 %collective-permute-start.4 = (bf16[8,14336]{1,0:T(8,128)(2,1)S(1)}, bf16[8,14336]{1,0:T(8,128)(2,1)S(1)}, u32[]{:S(2)}, u32[]{:S(2)}) collective-permute-start(bf16[8,14336]{1,0:T(8,128)(2,1)S(1)} %collective-permute-done.2.refs_3_), channel_id=1, source_target_pairs={{0,4},{1,3},{2,0},{3,7},{4,8},{5,1},{6,2},{7,11},{8,12},{9,5},{10,... | collective-permute-start | bytes 688136 | tf_op jit(solution)/shard_map/ppermute | solution.py:155
  17.3 8.1 %collective-permute-start.7 = (bf16[8,14336]{1,0:T(8,128)(2,1)}, bf16[8,14336]{1,0:T(8,128)(2,1)S(1)}, u32[]{:S(2)}, u32[]{:S(2)}) collective-permute-start(bf16[8,14336]{1,0:T(8,128)(2,1)} %refs_0_.1), channel_id=1, source_target_pairs={{0,1},{1,0},{2,3},{3,2},{4,5},{5,4},{6,7},{7,6},{8,9},{9,8},{10,11... | collective-permute-start | bytes 688136 | tf_op jit(solution)/shard_map/ppermute | solution.py:155
  17.4 8.2 %collective-permute-start.9 = (bf16[8,14336]{1,0:T(8,128)(2,1)S(1)}, bf16[8,14336]{1,0:T(8,128)(2,1)S(1)}, u32[]{:S(2)}, u32[]{:S(2)}) collective-permute-start(bf16[8,14336]{1,0:T(8,128)(2,1)S(1)} %collective-permute-done.1.refs_2_), channel_id=1, source_target_pairs={{0,1},{1,0},{2,3},{3,2},{4,5},{5,4},{6,7},{7,6},{8,9},{9,8},{10,11... | collective-permute-start | bytes 688136 | tf_op jit(solution)/shard_map/ppermute | solution.py:155
  17.9 8.2 %collective-permute-start.8 = (bf16[8,14336]{1,0:T(8,128)(2,1)S(1)}, bf16[8,14336]{1,0:T(8,128)(2,1)S(1)}, u32[]{:S(2)}, u32[]{:S(2)}) collective-permute-start(bf16[8,14336]{1,0:T(8,128)(2,1)S(1)} %collective-permute-done.refs_1_), channel_id=1, source_target_pairs={{0,1},{1,0},{2,3},{3,2},{4,5},{5,4},{6,7},{7,6},{8,9},{9,8},{10,11... | collective-permute-start | bytes 688136 | tf_op jit(solution)/shard_map/ppermute | solution.py:155
  18.7 8.4 %collective-permute-start.5 = (bf16[8,14336]{1,0:T(8,128)(2,1)S(1)}, bf16[8,14336]{1,0:T(8,128)(2,1)S(1)}, u32[]{:S(2)}, u32[]{:S(2)}) collective-permute-start(bf16[8,14336]{1,0:T(8,128)(2,1)S(1)} %collective-permute-done.3.refs_4_), channel_id=1, source_target_pairs={{0,2},{1,5},{2,6},{3,1},{4,0},{5,9},{6,10},{7,3},{8,4},{9,13},{10,... | collective-permute-start | bytes 688136 | tf_op jit(solution)/shard_map/ppermute | solution.py:155
  25.5 6.0 %collective-permute-start.6 = (bf16[8,14336]{1,0:T(8,128)(2,1)S(1)}, bf16[8,14336]{1,0:T(8,128)(2,1)S(1)}, u32[]{:S(2)}, u32[]{:S(2)}) collective-permute-start(bf16[8,14336]{1,0:T(8,128)(2,1)S(1)} %collective-permute-done.4.refs_5_), channel_id=1, source_target_pairs={{0,4},{1,3},{2,0},{3,7},{4,8},{5,1},{6,2},{7,11},{8,12},{9,5},{10,... | collective-permute-start | bytes 688136 | tf_op jit(solution)/shard_map/ppermute | solution.py:155
  25.5 10.0 %collective-permute-start.11 = (bf16[8,14336]{1,0:T(8,128)(2,1)S(1)}, bf16[8,14336]{1,0:T(8,128)(2,1)S(1)}, u32[]{:S(2)}, u32[]{:S(2)}) collective-permute-start(bf16[8,14336]{1,0:T(8,128)(2,1)S(1)} %collective-permute-done.3.refs_4_), channel_id=1, source_target_pairs={{0,1},{1,0},{2,3},{3,2},{4,5},{5,4},{6,7},{7,6},{8,9},{9,8},{10,11... | collective-permute-start | bytes 688136 | tf_op jit(solution)/shard_map/ppermute | solution.py:155
  25.5 10.0 %collective-permute-start.10 = (bf16[8,14336]{1,0:T(8,128)(2,1)S(1)}, bf16[8,14336]{1,0:T(8,128)(2,1)S(1)}, u32[]{:S(2)}, u32[]{:S(2)}) collective-permute-start(bf16[8,14336]{1,0:T(8,128)(2,1)S(1)} %collective-permute-done.2.refs_3_), channel_id=1, source_target_pairs={{0,1},{1,0},{2,3},{3,2},{4,5},{5,4},{6,7},{7,6},{8,9},{9,8},{10,11... | collective-permute-start | bytes 688136 | tf_op jit(solution)/shard_map/ppermute | solution.py:155
  26.0 9.6 %collective-permute-start.12 = (bf16[8,14336]{1,0:T(8,128)(2,1)S(1)}, bf16[8,14336]{1,0:T(8,128)(2,1)S(1)}, u32[]{:S(2)}, u32[]{:S(2)}) collective-permute-start(bf16[8,14336]{1,0:T(8,128)(2,1)S(1)} %collective-permute-done.4.refs_5_), channel_id=1, source_target_pairs={{0,1},{1,0},{2,3},{3,2},{4,5},{5,4},{6,7},{7,6},{8,9},{9,8},{10,11... | collective-permute-start | bytes 688136 | tf_op jit(solution)/shard_map/ppermute | solution.py:155
  27.1 8.5 %collective-permute-start.13 = (bf16[8,14336]{1,0:T(8,128)(2,1)S(1)}, bf16[8,14336]{1,0:T(8,128)(2,1)S(1)}, u32[]{:S(2)}, u32[]{:S(2)}) collective-permute-start(bf16[8,14336]{1,0:T(8,128)(2,1)S(1)} %collective-permute-done.5.refs_6_), channel_id=1, source_target_pairs={{0,1},{1,0},{2,3},{3,2},{4,5},{5,4},{6,7},{7,6},{8,9},{9,8},{10,11... | collective-permute-start | bytes 688136 | tf_op jit(solution)/shard_map/ppermute | solution.py:155
  31.5 4.1 %collective-permute-start.14 = (bf16[8,14336]{1,0:T(8,128)(2,1)S(1)}, bf16[8,14336]{1,0:T(8,128)(2,1)S(1)}, u32[]{:S(2)}, u32[]{:S(2)}) collective-permute-start(bf16[8,14336]{1,0:T(8,128)(2,1)S(1)} %collective-permute-done.6.refs_7_), channel_id=1, source_target_pairs={{0,1},{1,0},{2,3},{3,2},{4,5},{5,4},{6,7},{7,6},{8,9},{9,8},{10,11... | collective-permute-start | bytes 688136 | tf_op jit(solution)/shard_map/ppermute | solution.py:155
  35.6 0.9 %copy-start = (bf16[8,14336]{1,0:T(8,128)(2,1)S(1)}, bf16[8,14336]{1,0:T(8,128)(2,1)}, u32[]{:S(2)}) copy-start(bf16[8,14336]{1,0:T(8,128)(2,1)} %refs_0_.1) | copy-start | bytes 688132
  36.5 0.7 %copy-start.1 = (s32[136]{0:T(256)S(1)}, s32[136]{0:T(256)}, u32[]{:S(2)}) copy-start(s32[136]{0:T(256)} %owner_ref.1) | copy-start | bytes 1636

commit v2 on v1

--- a/solution.py
+++ b/solution.py
@@ -2,7 +2,6 @@
 
 import jax
 import jax.numpy as jnp
-import numpy as np
 from jax import lax
 from jax.experimental import pallas as pl
 from jax.experimental.pallas import tpu as pltpu
@@ -106,12 +105,13 @@
     lax.fori_loop(count, slots, end_clear, 0)
 
 
-def gathered_form(tokens, slab_lengths, tile_owner, devices, device, slots, scale):
+def gathered_form(tokens, slab_lengths, tile_owner, devices, device, slots):
     slab, units = tokens.shape
     rows = slab * devices
     width = units // devices
     x = lax.all_gather(tokens, "col", axis=0, tiled=True)
     x = x.reshape(rows, devices, width).transpose(1, 0, 2)
+    scale = 1.0 / jnp.sum(slab_lengths).astype(jnp.float32)
     valid = jnp.arange(slab, dtype=jnp.int32)[None, :] < slab_lengths[:, None]
     mask = jnp.broadcast_to(valid.reshape(rows, 1), (rows, width)).astype(jnp.bfloat16)
     return pl.pallas_call(
@@ -146,45 +146,46 @@
     return onward, backward
 
 
-def ring_gather(tokens, devices):
+def ring_gather(parts, devices):
     onward, backward = ring_plan(devices)
     sibling = [device ^ 1 for device in range(devices)]
-    here = list(range(devices))
-
-    def send(value, target):
-        return lax.ppermute(value, "col", list(enumerate(target)))
-
-    def received(source, target):
-        return [source[target.index(device)] for device in range(devices)]
+
+    def send(values, target):
+        return [lax.ppermute(value, "col", list(enumerate(target))) for value in values]
 
     chips = devices // 2
-    ahead, back = tokens, tokens
-    ahead_from, back_from = here, here
-    slabs, sources = [tokens], [here]
+    ahead, back = parts, parts
+    slabs = [parts]
     for step in range(1, chips // 2 + 1):
         ahead = send(ahead, onward)
-        ahead_from = received(ahead_from, onward)
         slabs.append(ahead)
-        sources.append(ahead_from)
         if 2 * step < chips:
             back = send(back, backward)
-            back_from = received(back_from, backward)
             slabs.append(back)
-            sources.append(back_from)
-    for value, source in list(zip(slabs, sources)):
-        slabs.append(send(value, sibling))
-        sources.append(received(source, sibling))
-    return slabs, np.array(sources, np.int32).T
-
-
-def ring_kernel(devices, slots, count_in, owner_ref, device_ref, kept_ref, scale_ref, *refs):
-    slabs = refs[:count_in]
-    out_ref, pair, tiles, zeros, out_sems, zero_sems = refs[count_in:]
+    slabs += [send(values, sibling) for values in slabs]
+    return [list(part) for part in zip(*slabs)]
+
+
+def slab_origin(devices, device, number):
+    chips = devices // 2
+    number, flip = number % chips, number // chips
+    hops = (number + 1) // 2 if number % 2 else -(number // 2)
+    chip, core = device // 2, device % 2
+    core = 1 - core if flip else core
+    place = jnp.where(chip % 2 == 0, chip // 2, chips - 1 - chip // 2)
+    place = (place - (1 - 2 * core) * hops + chips) % chips
+    chip = jnp.where(2 * place < chips, 2 * place, 2 * (chips - 1 - place) + 1)
+    return 2 * chip + core
+
+
+def ring_kernel(devices, slots, cuts, device_ref, table_ref, *refs):
+    slabs = [refs[at * devices:(at + 1) * devices] for at in range(len(cuts))]
+    out_ref, pair, tiles, zeros, out_sems, zero_sems = refs[len(cuts) * devices:]
     device = device_ref[0]
-    slab, width = slabs[0].shape[0], pair.shape[2]
+    slab, width = slabs[0][0].shape[0], pair.shape[2]
 
     def owned(partner):
-        return owner_ref[tile_number(devices, device, partner)] == device
+        return table_ref[devices + tile_number(devices, device, partner)] == device
 
     def put(buffer, slot):
         return pltpu.make_async_copy(tiles.at[buffer], out_ref.at[slot], out_sems.at[buffer])
@@ -192,16 +193,19 @@
     def clear(slot):
         return pltpu.make_async_copy(zeros, out_ref.at[slot], zero_sems.at[slot])
 
-    def column_block(partner, masked):
-        columns = pl.ds(pl.multiple_of(partner * width, 128), width)
-        parts = []
-        for at, ref in enumerate(slabs):
-            part = ref[:, columns].astype(jnp.float32)
-            if masked:
-                row = lax.broadcasted_iota(jnp.int32, (slab, width), 0)
-                part = jnp.where(row < kept_ref[at], part, 0.0)
-            parts.append(part)
-        return jnp.concatenate(parts, axis=0).astype(jnp.bfloat16)
+    def load_block(partner, masked):
+        for (start, size), refs_of_part in zip(cuts, slabs):
+            columns = pl.ds(pl.multiple_of(partner * size, 128), size)
+            parts = []
+            for at, ref in enumerate(refs_of_part):
+                part = ref[:, columns].astype(jnp.float32)
+                if masked:
+                    row = lax.broadcasted_iota(jnp.int32, (slab, size), 0)
+                    kept = table_ref[slab_origin(devices, device, at)]
+                    part = jnp.where(row < kept, part, 0.0)
+                parts.append(part)
+            block = jnp.concatenate(parts, axis=0).astype(jnp.bfloat16)
+            pair[0 if masked else 1, :, start:start + size] = block
 
     count = lax.fori_loop(
         0, devices, lambda partner, total: total + owned(partner).astype(jnp.int32), jnp.int32(0)
@@ -217,8 +221,9 @@
 
     lax.fori_loop(count, slots, start_clear, 0)
 
-    pair[0] = column_block(device, True)
-    scale = scale_ref[0]
+    load_block(device, True)
+    valid_count = lax.fori_loop(0, devices, lambda at, total: total + table_ref[at], jnp.int32(0))
+    scale = 1.0 / jnp.full((128, width), valid_count.astype(jnp.float32))
 
     def visit(partner, slot):
         mine = owned(partner)
@@ -226,7 +231,7 @@
         @pl.when(mine)
         def _():
             buffer = lax.rem(slot, BUFFERS)
-            pair[1] = column_block(partner, False)
+            load_block(partner, False)
 
             @pl.when(slot >= BUFFERS)
             def _():
@@ -234,12 +239,15 @@
 
             left = (partner <= device).astype(jnp.int32)
             for row in range(0, width, 128):
+                strip = pl.ds(row, 128)
                 product = lax.dot_general(
                     pair[left, :, row:row + 128], pair[1 - left], (((0,), (0,)), ((), ())),
                     preferred_element_type=jnp.float32,
                 )
-                tiles[buffer, row:row + 128, :] = product * scale
-            put(buffer, slot).start()
+                tiles[buffer, strip, :] = product * scale
+                pltpu.make_async_copy(
+                    tiles.at[buffer, strip], out_ref.at[slot, strip], out_sems.at[buffer]
+                ).start()
 
         return slot + mine.astype(jnp.int32)
 
@@ -258,16 +266,20 @@
     lax.fori_loop(count, slots, end_clear, 0)
 
 
-def ring_form(tokens, slab_lengths, tile_owner, devices, device, slots, scale):
+def ring_form(tokens, slab_lengths, tile_owner, devices, device, slots):
     slab, units = tokens.shape
     width = units // devices
-    slabs, sources = ring_gather(tokens, devices)
-    kept = slab_lengths[jnp.asarray(sources)[device]]
+    first = -(-width // 256) * 128
+    cuts = [(0, first), (first, width - first)] if first < width else [(0, width)]
+    by_block = tokens.reshape(slab, devices, width)
+    parts = [by_block[:, :, start:start + size].reshape(slab, devices * size) for start, size in cuts]
+    slabs = ring_gather(parts, devices)
+    table = jnp.concatenate([slab_lengths, tile_owner])
     return pl.pallas_call(
-        functools.partial(ring_kernel, devices, slots, len(slabs)),
+        functools.partial(ring_kernel, devices, slots, cuts),
         out_shape=jax.ShapeDtypeStruct((slots, width, width), jnp.float32),
-        in_specs=[pl.BlockSpec(memory_space=pltpu.SMEM)] * 4
-        + [pl.BlockSpec(memory_space=pltpu.VMEM)] * len(slabs),
+        in_specs=[pl.BlockSpec(memory_space=pltpu.SMEM)] * 2
+        + [pl.BlockSpec(memory_space=pltpu.VMEM)] * (len(cuts) * devices),
         out_specs=pl.BlockSpec(memory_space=pl.ANY),
         scratch_shapes=[
             pltpu.VMEM((2, slab * devices, width), jnp.bfloat16),
@@ -282,7 +294,7 @@
             bytes_accessed=4 * slots * width * width,
             transcendentals=0,
         ),
-    )(tile_owner, device.reshape(1), kept, scale.reshape(1), *slabs)
+    )(device.reshape(1), table, *sum(slabs, []))
 
 
 def per_device(tokens, slab_lengths, tile_owner):
@@ -290,9 +302,8 @@
     device = lax.axis_index("col").astype(jnp.int32)
     slots = devices // 2 + devices // 8 + 1
     width = tokens.shape[1] // devices
-    scale = 1.0 / jnp.sum(slab_lengths).astype(jnp.float32)
     form = ring_form if devices <= RING_LIMIT and width % 128 == 0 else gathered_form
-    return form(tokens, slab_lengths, tile_owner, devices, device, slots, scale)
+    return form(tokens, slab_lengths, tile_owner, devices, device, slots)
 
 
 def solution(mesh):

time: 50.5 us -> 48.7 us (0.964)
  starting transfers between devices: 7.74 us -> 18.8 us
  waiting for transfers between devices: 23.8 us -> 14.3 us
  other arithmetic: 2 us -> 0.76 us
  local copies, waits for them, and re-layouts: 2.93 us -> 1.82 us
  between operations: 0.78 us -> 0.06 us
    ppermute x15 -> x30, starting transfers between devices: 7.74 us -> 18.8 us  [send(): lax.ppermute(value, 'col', list(enumerate(target)))]
    ppermute x15 -> x30, waiting for transfers between devices: 23.8 us -> 14.3 us  [send(): lax.ppermute(value, 'col', list(enumerate(target)))]
    slice x0 -> x2, local copies, waits for them, and re-layouts: none -> 1.82 us  [ring_form(): by_block[:, :, start:start + size].reshape(slab, devices * size)]
    unnamed x4 -> x0, local copies, waits for them, and re-layouts: 1.61 us -> none
    gather x1 -> x0, local copies, waits for them, and re-layouts: 1.31 us -> none  [ring_form(): kept = slab_lengths[jnp.asarray(sources)[device]]]
    reduce_sum x1 -> x0, other arithmetic: 1.29 us -> none  [per_device(): scale = 1.0 / jnp.sum(slab_lengths).astype(jnp.float32)]
    concatenate x0 -> x1, other arithmetic: none -> 0.76 us  [ring_form(): table = jnp.concatenate([slab_lengths, tile_owner])]
    select_n x1 -> x0, other arithmetic: 0.7 us -> none  [ring_form(): kept = slab_lengths[jnp.asarray(sources)[device]]]
  transfers between devices with their start and end apart: 15 -> 30, of which waited for: 6 -> 9; matrix products, arithmetic and copies ran while one was open for 7% -> 3% of each run, Pallas kernels for 0% -> 0%
where the time goes in v2:
time: 48.7 us; the launch traced here: 48.6 us
  starting transfers between devices  18.8 us (39%)
  waiting for transfers between devices  14.3 us (29%)
  Pallas kernels  12.9 us (26%)
  local copies, waits for them, and re-layouts  1.82 us (4%)
  other arithmetic  0.76 us (2%)
    ppermute x30, starting transfers between devices, send(): lax.ppermute(value, 'col', list(enumerate(target)))  18.8 us
    ppermute x30, waiting for transfers between devices, send(): lax.ppermute(value, 'col', list(enumerate(target)))  14.3 us
    pallas_call x1, Pallas kernels, ring_form(): pl.pallas_call(functools.partial(ring_kernel, devices, slots, cuts), out_...  12.9 us
    slice x2, local copies, waits for them, and re-layouts, ring_form(): by_block[:, :, start:start + size].reshape(slab, devices * size)  1.82 us
  transfers between devices with their start and end apart: 30, of which 9 were waited for; matrix products, arithmetic and copies ran while one was open for 3% of the time, Pallas kernels for 0%

profile of v2, /device:TPU:0, one launch (start us, length us, event | category | flops | bytes accessed | tf_op | source)
XLA Modules:
  0.0 48.6 jit_solution(7338077098657570331)
XLA Ops:
  0.0 0.9 %slice.9 = bf16[8,16,384]{2,0,1:T(8,128)(2,1)S(1)} slice(bf16[8,16,896]{2,0,1:T(8,128)(2,1)} %bitcast.12), slice={[0:8], [0:16], [512:896]} | slice | bytes 196608 | tf_op jit(solution)/shard_map/slice | solution.py:275
  0.9 0.5 %collective-permute-start.22 = (bf16[8,6144]{1,0:T(8,128)(2,1)S(1)}, bf16[8,6144]{1,0:T(8,128)(2,1)S(1)}, u32[]{:S(2)}, u32[]{:S(2)}) collective-permute-start(bf16[8,6144]{1,0:T(8,128)(2,1)S(1)} %bitcast.8), channel_id=1, source_target_pairs={{0,1},{1,0},{2,3},{3,2},{4,5},{5,4},{6,7},{7,6},{8,9},{9,8},{10,11... | collective-permute-start | bytes 294920 | tf_op jit(solution)/shard_map/ppermute | solution.py:154
  1.4 0.9 %slice.8 = bf16[8,16,512]{2,0,1:T(8,128)(2,1)S(1)} slice(bf16[8,16,896]{2,0,1:T(8,128)(2,1)} %bitcast.13), slice={[0:8], [0:16], [0:512]} | slice | bytes 262144 | tf_op jit(solution)/shard_map/slice | solution.py:275
  2.3 0.1 collective-permute-start.7
  2.5 2.9 %collective-permute-start.16 = (bf16[8,6144]{1,0:T(8,128)(2,1)S(1)}, bf16[8,6144]{1,0:T(8,128)(2,1)S(1)}, u32[]{:S(2)}, u32[]{:S(2)}) collective-permute-start(bf16[8,6144]{1,0:T(8,128)(2,1)S(1)} %bitcast.9), channel_id=1, source_target_pairs={{0,2},{1,5},{2,6},{3,1},{4,0},{5,9},{6,10},{7,3},{8,4},{9,13},{10,... | collective-permute-start | bytes 294920 | tf_op jit(solution)/shard_map/ppermute | solution.py:154
  5.4 0.1 collective-permute-start.15
  5.5 2.0 %collective-permute-start = (bf16[8,8192]{1,0:T(8,128)(2,1)S(1)}, bf16[8,8192]{1,0:T(8,128)(2,1)S(1)}, u32[]{:S(2)}, u32[]{:S(2)}) collective-permute-start(bf16[8,8192]{1,0:T(8,128)(2,1)S(1)} %bitcast.5), channel_id=1, source_target_pairs={{0,4},{1,3},{2,0},{3,7},{4,8},{5,1},{6,2},{7,11},{8,12},{9,5},{10,... | collective-permute-start | bytes 393224 | tf_op jit(solution)/shard_map/ppermute | solution.py:154
  7.5 0.0 collective-permute-start.1
  7.5 1.0 %collective-permute-done.16.refs_18_ = bf16[8,6144]{1,0:T(8,128)(2,1)S(1)} collective-permute-done((bf16[8,6144]{1,0:T(8,128)(2,1)S(1)}, bf16[8,6144]{1,0:T(8,128)(2,1)S(1)}, u32[]{:S(2)}, u32[]{:S(2)}) %collective-permute-start.16) | collective-permute-done | bytes 98336 | tf_op jit(solution)/shard_map/ppermute | solution.py:154
  8.5 2.3 %collective-permute-done.15.refs_17_ = bf16[8,6144]{1,0:T(8,128)(2,1)S(1)} collective-permute-done((bf16[8,6144]{1,0:T(8,128)(2,1)S(1)}, bf16[8,6144]{1,0:T(8,128)(2,1)S(1)}, u32[]{:S(2)}, u32[]{:S(2)}) %collective-permute-start.15) | collective-permute-done | bytes 98336 | tf_op jit(solution)/shard_map/ppermute | solution.py:154
  10.8 1.6 %collective-permute-start.18 = (bf16[8,6144]{1,0:T(8,128)(2,1)S(1)}, bf16[8,6144]{1,0:T(8,128)(2,1)S(1)}, u32[]{:S(2)}, u32[]{:S(2)}) collective-permute-start(bf16[8,6144]{1,0:T(8,128)(2,1)S(1)} %collective-permute-done.16.refs_18_), channel_id=1, source_target_pairs={{0,2},{1,5},{2,6},{3,1},{4,0},{5,9},{6,10},{7,3},{8,4},{9,13},{10,... | collective-permute-start | bytes 294920 | tf_op jit(solution)/shard_map/ppermute | solution.py:154
  12.4 0.0 collective-permute-start.23
  12.4 0.9 %collective-permute-done.refs_1_ = bf16[8,8192]{1,0:T(8,128)(2,1)S(1)} collective-permute-done((bf16[8,8192]{1,0:T(8,128)(2,1)S(1)}, bf16[8,8192]{1,0:T(8,128)(2,1)S(1)}, u32[]{:S(2)}, u32[]{:S(2)}) %collective-permute-start) | collective-permute-done | bytes 131104 | tf_op jit(solution)/shard_map/ppermute | solution.py:154
  13.2 1.7 %collective-permute-start.17 = (bf16[8,6144]{1,0:T(8,128)(2,1)S(1)}, bf16[8,6144]{1,0:T(8,128)(2,1)S(1)}, u32[]{:S(2)}, u32[]{:S(2)}) collective-permute-start(bf16[8,6144]{1,0:T(8,128)(2,1)S(1)} %collective-permute-done.15.refs_17_), channel_id=1, source_target_pairs={{0,4},{1,3},{2,0},{3,7},{4,8},{5,1},{6,2},{7,11},{8,12},{9,5},{10,... | collective-permute-start | bytes 294920 | tf_op jit(solution)/shard_map/ppermute | solution.py:154
  14.9 0.5 %collective-permute-start.9 = (bf16[8,8192]{1,0:T(8,128)(2,1)S(1)}, bf16[8,8192]{1,0:T(8,128)(2,1)S(1)}, u32[]{:S(2)}, u32[]{:S(2)}) collective-permute-start(bf16[8,8192]{1,0:T(8,128)(2,1)S(1)} %collective-permute-done.1.refs_2_), channel_id=1, source_target_pairs={{0,1},{1,0},{2,3},{3,2},{4,5},{5,4},{6,7},{7,6},{8,9},{9,8},{10,11... | collective-permute-start | bytes 393224 | tf_op jit(solution)/shard_map/ppermute | solution.py:154
  15.5 0.0 collective-permute-done.18.refs_20_
  15.5 1.5 %collective-permute-start.3 = (bf16[8,8192]{1,0:T(8,128)(2,1)S(1)}, bf16[8,8192]{1,0:T(8,128)(2,1)S(1)}, u32[]{:S(2)}, u32[]{:S(2)}) collective-permute-start(bf16[8,8192]{1,0:T(8,128)(2,1)S(1)} %collective-permute-done.1.refs_2_), channel_id=1, source_target_pairs={{0,2},{1,5},{2,6},{3,1},{4,0},{5,9},{6,10},{7,3},{8,4},{9,13},{10,... | collective-permute-start | bytes 393224 | tf_op jit(solution)/shard_map/ppermute | solution.py:154
  17.0 0.0 collective-permute-done.23.refs_25_
  17.0 3.4 %collective-permute-done.17.refs_19_ = bf16[8,6144]{1,0:T(8,128)(2,1)S(1)} collective-permute-done((bf16[8,6144]{1,0:T(8,128)(2,1)S(1)}, bf16[8,6144]{1,0:T(8,128)(2,1)S(1)}, u32[]{:S(2)}, u32[]{:S(2)}) %collective-permute-start.17) | collective-permute-done | bytes 98336 | tf_op jit(solution)/shard_map/ppermute | solution.py:154
  20.3 0.0 collective-permute-start.26
  20.3 0.0 collective-permute-done.2.refs_3_
  20.3 0.0 collective-permute-start.4
  20.4 0.0 collective-permute-done.9.refs_10_
  20.4 2.0 %collective-permute-start.20 = (bf16[8,6144]{1,0:T(8,128)(2,1)S(1)}, bf16[8,6144]{1,0:T(8,128)(2,1)S(1)}, u32[]{:S(2)}, u32[]{:S(2)}) collective-permute-start(bf16[8,6144]{1,0:T(8,128)(2,1)S(1)} %collective-permute-done.18.refs_20_), channel_id=1, source_target_pairs={{0,2},{1,5},{2,6},{3,1},{4,0},{5,9},{6,10},{7,3},{8,4},{9,13},{10,... | collective-permute-start | bytes 294920 | tf_op jit(solution)/shard_map/ppermute | solution.py:154
  22.4 0.0 collective-permute-start.25
  22.4 0.5 %collective-permute-start.11 = (bf16[8,8192]{1,0:T(8,128)(2,1)S(1)}, bf16[8,8192]{1,0:T(8,128)(2,1)S(1)}, u32[]{:S(2)}, u32[]{:S(2)}) collective-permute-start(bf16[8,8192]{1,0:T(8,128)(2,1)S(1)} %collective-permute-done.3.refs_4_), channel_id=1, source_target_pairs={{0,1},{1,0},{2,3},{3,2},{4,5},{5,4},{6,7},{7,6},{8,9},{9,8},{10,11... | collective-permute-start | bytes 393224 | tf_op jit(solution)/shard_map/ppermute | solution.py:154
  22.9 0.1 collective-permute-start.19
  23.0 3.1 %collective-permute-done.20.refs_22_ = bf16[8,6144]{1,0:T(8,128)(2,1)S(1)} collective-permute-done((bf16[8,6144]{1,0:T(8,128)(2,1)S(1)}, bf16[8,6144]{1,0:T(8,128)(2,1)S(1)}, u32[]{:S(2)}, u32[]{:S(2)}) %collective-permute-start.20) | collective-permute-done | bytes 98336 | tf_op jit(solution)/shard_map/ppermute | solution.py:154
  26.0 1.9 %collective-permute-start.5 = (bf16[8,8192]{1,0:T(8,128)(2,1)S(1)}, bf16[8,8192]{1,0:T(8,128)(2,1)S(1)}, u32[]{:S(2)}, u32[]{:S(2)}) collective-permute-start(bf16[8,8192]{1,0:T(8,128)(2,1)S(1)} %collective-permute-done.3.refs_4_), channel_id=1, source_target_pairs={{0,2},{1,5},{2,6},{3,1},{4,0},{5,9},{6,10},{7,3},{8,4},{9,13},{10,... | collective-permute-start | bytes 393224 | tf_op jit(solution)/shard_map/ppermute | solution.py:154
  27.9 0.0 collective-permute-done.25.refs_27_
  27.9 0.0 collective-permute-start.10
  27.9 0.0 collective-permute-done.4.refs_5_
  27.9 0.2 collective-permute-start.6
  28.1 1.6 %collective-permute-start.28 = (bf16[8,6144]{1,0:T(8,128)(2,1)S(1)}, bf16[8,6144]{1,0:T(8,128)(2,1)S(1)}, u32[]{:S(2)}, u32[]{:S(2)}) collective-permute-start(bf16[8,6144]{1,0:T(8,128)(2,1)S(1)} %collective-permute-done.20.refs_22_), channel_id=1, source_target_pairs={{0,1},{1,0},{2,3},{3,2},{4,5},{5,4},{6,7},{7,6},{8,9},{9,8},{10,11... | collective-permute-start | bytes 294920 | tf_op jit(solution)/shard_map/ppermute | solution.py:154
  29.7 0.5 collective-permute-start.21
  30.2 0.8 %collective-permute-done.5.refs_6_ = bf16[8,8192]{1,0:T(8,128)(2,1)S(1)} collective-permute-done((bf16[8,8192]{1,0:T(8,128)(2,1)S(1)}, bf16[8,8192]{1,0:T(8,128)(2,1)S(1)}, u32[]{:S(2)}, u32[]{:S(2)}) %collective-permute-start.5) | collective-permute-done | bytes 131104 | tf_op jit(solution)/shard_map/ppermute | solution.py:154
  31.0 0.1 collective-permute-start.12
  31.1 0.4 collective-permute-start.13
  31.5 1.5 %collective-permute-done.6.refs_7_ = bf16[8,8192]{1,0:T(8,128)(2,1)S(1)} collective-permute-done((bf16[8,8192]{1,0:T(8,128)(2,1)S(1)}, bf16[8,8192]{1,0:T(8,128)(2,1)S(1)}, u32[]{:S(2)}, u32[]{:S(2)}) %collective-permute-start.6) | collective-permute-done | bytes 131104 | tf_op jit(solution)/shard_map/ppermute | solution.py:154
  33.0 0.0 collective-permute-start.14
  33.0 0.5 %collective-permute-start.27 = (bf16[8,6144]{1,0:T(8,128)(2,1)S(1)}, bf16[8,6144]{1,0:T(8,128)(2,1)S(1)}, u32[]{:S(2)}, u32[]{:S(2)}) collective-permute-start(bf16[8,6144]{1,0:T(8,128)(2,1)S(1)} %collective-permute-done.19.refs_21_), channel_id=1, source_target_pairs={{0,1},{1,0},{2,3},{3,2},{4,5},{5,4},{6,7},{7,6},{8,9},{9,8},{10,11... | collective-permute-start | bytes 294920 | tf_op jit(solution)/shard_map/ppermute | solution.py:154
  33.5 0.9 %collective-permute-done.21.refs_23_ = bf16[8,6144]{1,0:T(8,128)(2,1)S(1)} collective-permute-done((bf16[8,6144]{1,0:T(8,128)(2,1)S(1)}, bf16[8,6144]{1,0:T(8,128)(2,1)S(1)}, u32[]{:S(2)}, u32[]{:S(2)}) %collective-permute-start.21) | collective-permute-done | bytes 98336 | tf_op jit(solution)/shard_map/ppermute | solution.py:154
  34.4 0.0 collective-permute-start.29
  34.4 0.8 %pad_add_fusion.table_ref = s32[152]{0:T(256)S(1)} fusion(s32[136]{0:T(256)} %param.5, s32[16]{0:T(128)} %param.4), kind=kLoop, calls=%fused_computation | loop fusion | flops 152 | bytes 1216 | tf_op jit(solution)/shard_map/concatenate | solution.py:277
  35.1 0.0 collective-permute-done.27.refs_29_
  35.1 0.5 %collective-permute-done.29.refs_31_ = bf16[8,6144]{1,0:T(8,128)(2,1)S(1)} collective-permute-done((bf16[8,6144]{1,0:T(8,128)(2,1)S(1)}, bf16[8,6144]{1,0:T(8,128)(2,1)S(1)}, u32[]{:S(2)}, u32[]{:S(2)}) %collective-permute-start.29) | collective-permute-done | bytes 98336 | tf_op jit(solution)/shard_map/ppermute | solution.py:154
  35.7 0.0 collective-permute-done.12.refs_13_
  35.7 12.9 %shard_map.37 = f32[11,896,896]{2,1,0:T(8,128)} custom-call(s32[1]{0:T(128)} %bitcast.device_ref, s32[152]{0:T(256)S(1)} %pad_add_fusion.table_ref, bf16[8,8192]{1,0:T(8,128)(2,1)S(1)} %bitcast.7, bf16[8,8192]{1,0:T(8,128)(2,1)S(1)} %collective-permute-done.refs_1_, bf16[8,8192]{1,0:T(8,128)(2,1)S(1)} %collective-permute-done.1.refs_2_, ...), custom_call_target="tpu_custom_call" | custom-call | flops 2260729856 | bytes 35323904 | tf_op jit(solution)/shard_map/pallas_call | solution.py:278
  (16 shorter events, 0.0 us)
Async XLA Ops:
  0.9 6.6 %collective-permute-start.22 = (bf16[8,6144]{1,0:T(8,128)(2,1)S(1)}, bf16[8,6144]{1,0:T(8,128)(2,1)S(1)}, u32[]{:S(2)}, u32[]{:S(2)}) collective-permute-start(bf16[8,6144]{1,0:T(8,128)(2,1)S(1)} %bitcast.8), channel_id=1, source_target_pairs={{0,1},{1,0},{2,3},{3,2},{4,5},{5,4},{6,7},{7,6},{8,9},{9,8},{10,11... | collective-permute-start | bytes 294920 | tf_op jit(solution)/shard_map/ppermute | solution.py:154
  2.3 10.0 %collective-permute-start.7 = (bf16[8,8192]{1,0:T(8,128)(2,1)S(1)}, bf16[8,8192]{1,0:T(8,128)(2,1)S(1)}, u32[]{:S(2)}, u32[]{:S(2)}) collective-permute-start(bf16[8,8192]{1,0:T(8,128)(2,1)S(1)} %bitcast.4), channel_id=1, source_target_pairs={{0,1},{1,0},{2,3},{3,2},{4,5},{5,4},{6,7},{7,6},{8,9},{9,8},{10,11... | collective-permute-start | bytes 393224 | tf_op jit(solution)/shard_map/ppermute | solution.py:154
  2.5 6.0 %collective-permute-start.16 = (bf16[8,6144]{1,0:T(8,128)(2,1)S(1)}, bf16[8,6144]{1,0:T(8,128)(2,1)S(1)}, u32[]{:S(2)}, u32[]{:S(2)}) collective-permute-start(bf16[8,6144]{1,0:T(8,128)(2,1)S(1)} %bitcast.9), channel_id=1, source_target_pairs={{0,2},{1,5},{2,6},{3,1},{4,0},{5,9},{6,10},{7,3},{8,4},{9,13},{10,... | collective-permute-start | bytes 294920 | tf_op jit(solution)/shard_map/ppermute | solution.py:154
  5.4 5.4 %collective-permute-start.15 = (bf16[8,6144]{1,0:T(8,128)(2,1)S(1)}, bf16[8,6144]{1,0:T(8,128)(2,1)S(1)}, u32[]{:S(2)}, u32[]{:S(2)}) collective-permute-start(bf16[8,6144]{1,0:T(8,128)(2,1)S(1)} %bitcast.10), channel_id=1, source_target_pairs={{0,4},{1,3},{2,0},{3,7},{4,8},{5,1},{6,2},{7,11},{8,12},{9,5},{10,... | collective-permute-start | bytes 294920 | tf_op jit(solution)/shard_map/ppermute | solution.py:154
  5.5 7.7 %collective-permute-start = (bf16[8,8192]{1,0:T(8,128)(2,1)S(1)}, bf16[8,8192]{1,0:T(8,128)(2,1)S(1)}, u32[]{:S(2)}, u32[]{:S(2)}) collective-permute-start(bf16[8,8192]{1,0:T(8,128)(2,1)S(1)} %bitcast.5), channel_id=1, source_target_pairs={{0,4},{1,3},{2,0},{3,7},{4,8},{5,1},{6,2},{7,11},{8,12},{9,5},{10,... | collective-permute-start | bytes 393224 | tf_op jit(solution)/shard_map/ppermute | solution.py:154
  7.5 5.7 %collective-permute-start.1 = (bf16[8,8192]{1,0:T(8,128)(2,1)S(1)}, bf16[8,8192]{1,0:T(8,128)(2,1)S(1)}, u32[]{:S(2)}, u32[]{:S(2)}) collective-permute-start(bf16[8,8192]{1,0:T(8,128)(2,1)S(1)} %bitcast.6), channel_id=1, source_target_pairs={{0,2},{1,5},{2,6},{3,1},{4,0},{5,9},{6,10},{7,3},{8,4},{9,13},{10,... | collective-permute-start | bytes 393224 | tf_op jit(solution)/shard_map/ppermute | solution.py:154
  8.5 6.4 %collective-permute-start.24 = (bf16[8,6144]{1,0:T(8,128)(2,1)S(1)}, bf16[8,6144]{1,0:T(8,128)(2,1)S(1)}, u32[]{:S(2)}, u32[]{:S(2)}) collective-permute-start(bf16[8,6144]{1,0:T(8,128)(2,1)S(1)} %collective-permute-done.16.refs_18_), channel_id=1, source_target_pairs={{0,1},{1,0},{2,3},{3,2},{4,5},{5,4},{6,7},{7,6},{8,9},{9,8},{10,11... | collective-permute-start | bytes 294920 | tf_op jit(solution)/shard_map/ppermute | solution.py:154
  10.8 4.7 %collective-permute-start.18 = (bf16[8,6144]{1,0:T(8,128)(2,1)S(1)}, bf16[8,6144]{1,0:T(8,128)(2,1)S(1)}, u32[]{:S(2)}, u32[]{:S(2)}) collective-permute-start(bf16[8,6144]{1,0:T(8,128)(2,1)S(1)} %collective-permute-done.16.refs_18_), channel_id=1, source_target_pairs={{0,2},{1,5},{2,6},{3,1},{4,0},{5,9},{6,10},{7,3},{8,4},{9,13},{10,... | collective-permute-start | bytes 294920 | tf_op jit(solution)/shard_map/ppermute | solution.py:154
  12.4 4.6 %collective-permute-start.23 = (bf16[8,6144]{1,0:T(8,128)(2,1)S(1)}, bf16[8,6144]{1,0:T(8,128)(2,1)S(1)}, u32[]{:S(2)}, u32[]{:S(2)}) collective-permute-start(bf16[8,6144]{1,0:T(8,128)(2,1)S(1)} %collective-permute-done.15.refs_17_), channel_id=1, source_target_pairs={{0,1},{1,0},{2,3},{3,2},{4,5},{5,4},{6,7},{7,6},{8,9},{9,8},{10,11... | collective-permute-start | bytes 294920 | tf_op jit(solution)/shard_map/ppermute | solution.py:154
  13.2 7.1 %collective-permute-start.2 = (bf16[8,8192]{1,0:T(8,128)(2,1)S(1)}, bf16[8,8192]{1,0:T(8,128)(2,1)S(1)}, u32[]{:S(2)}, u32[]{:S(2)}) collective-permute-start(bf16[8,8192]{1,0:T(8,128)(2,1)S(1)} %collective-permute-done.refs_1_), channel_id=1, source_target_pairs={{0,4},{1,3},{2,0},{3,7},{4,8},{5,1},{6,2},{7,11},{8,12},{9,5},{10,... | collective-permute-start | bytes 393224 | tf_op jit(solution)/shard_map/ppermute | solution.py:154
  13.2 7.1 %collective-permute-start.17 = (bf16[8,6144]{1,0:T(8,128)(2,1)S(1)}, bf16[8,6144]{1,0:T(8,128)(2,1)S(1)}, u32[]{:S(2)}, u32[]{:S(2)}) collective-permute-start(bf16[8,6144]{1,0:T(8,128)(2,1)S(1)} %collective-permute-done.15.refs_17_), channel_id=1, source_target_pairs={{0,4},{1,3},{2,0},{3,7},{4,8},{5,1},{6,2},{7,11},{8,12},{9,5},{10,... | collective-permute-start | bytes 294920 | tf_op jit(solution)/shard_map/ppermute | solution.py:154
  14.9 5.4 %collective-permute-start.9 = (bf16[8,8192]{1,0:T(8,128)(2,1)S(1)}, bf16[8,8192]{1,0:T(8,128)(2,1)S(1)}, u32[]{:S(2)}, u32[]{:S(2)}) collective-permute-start(bf16[8,8192]{1,0:T(8,128)(2,1)S(1)} %collective-permute-done.1.refs_2_), channel_id=1, source_target_pairs={{0,1},{1,0},{2,3},{3,2},{4,5},{5,4},{6,7},{7,6},{8,9},{9,8},{10,11... | collective-permute-start | bytes 393224 | tf_op jit(solution)/shard_map/ppermute | solution.py:154
  15.5 6.9 %collective-permute-start.3 = (bf16[8,8192]{1,0:T(8,128)(2,1)S(1)}, bf16[8,8192]{1,0:T(8,128)(2,1)S(1)}, u32[]{:S(2)}, u32[]{:S(2)}) collective-permute-start(bf16[8,8192]{1,0:T(8,128)(2,1)S(1)} %collective-permute-done.1.refs_2_), channel_id=1, source_target_pairs={{0,2},{1,5},{2,6},{3,1},{4,0},{5,9},{6,10},{7,3},{8,4},{9,13},{10,... | collective-permute-start | bytes 393224 | tf_op jit(solution)/shard_map/ppermute | solution.py:154
  17.0 5.4 %collective-permute-start.8 = (bf16[8,8192]{1,0:T(8,128)(2,1)S(1)}, bf16[8,8192]{1,0:T(8,128)(2,1)S(1)}, u32[]{:S(2)}, u32[]{:S(2)}) collective-permute-start(bf16[8,8192]{1,0:T(8,128)(2,1)S(1)} %collective-permute-done.refs_1_), channel_id=1, source_target_pairs={{0,1},{1,0},{2,3},{3,2},{4,5},{5,4},{6,7},{7,6},{8,9},{9,8},{10,11... | collective-permute-start | bytes 393224 | tf_op jit(solution)/shard_map/ppermute | solution.py:154
  20.3 2.6 %collective-permute-start.26 = (bf16[8,6144]{1,0:T(8,128)(2,1)S(1)}, bf16[8,6144]{1,0:T(8,128)(2,1)S(1)}, u32[]{:S(2)}, u32[]{:S(2)}) collective-permute-start(bf16[8,6144]{1,0:T(8,128)(2,1)S(1)} %collective-permute-done.18.refs_20_), channel_id=1, source_target_pairs={{0,1},{1,0},{2,3},{3,2},{4,5},{5,4},{6,7},{7,6},{8,9},{9,8},{10,11... | collective-permute-start | bytes 294920 | tf_op jit(solution)/shard_map/ppermute | solution.py:154
  20.3 7.6 %collective-permute-start.4 = (bf16[8,8192]{1,0:T(8,128)(2,1)S(1)}, bf16[8,8192]{1,0:T(8,128)(2,1)S(1)}, u32[]{:S(2)}, u32[]{:S(2)}) collective-permute-start(bf16[8,8192]{1,0:T(8,128)(2,1)S(1)} %collective-permute-done.2.refs_3_), channel_id=1, source_target_pairs={{0,4},{1,3},{2,0},{3,7},{4,8},{5,1},{6,2},{7,11},{8,12},{9,5},{10,... | collective-permute-start | bytes 393224 | tf_op jit(solution)/shard_map/ppermute | solution.py:154
  20.4 5.7 %collective-permute-start.20 = (bf16[8,6144]{1,0:T(8,128)(2,1)S(1)}, bf16[8,6144]{1,0:T(8,128)(2,1)S(1)}, u32[]{:S(2)}, u32[]{:S(2)}) collective-permute-start(bf16[8,6144]{1,0:T(8,128)(2,1)S(1)} %collective-permute-done.18.refs_20_), channel_id=1, source_target_pairs={{0,2},{1,5},{2,6},{3,1},{4,0},{5,9},{6,10},{7,3},{8,4},{9,13},{10,... | collective-permute-start | bytes 294920 | tf_op jit(solution)/shard_map/ppermute | solution.py:154
  22.4 5.6 %collective-permute-start.25 = (bf16[8,6144]{1,0:T(8,128)(2,1)S(1)}, bf16[8,6144]{1,0:T(8,128)(2,1)S(1)}, u32[]{:S(2)}, u32[]{:S(2)}) collective-permute-start(bf16[8,6144]{1,0:T(8,128)(2,1)S(1)} %collective-permute-done.17.refs_19_), channel_id=1, source_target_pairs={{0,1},{1,0},{2,3},{3,2},{4,5},{5,4},{6,7},{7,6},{8,9},{9,8},{10,11... | collective-permute-start | bytes 294920 | tf_op jit(solution)/shard_map/ppermute | solution.py:154
  22.4 7.3 %collective-permute-start.11 = (bf16[8,8192]{1,0:T(8,128)(2,1)S(1)}, bf16[8,8192]{1,0:T(8,128)(2,1)S(1)}, u32[]{:S(2)}, u32[]{:S(2)}) collective-permute-start(bf16[8,8192]{1,0:T(8,128)(2,1)S(1)} %collective-permute-done.3.refs_4_), channel_id=1, source_target_pairs={{0,1},{1,0},{2,3},{3,2},{4,5},{5,4},{6,7},{7,6},{8,9},{9,8},{10,11... | collective-permute-start | bytes 393224 | tf_op jit(solution)/shard_map/ppermute | solution.py:154
  22.9 5.2 %collective-permute-start.19 = (bf16[8,6144]{1,0:T(8,128)(2,1)S(1)}, bf16[8,6144]{1,0:T(8,128)(2,1)S(1)}, u32[]{:S(2)}, u32[]{:S(2)}) collective-permute-start(bf16[8,6144]{1,0:T(8,128)(2,1)S(1)} %collective-permute-done.17.refs_19_), channel_id=1, source_target_pairs={{0,4},{1,3},{2,0},{3,7},{4,8},{5,1},{6,2},{7,11},{8,12},{9,5},{10,... | collective-permute-start | bytes 294920 | tf_op jit(solution)/shard_map/ppermute | solution.py:154
  26.0 5.0 %collective-permute-start.5 = (bf16[8,8192]{1,0:T(8,128)(2,1)S(1)}, bf16[8,8192]{1,0:T(8,128)(2,1)S(1)}, u32[]{:S(2)}, u32[]{:S(2)}) collective-permute-start(bf16[8,8192]{1,0:T(8,128)(2,1)S(1)} %collective-permute-done.3.refs_4_), channel_id=1, source_target_pairs={{0,2},{1,5},{2,6},{3,1},{4,0},{5,9},{6,10},{7,3},{8,4},{9,13},{10,... | collective-permute-start | bytes 393224 | tf_op jit(solution)/shard_map/ppermute | solution.py:154
  27.9 3.2 %collective-permute-start.10 = (bf16[8,8192]{1,0:T(8,128)(2,1)S(1)}, bf16[8,8192]{1,0:T(8,128)(2,1)S(1)}, u32[]{:S(2)}, u32[]{:S(2)}) collective-permute-start(bf16[8,8192]{1,0:T(8,128)(2,1)S(1)} %collective-permute-done.2.refs_3_), channel_id=1, source_target_pairs={{0,1},{1,0},{2,3},{3,2},{4,5},{5,4},{6,7},{7,6},{8,9},{9,8},{10,11... | collective-permute-start | bytes 393224 | tf_op jit(solution)/shard_map/ppermute | solution.py:154
  27.9 5.0 %collective-permute-start.6 = (bf16[8,8192]{1,0:T(8,128)(2,1)S(1)}, bf16[8,8192]{1,0:T(8,128)(2,1)S(1)}, u32[]{:S(2)}, u32[]{:S(2)}) collective-permute-start(bf16[8,8192]{1,0:T(8,128)(2,1)S(1)} %collective-permute-done.4.refs_5_), channel_id=1, source_target_pairs={{0,4},{1,3},{2,0},{3,7},{4,8},{5,1},{6,2},{7,11},{8,12},{9,5},{10,... | collective-permute-start | bytes 393224 | tf_op jit(solution)/shard_map/ppermute | solution.py:154
  28.1 4.9 %collective-permute-start.28 = (bf16[8,6144]{1,0:T(8,128)(2,1)S(1)}, bf16[8,6144]{1,0:T(8,128)(2,1)S(1)}, u32[]{:S(2)}, u32[]{:S(2)}) collective-permute-start(bf16[8,6144]{1,0:T(8,128)(2,1)S(1)} %collective-permute-done.20.refs_22_), channel_id=1, source_target_pairs={{0,1},{1,0},{2,3},{3,2},{4,5},{5,4},{6,7},{7,6},{8,9},{9,8},{10,11... | collective-permute-start | bytes 294920 | tf_op jit(solution)/shard_map/ppermute | solution.py:154
  29.7 4.6 %collective-permute-start.21 = (bf16[8,6144]{1,0:T(8,128)(2,1)S(1)}, bf16[8,6144]{1,0:T(8,128)(2,1)S(1)}, u32[]{:S(2)}, u32[]{:S(2)}) collective-permute-start(bf16[8,6144]{1,0:T(8,128)(2,1)S(1)} %collective-permute-done.19.refs_21_), channel_id=1, source_target_pairs={{0,4},{1,3},{2,0},{3,7},{4,8},{5,1},{6,2},{7,11},{8,12},{9,5},{10,... | collective-permute-start | bytes 294920 | tf_op jit(solution)/shard_map/ppermute | solution.py:154
  31.0 4.7 %collective-permute-start.12 = (bf16[8,8192]{1,0:T(8,128)(2,1)S(1)}, bf16[8,8192]{1,0:T(8,128)(2,1)S(1)}, u32[]{:S(2)}, u32[]{:S(2)}) collective-permute-start(bf16[8,8192]{1,0:T(8,128)(2,1)S(1)} %collective-permute-done.4.refs_5_), channel_id=1, source_target_pairs={{0,1},{1,0},{2,3},{3,2},{4,5},{5,4},{6,7},{7,6},{8,9},{9,8},{10,11... | collective-permute-start | bytes 393224 | tf_op jit(solution)/shard_map/ppermute | solution.py:154
  31.1 4.6 %collective-permute-start.13 = (bf16[8,8192]{1,0:T(8,128)(2,1)S(1)}, bf16[8,8192]{1,0:T(8,128)(2,1)S(1)}, u32[]{:S(2)}, u32[]{:S(2)}) collective-permute-start(bf16[8,8192]{1,0:T(8,128)(2,1)S(1)} %collective-permute-done.5.refs_6_), channel_id=1, source_target_pairs={{0,1},{1,0},{2,3},{3,2},{4,5},{5,4},{6,7},{7,6},{8,9},{9,8},{10,11... | collective-permute-start | bytes 393224 | tf_op jit(solution)/shard_map/ppermute | solution.py:154
  33.0 2.7 %collective-permute-start.14 = (bf16[8,8192]{1,0:T(8,128)(2,1)S(1)}, bf16[8,8192]{1,0:T(8,128)(2,1)S(1)}, u32[]{:S(2)}, u32[]{:S(2)}) collective-permute-start(bf16[8,8192]{1,0:T(8,128)(2,1)S(1)} %collective-permute-done.6.refs_7_), channel_id=1, source_target_pairs={{0,1},{1,0},{2,3},{3,2},{4,5},{5,4},{6,7},{7,6},{8,9},{9,8},{10,11... | collective-permute-start | bytes 393224 | tf_op jit(solution)/shard_map/ppermute | solution.py:154
  33.0 2.1 %collective-permute-start.27 = (bf16[8,6144]{1,0:T(8,128)(2,1)S(1)}, bf16[8,6144]{1,0:T(8,128)(2,1)S(1)}, u32[]{:S(2)}, u32[]{:S(2)}) collective-permute-start(bf16[8,6144]{1,0:T(8,128)(2,1)S(1)} %collective-permute-done.19.refs_21_), channel_id=1, source_target_pairs={{0,1},{1,0},{2,3},{3,2},{4,5},{5,4},{6,7},{7,6},{8,9},{9,8},{10,11... | collective-permute-start | bytes 294920 | tf_op jit(solution)/shard_map/ppermute | solution.py:154
  34.4 1.3 %collective-permute-start.29 = (bf16[8,6144]{1,0:T(8,128)(2,1)S(1)}, bf16[8,6144]{1,0:T(8,128)(2,1)S(1)}, u32[]{:S(2)}, u32[]{:S(2)}) collective-permute-start(bf16[8,6144]{1,0:T(8,128)(2,1)S(1)} %collective-permute-done.21.refs_23_), channel_id=1, source_target_pairs={{0,1},{1,0},{2,3},{3,2},{4,5},{5,4},{6,7},{7,6},{8,9},{9,8},{10,11... | collective-permute-start | bytes 294920 | tf_op jit(solution)/shard_map/ppermute | solution.py:154

commit v3 on v2

--- a/solution.py
+++ b/solution.py
@@ -146,24 +146,27 @@
     return onward, backward
 
 
-def ring_gather(parts, devices):
+def ring_gather(tokens, devices):
     onward, backward = ring_plan(devices)
     sibling = [device ^ 1 for device in range(devices)]
 
-    def send(values, target):
-        return [lax.ppermute(value, "col", list(enumerate(target))) for value in values]
+    def send(value, target):
+        return lax.ppermute(value, "col", list(enumerate(target)))
 
     chips = devices // 2
-    ahead, back = parts, parts
-    slabs = [parts]
+    beside = send(tokens, sibling)
+    later, beside = lax.optimization_barrier((tokens, beside))
+    ahead, back = tokens, later
+    slabs, passed = [tokens], [beside]
     for step in range(1, chips // 2 + 1):
         ahead = send(ahead, onward)
         slabs.append(ahead)
+        passed.append(send(ahead, sibling))
         if 2 * step < chips:
             back = send(back, backward)
             slabs.append(back)
-    slabs += [send(values, sibling) for values in slabs]
-    return [list(part) for part in zip(*slabs)]
+            passed.append(send(back, sibling))
+    return slabs + passed
 
 
 def slab_origin(devices, device, number):
@@ -178,11 +181,11 @@
     return 2 * chip + core
 
 
-def ring_kernel(devices, slots, cuts, device_ref, table_ref, *refs):
-    slabs = [refs[at * devices:(at + 1) * devices] for at in range(len(cuts))]
-    out_ref, pair, tiles, zeros, out_sems, zero_sems = refs[len(cuts) * devices:]
+def ring_kernel(devices, slots, device_ref, table_ref, *refs):
+    slabs = refs[:devices]
+    out_ref, pair, tiles, zeros, out_sems, zero_sems = refs[devices:]
     device = device_ref[0]
-    slab, width = slabs[0][0].shape[0], pair.shape[2]
+    slab, width = slabs[0].shape[0], pair.shape[2]
 
     def owned(partner):
         return table_ref[devices + tile_number(devices, device, partner)] == device
@@ -194,18 +197,15 @@
         return pltpu.make_async_copy(zeros, out_ref.at[slot], zero_sems.at[slot])
 
     def load_block(partner, masked):
-        for (start, size), refs_of_part in zip(cuts, slabs):
-            columns = pl.ds(pl.multiple_of(partner * size, 128), size)
-            parts = []
-            for at, ref in enumerate(refs_of_part):
-                part = ref[:, columns].astype(jnp.float32)
-                if masked:
-                    row = lax.broadcasted_iota(jnp.int32, (slab, size), 0)
-                    kept = table_ref[slab_origin(devices, device, at)]
-                    part = jnp.where(row < kept, part, 0.0)
-                parts.append(part)
-            block = jnp.concatenate(parts, axis=0).astype(jnp.bfloat16)
-            pair[0 if masked else 1, :, start:start + size] = block
+        columns = pl.ds(pl.multiple_of(partner * width, 128), width)
+        parts = []
+        for at, ref in enumerate(slabs):
+            part = ref[:, columns].astype(jnp.float32)
+            if masked:
+                row = lax.broadcasted_iota(jnp.int32, (slab, width), 0)
+                part = jnp.where(row < table_ref[slab_origin(devices, device, at)], part, 0.0)
+            parts.append(part)
+        pair[0 if masked else 1] = jnp.concatenate(parts, axis=0).astype(jnp.bfloat16)
 
     count = lax.fori_loop(
         0, devices, lambda partner, total: total + owned(partner).astype(jnp.int32), jnp.int32(0)
@@ -269,17 +269,15 @@
 def ring_form(tokens, slab_lengths, tile_owner, devices, device, slots):
     slab, units = tokens.shape
     width = units // devices
-    first = -(-width // 256) * 128
-    cuts = [(0, first), (first, width - first)] if first < width else [(0, width)]
-    by_block = tokens.reshape(slab, devices, width)
-    parts = [by_block[:, :, start:start + size].reshape(slab, devices * size) for start, size in cuts]
-    slabs = ring_gather(parts, devices)
+    slabs = ring_gather(tokens, devices)
+    kept = jnp.arange(slab, dtype=jnp.int32)[:, None] < slab_lengths[device]
+    slabs[0] = jnp.where(kept, tokens, jnp.zeros_like(tokens))
     table = jnp.concatenate([slab_lengths, tile_owner])
     return pl.pallas_call(
-        functools.partial(ring_kernel, devices, slots, cuts),
+        functools.partial(ring_kernel, devices, slots),
         out_shape=jax.ShapeDtypeStruct((slots, width, width), jnp.float32),
         in_specs=[pl.BlockSpec(memory_space=pltpu.SMEM)] * 2
-        + [pl.BlockSpec(memory_space=pltpu.VMEM)] * (len(cuts) * devices),
+        + [pl.BlockSpec(memory_space=pltpu.VMEM)] * devices,
         out_specs=pl.BlockSpec(memory_space=pl.ANY),
         scratch_shapes=[
             pltpu.VMEM((2, slab * devices, width), jnp.bfloat16),
@@ -294,7 +292,7 @@
             bytes_accessed=4 * slots * width * width,
             transcendentals=0,
         ),
-    )(device.reshape(1), table, *sum(slabs, []))
+    )(device.reshape(1), table, *slabs)
 
 
 def per_device(tokens, slab_lengths, tile_owner):

time: 48.7 us -> 45.8 us (0.940)
  starting transfers between devices: 18.8 us -> 9.56 us
  waiting for transfers between devices: 14.3 us -> 19.5 us
  other arithmetic: 0.76 us -> 2.43 us
  local copies, waits for them, and re-layouts: 1.82 us -> 1.24 us
    ppermute x30 -> x15, starting transfers between devices: 18.8 us -> 9.56 us  [send(): return lax.ppermute(value, 'col', list(enumerate(target)))]
    ppermute x30 -> x15, waiting for transfers between devices: 14.3 us -> 19.5 us  [send(): return lax.ppermute(value, 'col', list(enumerate(target)))]
    slice x2 -> x0, local copies, waits for them, and re-layouts: 1.82 us -> none  [ring_form(): by_block[:, :, start:start + size].reshape(slab, devices * size)]
    dynamic_slice x0 -> x1, local copies, waits for them, and re-layouts: none -> 1.24 us  [ring_form(): kept = jnp.arange(slab, dtype=jnp.int32)[:, None] < slab_lengths[device]]
    select_n x0 -> x1, other arithmetic: none -> 1.02 us  [ring_form(): slabs[0] = jnp.where(kept, tokens, jnp.zeros_like(tokens))]
    lt x0 -> x1, other arithmetic: none -> 0.65 us  [ring_form(): kept = jnp.arange(slab, dtype=jnp.int32)[:, None] < slab_lengths[device]]
  transfers between devices with their start and end apart: 30 -> 15, of which waited for: 9 -> 6; matrix products, arithmetic and copies ran while one was open for 3% -> 8% of each run, Pallas kernels for 0% -> 0%
where the time goes in v3:
time: 45.8 us; the launch traced here: 45.5 us
  waiting for transfers between devices  19.5 us (43%)
  Pallas kernels  12.7 us (28%)
  starting transfers between devices  9.56 us (21%)
  other arithmetic  2.43 us (5%)
  local copies, waits for them, and re-layouts  1.24 us (3%)
    ppermute x15, waiting for transfers between devices, send(): return lax.ppermute(value, 'col', list(enumerate(target)))  19.5 us
    pallas_call x1, Pallas kernels, ring_form(): pl.pallas_call(functools.partial(ring_kernel, devices, slots), out_shape=...  12.7 us
    ppermute x15, starting transfers between devices, send(): return lax.ppermute(value, 'col', list(enumerate(target)))  9.56 us
    dynamic_slice x1, local copies, waits for them, and re-layouts, ring_form(): kept = jnp.arange(slab, dtype=jnp.int32)[:, None] < slab_lengths[device]  1.24 us
    select_n x1, other arithmetic, ring_form(): slabs[0] = jnp.where(kept, tokens, jnp.zeros_like(tokens))  1.02 us
  transfers between devices with their start and end apart: 15, of which 6 were waited for; matrix products, arithmetic and copies ran while one was open for 8% of the time, Pallas kernels for 0%

profile of v3, /device:TPU:0, one launch (start us, length us, event | category | flops | bytes accessed | tf_op | source)
XLA Modules:
  0.0 45.5 jit_solution(14598969440191727377)
XLA Ops:
  0.0 0.5 collective-permute-start.1
  0.5 2.6 %collective-permute-start = (bf16[8,14336]{1,0:T(8,128)(2,1)}, bf16[8,14336]{1,0:T(8,128)(2,1)S(1)}, u32[]{:S(2)}, u32[]{:S(2)}) collective-permute-start(bf16[8,14336]{1,0:T(8,128)(2,1)} %param.3), channel_id=1, source_target_pairs={{0,4},{1,3},{2,0},{3,7},{4,8},{5,1},{6,2},{7,11},{8,12},{9,5},{10,... | collective-permute-start | bytes 688136 | tf_op jit(solution)/shard_map/ppermute | solution.py:154
  3.0 0.0 collective-permute-done.1.refs_8_
  3.0 4.1 %collective-permute-done.refs_1_ = bf16[8,14336]{1,0:T(8,128)(2,1)S(1)} collective-permute-done((bf16[8,14336]{1,0:T(8,128)(2,1)}, bf16[8,14336]{1,0:T(8,128)(2,1)S(1)}, u32[]{:S(2)}, u32[]{:S(2)}) %collective-permute-start) | collective-permute-done | bytes 229408 | tf_op jit(solution)/shard_map/ppermute | solution.py:154
  7.2 2.1 %collective-permute-start.3 = (bf16[8,14336]{1,0:T(8,128)(2,1)S(1)}, bf16[8,14336]{1,0:T(8,128)(2,1)S(1)}, u32[]{:S(2)}, u32[]{:S(2)}) collective-permute-start(bf16[8,14336]{1,0:T(8,128)(2,1)S(1)} %collective-permute-done.refs_1_), channel_id=1, source_target_pairs={{0,4},{1,3},{2,0},{3,7},{4,8},{5,1},{6,2},{7,11},{8,12},{9,5},{10,... | collective-permute-start | bytes 688136 | tf_op jit(solution)/shard_map/ppermute | solution.py:154
  9.3 0.0 collective-permute-start.2
  9.3 5.8 %collective-permute-done.3.refs_3_ = bf16[8,14336]{1,0:T(8,128)(2,1)S(1)} collective-permute-done((bf16[8,14336]{1,0:T(8,128)(2,1)S(1)}, bf16[8,14336]{1,0:T(8,128)(2,1)S(1)}, u32[]{:S(2)}, u32[]{:S(2)}) %collective-permute-start.3) | collective-permute-done | bytes 229408 | tf_op jit(solution)/shard_map/ppermute | solution.py:154
  15.0 1.6 %collective-permute-start.5 = (bf16[8,14336]{1,0:T(8,128)(2,1)S(1)}, bf16[8,14336]{1,0:T(8,128)(2,1)S(1)}, u32[]{:S(2)}, u32[]{:S(2)}) collective-permute-start(bf16[8,14336]{1,0:T(8,128)(2,1)S(1)} %collective-permute-done.3.refs_3_), channel_id=1, source_target_pairs={{0,4},{1,3},{2,0},{3,7},{4,8},{5,1},{6,2},{7,11},{8,12},{9,5},{10,... | collective-permute-start | bytes 688136 | tf_op jit(solution)/shard_map/ppermute | solution.py:154
  16.6 0.0 collective-permute-done.2.refs_2_
  16.6 0.8 %collective-permute-start.4 = (bf16[8,14336]{1,0:T(8,128)(2,1)S(1)}, bf16[8,14336]{1,0:T(8,128)(2,1)S(1)}, u32[]{:S(2)}, u32[]{:S(2)}) collective-permute-start(bf16[8,14336]{1,0:T(8,128)(2,1)S(1)} %collective-permute-done.2.refs_2_), channel_id=1, source_target_pairs={{0,2},{1,5},{2,6},{3,1},{4,0},{5,9},{6,10},{7,3},{8,4},{9,13},{10,... | collective-permute-start | bytes 688136 | tf_op jit(solution)/shard_map/ppermute | solution.py:154
  17.5 0.0 collective-permute-start.8
  17.5 0.5 %collective-permute-start.10 = (bf16[8,14336]{1,0:T(8,128)(2,1)S(1)}, bf16[8,14336]{1,0:T(8,128)(2,1)S(1)}, u32[]{:S(2)}, u32[]{:S(2)}) collective-permute-start(bf16[8,14336]{1,0:T(8,128)(2,1)S(1)} %collective-permute-done.3.refs_3_), channel_id=1, source_target_pairs={{0,1},{1,0},{2,3},{3,2},{4,5},{5,4},{6,7},{7,6},{8,9},{9,8},{10,11... | collective-permute-start | bytes 688136 | tf_op jit(solution)/shard_map/ppermute | solution.py:154
  18.0 5.4 %collective-permute-done.5.refs_5_ = bf16[8,14336]{1,0:T(8,128)(2,1)S(1)} collective-permute-done((bf16[8,14336]{1,0:T(8,128)(2,1)S(1)}, bf16[8,14336]{1,0:T(8,128)(2,1)S(1)}, u32[]{:S(2)}, u32[]{:S(2)}) %collective-permute-start.5) | collective-permute-done | bytes 229408 | tf_op jit(solution)/shard_map/ppermute | solution.py:154
  23.3 0.2 collective-permute-start.7
  23.5 1.3 %collective-permute-done.4.refs_4_ = bf16[8,14336]{1,0:T(8,128)(2,1)S(1)} collective-permute-done((bf16[8,14336]{1,0:T(8,128)(2,1)S(1)}, bf16[8,14336]{1,0:T(8,128)(2,1)S(1)}, u32[]{:S(2)}, u32[]{:S(2)}) %collective-permute-start.4) | collective-permute-done | bytes 229408 | tf_op jit(solution)/shard_map/ppermute | solution.py:154
  24.8 0.5 %collective-permute-start.6 = (bf16[8,14336]{1,0:T(8,128)(2,1)S(1)}, bf16[8,14336]{1,0:T(8,128)(2,1)S(1)}, u32[]{:S(2)}, u32[]{:S(2)}) collective-permute-start(bf16[8,14336]{1,0:T(8,128)(2,1)S(1)} %collective-permute-done.4.refs_4_), channel_id=1, source_target_pairs={{0,2},{1,5},{2,6},{3,1},{4,0},{5,9},{6,10},{7,3},{8,4},{9,13},{10,... | collective-permute-start | bytes 688136 | tf_op jit(solution)/shard_map/ppermute | solution.py:154
  25.4 1.2 %dynamic_slice.3 = s32[1]{0:T(128)} dynamic-slice(s32[16]{0:T(128)} %param.4, s32[]{:T(128)S(6)} %select_n.7), dynamic_slice_sizes={1} | dynamic-slice | bytes 12 | tf_op jit(solution)/shard_map/dynamic_slice | solution.py:273
  26.6 0.6 %iota_compare_fusion = pred[8]{0:T(512)(128)(4,1)S(1)} fusion(s32[]{:T(128)} %bitcast.1), kind=kLoop, calls=%fused_computation.2 | loop fusion | flops 8 | bytes 12 | tf_op jit(solution)/shard_map/lt | solution.py:273
  27.3 0.1 collective-permute-start.9
  27.3 0.0 collective-permute-done.8.refs_9_
  27.4 0.5 %collective-permute-start.12 = (bf16[8,14336]{1,0:T(8,128)(2,1)S(1)}, bf16[8,14336]{1,0:T(8,128)(2,1)S(1)}, u32[]{:S(2)}, u32[]{:S(2)}) collective-permute-start(bf16[8,14336]{1,0:T(8,128)(2,1)S(1)} %collective-permute-done.5.refs_5_), channel_id=1, source_target_pairs={{0,1},{1,0},{2,3},{3,2},{4,5},{5,4},{6,7},{7,6},{8,9},{9,8},{10,11... | collective-permute-start | bytes 688136 | tf_op jit(solution)/shard_map/ppermute | solution.py:154
  27.8 0.0 collective-permute-done.10.refs_11_
  27.9 0.1 collective-permute-start.11
  27.9 2.5 %collective-permute-done.7.refs_7_ = bf16[8,14336]{1,0:T(8,128)(2,1)S(1)} collective-permute-done((bf16[8,14336]{1,0:T(8,128)(2,1)S(1)}, bf16[8,14336]{1,0:T(8,128)(2,1)S(1)}, u32[]{:S(2)}, u32[]{:S(2)}) %collective-permute-start.7) | collective-permute-done | bytes 229408 | tf_op jit(solution)/shard_map/ppermute | solution.py:154
  30.5 0.0 collective-permute-start.14
  30.5 0.4 collective-permute-done.6.refs_6_
  30.9 0.1 collective-permute-start.13
  31.0 1.0 %broadcast_select_fusion.refs_0_ = bf16[8,14336]{1,0:T(8,128)(2,1)S(1)} fusion(bf16[8,14336]{1,0:T(8,128)(2,1)} %param.3, pred[8]{0:T(512)(128)(4,1)S(1)} %iota_compare_fusion), kind=kLoop, calls=%fused_computation | loop fusion | flops 114688 | bytes 458760 | tf_op jit(solution)/shard_map/jit(_where)/select_n | solution.py:274
  32.0 0.8 %pad_add_fusion.table_ref = s32[152]{0:T(256)S(1)} fusion(s32[136]{0:T(256)} %param.5, s32[16]{0:T(128)} %param.4), kind=kLoop, calls=%fused_computation.1 | loop fusion | flops 152 | bytes 1216 | tf_op jit(solution)/shard_map/concatenate | solution.py:275
  32.8 0.0 collective-permute-done.9.refs_10_
  32.8 0.0 collective-permute-done.12.refs_13_
  32.8 0.0 collective-permute-done.11.refs_12_
  32.8 0.0 collective-permute-done.14.refs_15_
  32.8 0.0 collective-permute-done.13.refs_14_
  32.8 12.7 %shard_map.37 = f32[11,896,896]{2,1,0:T(8,128)} custom-call(s32[1]{0:T(128)} %bitcast.device_ref, s32[152]{0:T(256)S(1)} %pad_add_fusion.table_ref, bf16[8,14336]{1,0:T(8,128)(2,1)S(1)} %broadcast_select_fusion.refs_0_, bf16[8,14336]{1,0:T(8,128)(2,1)S(1)} %collective-permute-done.refs_1_, bf16[8,14336]{1,0:T(8,128)(2,1)S(1)} %collective-permute-done.2.refs_2_, ...), custom_call_target="tpu_custom_call" | custom-call | flops 2260729856 | bytes 35323904 | tf_op jit(solution)/shard_map/pallas_call | solution.py:276
Async XLA Ops:
  0.0 3.0 %collective-permute-start.1 = (bf16[8,14336]{1,0:T(8,128)(2,1)}, bf16[8,14336]{1,0:T(8,128)(2,1)S(1)}, u32[]{:S(2)}, u32[]{:S(2)}) collective-permute-start(bf16[8,14336]{1,0:T(8,128)(2,1)} %param.3), channel_id=1, source_target_pairs={{0,1},{1,0},{2,3},{3,2},{4,5},{5,4},{6,7},{7,6},{8,9},{9,8},{10,11... | collective-permute-start | bytes 688136 | tf_op jit(solution)/shard_map/ppermute | solution.py:154
  0.5 6.7 %collective-permute-start = (bf16[8,14336]{1,0:T(8,128)(2,1)}, bf16[8,14336]{1,0:T(8,128)(2,1)S(1)}, u32[]{:S(2)}, u32[]{:S(2)}) collective-permute-start(bf16[8,14336]{1,0:T(8,128)(2,1)} %param.3), channel_id=1, source_target_pairs={{0,4},{1,3},{2,0},{3,7},{4,8},{5,1},{6,2},{7,11},{8,12},{9,5},{10,... | collective-permute-start | bytes 688136 | tf_op jit(solution)/shard_map/ppermute | solution.py:154
  7.2 7.9 %collective-permute-start.3 = (bf16[8,14336]{1,0:T(8,128)(2,1)S(1)}, bf16[8,14336]{1,0:T(8,128)(2,1)S(1)}, u32[]{:S(2)}, u32[]{:S(2)}) collective-permute-start(bf16[8,14336]{1,0:T(8,128)(2,1)S(1)} %collective-permute-done.refs_1_), channel_id=1, source_target_pairs={{0,4},{1,3},{2,0},{3,7},{4,8},{5,1},{6,2},{7,11},{8,12},{9,5},{10,... | collective-permute-start | bytes 688136 | tf_op jit(solution)/shard_map/ppermute | solution.py:154
  9.3 7.4 %collective-permute-start.2 = (bf16[8,14336]{1,0:T(8,128)(2,1)}, bf16[8,14336]{1,0:T(8,128)(2,1)S(1)}, u32[]{:S(2)}, u32[]{:S(2)}) collective-permute-start(bf16[8,14336]{1,0:T(8,128)(2,1)} %param.3), channel_id=1, source_target_pairs={{0,2},{1,5},{2,6},{3,1},{4,0},{5,9},{6,10},{7,3},{8,4},{9,13},{10,... | collective-permute-start | bytes 688136 | tf_op jit(solution)/shard_map/ppermute | solution.py:154
  15.0 8.3 %collective-permute-start.5 = (bf16[8,14336]{1,0:T(8,128)(2,1)S(1)}, bf16[8,14336]{1,0:T(8,128)(2,1)S(1)}, u32[]{:S(2)}, u32[]{:S(2)}) collective-permute-start(bf16[8,14336]{1,0:T(8,128)(2,1)S(1)} %collective-permute-done.3.refs_3_), channel_id=1, source_target_pairs={{0,4},{1,3},{2,0},{3,7},{4,8},{5,1},{6,2},{7,11},{8,12},{9,5},{10,... | collective-permute-start | bytes 688136 | tf_op jit(solution)/shard_map/ppermute | solution.py:154
  16.6 8.2 %collective-permute-start.4 = (bf16[8,14336]{1,0:T(8,128)(2,1)S(1)}, bf16[8,14336]{1,0:T(8,128)(2,1)S(1)}, u32[]{:S(2)}, u32[]{:S(2)}) collective-permute-start(bf16[8,14336]{1,0:T(8,128)(2,1)S(1)} %collective-permute-done.2.refs_2_), channel_id=1, source_target_pairs={{0,2},{1,5},{2,6},{3,1},{4,0},{5,9},{6,10},{7,3},{8,4},{9,13},{10,... | collective-permute-start | bytes 688136 | tf_op jit(solution)/shard_map/ppermute | solution.py:154
  17.5 9.9 %collective-permute-start.8 = (bf16[8,14336]{1,0:T(8,128)(2,1)S(1)}, bf16[8,14336]{1,0:T(8,128)(2,1)S(1)}, u32[]{:S(2)}, u32[]{:S(2)}) collective-permute-start(bf16[8,14336]{1,0:T(8,128)(2,1)S(1)} %collective-permute-done.refs_1_), channel_id=1, source_target_pairs={{0,1},{1,0},{2,3},{3,2},{4,5},{5,4},{6,7},{7,6},{8,9},{9,8},{10,11... | collective-permute-start | bytes 688136 | tf_op jit(solution)/shard_map/ppermute | solution.py:154
  17.5 10.4 %collective-permute-start.10 = (bf16[8,14336]{1,0:T(8,128)(2,1)S(1)}, bf16[8,14336]{1,0:T(8,128)(2,1)S(1)}, u32[]{:S(2)}, u32[]{:S(2)}) collective-permute-start(bf16[8,14336]{1,0:T(8,128)(2,1)S(1)} %collective-permute-done.3.refs_3_), channel_id=1, source_target_pairs={{0,1},{1,0},{2,3},{3,2},{4,5},{5,4},{6,7},{7,6},{8,9},{9,8},{10,11... | collective-permute-start | bytes 688136 | tf_op jit(solution)/shard_map/ppermute | solution.py:154
  23.3 7.1 %collective-permute-start.7 = (bf16[8,14336]{1,0:T(8,128)(2,1)S(1)}, bf16[8,14336]{1,0:T(8,128)(2,1)S(1)}, u32[]{:S(2)}, u32[]{:S(2)}) collective-permute-start(bf16[8,14336]{1,0:T(8,128)(2,1)S(1)} %collective-permute-done.5.refs_5_), channel_id=1, source_target_pairs={{0,4},{1,3},{2,0},{3,7},{4,8},{5,1},{6,2},{7,11},{8,12},{9,5},{10,... | collective-permute-start | bytes 688136 | tf_op jit(solution)/shard_map/ppermute | solution.py:154
  24.8 6.0 %collective-permute-start.6 = (bf16[8,14336]{1,0:T(8,128)(2,1)S(1)}, bf16[8,14336]{1,0:T(8,128)(2,1)S(1)}, u32[]{:S(2)}, u32[]{:S(2)}) collective-permute-start(bf16[8,14336]{1,0:T(8,128)(2,1)S(1)} %collective-permute-done.4.refs_4_), channel_id=1, source_target_pairs={{0,2},{1,5},{2,6},{3,1},{4,0},{5,9},{6,10},{7,3},{8,4},{9,13},{10,... | collective-permute-start | bytes 688136 | tf_op jit(solution)/shard_map/ppermute | solution.py:154
  27.3 5.5 %collective-permute-start.9 = (bf16[8,14336]{1,0:T(8,128)(2,1)S(1)}, bf16[8,14336]{1,0:T(8,128)(2,1)S(1)}, u32[]{:S(2)}, u32[]{:S(2)}) collective-permute-start(bf16[8,14336]{1,0:T(8,128)(2,1)S(1)} %collective-permute-done.2.refs_2_), channel_id=1, source_target_pairs={{0,1},{1,0},{2,3},{3,2},{4,5},{5,4},{6,7},{7,6},{8,9},{9,8},{10,11... | collective-permute-start | bytes 688136 | tf_op jit(solution)/shard_map/ppermute | solution.py:154
  27.4 5.4 %collective-permute-start.12 = (bf16[8,14336]{1,0:T(8,128)(2,1)S(1)}, bf16[8,14336]{1,0:T(8,128)(2,1)S(1)}, u32[]{:S(2)}, u32[]{:S(2)}) collective-permute-start(bf16[8,14336]{1,0:T(8,128)(2,1)S(1)} %collective-permute-done.5.refs_5_), channel_id=1, source_target_pairs={{0,1},{1,0},{2,3},{3,2},{4,5},{5,4},{6,7},{7,6},{8,9},{9,8},{10,11... | collective-permute-start | bytes 688136 | tf_op jit(solution)/shard_map/ppermute | solution.py:154
  27.9 4.9 %collective-permute-start.11 = (bf16[8,14336]{1,0:T(8,128)(2,1)S(1)}, bf16[8,14336]{1,0:T(8,128)(2,1)S(1)}, u32[]{:S(2)}, u32[]{:S(2)}) collective-permute-start(bf16[8,14336]{1,0:T(8,128)(2,1)S(1)} %collective-permute-done.4.refs_4_), channel_id=1, source_target_pairs={{0,1},{1,0},{2,3},{3,2},{4,5},{5,4},{6,7},{7,6},{8,9},{9,8},{10,11... | collective-permute-start | bytes 688136 | tf_op jit(solution)/shard_map/ppermute | solution.py:154
  30.5 2.3 %collective-permute-start.14 = (bf16[8,14336]{1,0:T(8,128)(2,1)S(1)}, bf16[8,14336]{1,0:T(8,128)(2,1)S(1)}, u32[]{:S(2)}, u32[]{:S(2)}) collective-permute-start(bf16[8,14336]{1,0:T(8,128)(2,1)S(1)} %collective-permute-done.7.refs_7_), channel_id=1, source_target_pairs={{0,1},{1,0},{2,3},{3,2},{4,5},{5,4},{6,7},{7,6},{8,9},{9,8},{10,11... | collective-permute-start | bytes 688136 | tf_op jit(solution)/shard_map/ppermute | solution.py:154
  30.9 1.9 %collective-permute-start.13 = (bf16[8,14336]{1,0:T(8,128)(2,1)S(1)}, bf16[8,14336]{1,0:T(8,128)(2,1)S(1)}, u32[]{:S(2)}, u32[]{:S(2)}) collective-permute-start(bf16[8,14336]{1,0:T(8,128)(2,1)S(1)} %collective-permute-done.6.refs_6_), channel_id=1, source_target_pairs={{0,1},{1,0},{2,3},{3,2},{4,5},{5,4},{6,7},{7,6},{8,9},{9,8},{10,11... | collective-permute-start | bytes 688136 | tf_op jit(solution)/shard_map/ppermute | solution.py:154

commit v4 on v3

--- a/solution.py
+++ b/solution.py
@@ -146,18 +146,16 @@
     return onward, backward
 
 
-def ring_gather(tokens, devices):
+def ring_gather(tokens, parts, devices):
     onward, backward = ring_plan(devices)
     sibling = [device ^ 1 for device in range(devices)]
 
-    def send(value, target):
-        return lax.ppermute(value, "col", list(enumerate(target)))
+    def send(values, target):
+        return [lax.ppermute(value, "col", list(enumerate(target))) for value in values]
 
     chips = devices // 2
-    beside = send(tokens, sibling)
-    later, beside = lax.optimization_barrier((tokens, beside))
-    ahead, back = tokens, later
-    slabs, passed = [tokens], [beside]
+    ahead, back = parts, [tokens]
+    slabs, passed = [], [send([tokens], sibling)]
     for step in range(1, chips // 2 + 1):
         ahead = send(ahead, onward)
         slabs.append(ahead)
@@ -181,11 +179,12 @@
     return 2 * chip + core
 
 
-def ring_kernel(devices, slots, device_ref, table_ref, *refs):
-    slabs = refs[:devices]
-    out_ref, pair, tiles, zeros, out_sems, zero_sems = refs[devices:]
+def ring_kernel(devices, slots, sizes, device_ref, table_ref, *refs):
+    refs = list(refs)
+    slabs = [[refs.pop(0) for _ in group] for group in sizes]
+    out_ref, pair, tiles, zeros, out_sems, zero_sems = refs
     device = device_ref[0]
-    slab, width = slabs[0].shape[0], pair.shape[2]
+    slab, width = slabs[0][0].shape[0], pair.shape[2]
 
     def owned(partner):
         return table_ref[devices + tile_number(devices, device, partner)] == device
@@ -197,10 +196,13 @@
         return pltpu.make_async_copy(zeros, out_ref.at[slot], zero_sems.at[slot])
 
     def load_block(partner, masked):
-        columns = pl.ds(pl.multiple_of(partner * width, 128), width)
         parts = []
-        for at, ref in enumerate(slabs):
-            part = ref[:, columns].astype(jnp.float32)
+        for at, (group, group_sizes) in enumerate(zip(slabs, sizes)):
+            pieces = [
+                ref[:, pl.ds(pl.multiple_of(partner * size, 128), size)].astype(jnp.float32)
+                for ref, size in zip(group, group_sizes)
+            ]
+            part = pieces[0] if len(pieces) == 1 else jnp.concatenate(pieces, axis=1)
             if masked:
                 row = lax.broadcasted_iota(jnp.int32, (slab, width), 0)
                 part = jnp.where(row < table_ref[slab_origin(devices, device, at)], part, 0.0)
@@ -269,15 +271,21 @@
 def ring_form(tokens, slab_lengths, tile_owner, devices, device, slots):
     slab, units = tokens.shape
     width = units // devices
-    slabs = ring_gather(tokens, devices)
+    first = -(-width // 256) * 128
+    by_block = tokens.reshape(slab, devices, width)
+    parts = [
+        by_block[:, :, start:stop].reshape(slab, devices * (stop - start))
+        for start, stop in ((0, first), (first, width)) if start < stop
+    ]
     kept = jnp.arange(slab, dtype=jnp.int32)[:, None] < slab_lengths[device]
-    slabs[0] = jnp.where(kept, tokens, jnp.zeros_like(tokens))
+    slabs = [[jnp.where(kept, tokens, jnp.zeros_like(tokens))]] + ring_gather(tokens, parts, devices)
+    sizes = [[value.shape[1] // devices for value in group] for group in slabs]
     table = jnp.concatenate([slab_lengths, tile_owner])
     return pl.pallas_call(
-        functools.partial(ring_kernel, devices, slots),
+        functools.partial(ring_kernel, devices, slots, sizes),
         out_shape=jax.ShapeDtypeStruct((slots, width, width), jnp.float32),
         in_specs=[pl.BlockSpec(memory_space=pltpu.SMEM)] * 2
-        + [pl.BlockSpec(memory_space=pltpu.VMEM)] * devices,
+        + [pl.BlockSpec(memory_space=pltpu.VMEM)] * sum(len(group) for group in slabs),
         out_specs=pl.BlockSpec(memory_space=pl.ANY),
         scratch_shapes=[
             pltpu.VMEM((2, slab * devices, width), jnp.bfloat16),
@@ -292,7 +300,7 @@
             bytes_accessed=4 * slots * width * width,
             transcendentals=0,
         ),
-    )(device.reshape(1), table, *slabs)
+    )(device.reshape(1), table, *sum(slabs, []))
 
 
 def per_device(tokens, slab_lengths, tile_owner):

time: 45.8 us -> 45.5 us (level)
  waiting for transfers between devices: 19.5 us -> 9.45 us
  starting transfers between devices: 9.56 us -> 17.4 us
  local copies, waits for them, and re-layouts: 1.24 us -> 3.09 us
    ppermute x15 -> x23, waiting for transfers between devices: 19.5 us -> 9.45 us  [send(): lax.ppermute(value, 'col', list(enumerate(target)))]
    ppermute x15 -> x23, starting transfers between devices: 9.56 us -> 17.4 us  [send(): lax.ppermute(value, 'col', list(enumerate(target)))]
    slice x0 -> x2, local copies, waits for them, and re-layouts: none -> 1.85 us  [ring_form(): by_block[:, :, start:stop].reshape(slab, devices * (stop - start))]
  transfers between devices with their start and end apart: 15 -> 23, of which waited for: 6 -> 7; matrix products, arithmetic and copies ran while one was open for 8% -> 12% of each run, Pallas kernels for 0% -> 0%
where the time goes in v4:
time: 45.5 us; the launch traced here: 45.2 us
  starting transfers between devices  17.4 us (38%)
  Pallas kernels  12.7 us (28%)
  waiting for transfers between devices  9.45 us (21%)
  local copies, waits for them, and re-layouts  3.09 us (7%)
  other arithmetic  2.43 us (5%)
    ppermute x23, starting transfers between devices, send(): lax.ppermute(value, 'col', list(enumerate(target)))  17.4 us
    pallas_call x1, Pallas kernels, ring_form(): pl.pallas_call(functools.partial(ring_kernel, devices, slots, sizes), out...  12.7 us
    ppermute x23, waiting for transfers between devices, send(): lax.ppermute(value, 'col', list(enumerate(target)))  9.45 us
    slice x2, local copies, waits for them, and re-layouts, ring_form(): by_block[:, :, start:stop].reshape(slab, devices * (stop - start))  1.85 us
    dynamic_slice x1, local copies, waits for them, and re-layouts, ring_form(): kept = jnp.arange(slab, dtype=jnp.int32)[:, None] < slab_lengths[device]  1.24 us
    select_n x1, other arithmetic, ring_form(): jnp.where(kept, tokens, jnp.zeros_like(tokens))  1.02 us
  transfers between devices with their start and end apart: 23, of which 7 were waited for; matrix products, arithmetic and copies ran while one was open for 12% of the time, Pallas kernels for 0%

profile of v4, /device:TPU:0, one launch (start us, length us, event | category | flops | bytes accessed | tf_op | source)
XLA Modules:
  0.0 45.2 jit_solution(15844499070423702662)
XLA Ops:
  0.0 2.9 %collective-permute-start.2 = (bf16[8,14336]{1,0:T(8,128)(2,1)}, bf16[8,14336]{1,0:T(8,128)(2,1)S(1)}, u32[]{:S(2)}, u32[]{:S(2)}) collective-permute-start(bf16[8,14336]{1,0:T(8,128)(2,1)} %param.3), channel_id=1, source_target_pairs={{0,2},{1,5},{2,6},{3,1},{4,0},{5,9},{6,10},{7,3},{8,4},{9,13},{10,... | collective-permute-start | bytes 688136 | tf_op jit(solution)/shard_map/ppermute | solution.py:154
  2.9 0.9 %slice.8 = bf16[8,16,512]{2,0,1:T(8,128)(2,1)S(1)} slice(bf16[8,16,896]{2,0,1:T(8,128)(2,1)} %bitcast.5), slice={[0:8], [0:16], [0:512]} | slice | bytes 262144 | tf_op jit(solution)/shard_map/slice | solution.py:277
  3.9 0.1 collective-permute-start
  4.0 0.9 %slice.9 = bf16[8,16,384]{2,0,1:T(8,128)(2,1)S(1)} slice(bf16[8,16,896]{2,0,1:T(8,128)(2,1)} %bitcast.6), slice={[0:8], [0:16], [512:896]} | slice | bytes 196608 | tf_op jit(solution)/shard_map/slice | solution.py:277
  4.9 2.1 %collective-permute-start.1 = (bf16[8,6144]{1,0:T(8,128)(2,1)S(1)}, bf16[8,6144]{1,0:T(8,128)(2,1)S(1)}, u32[]{:S(2)}, u32[]{:S(2)}) collective-permute-start(bf16[8,6144]{1,0:T(8,128)(2,1)S(1)} %bitcast.8), channel_id=1, source_target_pairs={{0,4},{1,3},{2,0},{3,7},{4,8},{5,1},{6,2},{7,11},{8,12},{9,5},{10,... | collective-permute-start | bytes 294920 | tf_op jit(solution)/shard_map/ppermute | solution.py:154
  7.0 2.0 %collective-permute-done.2.refs_3_ = bf16[8,14336]{1,0:T(8,128)(2,1)S(1)} collective-permute-done((bf16[8,14336]{1,0:T(8,128)(2,1)}, bf16[8,14336]{1,0:T(8,128)(2,1)S(1)}, u32[]{:S(2)}, u32[]{:S(2)}) %collective-permute-start.2) | collective-permute-done | bytes 229408 | tf_op jit(solution)/shard_map/ppermute | solution.py:154
  9.0 2.4 %collective-permute-start.5 = (bf16[8,14336]{1,0:T(8,128)(2,1)S(1)}, bf16[8,14336]{1,0:T(8,128)(2,1)S(1)}, u32[]{:S(2)}, u32[]{:S(2)}) collective-permute-start(bf16[8,14336]{1,0:T(8,128)(2,1)S(1)} %collective-permute-done.2.refs_3_), channel_id=1, source_target_pairs={{0,2},{1,5},{2,6},{3,1},{4,0},{5,9},{6,10},{7,3},{8,4},{9,13},{10,... | collective-permute-start | bytes 688136 | tf_op jit(solution)/shard_map/ppermute | solution.py:154
  11.4 0.0 collective-permute-start.11
  11.4 0.0 collective-permute-done.refs_1_
  11.4 0.0 collective-permute-start.3
  11.4 0.0 collective-permute-done.1.refs_2_
  11.4 1.9 %collective-permute-start.13 = (bf16[8,6144]{1,0:T(8,128)(2,1)S(1)}, bf16[8,6144]{1,0:T(8,128)(2,1)S(1)}, u32[]{:S(2)}, u32[]{:S(2)}) collective-permute-start(bf16[8,6144]{1,0:T(8,128)(2,1)S(1)} %collective-permute-done.1.refs_2_), channel_id=1, source_target_pairs={{0,1},{1,0},{2,3},{3,2},{4,5},{5,4},{6,7},{7,6},{8,9},{9,8},{10,11... | collective-permute-start | bytes 294920 | tf_op jit(solution)/shard_map/ppermute | solution.py:154
  13.3 0.4 collective-permute-start.4
  13.6 0.6 %collective-permute-done.13.refs_14_ = bf16[8,6144]{1,0:T(8,128)(2,1)S(1)} collective-permute-done((bf16[8,6144]{1,0:T(8,128)(2,1)S(1)}, bf16[8,6144]{1,0:T(8,128)(2,1)S(1)}, u32[]{:S(2)}, u32[]{:S(2)}) %collective-permute-start.13) | collective-permute-done | bytes 98336 | tf_op jit(solution)/shard_map/ppermute | solution.py:154
  14.2 0.4 collective-permute-start.12
  14.6 1.8 %collective-permute-done.3.refs_4_ = bf16[8,8192]{1,0:T(8,128)(2,1)S(1)} collective-permute-done((bf16[8,8192]{1,0:T(8,128)(2,1)S(1)}, bf16[8,8192]{1,0:T(8,128)(2,1)S(1)}, u32[]{:S(2)}, u32[]{:S(2)}) %collective-permute-start.3) | collective-permute-done | bytes 131104 | tf_op jit(solution)/shard_map/ppermute | solution.py:154
  16.4 0.0 collective-permute-start.6
  16.4 0.0 collective-permute-done.5.refs_6_
  16.4 2.3 %collective-permute-start.8 = (bf16[8,14336]{1,0:T(8,128)(2,1)S(1)}, bf16[8,14336]{1,0:T(8,128)(2,1)S(1)}, u32[]{:S(2)}, u32[]{:S(2)}) collective-permute-start(bf16[8,14336]{1,0:T(8,128)(2,1)S(1)} %collective-permute-done.5.refs_6_), channel_id=1, source_target_pairs={{0,2},{1,5},{2,6},{3,1},{4,0},{5,9},{6,10},{7,3},{8,4},{9,13},{10,... | collective-permute-start | bytes 688136 | tf_op jit(solution)/shard_map/ppermute | solution.py:154
  18.6 0.0 collective-permute-done.4.refs_5_
  18.6 0.5 %collective-permute-start.7 = (bf16[8,6144]{1,0:T(8,128)(2,1)S(1)}, bf16[8,6144]{1,0:T(8,128)(2,1)S(1)}, u32[]{:S(2)}, u32[]{:S(2)}) collective-permute-start(bf16[8,6144]{1,0:T(8,128)(2,1)S(1)} %collective-permute-done.4.refs_5_), channel_id=1, source_target_pairs={{0,4},{1,3},{2,0},{3,7},{4,8},{5,1},{6,2},{7,11},{8,12},{9,5},{10,... | collective-permute-start | bytes 294920 | tf_op jit(solution)/shard_map/ppermute | solution.py:154
  19.1 0.0 collective-permute-done.11.refs_12_
  19.1 1.0 %collective-permute-start.16 = (bf16[8,6144]{1,0:T(8,128)(2,1)S(1)}, bf16[8,6144]{1,0:T(8,128)(2,1)S(1)}, u32[]{:S(2)}, u32[]{:S(2)}) collective-permute-start(bf16[8,6144]{1,0:T(8,128)(2,1)S(1)} %collective-permute-done.4.refs_5_), channel_id=1, source_target_pairs={{0,1},{1,0},{2,3},{3,2},{4,5},{5,4},{6,7},{7,6},{8,9},{9,8},{10,11... | collective-permute-start | bytes 294920 | tf_op jit(solution)/shard_map/ppermute | solution.py:154
  20.1 0.0 collective-permute-done.12.refs_13_
  20.1 0.1 collective-permute-start.15
  20.2 1.2 %collective-permute-done.6.refs_7_ = bf16[8,8192]{1,0:T(8,128)(2,1)S(1)} collective-permute-done((bf16[8,8192]{1,0:T(8,128)(2,1)S(1)}, bf16[8,8192]{1,0:T(8,128)(2,1)S(1)}, u32[]{:S(2)}, u32[]{:S(2)}) %collective-permute-start.6) | collective-permute-done | bytes 131104 | tf_op jit(solution)/shard_map/ppermute | solution.py:154
  21.4 0.3 collective-permute-start.9
  21.6 1.2 %dynamic_slice.3 = s32[1]{0:T(128)} dynamic-slice(s32[16]{0:T(128)} %param.4, s32[]{:T(128)S(6)} %select_n.7), dynamic_slice_sizes={1} | dynamic-slice | bytes 12 | tf_op jit(solution)/shard_map/dynamic_slice | solution.py:280
  22.9 1.4 %collective-permute-done.7.refs_8_ = bf16[8,6144]{1,0:T(8,128)(2,1)S(1)} collective-permute-done((bf16[8,6144]{1,0:T(8,128)(2,1)S(1)}, bf16[8,6144]{1,0:T(8,128)(2,1)S(1)}, u32[]{:S(2)}, u32[]{:S(2)}) %collective-permute-start.7) | collective-permute-done | bytes 98336 | tf_op jit(solution)/shard_map/ppermute | solution.py:154
  24.3 0.5 %collective-permute-start.19 = (bf16[8,6144]{1,0:T(8,128)(2,1)S(1)}, bf16[8,6144]{1,0:T(8,128)(2,1)S(1)}, u32[]{:S(2)}, u32[]{:S(2)}) collective-permute-start(bf16[8,6144]{1,0:T(8,128)(2,1)S(1)} %collective-permute-done.7.refs_8_), channel_id=1, source_target_pairs={{0,1},{1,0},{2,3},{3,2},{4,5},{5,4},{6,7},{7,6},{8,9},{9,8},{10,11... | collective-permute-start | bytes 294920 | tf_op jit(solution)/shard_map/ppermute | solution.py:154
  24.8 0.0 collective-permute-done.16.refs_17_
  24.8 0.6 %collective-permute-start.10 = (bf16[8,6144]{1,0:T(8,128)(2,1)S(1)}, bf16[8,6144]{1,0:T(8,128)(2,1)S(1)}, u32[]{:S(2)}, u32[]{:S(2)}) collective-permute-start(bf16[8,6144]{1,0:T(8,128)(2,1)S(1)} %collective-permute-done.7.refs_8_), channel_id=1, source_target_pairs={{0,4},{1,3},{2,0},{3,7},{4,8},{5,1},{6,2},{7,11},{8,12},{9,5},{10,... | collective-permute-start | bytes 294920 | tf_op jit(solution)/shard_map/ppermute | solution.py:154
  25.4 0.6 %iota_compare_fusion = pred[8]{0:T(512)(128)(4,1)S(1)} fusion(s32[]{:T(128)} %bitcast.1), kind=kLoop, calls=%fused_computation.2 | loop fusion | flops 8 | bytes 12 | tf_op jit(solution)/shard_map/lt | solution.py:280
  26.0 0.0 collective-permute-done.15.refs_16_
  26.0 1.0 %collective-permute-start.14 = (bf16[8,14336]{1,0:T(8,128)(2,1)S(1)}, bf16[8,14336]{1,0:T(8,128)(2,1)S(1)}, u32[]{:S(2)}, u32[]{:S(2)}) collective-permute-start(bf16[8,14336]{1,0:T(8,128)(2,1)S(1)} %collective-permute-done.2.refs_3_), channel_id=1, source_target_pairs={{0,1},{1,0},{2,3},{3,2},{4,5},{5,4},{6,7},{7,6},{8,9},{9,8},{10,11... | collective-permute-start | bytes 688136 | tf_op jit(solution)/shard_map/ppermute | solution.py:154
  27.0 0.0 collective-permute-done.19.refs_20_
  27.0 0.1 collective-permute-start.18
  27.1 2.3 %collective-permute-done.10.refs_11_ = bf16[8,6144]{1,0:T(8,128)(2,1)S(1)} collective-permute-done((bf16[8,6144]{1,0:T(8,128)(2,1)S(1)}, bf16[8,6144]{1,0:T(8,128)(2,1)S(1)}, u32[]{:S(2)}, u32[]{:S(2)}) %collective-permute-start.10) | collective-permute-done | bytes 98336 | tf_op jit(solution)/shard_map/ppermute | solution.py:154
  29.4 0.0 collective-permute-start.17
  29.4 0.5 %collective-permute-start.21 = (bf16[8,8192]{1,0:T(8,128)(2,1)S(1)}, bf16[8,8192]{1,0:T(8,128)(2,1)S(1)}, u32[]{:S(2)}, u32[]{:S(2)}) collective-permute-start(bf16[8,8192]{1,0:T(8,128)(2,1)S(1)} %collective-permute-done.9.refs_10_), channel_id=1, source_target_pairs={{0,1},{1,0},{2,3},{3,2},{4,5},{5,4},{6,7},{7,6},{8,9},{9,8},{10,11... | collective-permute-start | bytes 393224 | tf_op jit(solution)/shard_map/ppermute | solution.py:154
  29.9 0.1 collective-permute-start.20
  30.0 1.0 %broadcast_select_fusion.refs_0_ = bf16[8,14336]{1,0:T(8,128)(2,1)S(1)} fusion(bf16[8,14336]{1,0:T(8,128)(2,1)} %param.3, pred[8]{0:T(512)(128)(4,1)S(1)} %iota_compare_fusion), kind=kLoop, calls=%fused_computation | loop fusion | flops 114688 | bytes 458760 | tf_op jit(solution)/shard_map/jit(_where)/select_n | solution.py:281
  31.0 0.5 %collective-permute-start.22 = (bf16[8,6144]{1,0:T(8,128)(2,1)S(1)}, bf16[8,6144]{1,0:T(8,128)(2,1)S(1)}, u32[]{:S(2)}, u32[]{:S(2)}) collective-permute-start(bf16[8,6144]{1,0:T(8,128)(2,1)S(1)} %collective-permute-done.10.refs_11_), channel_id=1, source_target_pairs={{0,1},{1,0},{2,3},{3,2},{4,5},{5,4},{6,7},{7,6},{8,9},{9,8},{10,11... | collective-permute-start | bytes 294920 | tf_op jit(solution)/shard_map/ppermute | solution.py:154
  31.5 0.8 %pad_add_fusion.table_ref = s32[152]{0:T(256)S(1)} fusion(s32[136]{0:T(256)} %param.5, s32[16]{0:T(128)} %param.4), kind=kLoop, calls=%fused_computation.1 | loop fusion | flops 152 | bytes 1216 | tf_op jit(solution)/shard_map/concatenate | solution.py:283
  32.3 0.2 collective-permute-done.22.refs_23_
  32.5 0.0 collective-permute-done.21.refs_22_
  32.5 0.0 collective-permute-done.17.refs_18_
  32.5 12.7 %shard_map.37 = f32[11,896,896]{2,1,0:T(8,128)} custom-call(s32[1]{0:T(128)} %bitcast.device_ref, s32[152]{0:T(256)S(1)} %pad_add_fusion.table_ref, bf16[8,14336]{1,0:T(8,128)(2,1)S(1)} %broadcast_select_fusion.refs_0_, bf16[8,8192]{1,0:T(8,128)(2,1)S(1)} %collective-permute-done.refs_1_, bf16[8,6144]{1,0:T(8,128)(2,1)S(1)} %collective-permute-done.1.refs_2_, ...), custom_call_target="tpu_custom_call" | custom-call | flops 2260729856 | bytes 35323904 | tf_op jit(solution)/shard_map/pallas_call | solution.py:284
  (5 shorter events, 0.0 us)
Async XLA Ops:
  0.0 9.0 %collective-permute-start.2 = (bf16[8,14336]{1,0:T(8,128)(2,1)}, bf16[8,14336]{1,0:T(8,128)(2,1)S(1)}, u32[]{:S(2)}, u32[]{:S(2)}) collective-permute-start(bf16[8,14336]{1,0:T(8,128)(2,1)} %param.3), channel_id=1, source_target_pairs={{0,2},{1,5},{2,6},{3,1},{4,0},{5,9},{6,10},{7,3},{8,4},{9,13},{10,... | collective-permute-start | bytes 688136 | tf_op jit(solution)/shard_map/ppermute | solution.py:154
  3.9 7.5 %collective-permute-start = (bf16[8,8192]{1,0:T(8,128)(2,1)S(1)}, bf16[8,8192]{1,0:T(8,128)(2,1)S(1)}, u32[]{:S(2)}, u32[]{:S(2)}) collective-permute-start(bf16[8,8192]{1,0:T(8,128)(2,1)S(1)} %bitcast.7), channel_id=1, source_target_pairs={{0,4},{1,3},{2,0},{3,7},{4,8},{5,1},{6,2},{7,11},{8,12},{9,5},{10,... | collective-permute-start | bytes 393224 | tf_op jit(solution)/shard_map/ppermute | solution.py:154
  4.9 6.5 %collective-permute-start.1 = (bf16[8,6144]{1,0:T(8,128)(2,1)S(1)}, bf16[8,6144]{1,0:T(8,128)(2,1)S(1)}, u32[]{:S(2)}, u32[]{:S(2)}) collective-permute-start(bf16[8,6144]{1,0:T(8,128)(2,1)S(1)} %bitcast.8), channel_id=1, source_target_pairs={{0,4},{1,3},{2,0},{3,7},{4,8},{5,1},{6,2},{7,11},{8,12},{9,5},{10,... | collective-permute-start | bytes 294920 | tf_op jit(solution)/shard_map/ppermute | solution.py:154
  9.0 7.4 %collective-permute-start.5 = (bf16[8,14336]{1,0:T(8,128)(2,1)S(1)}, bf16[8,14336]{1,0:T(8,128)(2,1)S(1)}, u32[]{:S(2)}, u32[]{:S(2)}) collective-permute-start(bf16[8,14336]{1,0:T(8,128)(2,1)S(1)} %collective-permute-done.2.refs_3_), channel_id=1, source_target_pairs={{0,2},{1,5},{2,6},{3,1},{4,0},{5,9},{6,10},{7,3},{8,4},{9,13},{10,... | collective-permute-start | bytes 688136 | tf_op jit(solution)/shard_map/ppermute | solution.py:154
  11.4 7.7 %collective-permute-start.11 = (bf16[8,14336]{1,0:T(8,128)(2,1)}, bf16[8,14336]{1,0:T(8,128)(2,1)S(1)}, u32[]{:S(2)}, u32[]{:S(2)}) collective-permute-start(bf16[8,14336]{1,0:T(8,128)(2,1)} %param.3), channel_id=1, source_target_pairs={{0,1},{1,0},{2,3},{3,2},{4,5},{5,4},{6,7},{7,6},{8,9},{9,8},{10,11... | collective-permute-start | bytes 688136 | tf_op jit(solution)/shard_map/ppermute | solution.py:154
  11.4 5.0 %collective-permute-start.3 = (bf16[8,8192]{1,0:T(8,128)(2,1)S(1)}, bf16[8,8192]{1,0:T(8,128)(2,1)S(1)}, u32[]{:S(2)}, u32[]{:S(2)}) collective-permute-start(bf16[8,8192]{1,0:T(8,128)(2,1)S(1)} %collective-permute-done.refs_1_), channel_id=1, source_target_pairs={{0,4},{1,3},{2,0},{3,7},{4,8},{5,1},{6,2},{7,11},{8,12},{9,5},{10,... | collective-permute-start | bytes 393224 | tf_op jit(solution)/shard_map/ppermute | solution.py:154
  11.4 2.8 %collective-permute-start.13 = (bf16[8,6144]{1,0:T(8,128)(2,1)S(1)}, bf16[8,6144]{1,0:T(8,128)(2,1)S(1)}, u32[]{:S(2)}, u32[]{:S(2)}) collective-permute-start(bf16[8,6144]{1,0:T(8,128)(2,1)S(1)} %collective-permute-done.1.refs_2_), channel_id=1, source_target_pairs={{0,1},{1,0},{2,3},{3,2},{4,5},{5,4},{6,7},{7,6},{8,9},{9,8},{10,11... | collective-permute-start | bytes 294920 | tf_op jit(solution)/shard_map/ppermute | solution.py:154
  13.3 5.4 %collective-permute-start.4 = (bf16[8,6144]{1,0:T(8,128)(2,1)S(1)}, bf16[8,6144]{1,0:T(8,128)(2,1)S(1)}, u32[]{:S(2)}, u32[]{:S(2)}) collective-permute-start(bf16[8,6144]{1,0:T(8,128)(2,1)S(1)} %collective-permute-done.1.refs_2_), channel_id=1, source_target_pairs={{0,4},{1,3},{2,0},{3,7},{4,8},{5,1},{6,2},{7,11},{8,12},{9,5},{10,... | collective-permute-start | bytes 294920 | tf_op jit(solution)/shard_map/ppermute | solution.py:154
  14.2 5.9 %collective-permute-start.12 = (bf16[8,8192]{1,0:T(8,128)(2,1)S(1)}, bf16[8,8192]{1,0:T(8,128)(2,1)S(1)}, u32[]{:S(2)}, u32[]{:S(2)}) collective-permute-start(bf16[8,8192]{1,0:T(8,128)(2,1)S(1)} %collective-permute-done.refs_1_), channel_id=1, source_target_pairs={{0,1},{1,0},{2,3},{3,2},{4,5},{5,4},{6,7},{7,6},{8,9},{9,8},{10,11... | collective-permute-start | bytes 393224 | tf_op jit(solution)/shard_map/ppermute | solution.py:154
  16.4 5.0 %collective-permute-start.6 = (bf16[8,8192]{1,0:T(8,128)(2,1)S(1)}, bf16[8,8192]{1,0:T(8,128)(2,1)S(1)}, u32[]{:S(2)}, u32[]{:S(2)}) collective-permute-start(bf16[8,8192]{1,0:T(8,128)(2,1)S(1)} %collective-permute-done.3.refs_4_), channel_id=1, source_target_pairs={{0,4},{1,3},{2,0},{3,7},{4,8},{5,1},{6,2},{7,11},{8,12},{9,5},{10,... | collective-permute-start | bytes 393224 | tf_op jit(solution)/shard_map/ppermute | solution.py:154
  16.4 13.5 %collective-permute-start.8 = (bf16[8,14336]{1,0:T(8,128)(2,1)S(1)}, bf16[8,14336]{1,0:T(8,128)(2,1)S(1)}, u32[]{:S(2)}, u32[]{:S(2)}) collective-permute-start(bf16[8,14336]{1,0:T(8,128)(2,1)S(1)} %collective-permute-done.5.refs_6_), channel_id=1, source_target_pairs={{0,2},{1,5},{2,6},{3,1},{4,0},{5,9},{6,10},{7,3},{8,4},{9,13},{10,... | collective-permute-start | bytes 688136 | tf_op jit(solution)/shard_map/ppermute | solution.py:154
  18.6 5.7 %collective-permute-start.7 = (bf16[8,6144]{1,0:T(8,128)(2,1)S(1)}, bf16[8,6144]{1,0:T(8,128)(2,1)S(1)}, u32[]{:S(2)}, u32[]{:S(2)}) collective-permute-start(bf16[8,6144]{1,0:T(8,128)(2,1)S(1)} %collective-permute-done.4.refs_5_), channel_id=1, source_target_pairs={{0,4},{1,3},{2,0},{3,7},{4,8},{5,1},{6,2},{7,11},{8,12},{9,5},{10,... | collective-permute-start | bytes 294920 | tf_op jit(solution)/shard_map/ppermute | solution.py:154
  19.1 5.7 %collective-permute-start.16 = (bf16[8,6144]{1,0:T(8,128)(2,1)S(1)}, bf16[8,6144]{1,0:T(8,128)(2,1)S(1)}, u32[]{:S(2)}, u32[]{:S(2)}) collective-permute-start(bf16[8,6144]{1,0:T(8,128)(2,1)S(1)} %collective-permute-done.4.refs_5_), channel_id=1, source_target_pairs={{0,1},{1,0},{2,3},{3,2},{4,5},{5,4},{6,7},{7,6},{8,9},{9,8},{10,11... | collective-permute-start | bytes 294920 | tf_op jit(solution)/shard_map/ppermute | solution.py:154
  20.1 5.9 %collective-permute-start.15 = (bf16[8,8192]{1,0:T(8,128)(2,1)S(1)}, bf16[8,8192]{1,0:T(8,128)(2,1)S(1)}, u32[]{:S(2)}, u32[]{:S(2)}) collective-permute-start(bf16[8,8192]{1,0:T(8,128)(2,1)S(1)} %collective-permute-done.3.refs_4_), channel_id=1, source_target_pairs={{0,1},{1,0},{2,3},{3,2},{4,5},{5,4},{6,7},{7,6},{8,9},{9,8},{10,11... | collective-permute-start | bytes 393224 | tf_op jit(solution)/shard_map/ppermute | solution.py:154
  21.4 8.0 %collective-permute-start.9 = (bf16[8,8192]{1,0:T(8,128)(2,1)S(1)}, bf16[8,8192]{1,0:T(8,128)(2,1)S(1)}, u32[]{:S(2)}, u32[]{:S(2)}) collective-permute-start(bf16[8,8192]{1,0:T(8,128)(2,1)S(1)} %collective-permute-done.6.refs_7_), channel_id=1, source_target_pairs={{0,4},{1,3},{2,0},{3,7},{4,8},{5,1},{6,2},{7,11},{8,12},{9,5},{10,... | collective-permute-start | bytes 393224 | tf_op jit(solution)/shard_map/ppermute | solution.py:154
  24.3 2.7 %collective-permute-start.19 = (bf16[8,6144]{1,0:T(8,128)(2,1)S(1)}, bf16[8,6144]{1,0:T(8,128)(2,1)S(1)}, u32[]{:S(2)}, u32[]{:S(2)}) collective-permute-start(bf16[8,6144]{1,0:T(8,128)(2,1)S(1)} %collective-permute-done.7.refs_8_), channel_id=1, source_target_pairs={{0,1},{1,0},{2,3},{3,2},{4,5},{5,4},{6,7},{7,6},{8,9},{9,8},{10,11... | collective-permute-start | bytes 294920 | tf_op jit(solution)/shard_map/ppermute | solution.py:154
  24.8 4.6 %collective-permute-start.10 = (bf16[8,6144]{1,0:T(8,128)(2,1)S(1)}, bf16[8,6144]{1,0:T(8,128)(2,1)S(1)}, u32[]{:S(2)}, u32[]{:S(2)}) collective-permute-start(bf16[8,6144]{1,0:T(8,128)(2,1)S(1)} %collective-permute-done.7.refs_8_), channel_id=1, source_target_pairs={{0,4},{1,3},{2,0},{3,7},{4,8},{5,1},{6,2},{7,11},{8,12},{9,5},{10,... | collective-permute-start | bytes 294920 | tf_op jit(solution)/shard_map/ppermute | solution.py:154
  26.0 5.0 %collective-permute-start.14 = (bf16[8,14336]{1,0:T(8,128)(2,1)S(1)}, bf16[8,14336]{1,0:T(8,128)(2,1)S(1)}, u32[]{:S(2)}, u32[]{:S(2)}) collective-permute-start(bf16[8,14336]{1,0:T(8,128)(2,1)S(1)} %collective-permute-done.2.refs_3_), channel_id=1, source_target_pairs={{0,1},{1,0},{2,3},{3,2},{4,5},{5,4},{6,7},{7,6},{8,9},{9,8},{10,11... | collective-permute-start | bytes 688136 | tf_op jit(solution)/shard_map/ppermute | solution.py:154
  27.0 5.5 %collective-permute-start.18 = (bf16[8,8192]{1,0:T(8,128)(2,1)S(1)}, bf16[8,8192]{1,0:T(8,128)(2,1)S(1)}, u32[]{:S(2)}, u32[]{:S(2)}) collective-permute-start(bf16[8,8192]{1,0:T(8,128)(2,1)S(1)} %collective-permute-done.6.refs_7_), channel_id=1, source_target_pairs={{0,1},{1,0},{2,3},{3,2},{4,5},{5,4},{6,7},{7,6},{8,9},{9,8},{10,11... | collective-permute-start | bytes 393224 | tf_op jit(solution)/shard_map/ppermute | solution.py:154
  29.4 3.1 %collective-permute-start.17 = (bf16[8,14336]{1,0:T(8,128)(2,1)S(1)}, bf16[8,14336]{1,0:T(8,128)(2,1)S(1)}, u32[]{:S(2)}, u32[]{:S(2)}) collective-permute-start(bf16[8,14336]{1,0:T(8,128)(2,1)S(1)} %collective-permute-done.5.refs_6_), channel_id=1, source_target_pairs={{0,1},{1,0},{2,3},{3,2},{4,5},{5,4},{6,7},{7,6},{8,9},{9,8},{10,11... | collective-permute-start | bytes 688136 | tf_op jit(solution)/shard_map/ppermute | solution.py:154
  29.4 3.1 %collective-permute-start.21 = (bf16[8,8192]{1,0:T(8,128)(2,1)S(1)}, bf16[8,8192]{1,0:T(8,128)(2,1)S(1)}, u32[]{:S(2)}, u32[]{:S(2)}) collective-permute-start(bf16[8,8192]{1,0:T(8,128)(2,1)S(1)} %collective-permute-done.9.refs_10_), channel_id=1, source_target_pairs={{0,1},{1,0},{2,3},{3,2},{4,5},{5,4},{6,7},{7,6},{8,9},{9,8},{10,11... | collective-permute-start | bytes 393224 | tf_op jit(solution)/shard_map/ppermute | solution.py:154
  29.9 2.6 %collective-permute-start.20 = (bf16[8,14336]{1,0:T(8,128)(2,1)S(1)}, bf16[8,14336]{1,0:T(8,128)(2,1)S(1)}, u32[]{:S(2)}, u32[]{:S(2)}) collective-permute-start(bf16[8,14336]{1,0:T(8,128)(2,1)S(1)} %collective-permute-done.8.refs_9_), channel_id=1, source_target_pairs={{0,1},{1,0},{2,3},{3,2},{4,5},{5,4},{6,7},{7,6},{8,9},{9,8},{10,11... | collective-permute-start | bytes 688136 | tf_op jit(solution)/shard_map/ppermute | solution.py:154
  31.0 1.5 %collective-permute-start.22 = (bf16[8,6144]{1,0:T(8,128)(2,1)S(1)}, bf16[8,6144]{1,0:T(8,128)(2,1)S(1)}, u32[]{:S(2)}, u32[]{:S(2)}) collective-permute-start(bf16[8,6144]{1,0:T(8,128)(2,1)S(1)} %collective-permute-done.10.refs_11_), channel_id=1, source_target_pairs={{0,1},{1,0},{2,3},{3,2},{4,5},{5,4},{6,7},{7,6},{8,9},{9,8},{10,11... | collective-permute-start | bytes 294920 | tf_op jit(solution)/shard_map/ppermute | solution.py:154

commit v5 on v4

--- a/solution.py
+++ b/solution.py
@@ -153,18 +153,28 @@
     def send(values, target):
         return [lax.ppermute(value, "col", list(enumerate(target))) for value in values]
 
+    def after(values, others):
+        return list(lax.optimization_barrier((*values, *others))[:len(values)])
+
     chips = devices // 2
     ahead, back = parts, [tokens]
     slabs, passed = [], [send([tokens], sibling)]
     for step in range(1, chips // 2 + 1):
+        if step > 1:
+            ahead = ahead[:1] + after(ahead[1:], ahead[:1])
         ahead = send(ahead, onward)
         slabs.append(ahead)
-        passed.append(send(ahead, sibling))
         if 2 * step < chips:
-            back = send(back, backward)
+            back = send(back if step == 1 else after(back, ahead_before[-1:]), backward)
             slabs.append(back)
-            passed.append(send(back, sibling))
-    return slabs + passed
+            passed += [(ahead, back), (back, None)]
+        else:
+            passed.append((ahead, None))
+        ahead_before = ahead
+    beside = passed[:1]
+    for values, others in passed[1:]:
+        beside.append(send(after(values, others) if others else values, sibling))
+    return slabs + beside
 
 
 def slab_origin(devices, device, number):
@@ -277,8 +287,8 @@
         by_block[:, :, start:stop].reshape(slab, devices * (stop - start))
         for start, stop in ((0, first), (first, width)) if start < stop
     ]
-    kept = jnp.arange(slab, dtype=jnp.int32)[:, None] < slab_lengths[device]
-    slabs = [[jnp.where(kept, tokens, jnp.zeros_like(tokens))]] + ring_gather(tokens, parts, devices)
+    parts = list(lax.optimization_barrier(tuple(parts)))
+    slabs = [parts] + ring_gather(tokens, parts, devices)
     sizes = [[value.shape[1] // devices for value in group] for group in slabs]
     table = jnp.concatenate([slab_lengths, tile_owner])
     return pl.pallas_call(

time: 45.5 us -> 45.7 us (level)
  starting transfers between devices: 17.4 us -> 19.1 us
  other arithmetic: 2.43 us -> 0.75 us
    ppermute x23, starting transfers between devices: 17.4 us -> 19.1 us  [send(): lax.ppermute(value, 'col', list(enumerate(target)))]
    unnamed x0 -> x4, local copies, waits for them, and re-layouts: none -> 1.53 us
    dynamic_slice x1 -> x0, local copies, waits for them, and re-layouts: 1.24 us -> none  [ring_form(): kept = jnp.arange(slab, dtype=jnp.int32)[:, None] < slab_lengths[device]]
    select_n x1 -> x0, other arithmetic: 1.02 us -> none  [ring_form(): jnp.where(kept, tokens, jnp.zeros_like(tokens))]
    lt x1 -> x0, other arithmetic: 0.65 us -> none  [ring_form(): kept = jnp.arange(slab, dtype=jnp.int32)[:, None] < slab_lengths[device]]
  transfers between devices with their start and end apart: 23 -> 23, of which waited for: 7 -> 7; matrix products, arithmetic and copies ran while one was open for 12% -> 6% of each run, Pallas kernels for 0% -> 0%
where the time goes in v5:
time: 45.7 us; the launch traced here: 45.5 us
  starting transfers between devices  19.1 us (42%)
  Pallas kernels  12.7 us (28%)
  waiting for transfers between devices  9.6 us (21%)
  local copies, waits for them, and re-layouts  3.38 us (7%)
  other arithmetic  0.75 us (2%)
    ppermute x23, starting transfers between devices, send(): lax.ppermute(value, 'col', list(enumerate(target)))  19.1 us
    pallas_call x1, Pallas kernels, ring_form(): pl.pallas_call(functools.partial(ring_kernel, devices, slots, sizes), out...  12.7 us
    ppermute x23, waiting for transfers between devices, send(): lax.ppermute(value, 'col', list(enumerate(target)))  9.6 us
    slice x2, local copies, waits for them, and re-layouts, ring_form(): by_block[:, :, start:stop].reshape(slab, devices * (stop - start))  1.85 us
    unnamed x4, local copies, waits for them, and re-layouts  1.53 us
  transfers between devices with their start and end apart: 23, of which 7 were waited for; matrix products, arithmetic and copies ran while one was open for 6% of the time, Pallas kernels for 0%

profile of v5, /device:TPU:0, one launch (start us, length us, event | category | flops | bytes accessed | tf_op | source)
XLA Modules:
  0.0 45.5 jit_solution(8113730810621738035)
XLA Ops:
  0.0 2.9 %collective-permute-start.2 = (bf16[8,14336]{1,0:T(8,128)(2,1)}, bf16[8,14336]{1,0:T(8,128)(2,1)S(1)}, u32[]{:S(2)}, u32[]{:S(2)}) collective-permute-start(bf16[8,14336]{1,0:T(8,128)(2,1)} %param.3), channel_id=1, source_target_pairs={{0,2},{1,5},{2,6},{3,1},{4,0},{5,9},{6,10},{7,3},{8,4},{9,13},{10,... | collective-permute-start | bytes 688136 | tf_op jit(solution)/shard_map/ppermute | solution.py:154
  2.9 0.9 %slice.9 = bf16[8,16,384]{2,0,1:T(8,128)(2,1)S(1)} slice(bf16[8,16,896]{2,0,1:T(8,128)(2,1)} %bitcast.8), slice={[0:8], [0:16], [512:896]} | slice | bytes 196608 | tf_op jit(solution)/shard_map/slice | solution.py:287
  3.9 0.9 %slice.8 = bf16[8,16,512]{2,0,1:T(8,128)(2,1)S(1)} slice(bf16[8,16,896]{2,0,1:T(8,128)(2,1)} %bitcast.9), slice={[0:8], [0:16], [0:512]} | slice | bytes 262144 | tf_op jit(solution)/shard_map/slice | solution.py:287
  4.8 0.1 collective-permute-start.1
  4.9 2.0 %collective-permute-start = (bf16[8,8192]{1,0:T(8,128)(2,1)S(1)}, bf16[8,8192]{1,0:T(8,128)(2,1)S(1)}, u32[]{:S(2)}, u32[]{:S(2)}) collective-permute-start(bf16[8,8192]{1,0:T(8,128)(2,1)S(1)} %bitcast.4), channel_id=1, source_target_pairs={{0,4},{1,3},{2,0},{3,7},{4,8},{5,1},{6,2},{7,11},{8,12},{9,5},{10,... | collective-permute-start | bytes 393224 | tf_op jit(solution)/shard_map/ppermute | solution.py:154
  7.0 2.5 %collective-permute-done.1.refs_3_ = bf16[8,6144]{1,0:T(8,128)(2,1)S(1)} collective-permute-done((bf16[8,6144]{1,0:T(8,128)(2,1)S(1)}, bf16[8,6144]{1,0:T(8,128)(2,1)S(1)}, u32[]{:S(2)}, u32[]{:S(2)}) %collective-permute-start.1) | collective-permute-done | bytes 98336 | tf_op jit(solution)/shard_map/ppermute | solution.py:154
  9.5 0.0 collective-permute-done.2.refs_4_
  9.5 1.6 %collective-permute-start.5 = (bf16[8,14336]{1,0:T(8,128)(2,1)S(1)}, bf16[8,14336]{1,0:T(8,128)(2,1)S(1)}, u32[]{:S(2)}, u32[]{:S(2)}) collective-permute-start(bf16[8,14336]{1,0:T(8,128)(2,1)S(1)} %collective-permute-done.2.refs_4_), channel_id=1, source_target_pairs={{0,2},{1,5},{2,6},{3,1},{4,0},{5,9},{6,10},{7,3},{8,4},{9,13},{10,... | collective-permute-start | bytes 688136 | tf_op jit(solution)/shard_map/ppermute | solution.py:154
  11.0 0.0 collective-permute-start.11
  11.1 0.0 collective-permute-done.refs_2_
  11.1 0.9 %collective-permute-start.3 = (bf16[8,8192]{1,0:T(8,128)(2,1)S(1)}, bf16[8,8192]{1,0:T(8,128)(2,1)S(1)}, u32[]{:S(2)}, u32[]{:S(2)}) collective-permute-start(bf16[8,8192]{1,0:T(8,128)(2,1)S(1)} %collective-permute-done.refs_2_), channel_id=1, source_target_pairs={{0,4},{1,3},{2,0},{3,7},{4,8},{5,1},{6,2},{7,11},{8,12},{9,5},{10,... | collective-permute-start | bytes 393224 | tf_op jit(solution)/shard_map/ppermute | solution.py:154
  11.9 1.6 %collective-permute-start.4 = (bf16[8,6144]{1,0:T(8,128)(2,1)S(1)}, bf16[8,6144]{1,0:T(8,128)(2,1)S(1)}, u32[]{:S(2)}, u32[]{:S(2)}) collective-permute-start(bf16[8,6144]{1,0:T(8,128)(2,1)S(1)} %collective-permute-done.1.refs_3_), channel_id=1, source_target_pairs={{0,4},{1,3},{2,0},{3,7},{4,8},{5,1},{6,2},{7,11},{8,12},{9,5},{10,... | collective-permute-start | bytes 294920 | tf_op jit(solution)/shard_map/ppermute | solution.py:154
  13.5 2.5 %collective-permute-done.3.refs_5_ = bf16[8,8192]{1,0:T(8,128)(2,1)S(1)} collective-permute-done((bf16[8,8192]{1,0:T(8,128)(2,1)S(1)}, bf16[8,8192]{1,0:T(8,128)(2,1)S(1)}, u32[]{:S(2)}, u32[]{:S(2)}) %collective-permute-start.3) | collective-permute-done | bytes 131104 | tf_op jit(solution)/shard_map/ppermute | solution.py:154
  16.0 0.9 %collective-permute-start.6 = (bf16[8,8192]{1,0:T(8,128)(2,1)S(1)}, bf16[8,8192]{1,0:T(8,128)(2,1)S(1)}, u32[]{:S(2)}, u32[]{:S(2)}) collective-permute-start(bf16[8,8192]{1,0:T(8,128)(2,1)S(1)} %collective-permute-done.3.refs_5_), channel_id=1, source_target_pairs={{0,4},{1,3},{2,0},{3,7},{4,8},{5,1},{6,2},{7,11},{8,12},{9,5},{10,... | collective-permute-start | bytes 393224 | tf_op jit(solution)/shard_map/ppermute | solution.py:154
  16.9 0.2 collective-permute-done.4.refs_6_
  17.1 1.4 %collective-permute-start.7 = (bf16[8,6144]{1,0:T(8,128)(2,1)S(1)}, bf16[8,6144]{1,0:T(8,128)(2,1)S(1)}, u32[]{:S(2)}, u32[]{:S(2)}) collective-permute-start(bf16[8,6144]{1,0:T(8,128)(2,1)S(1)} %collective-permute-done.4.refs_6_), channel_id=1, source_target_pairs={{0,4},{1,3},{2,0},{3,7},{4,8},{5,1},{6,2},{7,11},{8,12},{9,5},{10,... | collective-permute-start | bytes 294920 | tf_op jit(solution)/shard_map/ppermute | solution.py:154
  18.5 1.1 %collective-permute-start.14 = (bf16[8,14336]{1,0:T(8,128)(2,1)S(1)}, bf16[8,14336]{1,0:T(8,128)(2,1)S(1)}, u32[]{:S(2)}, u32[]{:S(2)}) collective-permute-start(bf16[8,14336]{1,0:T(8,128)(2,1)S(1)} %collective-permute-done.2.refs_4_), channel_id=1, source_target_pairs={{0,1},{1,0},{2,3},{3,2},{4,5},{5,4},{6,7},{7,6},{8,9},{9,8},{10,11... | collective-permute-start | bytes 688136 | tf_op jit(solution)/shard_map/ppermute | solution.py:154
  19.6 0.0 collective-permute-done.5.refs_7_
  19.6 1.5 %collective-permute-start.8 = (bf16[8,14336]{1,0:T(8,128)(2,1)S(1)}, bf16[8,14336]{1,0:T(8,128)(2,1)S(1)}, u32[]{:S(2)}, u32[]{:S(2)}) collective-permute-start(bf16[8,14336]{1,0:T(8,128)(2,1)S(1)} %collective-permute-done.5.refs_7_), channel_id=1, source_target_pairs={{0,2},{1,5},{2,6},{3,1},{4,0},{5,9},{6,10},{7,3},{8,4},{9,13},{10,... | collective-permute-start | bytes 688136 | tf_op jit(solution)/shard_map/ppermute | solution.py:154
  21.1 0.0 collective-permute-done.11.refs_13_
  21.1 0.0 collective-permute-start.13
  21.1 0.9 %collective-permute-done.7.refs_9_ = bf16[8,6144]{1,0:T(8,128)(2,1)S(1)} collective-permute-done((bf16[8,6144]{1,0:T(8,128)(2,1)S(1)}, bf16[8,6144]{1,0:T(8,128)(2,1)S(1)}, u32[]{:S(2)}, u32[]{:S(2)}) %collective-permute-start.7) | collective-permute-done | bytes 98336 | tf_op jit(solution)/shard_map/ppermute | solution.py:154
  22.0 0.1 collective-permute-start.12
  22.2 0.0 collective-permute-done.6.refs_8_
  22.2 0.9 %collective-permute-start.9 = (bf16[8,8192]{1,0:T(8,128)(2,1)S(1)}, bf16[8,8192]{1,0:T(8,128)(2,1)S(1)}, u32[]{:S(2)}, u32[]{:S(2)}) collective-permute-start(bf16[8,8192]{1,0:T(8,128)(2,1)S(1)} %collective-permute-done.6.refs_8_), channel_id=1, source_target_pairs={{0,4},{1,3},{2,0},{3,7},{4,8},{5,1},{6,2},{7,11},{8,12},{9,5},{10,... | collective-permute-start | bytes 393224 | tf_op jit(solution)/shard_map/ppermute | solution.py:154
  23.1 0.0 collective-permute-done.13.refs_15_
  23.1 1.6 %collective-permute-start.10 = (bf16[8,6144]{1,0:T(8,128)(2,1)S(1)}, bf16[8,6144]{1,0:T(8,128)(2,1)S(1)}, u32[]{:S(2)}, u32[]{:S(2)}) collective-permute-start(bf16[8,6144]{1,0:T(8,128)(2,1)S(1)} %collective-permute-done.7.refs_9_), channel_id=1, source_target_pairs={{0,4},{1,3},{2,0},{3,7},{4,8},{5,1},{6,2},{7,11},{8,12},{9,5},{10,... | collective-permute-start | bytes 294920 | tf_op jit(solution)/shard_map/ppermute | solution.py:154
  24.7 0.8 %collective-permute-start.15 = (bf16[8,8192]{1,0:T(8,128)(2,1)S(1)}, bf16[8,8192]{1,0:T(8,128)(2,1)S(1)}, u32[]{:S(2)}, u32[]{:S(2)}) collective-permute-start(bf16[8,8192]{1,0:T(8,128)(2,1)S(1)} %collective-permute-done.3.refs_5_), channel_id=1, source_target_pairs={{0,1},{1,0},{2,3},{3,2},{4,5},{5,4},{6,7},{7,6},{8,9},{9,8},{10,11... | collective-permute-start | bytes 393224 | tf_op jit(solution)/shard_map/ppermute | solution.py:154
  25.5 0.0 collective-permute-done.14.refs_16_
  25.5 0.1 collective-permute-start.16
  25.5 2.6 %collective-permute-done.10.refs_12_ = bf16[8,6144]{1,0:T(8,128)(2,1)S(1)} collective-permute-done((bf16[8,6144]{1,0:T(8,128)(2,1)S(1)}, bf16[8,6144]{1,0:T(8,128)(2,1)S(1)}, u32[]{:S(2)}, u32[]{:S(2)}) %collective-permute-start.10) | collective-permute-done | bytes 98336 | tf_op jit(solution)/shard_map/ppermute | solution.py:154
  28.2 0.0 collective-permute-start.17
  28.2 0.0 collective-permute-done.9.refs_11_
  28.2 0.5 %collective-permute-start.22 = (bf16[8,6144]{1,0:T(8,128)(2,1)S(1)}, bf16[8,6144]{1,0:T(8,128)(2,1)S(1)}, u32[]{:S(2)}, u32[]{:S(2)}) collective-permute-start(bf16[8,6144]{1,0:T(8,128)(2,1)S(1)} %collective-permute-done.10.refs_12_), channel_id=1, source_target_pairs={{0,1},{1,0},{2,3},{3,2},{4,5},{5,4},{6,7},{7,6},{8,9},{9,8},{10,11... | collective-permute-start | bytes 294920 | tf_op jit(solution)/shard_map/ppermute | solution.py:154
  28.7 0.0 collective-permute-done.8.refs_10_
  28.7 0.1 collective-permute-start.20
  28.8 0.4 collective-permute-start.21
  29.2 0.6 %collective-permute-done.22.refs_24_ = bf16[8,6144]{1,0:T(8,128)(2,1)S(1)} collective-permute-done((bf16[8,6144]{1,0:T(8,128)(2,1)S(1)}, bf16[8,6144]{1,0:T(8,128)(2,1)S(1)}, u32[]{:S(2)}, u32[]{:S(2)}) %collective-permute-start.22) | collective-permute-done | bytes 98336 | tf_op jit(solution)/shard_map/ppermute | solution.py:154
  29.8 0.6 %copy-done = bf16[8,6144]{1,0:T(8,128)(2,1)} copy-done((bf16[8,6144]{1,0:T(8,128)(2,1)}, bf16[8,6144]{1,0:T(8,128)(2,1)S(1)}, u32[]{:S(2)}) %copy-start) | copy-done | bytes 98328
  30.5 0.2 collective-permute-start.18
  30.6 0.0 collective-permute-done.15.refs_17_
  30.6 0.3 collective-permute-start.19
  31.0 0.8 %pad_add_fusion.table_ref = s32[152]{0:T(256)S(1)} fusion(s32[136]{0:T(256)} %param.5, s32[16]{0:T(128)} %param.4), kind=kLoop, calls=%fused_computation | loop fusion | flops 152 | bytes 1216 | tf_op jit(solution)/shard_map/concatenate | solution.py:293
  31.7 0.0 collective-permute-done.21.refs_23_
  31.7 0.0 collective-permute-done.17.refs_19_
  31.7 0.2 collective-permute-done.19.refs_21_
  32.0 0.9 %copy-done.1 = bf16[8,6144]{1,0:T(8,128)(2,1)S(1)} copy-done((bf16[8,6144]{1,0:T(8,128)(2,1)S(1)}, bf16[8,6144]{1,0:T(8,128)(2,1)}, u32[]{:S(2)}) %copy-start.1) | copy-done | bytes 98328
  32.9 12.7 %shard_map.37 = f32[11,896,896]{2,1,0:T(8,128)} custom-call(s32[1]{0:T(128)} %bitcast.device_ref, s32[152]{0:T(256)S(1)} %pad_add_fusion.table_ref, bf16[8,8192]{1,0:T(8,128)(2,1)S(1)} %bitcast.5, bf16[8,6144]{1,0:T(8,128)(2,1)S(1)} %bitcast.7, bf16[8,8192]{1,0:T(8,128)(2,1)S(1)} %collective-permute-done.refs_2_, ...), custom_call_target="tpu_custom_call" | custom-call | flops 2260729856 | bytes 35323904 | tf_op jit(solution)/shard_map/pallas_call | solution.py:294
  (6 shorter events, 0.0 us)
Async XLA Ops:
  0.0 9.5 %collective-permute-start.2 = (bf16[8,14336]{1,0:T(8,128)(2,1)}, bf16[8,14336]{1,0:T(8,128)(2,1)S(1)}, u32[]{:S(2)}, u32[]{:S(2)}) collective-permute-start(bf16[8,14336]{1,0:T(8,128)(2,1)} %param.3), channel_id=1, source_target_pairs={{0,2},{1,5},{2,6},{3,1},{4,0},{5,9},{6,10},{7,3},{8,4},{9,13},{10,... | collective-permute-start | bytes 688136 | tf_op jit(solution)/shard_map/ppermute | solution.py:154
  4.8 4.7 %collective-permute-start.1 = (bf16[8,6144]{1,0:T(8,128)(2,1)S(1)}, bf16[8,6144]{1,0:T(8,128)(2,1)S(1)}, u32[]{:S(2)}, u32[]{:S(2)}) collective-permute-start(bf16[8,6144]{1,0:T(8,128)(2,1)S(1)} %bitcast.6), channel_id=1, source_target_pairs={{0,4},{1,3},{2,0},{3,7},{4,8},{5,1},{6,2},{7,11},{8,12},{9,5},{10,... | collective-permute-start | bytes 294920 | tf_op jit(solution)/shard_map/ppermute | solution.py:154
  4.9 6.1 %collective-permute-start = (bf16[8,8192]{1,0:T(8,128)(2,1)S(1)}, bf16[8,8192]{1,0:T(8,128)(2,1)S(1)}, u32[]{:S(2)}, u32[]{:S(2)}) collective-permute-start(bf16[8,8192]{1,0:T(8,128)(2,1)S(1)} %bitcast.4), channel_id=1, source_target_pairs={{0,4},{1,3},{2,0},{3,7},{4,8},{5,1},{6,2},{7,11},{8,12},{9,5},{10,... | collective-permute-start | bytes 393224 | tf_op jit(solution)/shard_map/ppermute | solution.py:154
  9.5 10.1 %collective-permute-start.5 = (bf16[8,14336]{1,0:T(8,128)(2,1)S(1)}, bf16[8,14336]{1,0:T(8,128)(2,1)S(1)}, u32[]{:S(2)}, u32[]{:S(2)}) collective-permute-start(bf16[8,14336]{1,0:T(8,128)(2,1)S(1)} %collective-permute-done.2.refs_4_), channel_id=1, source_target_pairs={{0,2},{1,5},{2,6},{3,1},{4,0},{5,9},{6,10},{7,3},{8,4},{9,13},{10,... | collective-permute-start | bytes 688136 | tf_op jit(solution)/shard_map/ppermute | solution.py:154
  11.0 10.1 %collective-permute-start.11 = (bf16[8,14336]{1,0:T(8,128)(2,1)}, bf16[8,14336]{1,0:T(8,128)(2,1)S(1)}, u32[]{:S(2)}, u32[]{:S(2)}) collective-permute-start(bf16[8,14336]{1,0:T(8,128)(2,1)} %param.3), channel_id=1, source_target_pairs={{0,1},{1,0},{2,3},{3,2},{4,5},{5,4},{6,7},{7,6},{8,9},{9,8},{10,11... | collective-permute-start | bytes 688136 | tf_op jit(solution)/shard_map/ppermute | solution.py:154
  11.1 5.0 %collective-permute-start.3 = (bf16[8,8192]{1,0:T(8,128)(2,1)S(1)}, bf16[8,8192]{1,0:T(8,128)(2,1)S(1)}, u32[]{:S(2)}, u32[]{:S(2)}) collective-permute-start(bf16[8,8192]{1,0:T(8,128)(2,1)S(1)} %collective-permute-done.refs_2_), channel_id=1, source_target_pairs={{0,4},{1,3},{2,0},{3,7},{4,8},{5,1},{6,2},{7,11},{8,12},{9,5},{10,... | collective-permute-start | bytes 393224 | tf_op jit(solution)/shard_map/ppermute | solution.py:154
  11.9 5.1 %collective-permute-start.4 = (bf16[8,6144]{1,0:T(8,128)(2,1)S(1)}, bf16[8,6144]{1,0:T(8,128)(2,1)S(1)}, u32[]{:S(2)}, u32[]{:S(2)}) collective-permute-start(bf16[8,6144]{1,0:T(8,128)(2,1)S(1)} %collective-permute-done.1.refs_3_), channel_id=1, source_target_pairs={{0,4},{1,3},{2,0},{3,7},{4,8},{5,1},{6,2},{7,11},{8,12},{9,5},{10,... | collective-permute-start | bytes 294920 | tf_op jit(solution)/shard_map/ppermute | solution.py:154
  16.0 6.1 %collective-permute-start.6 = (bf16[8,8192]{1,0:T(8,128)(2,1)S(1)}, bf16[8,8192]{1,0:T(8,128)(2,1)S(1)}, u32[]{:S(2)}, u32[]{:S(2)}) collective-permute-start(bf16[8,8192]{1,0:T(8,128)(2,1)S(1)} %collective-permute-done.3.refs_5_), channel_id=1, source_target_pairs={{0,4},{1,3},{2,0},{3,7},{4,8},{5,1},{6,2},{7,11},{8,12},{9,5},{10,... | collective-permute-start | bytes 393224 | tf_op jit(solution)/shard_map/ppermute | solution.py:154
  17.1 5.0 %collective-permute-start.7 = (bf16[8,6144]{1,0:T(8,128)(2,1)S(1)}, bf16[8,6144]{1,0:T(8,128)(2,1)S(1)}, u32[]{:S(2)}, u32[]{:S(2)}) collective-permute-start(bf16[8,6144]{1,0:T(8,128)(2,1)S(1)} %collective-permute-done.4.refs_6_), channel_id=1, source_target_pairs={{0,4},{1,3},{2,0},{3,7},{4,8},{5,1},{6,2},{7,11},{8,12},{9,5},{10,... | collective-permute-start | bytes 294920 | tf_op jit(solution)/shard_map/ppermute | solution.py:154
  18.5 7.0 %collective-permute-start.14 = (bf16[8,14336]{1,0:T(8,128)(2,1)S(1)}, bf16[8,14336]{1,0:T(8,128)(2,1)S(1)}, u32[]{:S(2)}, u32[]{:S(2)}) collective-permute-start(bf16[8,14336]{1,0:T(8,128)(2,1)S(1)} %collective-permute-done.2.refs_4_), channel_id=1, source_target_pairs={{0,1},{1,0},{2,3},{3,2},{4,5},{5,4},{6,7},{7,6},{8,9},{9,8},{10,11... | collective-permute-start | bytes 688136 | tf_op jit(solution)/shard_map/ppermute | solution.py:154
  19.6 9.1 %collective-permute-start.8 = (bf16[8,14336]{1,0:T(8,128)(2,1)S(1)}, bf16[8,14336]{1,0:T(8,128)(2,1)S(1)}, u32[]{:S(2)}, u32[]{:S(2)}) collective-permute-start(bf16[8,14336]{1,0:T(8,128)(2,1)S(1)} %collective-permute-done.5.refs_7_), channel_id=1, source_target_pairs={{0,2},{1,5},{2,6},{3,1},{4,0},{5,9},{6,10},{7,3},{8,4},{9,13},{10,... | collective-permute-start | bytes 688136 | tf_op jit(solution)/shard_map/ppermute | solution.py:154
  21.1 2.0 %collective-permute-start.13 = (bf16[8,6144]{1,0:T(8,128)(2,1)S(1)}, bf16[8,6144]{1,0:T(8,128)(2,1)S(1)}, u32[]{:S(2)}, u32[]{:S(2)}) collective-permute-start(bf16[8,6144]{1,0:T(8,128)(2,1)S(1)} %collective-permute-done.1.refs_3_), channel_id=1, source_target_pairs={{0,1},{1,0},{2,3},{3,2},{4,5},{5,4},{6,7},{7,6},{8,9},{9,8},{10,11... | collective-permute-start | bytes 294920 | tf_op jit(solution)/shard_map/ppermute | solution.py:154
  22.0 2.7 %collective-permute-start.12 = (bf16[8,8192]{1,0:T(8,128)(2,1)S(1)}, bf16[8,8192]{1,0:T(8,128)(2,1)S(1)}, u32[]{:S(2)}, u32[]{:S(2)}) collective-permute-start(bf16[8,8192]{1,0:T(8,128)(2,1)S(1)} %collective-permute-done.refs_2_), channel_id=1, source_target_pairs={{0,1},{1,0},{2,3},{3,2},{4,5},{5,4},{6,7},{7,6},{8,9},{9,8},{10,11... | collective-permute-start | bytes 393224 | tf_op jit(solution)/shard_map/ppermute | solution.py:154
  22.2 6.0 %collective-permute-start.9 = (bf16[8,8192]{1,0:T(8,128)(2,1)S(1)}, bf16[8,8192]{1,0:T(8,128)(2,1)S(1)}, u32[]{:S(2)}, u32[]{:S(2)}) collective-permute-start(bf16[8,8192]{1,0:T(8,128)(2,1)S(1)} %collective-permute-done.6.refs_8_), channel_id=1, source_target_pairs={{0,4},{1,3},{2,0},{3,7},{4,8},{5,1},{6,2},{7,11},{8,12},{9,5},{10,... | collective-permute-start | bytes 393224 | tf_op jit(solution)/shard_map/ppermute | solution.py:154
  23.1 5.1 %collective-permute-start.10 = (bf16[8,6144]{1,0:T(8,128)(2,1)S(1)}, bf16[8,6144]{1,0:T(8,128)(2,1)S(1)}, u32[]{:S(2)}, u32[]{:S(2)}) collective-permute-start(bf16[8,6144]{1,0:T(8,128)(2,1)S(1)} %collective-permute-done.7.refs_9_), channel_id=1, source_target_pairs={{0,4},{1,3},{2,0},{3,7},{4,8},{5,1},{6,2},{7,11},{8,12},{9,5},{10,... | collective-permute-start | bytes 294920 | tf_op jit(solution)/shard_map/ppermute | solution.py:154
  24.7 5.9 %collective-permute-start.15 = (bf16[8,8192]{1,0:T(8,128)(2,1)S(1)}, bf16[8,8192]{1,0:T(8,128)(2,1)S(1)}, u32[]{:S(2)}, u32[]{:S(2)}) collective-permute-start(bf16[8,8192]{1,0:T(8,128)(2,1)S(1)} %collective-permute-done.3.refs_5_), channel_id=1, source_target_pairs={{0,1},{1,0},{2,3},{3,2},{4,5},{5,4},{6,7},{7,6},{8,9},{9,8},{10,11... | collective-permute-start | bytes 393224 | tf_op jit(solution)/shard_map/ppermute | solution.py:154
  25.5 3.3 %collective-permute-start.16 = (bf16[8,6144]{1,0:T(8,128)(2,1)S(1)}, bf16[8,6144]{1,0:T(8,128)(2,1)S(1)}, u32[]{:S(2)}, u32[]{:S(2)}) collective-permute-start(bf16[8,6144]{1,0:T(8,128)(2,1)S(1)} %collective-permute-done.4.refs_6_), channel_id=1, source_target_pairs={{0,1},{1,0},{2,3},{3,2},{4,5},{5,4},{6,7},{7,6},{8,9},{9,8},{10,11... | collective-permute-start | bytes 294920 | tf_op jit(solution)/shard_map/ppermute | solution.py:154
  28.2 3.5 %collective-permute-start.17 = (bf16[8,14336]{1,0:T(8,128)(2,1)S(1)}, bf16[8,14336]{1,0:T(8,128)(2,1)S(1)}, u32[]{:S(2)}, u32[]{:S(2)}) collective-permute-start(bf16[8,14336]{1,0:T(8,128)(2,1)S(1)} %collective-permute-done.5.refs_7_), channel_id=1, source_target_pairs={{0,1},{1,0},{2,3},{3,2},{4,5},{5,4},{6,7},{7,6},{8,9},{9,8},{10,11... | collective-permute-start | bytes 688136 | tf_op jit(solution)/shard_map/ppermute | solution.py:154
  28.2 1.6 %collective-permute-start.22 = (bf16[8,6144]{1,0:T(8,128)(2,1)S(1)}, bf16[8,6144]{1,0:T(8,128)(2,1)S(1)}, u32[]{:S(2)}, u32[]{:S(2)}) collective-permute-start(bf16[8,6144]{1,0:T(8,128)(2,1)S(1)} %collective-permute-done.10.refs_12_), channel_id=1, source_target_pairs={{0,1},{1,0},{2,3},{3,2},{4,5},{5,4},{6,7},{7,6},{8,9},{9,8},{10,11... | collective-permute-start | bytes 294920 | tf_op jit(solution)/shard_map/ppermute | solution.py:154
  28.7 3.3 %collective-permute-start.20 = (bf16[8,14336]{1,0:T(8,128)(2,1)S(1)}, bf16[8,14336]{1,0:T(8,128)(2,1)S(1)}, u32[]{:S(2)}, u32[]{:S(2)}) collective-permute-start(bf16[8,14336]{1,0:T(8,128)(2,1)S(1)} %collective-permute-done.8.refs_10_), channel_id=1, source_target_pairs={{0,1},{1,0},{2,3},{3,2},{4,5},{5,4},{6,7},{7,6},{8,9},{9,8},{10,11... | collective-permute-start | bytes 688136 | tf_op jit(solution)/shard_map/ppermute | solution.py:154
  28.8 3.0 %collective-permute-start.21 = (bf16[8,8192]{1,0:T(8,128)(2,1)S(1)}, bf16[8,8192]{1,0:T(8,128)(2,1)S(1)}, u32[]{:S(2)}, u32[]{:S(2)}) collective-permute-start(bf16[8,8192]{1,0:T(8,128)(2,1)S(1)} %collective-permute-done.9.refs_11_), channel_id=1, source_target_pairs={{0,1},{1,0},{2,3},{3,2},{4,5},{5,4},{6,7},{7,6},{8,9},{9,8},{10,11... | collective-permute-start | bytes 393224 | tf_op jit(solution)/shard_map/ppermute | solution.py:154
  29.8 0.6 %copy-start = (bf16[8,6144]{1,0:T(8,128)(2,1)}, bf16[8,6144]{1,0:T(8,128)(2,1)S(1)}, u32[]{:S(2)}) copy-start(bf16[8,6144]{1,0:T(8,128)(2,1)S(1)} %collective-permute-done.22.refs_24_) | copy-start | bytes 294916
  30.5 1.5 %collective-permute-start.18 = (bf16[8,8192]{1,0:T(8,128)(2,1)S(1)}, bf16[8,8192]{1,0:T(8,128)(2,1)S(1)}, u32[]{:S(2)}, u32[]{:S(2)}) collective-permute-start(bf16[8,8192]{1,0:T(8,128)(2,1)S(1)} %collective-permute-done.6.refs_8_), channel_id=1, source_target_pairs={{0,1},{1,0},{2,3},{3,2},{4,5},{5,4},{6,7},{7,6},{8,9},{9,8},{10,11... | collective-permute-start | bytes 393224 | tf_op jit(solution)/shard_map/ppermute | solution.py:154
  30.6 1.3 %collective-permute-start.19 = (bf16[8,6144]{1,0:T(8,128)(2,1)S(1)}, bf16[8,6144]{1,0:T(8,128)(2,1)S(1)}, u32[]{:S(2)}, u32[]{:S(2)}) collective-permute-start(bf16[8,6144]{1,0:T(8,128)(2,1)S(1)} %collective-permute-done.7.refs_9_), channel_id=1, source_target_pairs={{0,1},{1,0},{2,3},{3,2},{4,5},{5,4},{6,7},{7,6},{8,9},{9,8},{10,11... | collective-permute-start | bytes 294920 | tf_op jit(solution)/shard_map/ppermute | solution.py:154
  32.0 0.9 %copy-start.1 = (bf16[8,6144]{1,0:T(8,128)(2,1)S(1)}, bf16[8,6144]{1,0:T(8,128)(2,1)}, u32[]{:S(2)}) copy-start(bf16[8,6144]{1,0:T(8,128)(2,1)} %copy-done) | copy-start | bytes 294916

commit v6 on v3

--- a/solution.py
+++ b/solution.py
@@ -8,7 +8,7 @@
 from jax.sharding import PartitionSpec as P
 
 BUFFERS = 4
-RING_LIMIT = 16
+RING_DEVICES = 16
 
 
 def tile_number(devices, device, partner):
@@ -137,36 +137,46 @@
     chips = devices // 2
     order = list(range(0, chips, 2)) + list(range(1, chips, 2))[::-1]
     place = {chip: at for at, chip in enumerate(order)}
-    onward = []
-    for device in range(devices):
+
+    def moved(device, hops):
         chip, core = divmod(device, 2)
-        step = 1 if core == 0 else -1
-        onward.append(order[(place[chip] + step) % chips] * 2 + core)
-    backward = [onward.index(device) for device in range(devices)]
-    return onward, backward
-
-
-def ring_gather(tokens, devices):
-    onward, backward = ring_plan(devices)
+        return order[(place[chip] + (hops if core == 0 else -hops)) % chips] * 2 + core
+
+    def target(hops):
+        return [moved(device, hops) for device in range(devices)]
+
+    return target, place
+
+
+def ring_gather(tokens, device, devices):
+    target, place = ring_plan(devices)
     sibling = [device ^ 1 for device in range(devices)]
+    corner = [place[at // 2] in (0, 3, 4, 7) for at in range(devices)]
+    across = [at ^ 2 for at in range(devices)]
 
     def send(value, target):
         return lax.ppermute(value, "col", list(enumerate(target)))
 
-    chips = devices // 2
-    beside = send(tokens, sibling)
-    later, beside = lax.optimization_barrier((tokens, beside))
-    ahead, back = tokens, later
-    slabs, passed = [tokens], [beside]
-    for step in range(1, chips // 2 + 1):
-        ahead = send(ahead, onward)
-        slabs.append(ahead)
-        passed.append(send(ahead, sibling))
-        if 2 * step < chips:
-            back = send(back, backward)
-            slabs.append(back)
-            passed.append(send(back, sibling))
-    return slabs + passed
+    def after(value, *others):
+        return lax.optimization_barrier((value, *others))[0]
+
+    straight = send(tokens, [there if corner[at] else at for at, there in enumerate(target(4))])
+    own = send(tokens, list(range(devices)))
+    ahead, back = [tokens], [tokens]
+    for _ in range(3):
+        ahead.append(send(ahead[-1], target(1)))
+        back.append(send(back[-1], target(-1)))
+    chip, core = device // 2, device % 2
+    at_corner = (chip < 2) | (chip >= devices // 2 - 2)
+    came_ahead = ((chip == 3) | (chip == 4)) == (core == 0)
+    held = jnp.where(at_corner, after(straight, ahead[2], back[2]), jnp.where(came_ahead, ahead[1], back[1]))
+    half = send(held, [at if corner[at] else across[at] for at in range(devices)])
+    slabs = [own, ahead[1], back[1], ahead[2], back[2], ahead[3], back[3], half]
+    beside = [
+        tokens, after(ahead[1], back[1]), after(back[1], ahead[1]), after(ahead[2], back[2]),
+        after(back[2], ahead[2]), ahead[3], back[3], half,
+    ]
+    return slabs + [send(value, sibling) for value in beside]
 
 
 def slab_origin(devices, device, number):
@@ -269,9 +279,7 @@
 def ring_form(tokens, slab_lengths, tile_owner, devices, device, slots):
     slab, units = tokens.shape
     width = units // devices
-    slabs = ring_gather(tokens, devices)
-    kept = jnp.arange(slab, dtype=jnp.int32)[:, None] < slab_lengths[device]
-    slabs[0] = jnp.where(kept, tokens, jnp.zeros_like(tokens))
+    slabs = ring_gather(tokens, device, devices)
     table = jnp.concatenate([slab_lengths, tile_owner])
     return pl.pallas_call(
         functools.partial(ring_kernel, devices, slots),
@@ -300,7 +308,7 @@
     device = lax.axis_index("col").astype(jnp.int32)
     slots = devices // 2 + devices // 8 + 1
     width = tokens.shape[1] // devices
-    form = ring_form if devices <= RING_LIMIT and width % 128 == 0 else gathered_form
+    form = ring_form if devices == RING_DEVICES and width % 128 == 0 else gathered_form
     return form(tokens, slab_lengths, tile_owner, devices, device, slots)
 
 

time: 45.8 us -> 45.6 us (level)
  starting transfers between devices: 9.56 us -> 16.8 us
  waiting for transfers between devices: 19.5 us -> 14.9 us
  other arithmetic: 2.43 us -> 0.79 us
  local copies, waits for them, and re-layouts: 1.24 us -> 0 us
    ppermute x15 -> x17, starting transfers between devices: 9.56 us -> 16.8 us  [send(): return lax.ppermute(value, 'col', list(enumerate(target)))]
    ppermute x15 -> x17, waiting for transfers between devices: 19.5 us -> 14.9 us  [send(): return lax.ppermute(value, 'col', list(enumerate(target)))]
    dynamic_slice x1 -> x0, local copies, waits for them, and re-layouts: 1.24 us -> none  [ring_form(): kept = jnp.arange(slab, dtype=jnp.int32)[:, None] < slab_lengths[device]]
    select_n x1, other arithmetic: 1.02 us -> 0.03 us  [ring_gather(): jnp.where(at_corner, after(straight, ahead[2], back[2]), jnp.where(came_a...]
    lt x1 -> x0, other arithmetic: 0.65 us -> none  [ring_form(): kept = jnp.arange(slab, dtype=jnp.int32)[:, None] < slab_lengths[device]]
  transfers between devices with their start and end apart: 15 -> 17, of which waited for: 6 -> 6; matrix products, arithmetic and copies ran while one was open for 8% -> 2% of each run, Pallas kernels for 0% -> 0%
where the time goes in v6:
time: 45.6 us; the launch traced here: 45.2 us
  starting transfers between devices  16.8 us (37%)
  waiting for transfers between devices  14.9 us (33%)
  Pallas kernels  12.7 us (28%)
  other arithmetic  0.79 us (2%)
    ppermute x17, starting transfers between devices, send(): return lax.ppermute(value, 'col', list(enumerate(target)))  16.8 us
    ppermute x17, waiting for transfers between devices, send(): return lax.ppermute(value, 'col', list(enumerate(target)))  14.9 us
    pallas_call x1, Pallas kernels, ring_form(): pl.pallas_call(functools.partial(ring_kernel, devices, slots), out_shape=...  12.7 us
  transfers between devices with their start and end apart: 17, of which 6 were waited for; matrix products, arithmetic and copies ran while one was open for 2% of the time, Pallas kernels for 0%

profile of v6, /device:TPU:0, one launch (start us, length us, event | category | flops | bytes accessed | tf_op | source)
XLA Modules:
  0.0 45.2 jit_solution(5904732923244263312)
XLA Ops:
  0.0 2.9 %collective-permute-start.2 = (bf16[8,14336]{1,0:T(8,128)(2,1)}, bf16[8,14336]{1,0:T(8,128)(2,1)S(1)}, u32[]{:S(2)}, u32[]{:S(2)}) collective-permute-start(bf16[8,14336]{1,0:T(8,128)(2,1)} %param.3), channel_id=1, source_target_pairs={{0,2},{1,5},{2,6},{3,1},{4,0},{5,9},{6,10},{7,3},{8,4},{9,13},{10,... | collective-permute-start | bytes 688136 | tf_op jit(solution)/shard_map/ppermute | solution.py:158
  2.9 0.1 collective-permute-start.1
  3.0 6.9 %collective-permute-start.7 = (bf16[8,14336]{1,0:T(8,128)(2,1)}, bf16[8,14336]{1,0:T(8,128)(2,1)S(1)}, u32[]{:S(2)}, u32[]{:S(2)}) collective-permute-start(bf16[8,14336]{1,0:T(8,128)(2,1)} %param.3), channel_id=1, source_target_pairs={{0,14},{1,15},{2,12},{3,13},{4,4},{5,5},{6,6},{7,7},{8,8},{9,9},{1... | collective-permute-start | bytes 688136 | tf_op jit(solution)/shard_map/ppermute | solution.py:158
  9.9 0.0 collective-permute-done.2.refs_2_
  9.9 0.7 %collective-permute-start.4 = (bf16[8,14336]{1,0:T(8,128)(2,1)S(1)}, bf16[8,14336]{1,0:T(8,128)(2,1)S(1)}, u32[]{:S(2)}, u32[]{:S(2)}) collective-permute-start(bf16[8,14336]{1,0:T(8,128)(2,1)S(1)} %collective-permute-done.2.refs_2_), channel_id=1, source_target_pairs={{0,2},{1,5},{2,6},{3,1},{4,0},{5,9},{6,10},{7,3},{8,4},{9,13},{10,... | collective-permute-start | bytes 688136 | tf_op jit(solution)/shard_map/ppermute | solution.py:158
  10.6 0.0 collective-permute-done.1.refs_1_
  10.6 1.4 %collective-permute-start.3 = (bf16[8,14336]{1,0:T(8,128)(2,1)S(1)}, bf16[8,14336]{1,0:T(8,128)(2,1)S(1)}, u32[]{:S(2)}, u32[]{:S(2)}) collective-permute-start(bf16[8,14336]{1,0:T(8,128)(2,1)S(1)} %collective-permute-done.1.refs_1_), channel_id=1, source_target_pairs={{0,4},{1,3},{2,0},{3,7},{4,8},{5,1},{6,2},{7,11},{8,12},{9,5},{10,... | collective-permute-start | bytes 688136 | tf_op jit(solution)/shard_map/ppermute | solution.py:158
  12.0 0.9 %collective-permute-start = (bf16[8,14336]{1,0:T(8,128)(2,1)}, bf16[8,14336]{1,0:T(8,128)(2,1)S(1)}, u32[]{:S(2)}, u32[]{:S(2)}) collective-permute-start(bf16[8,14336]{1,0:T(8,128)(2,1)} %param.3), channel_id=1, source_target_pairs={{0,0},{1,1},{2,2},{3,3},{4,4},{5,5},{6,6},{7,7},{8,8},{9,9},{10,10... | collective-permute-start | bytes 688136 | tf_op jit(solution)/shard_map/ppermute | solution.py:158
  12.9 0.0 collective-permute-start.9
  12.9 6.2 %collective-permute-done.7 = bf16[8,14336]{1,0:T(8,128)(2,1)S(1)} collective-permute-done((bf16[8,14336]{1,0:T(8,128)(2,1)}, bf16[8,14336]{1,0:T(8,128)(2,1)S(1)}, u32[]{:S(2)}, u32[]{:S(2)}) %collective-permute-start.7) | collective-permute-done | bytes 229408 | tf_op jit(solution)/shard_map/ppermute | solution.py:158
  19.2 0.0 collective-permute-start.10
  19.2 2.8 %collective-permute-done.4.refs_4_ = bf16[8,14336]{1,0:T(8,128)(2,1)S(1)} collective-permute-done((bf16[8,14336]{1,0:T(8,128)(2,1)S(1)}, bf16[8,14336]{1,0:T(8,128)(2,1)S(1)}, u32[]{:S(2)}, u32[]{:S(2)}) %collective-permute-start.4) | collective-permute-done | bytes 229408 | tf_op jit(solution)/shard_map/ppermute | solution.py:158
  22.0 0.0 collective-permute-start.11
  22.0 0.0 collective-permute-done.3.refs_3_
  22.0 1.1 %collective-permute-start.6 = (bf16[8,14336]{1,0:T(8,128)(2,1)S(1)}, bf16[8,14336]{1,0:T(8,128)(2,1)S(1)}, u32[]{:S(2)}, u32[]{:S(2)}) collective-permute-start(bf16[8,14336]{1,0:T(8,128)(2,1)S(1)} %collective-permute-done.4.refs_4_), channel_id=1, source_target_pairs={{0,2},{1,5},{2,6},{3,1},{4,0},{5,9},{6,10},{7,3},{8,4},{9,13},{10,... | collective-permute-start | bytes 688136 | tf_op jit(solution)/shard_map/ppermute | solution.py:158
  23.2 0.0 collective-permute-done.refs_0_
  23.2 0.9 %collective-permute-start.5 = (bf16[8,14336]{1,0:T(8,128)(2,1)S(1)}, bf16[8,14336]{1,0:T(8,128)(2,1)S(1)}, u32[]{:S(2)}, u32[]{:S(2)}) collective-permute-start(bf16[8,14336]{1,0:T(8,128)(2,1)S(1)} %collective-permute-done.3.refs_3_), channel_id=1, source_target_pairs={{0,4},{1,3},{2,0},{3,7},{4,8},{5,1},{6,2},{7,11},{8,12},{9,5},{10,... | collective-permute-start | bytes 688136 | tf_op jit(solution)/shard_map/ppermute | solution.py:158
  24.1 0.0 collective-permute-done.9.refs_8_
  24.1 0.7 %collective-permute-start.8 = (bf16[8,14336]{1,0:T(8,128)(2,1)S(1)}, bf16[8,14336]{1,0:T(8,128)(2,1)S(1)}, u32[]{:S(2)}, u32[]{:S(2)}) collective-permute-start(bf16[8,14336]{1,0:T(8,128)(2,1)S(1)} %select_select_fusion), channel_id=1, source_target_pairs={{0,0},{1,1},{2,2},{3,3},{4,6},{5,7},{6,4},{7,5},{8,10},{9,11},{10,... | collective-permute-start | bytes 688136 | tf_op jit(solution)/shard_map/ppermute | solution.py:158
  24.8 0.0 collective-permute-done.10.refs_9_
  24.8 0.1 collective-permute-start.12
  24.9 0.0 collective-permute-done.11.refs_10_
  24.9 0.5 %collective-permute-start.13 = (bf16[8,14336]{1,0:T(8,128)(2,1)S(1)}, bf16[8,14336]{1,0:T(8,128)(2,1)S(1)}, u32[]{:S(2)}, u32[]{:S(2)}) collective-permute-start(bf16[8,14336]{1,0:T(8,128)(2,1)S(1)} %collective-permute-done.4.refs_4_), channel_id=1, source_target_pairs={{0,1},{1,0},{2,3},{3,2},{4,5},{5,4},{6,7},{7,6},{8,9},{9,8},{10,11... | collective-permute-start | bytes 688136 | tf_op jit(solution)/shard_map/ppermute | solution.py:158
  25.4 5.0 %collective-permute-done.6.refs_6_ = bf16[8,14336]{1,0:T(8,128)(2,1)S(1)} collective-permute-done((bf16[8,14336]{1,0:T(8,128)(2,1)S(1)}, bf16[8,14336]{1,0:T(8,128)(2,1)S(1)}, u32[]{:S(2)}, u32[]{:S(2)}) %collective-permute-start.6) | collective-permute-done | bytes 229408 | tf_op jit(solution)/shard_map/ppermute | solution.py:158
  30.4 0.0 collective-permute-start.15
  30.4 0.0 collective-permute-done.5.refs_5_
  30.4 0.5 %collective-permute-start.14 = (bf16[8,14336]{1,0:T(8,128)(2,1)S(1)}, bf16[8,14336]{1,0:T(8,128)(2,1)S(1)}, u32[]{:S(2)}, u32[]{:S(2)}) collective-permute-start(bf16[8,14336]{1,0:T(8,128)(2,1)S(1)} %collective-permute-done.5.refs_5_), channel_id=1, source_target_pairs={{0,1},{1,0},{2,3},{3,2},{4,5},{5,4},{6,7},{7,6},{8,9},{9,8},{10,11... | collective-permute-start | bytes 688136 | tf_op jit(solution)/shard_map/ppermute | solution.py:158
  30.9 0.0 collective-permute-done.8.refs_7_
  30.9 0.1 collective-permute-start.16
  31.0 0.8 %pad_add_fusion.table_ref = s32[152]{0:T(256)S(1)} fusion(s32[136]{0:T(256)} %param.5, s32[16]{0:T(128)} %param.4), kind=kLoop, calls=%fused_computation.1 | loop fusion | flops 152 | bytes 1216 | tf_op jit(solution)/shard_map/concatenate | solution.py:283
  31.7 0.0 collective-permute-done.12.refs_11_
  31.7 0.0 collective-permute-done.13.refs_12_
  31.8 0.1 collective-permute-done.15.refs_14_
  31.9 0.3 collective-permute-done.14.refs_13_
  32.2 0.3 collective-permute-done.16.refs_15_
  32.5 12.7 %shard_map.37 = f32[11,896,896]{2,1,0:T(8,128)} custom-call(s32[1]{0:T(128)} %bitcast.device_ref, s32[152]{0:T(256)S(1)} %pad_add_fusion.table_ref, bf16[8,14336]{1,0:T(8,128)(2,1)S(1)} %collective-permute-done.refs_0_, bf16[8,14336]{1,0:T(8,128)(2,1)S(1)} %collective-permute-done.1.refs_1_, bf16[8,14336]{1,0:T(8,128)(2,1)S(1)} %collective-permute-done.2.refs_2_, ...), custom_call_target="tpu_custom_call" | custom-call | flops 2260729856 | bytes 35323904 | tf_op jit(solution)/shard_map/pallas_call | solution.py:284
  (1 shorter events, 0.0 us)
Async XLA Ops:
  0.0 9.9 %collective-permute-start.2 = (bf16[8,14336]{1,0:T(8,128)(2,1)}, bf16[8,14336]{1,0:T(8,128)(2,1)S(1)}, u32[]{:S(2)}, u32[]{:S(2)}) collective-permute-start(bf16[8,14336]{1,0:T(8,128)(2,1)} %param.3), channel_id=1, source_target_pairs={{0,2},{1,5},{2,6},{3,1},{4,0},{5,9},{6,10},{7,3},{8,4},{9,13},{10,... | collective-permute-start | bytes 688136 | tf_op jit(solution)/shard_map/ppermute | solution.py:158
  2.9 7.7 %collective-permute-start.1 = (bf16[8,14336]{1,0:T(8,128)(2,1)}, bf16[8,14336]{1,0:T(8,128)(2,1)S(1)}, u32[]{:S(2)}, u32[]{:S(2)}) collective-permute-start(bf16[8,14336]{1,0:T(8,128)(2,1)} %param.3), channel_id=1, source_target_pairs={{0,4},{1,3},{2,0},{3,7},{4,8},{5,1},{6,2},{7,11},{8,12},{9,5},{10,... | collective-permute-start | bytes 688136 | tf_op jit(solution)/shard_map/ppermute | solution.py:158
  3.0 16.2 %collective-permute-start.7 = (bf16[8,14336]{1,0:T(8,128)(2,1)}, bf16[8,14336]{1,0:T(8,128)(2,1)S(1)}, u32[]{:S(2)}, u32[]{:S(2)}) collective-permute-start(bf16[8,14336]{1,0:T(8,128)(2,1)} %param.3), channel_id=1, source_target_pairs={{0,14},{1,15},{2,12},{3,13},{4,4},{5,5},{6,6},{7,7},{8,8},{9,9},{1... | collective-permute-start | bytes 688136 | tf_op jit(solution)/shard_map/ppermute | solution.py:158
  9.9 12.1 %collective-permute-start.4 = (bf16[8,14336]{1,0:T(8,128)(2,1)S(1)}, bf16[8,14336]{1,0:T(8,128)(2,1)S(1)}, u32[]{:S(2)}, u32[]{:S(2)}) collective-permute-start(bf16[8,14336]{1,0:T(8,128)(2,1)S(1)} %collective-permute-done.2.refs_2_), channel_id=1, source_target_pairs={{0,2},{1,5},{2,6},{3,1},{4,0},{5,9},{6,10},{7,3},{8,4},{9,13},{10,... | collective-permute-start | bytes 688136 | tf_op jit(solution)/shard_map/ppermute | solution.py:158
  10.6 11.4 %collective-permute-start.3 = (bf16[8,14336]{1,0:T(8,128)(2,1)S(1)}, bf16[8,14336]{1,0:T(8,128)(2,1)S(1)}, u32[]{:S(2)}, u32[]{:S(2)}) collective-permute-start(bf16[8,14336]{1,0:T(8,128)(2,1)S(1)} %collective-permute-done.1.refs_1_), channel_id=1, source_target_pairs={{0,4},{1,3},{2,0},{3,7},{4,8},{5,1},{6,2},{7,11},{8,12},{9,5},{10,... | collective-permute-start | bytes 688136 | tf_op jit(solution)/shard_map/ppermute | solution.py:158
  12.0 11.2 %collective-permute-start = (bf16[8,14336]{1,0:T(8,128)(2,1)}, bf16[8,14336]{1,0:T(8,128)(2,1)S(1)}, u32[]{:S(2)}, u32[]{:S(2)}) collective-permute-start(bf16[8,14336]{1,0:T(8,128)(2,1)} %param.3), channel_id=1, source_target_pairs={{0,0},{1,1},{2,2},{3,3},{4,4},{5,5},{6,6},{7,7},{8,8},{9,9},{10,10... | collective-permute-start | bytes 688136 | tf_op jit(solution)/shard_map/ppermute | solution.py:158
  12.9 11.2 %collective-permute-start.9 = (bf16[8,14336]{1,0:T(8,128)(2,1)}, bf16[8,14336]{1,0:T(8,128)(2,1)S(1)}, u32[]{:S(2)}, u32[]{:S(2)}) collective-permute-start(bf16[8,14336]{1,0:T(8,128)(2,1)} %param.3), channel_id=1, source_target_pairs={{0,1},{1,0},{2,3},{3,2},{4,5},{5,4},{6,7},{7,6},{8,9},{9,8},{10,11... | collective-permute-start | bytes 688136 | tf_op jit(solution)/shard_map/ppermute | solution.py:158
  19.2 5.6 %collective-permute-start.10 = (bf16[8,14336]{1,0:T(8,128)(2,1)S(1)}, bf16[8,14336]{1,0:T(8,128)(2,1)S(1)}, u32[]{:S(2)}, u32[]{:S(2)}) collective-permute-start(bf16[8,14336]{1,0:T(8,128)(2,1)S(1)} %collective-permute-done.1.refs_1_), channel_id=1, source_target_pairs={{0,1},{1,0},{2,3},{3,2},{4,5},{5,4},{6,7},{7,6},{8,9},{9,8},{10,11... | collective-permute-start | bytes 688136 | tf_op jit(solution)/shard_map/ppermute | solution.py:158
  22.0 2.9 %collective-permute-start.11 = (bf16[8,14336]{1,0:T(8,128)(2,1)S(1)}, bf16[8,14336]{1,0:T(8,128)(2,1)S(1)}, u32[]{:S(2)}, u32[]{:S(2)}) collective-permute-start(bf16[8,14336]{1,0:T(8,128)(2,1)S(1)} %collective-permute-done.2.refs_2_), channel_id=1, source_target_pairs={{0,1},{1,0},{2,3},{3,2},{4,5},{5,4},{6,7},{7,6},{8,9},{9,8},{10,11... | collective-permute-start | bytes 688136 | tf_op jit(solution)/shard_map/ppermute | solution.py:158
  22.0 8.4 %collective-permute-start.6 = (bf16[8,14336]{1,0:T(8,128)(2,1)S(1)}, bf16[8,14336]{1,0:T(8,128)(2,1)S(1)}, u32[]{:S(2)}, u32[]{:S(2)}) collective-permute-start(bf16[8,14336]{1,0:T(8,128)(2,1)S(1)} %collective-permute-done.4.refs_4_), channel_id=1, source_target_pairs={{0,2},{1,5},{2,6},{3,1},{4,0},{5,9},{6,10},{7,3},{8,4},{9,13},{10,... | collective-permute-start | bytes 688136 | tf_op jit(solution)/shard_map/ppermute | solution.py:158
  23.2 7.2 %collective-permute-start.5 = (bf16[8,14336]{1,0:T(8,128)(2,1)S(1)}, bf16[8,14336]{1,0:T(8,128)(2,1)S(1)}, u32[]{:S(2)}, u32[]{:S(2)}) collective-permute-start(bf16[8,14336]{1,0:T(8,128)(2,1)S(1)} %collective-permute-done.3.refs_3_), channel_id=1, source_target_pairs={{0,4},{1,3},{2,0},{3,7},{4,8},{5,1},{6,2},{7,11},{8,12},{9,5},{10,... | collective-permute-start | bytes 688136 | tf_op jit(solution)/shard_map/ppermute | solution.py:158
  24.1 6.8 %collective-permute-start.8 = (bf16[8,14336]{1,0:T(8,128)(2,1)S(1)}, bf16[8,14336]{1,0:T(8,128)(2,1)S(1)}, u32[]{:S(2)}, u32[]{:S(2)}) collective-permute-start(bf16[8,14336]{1,0:T(8,128)(2,1)S(1)} %select_select_fusion), channel_id=1, source_target_pairs={{0,0},{1,1},{2,2},{3,3},{4,6},{5,7},{6,4},{7,5},{8,10},{9,11},{10,... | collective-permute-start | bytes 688136 | tf_op jit(solution)/shard_map/ppermute | solution.py:158
  24.8 6.9 %collective-permute-start.12 = (bf16[8,14336]{1,0:T(8,128)(2,1)S(1)}, bf16[8,14336]{1,0:T(8,128)(2,1)S(1)}, u32[]{:S(2)}, u32[]{:S(2)}) collective-permute-start(bf16[8,14336]{1,0:T(8,128)(2,1)S(1)} %collective-permute-done.3.refs_3_), channel_id=1, source_target_pairs={{0,1},{1,0},{2,3},{3,2},{4,5},{5,4},{6,7},{7,6},{8,9},{9,8},{10,11... | collective-permute-start | bytes 688136 | tf_op jit(solution)/shard_map/ppermute | solution.py:158
  24.9 6.8 %collective-permute-start.13 = (bf16[8,14336]{1,0:T(8,128)(2,1)S(1)}, bf16[8,14336]{1,0:T(8,128)(2,1)S(1)}, u32[]{:S(2)}, u32[]{:S(2)}) collective-permute-start(bf16[8,14336]{1,0:T(8,128)(2,1)S(1)} %collective-permute-done.4.refs_4_), channel_id=1, source_target_pairs={{0,1},{1,0},{2,3},{3,2},{4,5},{5,4},{6,7},{7,6},{8,9},{9,8},{10,11... | collective-permute-start | bytes 688136 | tf_op jit(solution)/shard_map/ppermute | solution.py:158
  30.4 1.5 %collective-permute-start.15 = (bf16[8,14336]{1,0:T(8,128)(2,1)S(1)}, bf16[8,14336]{1,0:T(8,128)(2,1)S(1)}, u32[]{:S(2)}, u32[]{:S(2)}) collective-permute-start(bf16[8,14336]{1,0:T(8,128)(2,1)S(1)} %collective-permute-done.6.refs_6_), channel_id=1, source_target_pairs={{0,1},{1,0},{2,3},{3,2},{4,5},{5,4},{6,7},{7,6},{8,9},{9,8},{10,11... | collective-permute-start | bytes 688136 | tf_op jit(solution)/shard_map/ppermute | solution.py:158
  30.4 1.8 %collective-permute-start.14 = (bf16[8,14336]{1,0:T(8,128)(2,1)S(1)}, bf16[8,14336]{1,0:T(8,128)(2,1)S(1)}, u32[]{:S(2)}, u32[]{:S(2)}) collective-permute-start(bf16[8,14336]{1,0:T(8,128)(2,1)S(1)} %collective-permute-done.5.refs_5_), channel_id=1, source_target_pairs={{0,1},{1,0},{2,3},{3,2},{4,5},{5,4},{6,7},{7,6},{8,9},{9,8},{10,11... | collective-permute-start | bytes 688136 | tf_op jit(solution)/shard_map/ppermute | solution.py:158
  30.9 1.6 %collective-permute-start.16 = (bf16[8,14336]{1,0:T(8,128)(2,1)S(1)}, bf16[8,14336]{1,0:T(8,128)(2,1)S(1)}, u32[]{:S(2)}, u32[]{:S(2)}) collective-permute-start(bf16[8,14336]{1,0:T(8,128)(2,1)S(1)} %collective-permute-done.8.refs_7_), channel_id=1, source_target_pairs={{0,1},{1,0},{2,3},{3,2},{4,5},{5,4},{6,7},{7,6},{8,9},{9,8},{10,11... | collective-permute-start | bytes 688136 | tf_op jit(solution)/shard_map/ppermute | solution.py:158

commit v7 on v3

--- a/solution.py
+++ b/solution.py
@@ -8,7 +8,7 @@
 from jax.sharding import PartitionSpec as P
 
 BUFFERS = 4
-RING_LIMIT = 16
+RING_DEVICES = 16
 
 
 def tile_number(devices, device, partner):
@@ -146,27 +146,43 @@
     return onward, backward
 
 
-def ring_gather(tokens, devices):
+GROUPS = ((0, 1, 2), (8, 9, 10), (3, 4), (11, 12), (5, 6, 7), (13, 14, 15))
+EACH = len(GROUPS) - 2
+
+
+def ring_gather(tokens, cuts, devices):
     onward, backward = ring_plan(devices)
     sibling = [device ^ 1 for device in range(devices)]
+    slab, units = tokens.shape
+    width = units // devices
 
     def send(value, target):
         return lax.ppermute(value, "col", list(enumerate(target)))
 
-    chips = devices // 2
-    beside = send(tokens, sibling)
-    later, beside = lax.optimization_barrier((tokens, beside))
-    ahead, back = tokens, later
-    slabs, passed = [tokens], [beside]
-    for step in range(1, chips // 2 + 1):
-        ahead = send(ahead, onward)
-        slabs.append(ahead)
-        passed.append(send(ahead, sibling))
-        if 2 * step < chips:
-            back = send(back, backward)
-            slabs.append(back)
-            passed.append(send(back, sibling))
-    return slabs + passed
+    def after(value, *others):
+        return lax.optimization_barrier((value, *others))[0]
+
+    def part(value, cut):
+        start, stop = cut
+        return value.reshape(slab, devices, width)[:, :, start:stop].reshape(slab, -1)
+
+    ahead, back = send(tokens, onward), send(tokens, backward)
+    near = jnp.concatenate([tokens, ahead, back], axis=0)
+    groups = [near, send(near, sibling)]
+    hops = {}
+    for cut in cuts:
+        ahead_2, back_2 = send(part(ahead, cut), onward), send(part(back, cut), backward)
+        ahead_3, back_3 = send(ahead_2, onward), send(back_2, backward)
+        ahead_4 = send(after(ahead_3, groups[1]) if cut == cuts[0] else ahead_3, onward)
+        hops[cut] = (ahead_2, back_2, ahead_3, back_3, ahead_4)
+    two = [jnp.concatenate(hops[cut][:2], axis=0) for cut in cuts]
+    two = jnp.concatenate(two, axis=1)
+    groups += [two, send(after(two, groups[1]), sibling)]
+    by_cut = []
+    for cut in cuts:
+        three = jnp.concatenate(hops[cut][2:], axis=0)
+        by_cut.append([three, send(three, sibling)])
+    return groups, by_cut
 
 
 def slab_origin(devices, device, number):
@@ -181,45 +197,68 @@
     return 2 * chip + core
 
 
-def ring_kernel(devices, slots, device_ref, table_ref, *refs):
-    slabs = refs[:devices]
-    out_ref, pair, tiles, zeros, out_sems, zero_sems = refs[devices:]
+def ring_kernel(devices, slots, cuts, known, device_ref, table_ref, *refs):
+    whole, both, refs = refs[:2], refs[2:4], refs[4:]
+    by_cut = [refs[2 * at:2 * at + 2] for at in range(known + 1)]
+    refs = refs[2 * (known + 1):]
+    out_ref, pair, tiles, zeros, out_sems, zero_sems = refs[1:] if known else refs
     device = device_ref[0]
-    slab, width = slabs[0].shape[0], pair.shape[2]
+    slab, width = pair.shape[1] // devices, pair.shape[2]
+    done, end = cuts[known] if known else (0, cuts[0][1])
+    pieces = [(done, end, 0, end)] + ([(0, done, done, end)] if known else [])
 
     def owned(partner):
         return table_ref[devices + tile_number(devices, device, partner)] == device
 
-    def put(buffer, slot):
-        return pltpu.make_async_copy(tiles.at[buffer], out_ref.at[slot], out_sems.at[buffer])
+    def put(buffer, slot, piece, top, bottom):
+        _, _, left, right = pieces[piece]
+        rows, columns = pl.ds(top, bottom - top), pl.ds(left, right - left)
+        return pltpu.make_async_copy(
+            tiles.at[buffer, rows, columns], out_ref.at[slot, rows, columns], out_sems.at[buffer, piece]
+        )
+
+    def wait_put(buffer, slot):
+        for piece, (top, bottom, _, _) in enumerate(pieces):
+            put(buffer, slot, piece, top, bottom).wait()
 
     def clear(slot):
         return pltpu.make_async_copy(zeros, out_ref.at[slot], zero_sems.at[slot])
 
     def load_block(partner, masked):
-        columns = pl.ds(pl.multiple_of(partner * width, 128), width)
-        parts = []
-        for at, ref in enumerate(slabs):
-            part = ref[:, columns].astype(jnp.float32)
-            if masked:
-                row = lax.broadcasted_iota(jnp.int32, (slab, width), 0)
-                part = jnp.where(row < table_ref[slab_origin(devices, device, at)], part, 0.0)
-            parts.append(part)
-        pair[0 if masked else 1] = jnp.concatenate(parts, axis=0).astype(jnp.bfloat16)
+        for (start, stop), own_refs in zip(cuts, by_cut):
+            size = stop - start
+            parts = []
+            for at, (numbers, ref) in enumerate(zip(GROUPS, (*whole, *both, *own_refs))):
+                if at < len(whole):
+                    columns = pl.ds(pl.multiple_of(partner * width + start, 128), size)
+                elif at < len(whole) + len(both):
+                    columns = pl.ds(pl.multiple_of(devices * start + partner * size, 128), size)
+                else:
+                    columns = pl.ds(pl.multiple_of(partner * size, 128), size)
+                group = ref[:, columns].astype(jnp.float32)
+                for row, number in enumerate(numbers):
+                    part = group[row * slab:(row + 1) * slab]
+                    if masked:
+                        place = lax.broadcasted_iota(jnp.int32, (slab, size), 0)
+                        part = jnp.where(place < table_ref[slab_origin(devices, device, number)], part, 0.0)
+                    parts.append(part)
+            pair[0 if masked else 1, :, start:stop] = jnp.concatenate(parts, axis=0).astype(jnp.bfloat16)
 
     count = lax.fori_loop(
         0, devices, lambda partner, total: total + owned(partner).astype(jnp.int32), jnp.int32(0)
     )
 
-    @pl.when(count < slots)
-    def _():
-        zeros[...] = jnp.zeros_like(zeros)
-
-    def start_clear(slot, carry):
-        clear(slot).start()
-        return carry
-
-    lax.fori_loop(count, slots, start_clear, 0)
+    if not known:
+
+        @pl.when(count < slots)
+        def _():
+            zeros[...] = jnp.zeros_like(zeros)
+
+        def start_clear(slot, carry):
+            clear(slot).start()
+            return carry
+
+        lax.fori_loop(count, slots, start_clear, 0)
 
     load_block(device, True)
     valid_count = lax.fori_loop(0, devices, lambda at, total: total + table_ref[at], jnp.int32(0))
@@ -235,64 +274,71 @@
 
             @pl.when(slot >= BUFFERS)
             def _():
-                put(buffer, slot - BUFFERS).wait()
-
-            left = (partner <= device).astype(jnp.int32)
-            for row in range(0, width, 128):
-                strip = pl.ds(row, 128)
-                product = lax.dot_general(
-                    pair[left, :, row:row + 128], pair[1 - left], (((0,), (0,)), ((), ())),
-                    preferred_element_type=jnp.float32,
-                )
-                tiles[buffer, strip, :] = product * scale
-                pltpu.make_async_copy(
-                    tiles.at[buffer, strip], out_ref.at[slot, strip], out_sems.at[buffer]
-                ).start()
+                wait_put(buffer, slot - BUFFERS)
+
+            lower = (partner <= device).astype(jnp.int32)
+            for piece, (top, bottom, left, right) in enumerate(pieces):
+                for row in range(top, bottom, 128):
+                    product = lax.dot_general(
+                        pair[lower, :, row:row + 128], pair[1 - lower, :, left:right],
+                        (((0,), (0,)), ((), ())), preferred_element_type=jnp.float32,
+                    )
+                    tiles[buffer, row:row + 128, left:right] = product * scale[:, left:right]
+                    put(buffer, slot, piece, row, row + 128).start()
 
         return slot + mine.astype(jnp.int32)
 
     lax.fori_loop(0, devices, visit, jnp.int32(0))
 
     def drain(slot, carry):
-        put(lax.rem(slot, BUFFERS), slot).wait()
+        wait_put(lax.rem(slot, BUFFERS), slot)
         return carry
 
     lax.fori_loop(jnp.maximum(count - BUFFERS, 0), count, drain, 0)
 
-    def end_clear(slot, carry):
-        clear(slot).wait()
-        return carry
-
-    lax.fori_loop(count, slots, end_clear, 0)
+    if not known:
+
+        def end_clear(slot, carry):
+            clear(slot).wait()
+            return carry
+
+        lax.fori_loop(count, slots, end_clear, 0)
 
 
 def ring_form(tokens, slab_lengths, tile_owner, devices, device, slots):
     slab, units = tokens.shape
     width = units // devices
-    slabs = ring_gather(tokens, devices)
-    kept = jnp.arange(slab, dtype=jnp.int32)[:, None] < slab_lengths[device]
-    slabs[0] = jnp.where(kept, tokens, jnp.zeros_like(tokens))
+    first = -(-width // 256) * 128
+    cuts = [(0, first), (first, width)]
+    whole, by_cut = ring_gather(tokens, cuts, devices)
     table = jnp.concatenate([slab_lengths, tile_owner])
-    return pl.pallas_call(
-        functools.partial(ring_kernel, devices, slots),
-        out_shape=jax.ShapeDtypeStruct((slots, width, width), jnp.float32),
-        in_specs=[pl.BlockSpec(memory_space=pltpu.SMEM)] * 2
-        + [pl.BlockSpec(memory_space=pltpu.VMEM)] * devices,
-        out_specs=pl.BlockSpec(memory_space=pl.ANY),
-        scratch_shapes=[
-            pltpu.VMEM((2, slab * devices, width), jnp.bfloat16),
-            pltpu.VMEM((BUFFERS, width, width), jnp.float32),
-            pltpu.VMEM((width, width), jnp.float32),
-            pltpu.SemaphoreType.DMA((BUFFERS,)),
-            pltpu.SemaphoreType.DMA((slots,)),
-        ],
-        compiler_params=pltpu.CompilerParams(vmem_limit_bytes=32 * 1024 * 1024),
-        cost_estimate=pl.CostEstimate(
-            flops=2 * slots * slab * devices * width * width,
-            bytes_accessed=4 * slots * width * width,
-            transcendentals=0,
-        ),
-    )(device.reshape(1), table, *slabs)
+    result = None
+    for known in range(len(cuts)):
+        groups = whole + sum(by_cut[:known + 1], [])
+        made = cuts[known][1] ** 2 - (cuts[known][0] ** 2 if known else 0)
+        result = pl.pallas_call(
+            functools.partial(ring_kernel, devices, slots, cuts, known),
+            out_shape=jax.ShapeDtypeStruct((slots, width, width), jnp.float32),
+            in_specs=[pl.BlockSpec(memory_space=pltpu.SMEM)] * 2
+            + [pl.BlockSpec(memory_space=pltpu.VMEM)] * len(groups)
+            + [pl.BlockSpec(memory_space=pl.ANY)] * (known > 0),
+            out_specs=pl.BlockSpec(memory_space=pl.ANY),
+            input_output_aliases={2 + len(groups): 0} if known else {},
+            scratch_shapes=[
+                pltpu.VMEM((2, slab * devices, width), jnp.bfloat16),
+                pltpu.VMEM((BUFFERS, width, width), jnp.float32),
+                pltpu.VMEM((width, width), jnp.float32),
+                pltpu.SemaphoreType.DMA((BUFFERS, 2)),
+                pltpu.SemaphoreType.DMA((slots,)),
+            ],
+            compiler_params=pltpu.CompilerParams(vmem_limit_bytes=32 * 1024 * 1024),
+            cost_estimate=pl.CostEstimate(
+                flops=2 * slots * slab * devices * made,
+                bytes_accessed=4 * slots * made,
+                transcendentals=0,
+            ),
+        )(device.reshape(1), table, *groups, *([result] if known else []))
+    return result
 
 
 def per_device(tokens, slab_lengths, tile_owner):
@@ -300,7 +346,7 @@
     device = lax.axis_index("col").astype(jnp.int32)
     slots = devices // 2 + devices // 8 + 1
     width = tokens.shape[1] // devices
-    form = ring_form if devices <= RING_LIMIT and width % 128 == 0 else gathered_form
+    form = ring_form if devices == RING_DEVICES and width % 128 == 0 and width > 128 else gathered_form
     return form(tokens, slab_lengths, tile_owner, devices, device, slots)
 
 

time: 45.8 us -> 46.8 us (1.022)
  starting transfers between devices: 9.56 us -> 15.1 us
  waiting for transfers between devices: 19.5 us -> 14 us
  Pallas kernels: 12.7 us -> 15.4 us
  other arithmetic: 2.43 us -> 0.79 us
    ppermute x15 -> x16, starting transfers between devices: 9.56 us -> 15.1 us  [send(): return lax.ppermute(value, 'col', list(enumerate(target)))]
    ppermute x15 -> x16, waiting for transfers between devices: 19.5 us -> 14 us  [send(): return lax.ppermute(value, 'col', list(enumerate(target)))]
    pallas_call x1 -> x2, Pallas kernels: 12.7 us -> 15.4 us  [ring_form(): pl.pallas_call(functools.partial(ring_kernel, devices, slots, cuts, known...]
    dynamic_slice x1 -> x0, local copies, waits for them, and re-layouts: 1.24 us -> none  [ring_form(): kept = jnp.arange(slab, dtype=jnp.int32)[:, None] < slab_lengths[device]]
    unnamed x0 -> x6, local copies, waits for them, and re-layouts: none -> 1.07 us
    select_n x1 -> x0, other arithmetic: 1.02 us -> none  [ring_form(): slabs[0] = jnp.where(kept, tokens, jnp.zeros_like(tokens))]
    lt x1 -> x0, other arithmetic: 0.65 us -> none  [ring_form(): kept = jnp.arange(slab, dtype=jnp.int32)[:, None] < slab_lengths[device]]
  transfers between devices with their start and end apart: 15 -> 16, of which waited for: 6 -> 9; matrix products, arithmetic and copies ran while one was open for 8% -> 4% of each run, Pallas kernels for 0% -> 19%
where the time goes in v7:
time: 46.8 us; the launch traced here: 46.6 us
  Pallas kernels  15.4 us (33%)
  starting transfers between devices  15.1 us (32%)
  waiting for transfers between devices  14 us (30%)
  local copies, waits for them, and re-layouts  1.15 us (2%)
  other arithmetic  0.79 us (2%)
    pallas_call x2, Pallas kernels, ring_form(): pl.pallas_call(functools.partial(ring_kernel, devices, slots, cuts, known...  15.4 us
    ppermute x16, starting transfers between devices, send(): return lax.ppermute(value, 'col', list(enumerate(target)))  15.1 us
    ppermute x16, waiting for transfers between devices, send(): return lax.ppermute(value, 'col', list(enumerate(target)))  14 us
    unnamed x6, local copies, waits for them, and re-layouts  1.07 us
  transfers between devices with their start and end apart: 16, of which 9 were waited for; matrix products, arithmetic and copies ran while one was open for 4% of the time, Pallas kernels for 19%

profile of v7, /device:TPU:0, one launch (start us, length us, event | category | flops | bytes accessed | tf_op | source)
XLA Modules:
  0.0 46.6 jit_solution(950086006934744173)
XLA Ops:
  0.0 3.0 %collective-permute-start = (bf16[8,14336]{1,0:T(8,128)(2,1)}, bf16[8,14336]{1,0:T(8,128)(2,1)S(1)}, u32[]{:S(2)}, u32[]{:S(2)}) collective-permute-start(bf16[8,14336]{1,0:T(8,128)(2,1)} %param.3), channel_id=1, source_target_pairs={{0,4},{1,3},{2,0},{3,7},{4,8},{5,1},{6,2},{7,11},{8,12},{9,5},{10,... | collective-permute-start | bytes 688136 | tf_op jit(solution)/shard_map/ppermute | solution.py:160
  3.0 0.0 collective-permute-start.1
  3.0 1.0 %constant_dynamic-update-slice_fusion.2 = bf16[24,14336]{1,0:T(8,128)(2,1)S(1)} fusion(bf16[8,14336]{1,0:T(8,128)(2,1)} %param.3), kind=kLoop, calls=%fused_computation.3 | loop fusion | bytes 458752
  4.0 5.0 %collective-permute-done = bf16[8,14336]{1,0:T(8,128)(2,1)S(1)} collective-permute-done((bf16[8,14336]{1,0:T(8,128)(2,1)}, bf16[8,14336]{1,0:T(8,128)(2,1)S(1)}, u32[]{:S(2)}, u32[]{:S(2)}) %collective-permute-start) | collective-permute-done | bytes 229408 | tf_op jit(solution)/shard_map/ppermute | solution.py:160
  9.1 0.2 collective-permute-done.1
  9.3 1.6 %collective-permute-start.5 = (bf16[8,6144]{1,0:T(8,128)(2,1)S(1)}, bf16[8,6144]{1,0:T(8,128)(2,1)S(1)}, u32[]{:S(2)}, u32[]{:S(2)}) collective-permute-start(bf16[8,6144]{1,0:T(8,128)(2,1)S(1)} %bitcast.14), channel_id=1, source_target_pairs={{0,4},{1,3},{2,0},{3,7},{4,8},{5,1},{6,2},{7,11},{8,12},{9,5},{10,... | collective-permute-start | bytes 294920 | tf_op jit(solution)/shard_map/ppermute | solution.py:160
  10.9 1.6 %collective-permute-start.3 = (bf16[8,8192]{1,0:T(8,128)(2,1)S(1)}, bf16[8,8192]{1,0:T(8,128)(2,1)S(1)}, u32[]{:S(2)}, u32[]{:S(2)}) collective-permute-start(bf16[8,8192]{1,0:T(8,128)(2,1)S(1)} %bitcast.12), channel_id=1, source_target_pairs={{0,4},{1,3},{2,0},{3,7},{4,8},{5,1},{6,2},{7,11},{8,12},{9,5},{10,... | collective-permute-start | bytes 393224 | tf_op jit(solution)/shard_map/ppermute | solution.py:160
  12.5 0.4 collective-permute-start.6
  12.9 0.7 %collective-permute-start.4 = (bf16[8,8192]{1,0:T(8,128)(2,1)S(1)}, bf16[8,8192]{1,0:T(8,128)(2,1)S(1)}, u32[]{:S(2)}, u32[]{:S(2)}) collective-permute-start(bf16[8,8192]{1,0:T(8,128)(2,1)S(1)} %bitcast.11), channel_id=1, source_target_pairs={{0,2},{1,5},{2,6},{3,1},{4,0},{5,9},{6,10},{7,3},{8,4},{9,13},{10,... | collective-permute-start | bytes 393224 | tf_op jit(solution)/shard_map/ppermute | solution.py:160
  13.7 0.1 collective-permute-start.2
  13.8 0.4 collective-permute-done.5
  14.2 1.5 %collective-permute-start.12 = (bf16[8,6144]{1,0:T(8,128)(2,1)S(1)}, bf16[8,6144]{1,0:T(8,128)(2,1)S(1)}, u32[]{:S(2)}, u32[]{:S(2)}) collective-permute-start(bf16[8,6144]{1,0:T(8,128)(2,1)S(1)} %collective-permute-done.5), channel_id=1, source_target_pairs={{0,4},{1,3},{2,0},{3,7},{4,8},{5,1},{6,2},{7,11},{8,12},{9,5},{10,... | collective-permute-start | bytes 294920 | tf_op jit(solution)/shard_map/ppermute | solution.py:160
  15.7 1.7 %collective-permute-done.6 = bf16[8,6144]{1,0:T(8,128)(2,1)S(1)} collective-permute-done((bf16[8,6144]{1,0:T(8,128)(2,1)S(1)}, bf16[8,6144]{1,0:T(8,128)(2,1)S(1)}, u32[]{:S(2)}, u32[]{:S(2)}) %collective-permute-start.6) | collective-permute-done | bytes 98336 | tf_op jit(solution)/shard_map/ppermute | solution.py:160
  17.3 0.7 %collective-permute-start.13 = (bf16[8,6144]{1,0:T(8,128)(2,1)S(1)}, bf16[8,6144]{1,0:T(8,128)(2,1)S(1)}, u32[]{:S(2)}, u32[]{:S(2)}) collective-permute-start(bf16[8,6144]{1,0:T(8,128)(2,1)S(1)} %collective-permute-done.6), channel_id=1, source_target_pairs={{0,2},{1,5},{2,6},{3,1},{4,0},{5,9},{6,10},{7,3},{8,4},{9,13},{10,... | collective-permute-start | bytes 294920 | tf_op jit(solution)/shard_map/ppermute | solution.py:160
  18.0 0.0 collective-permute-done.3
  18.0 1.4 %collective-permute-start.8 = (bf16[8,8192]{1,0:T(8,128)(2,1)S(1)}, bf16[8,8192]{1,0:T(8,128)(2,1)S(1)}, u32[]{:S(2)}, u32[]{:S(2)}) collective-permute-start(bf16[8,8192]{1,0:T(8,128)(2,1)S(1)} %collective-permute-done.3), channel_id=1, source_target_pairs={{0,4},{1,3},{2,0},{3,7},{4,8},{5,1},{6,2},{7,11},{8,12},{9,5},{10,... | collective-permute-start | bytes 393224 | tf_op jit(solution)/shard_map/ppermute | solution.py:160
  19.4 0.2 collective-permute-done.4
  19.6 0.5 %collective-permute-start.9 = (bf16[8,8192]{1,0:T(8,128)(2,1)S(1)}, bf16[8,8192]{1,0:T(8,128)(2,1)S(1)}, u32[]{:S(2)}, u32[]{:S(2)}) collective-permute-start(bf16[8,8192]{1,0:T(8,128)(2,1)S(1)} %collective-permute-done.4), channel_id=1, source_target_pairs={{0,2},{1,5},{2,6},{3,1},{4,0},{5,9},{6,10},{7,3},{8,4},{9,13},{10,... | collective-permute-start | bytes 393224 | tf_op jit(solution)/shard_map/ppermute | solution.py:160
  20.1 0.0 collective-permute-done.12
  20.1 1.7 %collective-permute-start.14 = (bf16[8,6144]{1,0:T(8,128)(2,1)S(1)}, bf16[8,6144]{1,0:T(8,128)(2,1)S(1)}, u32[]{:S(2)}, u32[]{:S(2)}) collective-permute-start(bf16[8,6144]{1,0:T(8,128)(2,1)S(1)} %collective-permute-done.12), channel_id=1, source_target_pairs={{0,4},{1,3},{2,0},{3,7},{4,8},{5,1},{6,2},{7,11},{8,12},{9,5},{10,... | collective-permute-start | bytes 294920 | tf_op jit(solution)/shard_map/ppermute | solution.py:160
  21.8 0.6 %collective-permute-done.13 = bf16[8,6144]{1,0:T(8,128)(2,1)S(1)} collective-permute-done((bf16[8,6144]{1,0:T(8,128)(2,1)S(1)}, bf16[8,6144]{1,0:T(8,128)(2,1)S(1)}, u32[]{:S(2)}, u32[]{:S(2)}) %collective-permute-start.13) | collective-permute-done | bytes 98336 | tf_op jit(solution)/shard_map/ppermute | solution.py:160
  22.4 1.9 %collective-permute-done.8 = bf16[8,8192]{1,0:T(8,128)(2,1)S(1)} collective-permute-done((bf16[8,8192]{1,0:T(8,128)(2,1)S(1)}, bf16[8,8192]{1,0:T(8,128)(2,1)S(1)}, u32[]{:S(2)}, u32[]{:S(2)}) %collective-permute-start.8) | collective-permute-done | bytes 131104 | tf_op jit(solution)/shard_map/ppermute | solution.py:160
  24.3 0.0 collective-permute-done.2.refs_1_
  24.3 1.2 %collective-permute-start.10 = (bf16[8,8192]{1,0:T(8,128)(2,1)S(1)}, bf16[8,8192]{1,0:T(8,128)(2,1)S(1)}, u32[]{:S(2)}, u32[]{:S(2)}) collective-permute-start(bf16[8,8192]{1,0:T(8,128)(2,1)S(1)} %collective-permute-done.8), channel_id=1, source_target_pairs={{0,4},{1,3},{2,0},{3,7},{4,8},{5,1},{6,2},{7,11},{8,12},{9,5},{10,... | collective-permute-start | bytes 393224 | tf_op jit(solution)/shard_map/ppermute | solution.py:160
  25.5 0.0 collective-permute-done.9
  25.6 0.1 collective-permute-start.7
  25.6 3.7 %collective-permute-done.10 = bf16[8,8192]{1,0:T(8,128)(2,1)S(1)} collective-permute-done((bf16[8,8192]{1,0:T(8,128)(2,1)S(1)}, bf16[8,8192]{1,0:T(8,128)(2,1)S(1)}, u32[]{:S(2)}, u32[]{:S(2)}) %collective-permute-start.10) | collective-permute-done | bytes 131104 | tf_op jit(solution)/shard_map/ppermute | solution.py:160
  29.4 0.1 collective-permute-start.11
  29.4 0.0 collective-permute-done.14
  29.5 0.5 %collective-permute-start.15 = (bf16[24,6144]{1,0:T(8,128)(2,1)S(1)}, bf16[24,6144]{1,0:T(8,128)(2,1)}, u32[]{:S(2)}, u32[]{:S(2)}) collective-permute-start(bf16[24,6144]{1,0:T(8,128)(2,1)S(1)} %constant_dynamic-update-slice_fusion.6.refs_6_), channel_id=1, source_target_pairs={{0,1},{1,0},{2,3},{3,2},{4,5},{5,4},{6,7},{7,6},{8,9},{9,8},{10,11... | collective-permute-start | bytes 884744 | tf_op jit(solution)/shard_map/ppermute | solution.py:160
  30.0 0.8 %pad_add_fusion.table_ref = s32[152]{0:T(256)S(1)} fusion(s32[136]{0:T(256)} %param.5, s32[16]{0:T(128)} %param.4), kind=kLoop, calls=%fused_computation.10 | loop fusion | flops 152 | bytes 1216 | tf_op jit(solution)/shard_map/concatenate | solution.py:314
  30.8 0.0 collective-permute-done.7.refs_3_
  30.8 0.4 collective-permute-done.11.refs_5_
  31.2 8.7 %shard_map.37.refs_8_ = f32[11,896,896]{2,1,0:T(8,128)} custom-call(s32[1]{0:T(128)} %bitcast.device_ref, s32[152]{0:T(256)S(1)} %pad_add_fusion.table_ref, bf16[24,14336]{1,0:T(8,128)(2,1)S(1)} %constant_dynamic-update-slice_fusion.refs_0_, bf16[24,14336]{1,0:T(8,128)(2,1)S(1)} %collective-permute-done.2.refs_1_, ...), custom_call_target="tpu_custom_call" | custom-call | flops 738197504 | bytes 11534336 | tf_op jit(solution)/shard_map/pallas_call | solution.py:319
  39.9 0.0 collective-permute-done.15.refs_7_
  39.9 6.7 %shard_map.38 = f32[11,896,896]{2,1,0:T(8,128)} custom-call(s32[1]{0:T(128)} %bitcast.device_ref, s32[152]{0:T(256)S(1)} %pad_add_fusion.table_ref, bf16[24,14336]{1,0:T(8,128)(2,1)S(1)} %constant_dynamic-update-slice_fusion.refs_0_, bf16[24,14336]{1,0:T(8,128)(2,1)S(1)} %collective-permute-done.2.refs_1_, ...), custom_call_target="tpu_custom_call", output_to_operand_aliasing={{}: (10, {})} | custom-call | flops 1522532352 | bytes 23789568 | tf_op jit(solution)/shard_map/pallas_call | solution.py:319
  (13 shorter events, 0.2 us)
Async XLA Ops:
  0.0 9.1 %collective-permute-start = (bf16[8,14336]{1,0:T(8,128)(2,1)}, bf16[8,14336]{1,0:T(8,128)(2,1)S(1)}, u32[]{:S(2)}, u32[]{:S(2)}) collective-permute-start(bf16[8,14336]{1,0:T(8,128)(2,1)} %param.3), channel_id=1, source_target_pairs={{0,4},{1,3},{2,0},{3,7},{4,8},{5,1},{6,2},{7,11},{8,12},{9,5},{10,... | collective-permute-start | bytes 688136 | tf_op jit(solution)/shard_map/ppermute | solution.py:160
  3.0 6.2 %collective-permute-start.1 = (bf16[8,14336]{1,0:T(8,128)(2,1)}, bf16[8,14336]{1,0:T(8,128)(2,1)S(1)}, u32[]{:S(2)}, u32[]{:S(2)}) collective-permute-start(bf16[8,14336]{1,0:T(8,128)(2,1)} %param.3), channel_id=1, source_target_pairs={{0,2},{1,5},{2,6},{3,1},{4,0},{5,9},{6,10},{7,3},{8,4},{9,13},{10,... | collective-permute-start | bytes 688136 | tf_op jit(solution)/shard_map/ppermute | solution.py:160
  9.3 4.9 %collective-permute-start.5 = (bf16[8,6144]{1,0:T(8,128)(2,1)S(1)}, bf16[8,6144]{1,0:T(8,128)(2,1)S(1)}, u32[]{:S(2)}, u32[]{:S(2)}) collective-permute-start(bf16[8,6144]{1,0:T(8,128)(2,1)S(1)} %bitcast.14), channel_id=1, source_target_pairs={{0,4},{1,3},{2,0},{3,7},{4,8},{5,1},{6,2},{7,11},{8,12},{9,5},{10,... | collective-permute-start | bytes 294920 | tf_op jit(solution)/shard_map/ppermute | solution.py:160
  10.9 7.1 %collective-permute-start.3 = (bf16[8,8192]{1,0:T(8,128)(2,1)S(1)}, bf16[8,8192]{1,0:T(8,128)(2,1)S(1)}, u32[]{:S(2)}, u32[]{:S(2)}) collective-permute-start(bf16[8,8192]{1,0:T(8,128)(2,1)S(1)} %bitcast.12), channel_id=1, source_target_pairs={{0,4},{1,3},{2,0},{3,7},{4,8},{5,1},{6,2},{7,11},{8,12},{9,5},{10,... | collective-permute-start | bytes 393224 | tf_op jit(solution)/shard_map/ppermute | solution.py:160
  12.5 4.8 %collective-permute-start.6 = (bf16[8,6144]{1,0:T(8,128)(2,1)S(1)}, bf16[8,6144]{1,0:T(8,128)(2,1)S(1)}, u32[]{:S(2)}, u32[]{:S(2)}) collective-permute-start(bf16[8,6144]{1,0:T(8,128)(2,1)S(1)} %bitcast.13), channel_id=1, source_target_pairs={{0,2},{1,5},{2,6},{3,1},{4,0},{5,9},{6,10},{7,3},{8,4},{9,13},{10,... | collective-permute-start | bytes 294920 | tf_op jit(solution)/shard_map/ppermute | solution.py:160
  12.9 6.6 %collective-permute-start.4 = (bf16[8,8192]{1,0:T(8,128)(2,1)S(1)}, bf16[8,8192]{1,0:T(8,128)(2,1)S(1)}, u32[]{:S(2)}, u32[]{:S(2)}) collective-permute-start(bf16[8,8192]{1,0:T(8,128)(2,1)S(1)} %bitcast.11), channel_id=1, source_target_pairs={{0,2},{1,5},{2,6},{3,1},{4,0},{5,9},{6,10},{7,3},{8,4},{9,13},{10,... | collective-permute-start | bytes 393224 | tf_op jit(solution)/shard_map/ppermute | solution.py:160
  13.7 10.6 %collective-permute-start.2 = (bf16[24,14336]{1,0:T(8,128)(2,1)S(1)}, bf16[24,14336]{1,0:T(8,128)(2,1)S(1)}, u32[]{:S(2)}, u32[]{:S(2)}) collective-permute-start(bf16[24,14336]{1,0:T(8,128)(2,1)S(1)} %constant_dynamic-update-slice_fusion.refs_0_), channel_id=1, source_target_pairs={{0,1},{1,0},{2,3},{3,2},{4,5},{5,4},{6,7},{7,6},{8,9},{9,8},{10,11... | collective-permute-start | bytes 2064392 | tf_op jit(solution)/shard_map/ppermute | solution.py:160
  14.2 5.9 %collective-permute-start.12 = (bf16[8,6144]{1,0:T(8,128)(2,1)S(1)}, bf16[8,6144]{1,0:T(8,128)(2,1)S(1)}, u32[]{:S(2)}, u32[]{:S(2)}) collective-permute-start(bf16[8,6144]{1,0:T(8,128)(2,1)S(1)} %collective-permute-done.5), channel_id=1, source_target_pairs={{0,4},{1,3},{2,0},{3,7},{4,8},{5,1},{6,2},{7,11},{8,12},{9,5},{10,... | collective-permute-start | bytes 294920 | tf_op jit(solution)/shard_map/ppermute | solution.py:160
  17.3 5.0 %collective-permute-start.13 = (bf16[8,6144]{1,0:T(8,128)(2,1)S(1)}, bf16[8,6144]{1,0:T(8,128)(2,1)S(1)}, u32[]{:S(2)}, u32[]{:S(2)}) collective-permute-start(bf16[8,6144]{1,0:T(8,128)(2,1)S(1)} %collective-permute-done.6), channel_id=1, source_target_pairs={{0,2},{1,5},{2,6},{3,1},{4,0},{5,9},{6,10},{7,3},{8,4},{9,13},{10,... | collective-permute-start | bytes 294920 | tf_op jit(solution)/shard_map/ppermute | solution.py:160
  18.0 6.3 %collective-permute-start.8 = (bf16[8,8192]{1,0:T(8,128)(2,1)S(1)}, bf16[8,8192]{1,0:T(8,128)(2,1)S(1)}, u32[]{:S(2)}, u32[]{:S(2)}) collective-permute-start(bf16[8,8192]{1,0:T(8,128)(2,1)S(1)} %collective-permute-done.3), channel_id=1, source_target_pairs={{0,4},{1,3},{2,0},{3,7},{4,8},{5,1},{6,2},{7,11},{8,12},{9,5},{10,... | collective-permute-start | bytes 393224 | tf_op jit(solution)/shard_map/ppermute | solution.py:160
  19.6 5.9 %collective-permute-start.9 = (bf16[8,8192]{1,0:T(8,128)(2,1)S(1)}, bf16[8,8192]{1,0:T(8,128)(2,1)S(1)}, u32[]{:S(2)}, u32[]{:S(2)}) collective-permute-start(bf16[8,8192]{1,0:T(8,128)(2,1)S(1)} %collective-permute-done.4), channel_id=1, source_target_pairs={{0,2},{1,5},{2,6},{3,1},{4,0},{5,9},{6,10},{7,3},{8,4},{9,13},{10,... | collective-permute-start | bytes 393224 | tf_op jit(solution)/shard_map/ppermute | solution.py:160
  20.1 9.3 %collective-permute-start.14 = (bf16[8,6144]{1,0:T(8,128)(2,1)S(1)}, bf16[8,6144]{1,0:T(8,128)(2,1)S(1)}, u32[]{:S(2)}, u32[]{:S(2)}) collective-permute-start(bf16[8,6144]{1,0:T(8,128)(2,1)S(1)} %collective-permute-done.12), channel_id=1, source_target_pairs={{0,4},{1,3},{2,0},{3,7},{4,8},{5,1},{6,2},{7,11},{8,12},{9,5},{10,... | collective-permute-start | bytes 294920 | tf_op jit(solution)/shard_map/ppermute | solution.py:160
  24.3 5.0 %collective-permute-start.10 = (bf16[8,8192]{1,0:T(8,128)(2,1)S(1)}, bf16[8,8192]{1,0:T(8,128)(2,1)S(1)}, u32[]{:S(2)}, u32[]{:S(2)}) collective-permute-start(bf16[8,8192]{1,0:T(8,128)(2,1)S(1)} %collective-permute-done.8), channel_id=1, source_target_pairs={{0,4},{1,3},{2,0},{3,7},{4,8},{5,1},{6,2},{7,11},{8,12},{9,5},{10,... | collective-permute-start | bytes 393224 | tf_op jit(solution)/shard_map/ppermute | solution.py:160
  25.6 5.2 %collective-permute-start.7 = (bf16[16,14336]{1,0:T(8,128)(2,1)S(1)}, bf16[16,14336]{1,0:T(8,128)(2,1)S(1)}, u32[]{:S(2)}, u32[]{:S(2)}) collective-permute-start(bf16[16,14336]{1,0:T(8,128)(2,1)S(1)} %maximum_maximum_fusion.refs_2_), channel_id=1, source_target_pairs={{0,1},{1,0},{2,3},{3,2},{4,5},{5,4},{6,7},{7,6},{8,9},{9,8},{10,11... | collective-permute-start | bytes 1376264 | tf_op jit(solution)/shard_map/ppermute | solution.py:160
  29.4 1.8 %collective-permute-start.11 = (bf16[24,8192]{1,0:T(8,128)(2,1)S(1)}, bf16[24,8192]{1,0:T(8,128)(2,1)S(1)}, u32[]{:S(2)}, u32[]{:S(2)}) collective-permute-start(bf16[24,8192]{1,0:T(8,128)(2,1)S(1)} %constant_dynamic-update-slice_fusion.3.refs_4_), channel_id=1, source_target_pairs={{0,1},{1,0},{2,3},{3,2},{4,5},{5,4},{6,7},{7,6},{8,9},{9,8},{10,11... | collective-permute-start | bytes 1179656 | tf_op jit(solution)/shard_map/ppermute | solution.py:160
  29.5 10.4 %collective-permute-start.15 = (bf16[24,6144]{1,0:T(8,128)(2,1)S(1)}, bf16[24,6144]{1,0:T(8,128)(2,1)}, u32[]{:S(2)}, u32[]{:S(2)}) collective-permute-start(bf16[24,6144]{1,0:T(8,128)(2,1)S(1)} %constant_dynamic-update-slice_fusion.6.refs_6_), channel_id=1, source_target_pairs={{0,1},{1,0},{2,3},{3,2},{4,5},{5,4},{6,7},{7,6},{8,9},{9,8},{10,11... | collective-permute-start | bytes 884744 | tf_op jit(solution)/shard_map/ppermute | solution.py:160

commit v8 on v3

--- a/solution.py
+++ b/solution.py
@@ -8,7 +8,7 @@
 from jax.sharding import PartitionSpec as P
 
 BUFFERS = 4
-RING_LIMIT = 16
+RING_DEVICES = 16
 
 
 def tile_number(devices, device, partner):
@@ -146,28 +146,40 @@
     return onward, backward
 
 
-def ring_gather(tokens, devices):
+GROUPS = ((0, 1, 2), (8, 9, 10), (3, 4, 7), (11, 12, 15), (5, 6), (13, 14))
+
+
+def ring_gather(tokens, device, devices):
     onward, backward = ring_plan(devices)
     sibling = [device ^ 1 for device in range(devices)]
+    across = [device ^ 2 for device in range(devices)]
+    mirror = [(at, at ^ 12) for at in range(devices) if at // 4 in (0, 3)]
 
     def send(value, target):
         return lax.ppermute(value, "col", list(enumerate(target)))
 
-    chips = devices // 2
-    beside = send(tokens, sibling)
-    later, beside = lax.optimization_barrier((tokens, beside))
-    ahead, back = tokens, later
-    slabs, passed = [tokens], [beside]
-    for step in range(1, chips // 2 + 1):
-        ahead = send(ahead, onward)
-        slabs.append(ahead)
-        passed.append(send(ahead, sibling))
-        if 2 * step < chips:
-            back = send(back, backward)
-            slabs.append(back)
-            passed.append(send(back, sibling))
-    return slabs + passed
-
+    def after(value, *others):
+        return lax.optimization_barrier((value, *others))[0]
+
+    ahead, back = [tokens], [tokens]
+    for _ in range(2):
+        ahead.append(send(ahead[-1], onward))
+        back.append(send(back[-1], backward))
+    far = lax.ppermute(tokens, "col", mirror)
+    chip, core = device // 2, device % 2
+    at_end = (chip < 2) | (chip >= devices // 2 - 2)
+    came_ahead = (((chip == 3) | (chip == 4)) == (core == 0)) & ~at_end
+    held = jnp.where(at_end, far, jnp.where(came_ahead, ahead[1], back[1]))
+    half = send(held, across)
+    ahead.append(send(after(ahead[2], back[2]), onward))
+    back.append(send(after(back[2], ahead[2]), backward))
+    groups = []
+    for group, others in (
+        ((tokens, ahead[1], back[1]), (ahead[2], back[2])), ((ahead[2], back[2], half), (ahead[2], back[2])), ((ahead[3], back[3]), ()),
+    ):
+        group = jnp.concatenate(group, axis=0)
+        groups += [group, send(after(group, *others) if others else group, sibling)]
+    return groups
 
 def slab_origin(devices, device, number):
     chips = devices // 2
@@ -182,10 +194,10 @@
 
 
 def ring_kernel(devices, slots, device_ref, table_ref, *refs):
-    slabs = refs[:devices]
-    out_ref, pair, tiles, zeros, out_sems, zero_sems = refs[devices:]
+    groups = refs[:len(GROUPS)]
+    out_ref, pair, tiles, zeros, out_sems, zero_sems = refs[len(GROUPS):]
     device = device_ref[0]
-    slab, width = slabs[0].shape[0], pair.shape[2]
+    slab, width = pair.shape[1] // devices, pair.shape[2]
 
     def owned(partner):
         return table_ref[devices + tile_number(devices, device, partner)] == device
@@ -199,12 +211,14 @@
     def load_block(partner, masked):
         columns = pl.ds(pl.multiple_of(partner * width, 128), width)
         parts = []
-        for at, ref in enumerate(slabs):
-            part = ref[:, columns].astype(jnp.float32)
-            if masked:
-                row = lax.broadcasted_iota(jnp.int32, (slab, width), 0)
-                part = jnp.where(row < table_ref[slab_origin(devices, device, at)], part, 0.0)
-            parts.append(part)
+        for numbers, ref in zip(GROUPS, groups):
+            group = ref[:, columns].astype(jnp.float32)
+            for at, number in enumerate(numbers):
+                part = group[at * slab:(at + 1) * slab]
+                if masked:
+                    row = lax.broadcasted_iota(jnp.int32, (slab, width), 0)
+                    part = jnp.where(row < table_ref[slab_origin(devices, device, number)], part, 0.0)
+                parts.append(part)
         pair[0 if masked else 1] = jnp.concatenate(parts, axis=0).astype(jnp.bfloat16)
 
     count = lax.fori_loop(
@@ -269,15 +283,13 @@
 def ring_form(tokens, slab_lengths, tile_owner, devices, device, slots):
     slab, units = tokens.shape
     width = units // devices
-    slabs = ring_gather(tokens, devices)
-    kept = jnp.arange(slab, dtype=jnp.int32)[:, None] < slab_lengths[device]
-    slabs[0] = jnp.where(kept, tokens, jnp.zeros_like(tokens))
+    groups = ring_gather(tokens, device, devices)
     table = jnp.concatenate([slab_lengths, tile_owner])
     return pl.pallas_call(
         functools.partial(ring_kernel, devices, slots),
         out_shape=jax.ShapeDtypeStruct((slots, width, width), jnp.float32),
         in_specs=[pl.BlockSpec(memory_space=pltpu.SMEM)] * 2
-        + [pl.BlockSpec(memory_space=pltpu.VMEM)] * devices,
+        + [pl.BlockSpec(memory_space=pltpu.VMEM)] * len(groups),
         out_specs=pl.BlockSpec(memory_space=pl.ANY),
         scratch_shapes=[
             pltpu.VMEM((2, slab * devices, width), jnp.bfloat16),
@@ -292,7 +304,7 @@
             bytes_accessed=4 * slots * width * width,
             transcendentals=0,
         ),
-    )(device.reshape(1), table, *slabs)
+    )(device.reshape(1), table, *groups)
 
 
 def per_device(tokens, slab_lengths, tile_owner):
@@ -300,7 +312,7 @@
     device = lax.axis_index("col").astype(jnp.int32)
     slots = devices // 2 + devices // 8 + 1
     width = tokens.shape[1] // devices
-    form = ring_form if devices <= RING_LIMIT and width % 128 == 0 else gathered_form
+    form = ring_form if devices == RING_DEVICES and width % 128 == 0 else gathered_form
     return form(tokens, slab_lengths, tile_owner, devices, device, slots)
 
 

time: 45.8 us -> 44.4 us (0.969)
  starting transfers between devices: 9.56 us -> 16.5 us
  waiting for transfers between devices: 19.5 us -> 13.1 us
  other arithmetic: 2.43 us -> 0.84 us
    ppermute x15 -> x10, waiting for transfers between devices: 19.5 us -> 8.17 us  [send(): return lax.ppermute(value, 'col', list(enumerate(target)))]
    ppermute x0 -> x1, starting transfers between devices: none -> 5.94 us  [ring_gather(): far = lax.ppermute(tokens, 'col', mirror)]
    ppermute x0 -> x1, waiting for transfers between devices: none -> 4.97 us  [ring_gather(): far = lax.ppermute(tokens, 'col', mirror)]
    dynamic_slice x1 -> x0, local copies, waits for them, and re-layouts: 1.24 us -> none  [ring_form(): kept = jnp.arange(slab, dtype=jnp.int32)[:, None] < slab_lengths[device]]
    unnamed x0 -> x5, local copies, waits for them, and re-layouts: none -> 1.03 us
    ppermute x15 -> x10, starting transfers between devices: 9.56 us -> 10.5 us  [send(): return lax.ppermute(value, 'col', list(enumerate(target)))]
    select_n x1, other arithmetic: 1.02 us -> 0.08 us  [ring_gather(): held = jnp.where(at_end, far, jnp.where(came_ahead, ahead[1], back[1]))]
    lt x1 -> x0, other arithmetic: 0.65 us -> none  [ring_form(): kept = jnp.arange(slab, dtype=jnp.int32)[:, None] < slab_lengths[device]]
  transfers between devices with their start and end apart: 15 -> 11, of which waited for: 6 -> 5; matrix products, arithmetic and copies ran while one was open for 8% -> 4% of each run, Pallas kernels for 0% -> 0%
where the time goes in v8:
time: 44.4 us; the launch traced here: 44.2 us
  starting transfers between devices  16.5 us (37%)
  waiting for transfers between devices  13.1 us (30%)
  Pallas kernels  12.6 us (28%)
  local copies, waits for them, and re-layouts  1.06 us (2%)
  other arithmetic  0.84 us (2%)
    pallas_call x1, Pallas kernels, ring_form(): pl.pallas_call(functools.partial(ring_kernel, devices, slots), out_shape=...  12.6 us
    ppermute x10, starting transfers between devices, send(): return lax.ppermute(value, 'col', list(enumerate(target)))  10.5 us
    ppermute x10, waiting for transfers between devices, send(): return lax.ppermute(value, 'col', list(enumerate(target)))  8.17 us
    ppermute x1, starting transfers between devices, ring_gather(): far = lax.ppermute(tokens, 'col', mirror)  5.94 us
    ppermute x1, waiting for transfers between devices, ring_gather(): far = lax.ppermute(tokens, 'col', mirror)  4.97 us
    unnamed x5, local copies, waits for them, and re-layouts  1.03 us
  transfers between devices with their start and end apart: 11, of which 5 were waited for; matrix products, arithmetic and copies ran while one was open for 4% of the time, Pallas kernels for 0%

profile of v8, /device:TPU:0, one launch (start us, length us, event | category | flops | bytes accessed | tf_op | source)
XLA Modules:
  0.0 44.2 jit_solution(11639261473353628086)
XLA Ops:
  0.0 2.9 %collective-permute-start.1 = (bf16[8,14336]{1,0:T(8,128)(2,1)}, bf16[8,14336]{1,0:T(8,128)(2,1)S(1)}, u32[]{:S(2)}, u32[]{:S(2)}) collective-permute-start(bf16[8,14336]{1,0:T(8,128)(2,1)} %param.3), channel_id=1, source_target_pairs={{0,2},{1,5},{2,6},{3,1},{4,0},{5,9},{6,10},{7,3},{8,4},{9,13},{10,... | collective-permute-start | bytes 688136 | tf_op jit(solution)/shard_map/ppermute | solution.py:159
  2.9 0.1 collective-permute-start
  3.0 5.9 %collective-permute-start.5 = (bf16[8,14336]{1,0:T(8,128)(2,1)}, bf16[8,14336]{1,0:T(8,128)(2,1)S(1)}, u32[]{:S(2)}, u32[]{:S(2)}) collective-permute-start(bf16[8,14336]{1,0:T(8,128)(2,1)} %param.3), channel_id=1, source_target_pairs={{0,12},{1,13},{2,14},{3,15},{12,0},{13,1},{14,2},{15,3},{16,28},{1... | collective-permute-start | bytes 688136 | tf_op jit(solution)/shard_map/ppermute | solution.py:168
  9.0 1.0 %constant_dynamic-update-slice_fusion.2 = bf16[24,14336]{1,0:T(8,128)(2,1)S(1)} fusion(bf16[8,14336]{1,0:T(8,128)(2,1)} %param.3), kind=kLoop, calls=%fused_computation.3 | loop fusion | bytes 458752
  10.0 0.0 collective-permute-done.1
  10.0 1.5 %collective-permute-start.3 = (bf16[8,14336]{1,0:T(8,128)(2,1)S(1)}, bf16[8,14336]{1,0:T(8,128)(2,1)S(1)}, u32[]{:S(2)}, u32[]{:S(2)}) collective-permute-start(bf16[8,14336]{1,0:T(8,128)(2,1)S(1)} %collective-permute-done.1), channel_id=1, source_target_pairs={{0,2},{1,5},{2,6},{3,1},{4,0},{5,9},{6,10},{7,3},{8,4},{9,13},{10,... | collective-permute-start | bytes 688136 | tf_op jit(solution)/shard_map/ppermute | solution.py:159
  11.5 0.0 collective-permute-done
  11.5 0.5 %collective-permute-start.2 = (bf16[8,14336]{1,0:T(8,128)(2,1)S(1)}, bf16[8,14336]{1,0:T(8,128)(2,1)S(1)}, u32[]{:S(2)}, u32[]{:S(2)}) collective-permute-start(bf16[8,14336]{1,0:T(8,128)(2,1)S(1)} %collective-permute-done), channel_id=1, source_target_pairs={{0,4},{1,3},{2,0},{3,7},{4,8},{5,1},{6,2},{7,11},{8,12},{9,5},{10,... | collective-permute-start | bytes 688136 | tf_op jit(solution)/shard_map/ppermute | solution.py:159
  12.1 5.0 %collective-permute-done.5 = bf16[8,14336]{1,0:T(8,128)(2,1)S(1)} collective-permute-done((bf16[8,14336]{1,0:T(8,128)(2,1)}, bf16[8,14336]{1,0:T(8,128)(2,1)S(1)}, u32[]{:S(2)}, u32[]{:S(2)}) %collective-permute-start.5) | collective-permute-done | bytes 229408 | tf_op jit(solution)/shard_map/ppermute | solution.py:168
  17.1 0.1 select_select_fusion
  17.2 2.7 %collective-permute-start.6 = (bf16[8,14336]{1,0:T(8,128)(2,1)S(1)}, bf16[8,14336]{1,0:T(8,128)(2,1)S(1)}, u32[]{:S(2)}, u32[]{:S(2)}) collective-permute-start(bf16[8,14336]{1,0:T(8,128)(2,1)S(1)} %get-tuple-element.13), channel_id=1, source_target_pairs={{0,2},{1,3},{2,0},{3,1},{4,6},{5,7},{6,4},{7,5},{8,10},{9,11},{10,... | collective-permute-start | bytes 688136 | tf_op jit(solution)/shard_map/ppermute | solution.py:159
  19.9 2.1 %collective-permute-done.3 = bf16[8,14336]{1,0:T(8,128)(2,1)S(1)} collective-permute-done((bf16[8,14336]{1,0:T(8,128)(2,1)S(1)}, bf16[8,14336]{1,0:T(8,128)(2,1)S(1)}, u32[]{:S(2)}, u32[]{:S(2)}) %collective-permute-start.3) | collective-permute-done | bytes 229408 | tf_op jit(solution)/shard_map/ppermute | solution.py:159
  22.0 0.0 collective-permute-done.2
  22.0 0.6 %collective-permute-start.8 = (bf16[8,14336]{1,0:T(8,128)(2,1)S(1)}, bf16[8,14336]{1,0:T(8,128)(2,1)S(1)}, u32[]{:S(2)}, u32[]{:S(2)}) collective-permute-start(bf16[8,14336]{1,0:T(8,128)(2,1)S(1)} %collective-permute-done.2), channel_id=1, source_target_pairs={{0,4},{1,3},{2,0},{3,7},{4,8},{5,1},{6,2},{7,11},{8,12},{9,5},{10,... | collective-permute-start | bytes 688136 | tf_op jit(solution)/shard_map/ppermute | solution.py:159
  22.6 1.5 %collective-permute-start.9 = (bf16[8,14336]{1,0:T(8,128)(2,1)S(1)}, bf16[8,14336]{1,0:T(8,128)(2,1)S(1)}, u32[]{:S(2)}, u32[]{:S(2)}) collective-permute-start(bf16[8,14336]{1,0:T(8,128)(2,1)S(1)} %collective-permute-done.3), channel_id=1, source_target_pairs={{0,2},{1,5},{2,6},{3,1},{4,0},{5,9},{6,10},{7,3},{8,4},{9,13},{10,... | collective-permute-start | bytes 688136 | tf_op jit(solution)/shard_map/ppermute | solution.py:159
  24.1 0.8 %collective-permute-done.6 = bf16[8,14336]{1,0:T(8,128)(2,1)S(1)} collective-permute-done((bf16[8,14336]{1,0:T(8,128)(2,1)S(1)}, bf16[8,14336]{1,0:T(8,128)(2,1)S(1)}, u32[]{:S(2)}, u32[]{:S(2)}) %collective-permute-start.6) | collective-permute-done | bytes 229408 | tf_op jit(solution)/shard_map/ppermute | solution.py:159
  24.9 0.1 collective-permute-start.7
  25.0 0.5 %collective-permute-start.4 = (bf16[24,14336]{1,0:T(8,128)(2,1)S(1)}, bf16[24,14336]{1,0:T(8,128)(2,1)S(1)}, u32[]{:S(2)}, u32[]{:S(2)}) collective-permute-start(bf16[24,14336]{1,0:T(8,128)(2,1)S(1)} %get-tuple-element.9.refs_0_), channel_id=1, source_target_pairs={{0,1},{1,0},{2,3},{3,2},{4,5},{5,4},{6,7},{7,6},{8,9},{9,8},{10,11... | collective-permute-start | bytes 2064392 | tf_op jit(solution)/shard_map/ppermute | solution.py:159
  25.4 4.2 %collective-permute-done.8 = bf16[8,14336]{1,0:T(8,128)(2,1)S(1)} collective-permute-done((bf16[8,14336]{1,0:T(8,128)(2,1)S(1)}, bf16[8,14336]{1,0:T(8,128)(2,1)S(1)}, u32[]{:S(2)}, u32[]{:S(2)}) %collective-permute-start.8) | collective-permute-done | bytes 229408 | tf_op jit(solution)/shard_map/ppermute | solution.py:159
  29.7 0.0 collective-permute-done.9
  29.7 0.1 collective-permute-start.10
  29.8 0.8 %pad_add_fusion.table_ref = s32[152]{0:T(256)S(1)} fusion(s32[136]{0:T(256)} %param.5, s32[16]{0:T(128)} %param.4), kind=kLoop, calls=%fused_computation.9 | loop fusion | flops 152 | bytes 1216 | tf_op jit(solution)/shard_map/concatenate | solution.py:287
  30.6 1.0 %collective-permute-done.10.refs_5_ = bf16[16,14336]{1,0:T(8,128)(2,1)S(1)} collective-permute-done((bf16[16,14336]{1,0:T(8,128)(2,1)S(1)}, bf16[16,14336]{1,0:T(8,128)(2,1)S(1)}, u32[]{:S(2)}, u32[]{:S(2)}) %collective-permute-start.10) | collective-permute-done | bytes 458784 | tf_op jit(solution)/shard_map/ppermute | solution.py:159
  31.6 0.0 collective-permute-done.7.refs_3_
  31.6 0.0 collective-permute-done.4.refs_1_
  31.6 12.6 %shard_map.37 = f32[11,896,896]{2,1,0:T(8,128)} custom-call(s32[1]{0:T(128)} %bitcast.device_ref, s32[152]{0:T(256)S(1)} %pad_add_fusion.table_ref, bf16[24,14336]{1,0:T(8,128)(2,1)S(1)} %get-tuple-element.9.refs_0_, bf16[24,14336]{1,0:T(8,128)(2,1)S(1)} %collective-permute-done.4.refs_1_, bf16[24,14336]{1,0:T(8,128)(2,1)S(1)} %constant_dynamic-update-slice_fusion.3.refs_2_, ...), custom_call_target="tpu_custom_call" | custom-call | flops 2260729856 | bytes 35323904 | tf_op jit(solution)/shard_map/pallas_call | solution.py:288
  (6 shorter events, 0.1 us)
Async XLA Ops:
  0.0 10.0 %collective-permute-start.1 = (bf16[8,14336]{1,0:T(8,128)(2,1)}, bf16[8,14336]{1,0:T(8,128)(2,1)S(1)}, u32[]{:S(2)}, u32[]{:S(2)}) collective-permute-start(bf16[8,14336]{1,0:T(8,128)(2,1)} %param.3), channel_id=1, source_target_pairs={{0,2},{1,5},{2,6},{3,1},{4,0},{5,9},{6,10},{7,3},{8,4},{9,13},{10,... | collective-permute-start | bytes 688136 | tf_op jit(solution)/shard_map/ppermute | solution.py:159
  2.9 8.6 %collective-permute-start = (bf16[8,14336]{1,0:T(8,128)(2,1)}, bf16[8,14336]{1,0:T(8,128)(2,1)S(1)}, u32[]{:S(2)}, u32[]{:S(2)}) collective-permute-start(bf16[8,14336]{1,0:T(8,128)(2,1)} %param.3), channel_id=1, source_target_pairs={{0,4},{1,3},{2,0},{3,7},{4,8},{5,1},{6,2},{7,11},{8,12},{9,5},{10,... | collective-permute-start | bytes 688136 | tf_op jit(solution)/shard_map/ppermute | solution.py:159
  3.0 14.0 %collective-permute-start.5 = (bf16[8,14336]{1,0:T(8,128)(2,1)}, bf16[8,14336]{1,0:T(8,128)(2,1)S(1)}, u32[]{:S(2)}, u32[]{:S(2)}) collective-permute-start(bf16[8,14336]{1,0:T(8,128)(2,1)} %param.3), channel_id=1, source_target_pairs={{0,12},{1,13},{2,14},{3,15},{12,0},{13,1},{14,2},{15,3},{16,28},{1... | collective-permute-start | bytes 688136 | tf_op jit(solution)/shard_map/ppermute | solution.py:168
  10.0 12.0 %collective-permute-start.3 = (bf16[8,14336]{1,0:T(8,128)(2,1)S(1)}, bf16[8,14336]{1,0:T(8,128)(2,1)S(1)}, u32[]{:S(2)}, u32[]{:S(2)}) collective-permute-start(bf16[8,14336]{1,0:T(8,128)(2,1)S(1)} %collective-permute-done.1), channel_id=1, source_target_pairs={{0,2},{1,5},{2,6},{3,1},{4,0},{5,9},{6,10},{7,3},{8,4},{9,13},{10,... | collective-permute-start | bytes 688136 | tf_op jit(solution)/shard_map/ppermute | solution.py:159
  11.5 10.5 %collective-permute-start.2 = (bf16[8,14336]{1,0:T(8,128)(2,1)S(1)}, bf16[8,14336]{1,0:T(8,128)(2,1)S(1)}, u32[]{:S(2)}, u32[]{:S(2)}) collective-permute-start(bf16[8,14336]{1,0:T(8,128)(2,1)S(1)} %collective-permute-done), channel_id=1, source_target_pairs={{0,4},{1,3},{2,0},{3,7},{4,8},{5,1},{6,2},{7,11},{8,12},{9,5},{10,... | collective-permute-start | bytes 688136 | tf_op jit(solution)/shard_map/ppermute | solution.py:159
  17.2 7.7 %collective-permute-start.6 = (bf16[8,14336]{1,0:T(8,128)(2,1)S(1)}, bf16[8,14336]{1,0:T(8,128)(2,1)S(1)}, u32[]{:S(2)}, u32[]{:S(2)}) collective-permute-start(bf16[8,14336]{1,0:T(8,128)(2,1)S(1)} %get-tuple-element.13), channel_id=1, source_target_pairs={{0,2},{1,3},{2,0},{3,1},{4,6},{5,7},{6,4},{7,5},{8,10},{9,11},{10,... | collective-permute-start | bytes 688136 | tf_op jit(solution)/shard_map/ppermute | solution.py:159
  22.0 7.7 %collective-permute-start.8 = (bf16[8,14336]{1,0:T(8,128)(2,1)S(1)}, bf16[8,14336]{1,0:T(8,128)(2,1)S(1)}, u32[]{:S(2)}, u32[]{:S(2)}) collective-permute-start(bf16[8,14336]{1,0:T(8,128)(2,1)S(1)} %collective-permute-done.2), channel_id=1, source_target_pairs={{0,4},{1,3},{2,0},{3,7},{4,8},{5,1},{6,2},{7,11},{8,12},{9,5},{10,... | collective-permute-start | bytes 688136 | tf_op jit(solution)/shard_map/ppermute | solution.py:159
  22.6 7.1 %collective-permute-start.9 = (bf16[8,14336]{1,0:T(8,128)(2,1)S(1)}, bf16[8,14336]{1,0:T(8,128)(2,1)S(1)}, u32[]{:S(2)}, u32[]{:S(2)}) collective-permute-start(bf16[8,14336]{1,0:T(8,128)(2,1)S(1)} %collective-permute-done.3), channel_id=1, source_target_pairs={{0,2},{1,5},{2,6},{3,1},{4,0},{5,9},{6,10},{7,3},{8,4},{9,13},{10,... | collective-permute-start | bytes 688136 | tf_op jit(solution)/shard_map/ppermute | solution.py:159
  24.9 6.7 %collective-permute-start.7 = (bf16[24,14336]{1,0:T(8,128)(2,1)S(1)}, bf16[24,14336]{1,0:T(8,128)(2,1)S(1)}, u32[]{:S(2)}, u32[]{:S(2)}) collective-permute-start(bf16[24,14336]{1,0:T(8,128)(2,1)S(1)} %constant_dynamic-update-slice_fusion.3.refs_2_), channel_id=1, source_target_pairs={{0,1},{1,0},{2,3},{3,2},{4,5},{5,4},{6,7},{7,6},{8,9},{9,8},{10,11... | collective-permute-start | bytes 2064392 | tf_op jit(solution)/shard_map/ppermute | solution.py:159
  25.0 6.7 %collective-permute-start.4 = (bf16[24,14336]{1,0:T(8,128)(2,1)S(1)}, bf16[24,14336]{1,0:T(8,128)(2,1)S(1)}, u32[]{:S(2)}, u32[]{:S(2)}) collective-permute-start(bf16[24,14336]{1,0:T(8,128)(2,1)S(1)} %get-tuple-element.9.refs_0_), channel_id=1, source_target_pairs={{0,1},{1,0},{2,3},{3,2},{4,5},{5,4},{6,7},{7,6},{8,9},{9,8},{10,11... | collective-permute-start | bytes 2064392 | tf_op jit(solution)/shard_map/ppermute | solution.py:159
  29.7 1.9 %collective-permute-start.10 = (bf16[16,14336]{1,0:T(8,128)(2,1)S(1)}, bf16[16,14336]{1,0:T(8,128)(2,1)S(1)}, u32[]{:S(2)}, u32[]{:S(2)}) collective-permute-start(bf16[16,14336]{1,0:T(8,128)(2,1)S(1)} %constant_dynamic-update-slice_fusion.6.refs_4_), channel_id=1, source_target_pairs={{0,1},{1,0},{2,3},{3,2},{4,5},{5,4},{6,7},{7,6},{8,9},{9,8},{10,11... | collective-permute-start | bytes 1376264 | tf_op jit(solution)/shard_map/ppermute | solution.py:159

commit v9 on v8

--- a/solution.py
+++ b/solution.py
@@ -261,7 +261,7 @@
                 tiles[buffer, strip, :] = product * scale
                 pltpu.make_async_copy(
                     tiles.at[buffer, strip], out_ref.at[slot, strip], out_sems.at[buffer]
-                ).start()
+                ).start(priority=row // 128 % 2)
 
         return slot + mine.astype(jnp.int32)
 

time: 44.4 us -> 44.4 us (level)
  no operation moved by 1% of the time
where the time goes in v9:
time: 44.4 us; the launch traced here: 44.2 us
  starting transfers between devices  16.5 us (37%)
  waiting for transfers between devices  13.1 us (30%)
  Pallas kernels  12.6 us (28%)
  local copies, waits for them, and re-layouts  1.06 us (2%)
  other arithmetic  0.84 us (2%)
    pallas_call x1, Pallas kernels, ring_form(): pl.pallas_call(functools.partial(ring_kernel, devices, slots), out_shape=...  12.6 us
    ppermute x10, starting transfers between devices, send(): return lax.ppermute(value, 'col', list(enumerate(target)))  10.5 us
    ppermute x10, waiting for transfers between devices, send(): return lax.ppermute(value, 'col', list(enumerate(target)))  8.17 us
    ppermute x1, starting transfers between devices, ring_gather(): far = lax.ppermute(tokens, 'col', mirror)  5.94 us
    ppermute x1, waiting for transfers between devices, ring_gather(): far = lax.ppermute(tokens, 'col', mirror)  4.97 us
    unnamed x5, local copies, waits for them, and re-layouts  1.03 us
  transfers between devices with their start and end apart: 11, of which 5 were waited for; matrix products, arithmetic and copies ran while one was open for 4% of the time, Pallas kernels for 0%

profile of v9, /device:TPU:0, one launch (start us, length us, event | category | flops | bytes accessed | tf_op | source)
XLA Modules:
  0.0 44.2 jit_solution(4796595488093739655)
XLA Ops:
  0.0 2.9 %collective-permute-start.1 = (bf16[8,14336]{1,0:T(8,128)(2,1)}, bf16[8,14336]{1,0:T(8,128)(2,1)S(1)}, u32[]{:S(2)}, u32[]{:S(2)}) collective-permute-start(bf16[8,14336]{1,0:T(8,128)(2,1)} %param.3), channel_id=1, source_target_pairs={{0,2},{1,5},{2,6},{3,1},{4,0},{5,9},{6,10},{7,3},{8,4},{9,13},{10,... | collective-permute-start | bytes 688136 | tf_op jit(solution)/shard_map/ppermute | solution.py:159
  2.9 0.1 collective-permute-start
  3.0 5.9 %collective-permute-start.5 = (bf16[8,14336]{1,0:T(8,128)(2,1)}, bf16[8,14336]{1,0:T(8,128)(2,1)S(1)}, u32[]{:S(2)}, u32[]{:S(2)}) collective-permute-start(bf16[8,14336]{1,0:T(8,128)(2,1)} %param.3), channel_id=1, source_target_pairs={{0,12},{1,13},{2,14},{3,15},{12,0},{13,1},{14,2},{15,3},{16,28},{1... | collective-permute-start | bytes 688136 | tf_op jit(solution)/shard_map/ppermute | solution.py:168
  9.0 1.0 %constant_dynamic-update-slice_fusion.2 = bf16[24,14336]{1,0:T(8,128)(2,1)S(1)} fusion(bf16[8,14336]{1,0:T(8,128)(2,1)} %param.3), kind=kLoop, calls=%fused_computation.3 | loop fusion | bytes 458752
  10.0 0.0 collective-permute-done.1
  10.0 1.5 %collective-permute-start.3 = (bf16[8,14336]{1,0:T(8,128)(2,1)S(1)}, bf16[8,14336]{1,0:T(8,128)(2,1)S(1)}, u32[]{:S(2)}, u32[]{:S(2)}) collective-permute-start(bf16[8,14336]{1,0:T(8,128)(2,1)S(1)} %collective-permute-done.1), channel_id=1, source_target_pairs={{0,2},{1,5},{2,6},{3,1},{4,0},{5,9},{6,10},{7,3},{8,4},{9,13},{10,... | collective-permute-start | bytes 688136 | tf_op jit(solution)/shard_map/ppermute | solution.py:159
  11.5 0.0 collective-permute-done
  11.5 0.5 %collective-permute-start.2 = (bf16[8,14336]{1,0:T(8,128)(2,1)S(1)}, bf16[8,14336]{1,0:T(8,128)(2,1)S(1)}, u32[]{:S(2)}, u32[]{:S(2)}) collective-permute-start(bf16[8,14336]{1,0:T(8,128)(2,1)S(1)} %collective-permute-done), channel_id=1, source_target_pairs={{0,4},{1,3},{2,0},{3,7},{4,8},{5,1},{6,2},{7,11},{8,12},{9,5},{10,... | collective-permute-start | bytes 688136 | tf_op jit(solution)/shard_map/ppermute | solution.py:159
  12.1 5.0 %collective-permute-done.5 = bf16[8,14336]{1,0:T(8,128)(2,1)S(1)} collective-permute-done((bf16[8,14336]{1,0:T(8,128)(2,1)}, bf16[8,14336]{1,0:T(8,128)(2,1)S(1)}, u32[]{:S(2)}, u32[]{:S(2)}) %collective-permute-start.5) | collective-permute-done | bytes 229408 | tf_op jit(solution)/shard_map/ppermute | solution.py:168
  17.1 0.1 select_select_fusion
  17.2 2.7 %collective-permute-start.6 = (bf16[8,14336]{1,0:T(8,128)(2,1)S(1)}, bf16[8,14336]{1,0:T(8,128)(2,1)S(1)}, u32[]{:S(2)}, u32[]{:S(2)}) collective-permute-start(bf16[8,14336]{1,0:T(8,128)(2,1)S(1)} %get-tuple-element.13), channel_id=1, source_target_pairs={{0,2},{1,3},{2,0},{3,1},{4,6},{5,7},{6,4},{7,5},{8,10},{9,11},{10,... | collective-permute-start | bytes 688136 | tf_op jit(solution)/shard_map/ppermute | solution.py:159
  19.9 2.1 %collective-permute-done.3 = bf16[8,14336]{1,0:T(8,128)(2,1)S(1)} collective-permute-done((bf16[8,14336]{1,0:T(8,128)(2,1)S(1)}, bf16[8,14336]{1,0:T(8,128)(2,1)S(1)}, u32[]{:S(2)}, u32[]{:S(2)}) %collective-permute-start.3) | collective-permute-done | bytes 229408 | tf_op jit(solution)/shard_map/ppermute | solution.py:159
  22.0 0.0 collective-permute-done.2
  22.0 0.6 %collective-permute-start.8 = (bf16[8,14336]{1,0:T(8,128)(2,1)S(1)}, bf16[8,14336]{1,0:T(8,128)(2,1)S(1)}, u32[]{:S(2)}, u32[]{:S(2)}) collective-permute-start(bf16[8,14336]{1,0:T(8,128)(2,1)S(1)} %collective-permute-done.2), channel_id=1, source_target_pairs={{0,4},{1,3},{2,0},{3,7},{4,8},{5,1},{6,2},{7,11},{8,12},{9,5},{10,... | collective-permute-start | bytes 688136 | tf_op jit(solution)/shard_map/ppermute | solution.py:159
  22.6 1.5 %collective-permute-start.9 = (bf16[8,14336]{1,0:T(8,128)(2,1)S(1)}, bf16[8,14336]{1,0:T(8,128)(2,1)S(1)}, u32[]{:S(2)}, u32[]{:S(2)}) collective-permute-start(bf16[8,14336]{1,0:T(8,128)(2,1)S(1)} %collective-permute-done.3), channel_id=1, source_target_pairs={{0,2},{1,5},{2,6},{3,1},{4,0},{5,9},{6,10},{7,3},{8,4},{9,13},{10,... | collective-permute-start | bytes 688136 | tf_op jit(solution)/shard_map/ppermute | solution.py:159
  24.1 0.8 %collective-permute-done.6 = bf16[8,14336]{1,0:T(8,128)(2,1)S(1)} collective-permute-done((bf16[8,14336]{1,0:T(8,128)(2,1)S(1)}, bf16[8,14336]{1,0:T(8,128)(2,1)S(1)}, u32[]{:S(2)}, u32[]{:S(2)}) %collective-permute-start.6) | collective-permute-done | bytes 229408 | tf_op jit(solution)/shard_map/ppermute | solution.py:159
  24.9 0.1 collective-permute-start.7
  25.0 0.5 %collective-permute-start.4 = (bf16[24,14336]{1,0:T(8,128)(2,1)S(1)}, bf16[24,14336]{1,0:T(8,128)(2,1)S(1)}, u32[]{:S(2)}, u32[]{:S(2)}) collective-permute-start(bf16[24,14336]{1,0:T(8,128)(2,1)S(1)} %get-tuple-element.9.refs_0_), channel_id=1, source_target_pairs={{0,1},{1,0},{2,3},{3,2},{4,5},{5,4},{6,7},{7,6},{8,9},{9,8},{10,11... | collective-permute-start | bytes 2064392 | tf_op jit(solution)/shard_map/ppermute | solution.py:159
  25.4 4.2 %collective-permute-done.8 = bf16[8,14336]{1,0:T(8,128)(2,1)S(1)} collective-permute-done((bf16[8,14336]{1,0:T(8,128)(2,1)S(1)}, bf16[8,14336]{1,0:T(8,128)(2,1)S(1)}, u32[]{:S(2)}, u32[]{:S(2)}) %collective-permute-start.8) | collective-permute-done | bytes 229408 | tf_op jit(solution)/shard_map/ppermute | solution.py:159
  29.7 0.0 collective-permute-done.9
  29.7 0.1 collective-permute-start.10
  29.8 0.8 %pad_add_fusion.table_ref = s32[152]{0:T(256)S(1)} fusion(s32[136]{0:T(256)} %param.5, s32[16]{0:T(128)} %param.4), kind=kLoop, calls=%fused_computation.9 | loop fusion | flops 152 | bytes 1216 | tf_op jit(solution)/shard_map/concatenate | solution.py:287
  30.6 1.0 %collective-permute-done.10.refs_5_ = bf16[16,14336]{1,0:T(8,128)(2,1)S(1)} collective-permute-done((bf16[16,14336]{1,0:T(8,128)(2,1)S(1)}, bf16[16,14336]{1,0:T(8,128)(2,1)S(1)}, u32[]{:S(2)}, u32[]{:S(2)}) %collective-permute-start.10) | collective-permute-done | bytes 458784 | tf_op jit(solution)/shard_map/ppermute | solution.py:159
  31.6 0.0 collective-permute-done.7.refs_3_
  31.6 0.0 collective-permute-done.4.refs_1_
  31.6 12.6 %shard_map.37 = f32[11,896,896]{2,1,0:T(8,128)} custom-call(s32[1]{0:T(128)} %bitcast.device_ref, s32[152]{0:T(256)S(1)} %pad_add_fusion.table_ref, bf16[24,14336]{1,0:T(8,128)(2,1)S(1)} %get-tuple-element.9.refs_0_, bf16[24,14336]{1,0:T(8,128)(2,1)S(1)} %collective-permute-done.4.refs_1_, bf16[24,14336]{1,0:T(8,128)(2,1)S(1)} %constant_dynamic-update-slice_fusion.3.refs_2_, ...), custom_call_target="tpu_custom_call" | custom-call | flops 2260729856 | bytes 35323904 | tf_op jit(solution)/shard_map/pallas_call | solution.py:288
  (6 shorter events, 0.1 us)
Async XLA Ops:
  0.0 10.0 %collective-permute-start.1 = (bf16[8,14336]{1,0:T(8,128)(2,1)}, bf16[8,14336]{1,0:T(8,128)(2,1)S(1)}, u32[]{:S(2)}, u32[]{:S(2)}) collective-permute-start(bf16[8,14336]{1,0:T(8,128)(2,1)} %param.3), channel_id=1, source_target_pairs={{0,2},{1,5},{2,6},{3,1},{4,0},{5,9},{6,10},{7,3},{8,4},{9,13},{10,... | collective-permute-start | bytes 688136 | tf_op jit(solution)/shard_map/ppermute | solution.py:159
  2.9 8.6 %collective-permute-start = (bf16[8,14336]{1,0:T(8,128)(2,1)}, bf16[8,14336]{1,0:T(8,128)(2,1)S(1)}, u32[]{:S(2)}, u32[]{:S(2)}) collective-permute-start(bf16[8,14336]{1,0:T(8,128)(2,1)} %param.3), channel_id=1, source_target_pairs={{0,4},{1,3},{2,0},{3,7},{4,8},{5,1},{6,2},{7,11},{8,12},{9,5},{10,... | collective-permute-start | bytes 688136 | tf_op jit(solution)/shard_map/ppermute | solution.py:159
  3.0 14.0 %collective-permute-start.5 = (bf16[8,14336]{1,0:T(8,128)(2,1)}, bf16[8,14336]{1,0:T(8,128)(2,1)S(1)}, u32[]{:S(2)}, u32[]{:S(2)}) collective-permute-start(bf16[8,14336]{1,0:T(8,128)(2,1)} %param.3), channel_id=1, source_target_pairs={{0,12},{1,13},{2,14},{3,15},{12,0},{13,1},{14,2},{15,3},{16,28},{1... | collective-permute-start | bytes 688136 | tf_op jit(solution)/shard_map/ppermute | solution.py:168
  10.0 12.0 %collective-permute-start.3 = (bf16[8,14336]{1,0:T(8,128)(2,1)S(1)}, bf16[8,14336]{1,0:T(8,128)(2,1)S(1)}, u32[]{:S(2)}, u32[]{:S(2)}) collective-permute-start(bf16[8,14336]{1,0:T(8,128)(2,1)S(1)} %collective-permute-done.1), channel_id=1, source_target_pairs={{0,2},{1,5},{2,6},{3,1},{4,0},{5,9},{6,10},{7,3},{8,4},{9,13},{10,... | collective-permute-start | bytes 688136 | tf_op jit(solution)/shard_map/ppermute | solution.py:159
  11.5 10.5 %collective-permute-start.2 = (bf16[8,14336]{1,0:T(8,128)(2,1)S(1)}, bf16[8,14336]{1,0:T(8,128)(2,1)S(1)}, u32[]{:S(2)}, u32[]{:S(2)}) collective-permute-start(bf16[8,14336]{1,0:T(8,128)(2,1)S(1)} %collective-permute-done), channel_id=1, source_target_pairs={{0,4},{1,3},{2,0},{3,7},{4,8},{5,1},{6,2},{7,11},{8,12},{9,5},{10,... | collective-permute-start | bytes 688136 | tf_op jit(solution)/shard_map/ppermute | solution.py:159
  17.2 7.7 %collective-permute-start.6 = (bf16[8,14336]{1,0:T(8,128)(2,1)S(1)}, bf16[8,14336]{1,0:T(8,128)(2,1)S(1)}, u32[]{:S(2)}, u32[]{:S(2)}) collective-permute-start(bf16[8,14336]{1,0:T(8,128)(2,1)S(1)} %get-tuple-element.13), channel_id=1, source_target_pairs={{0,2},{1,3},{2,0},{3,1},{4,6},{5,7},{6,4},{7,5},{8,10},{9,11},{10,... | collective-permute-start | bytes 688136 | tf_op jit(solution)/shard_map/ppermute | solution.py:159
  22.0 7.7 %collective-permute-start.8 = (bf16[8,14336]{1,0:T(8,128)(2,1)S(1)}, bf16[8,14336]{1,0:T(8,128)(2,1)S(1)}, u32[]{:S(2)}, u32[]{:S(2)}) collective-permute-start(bf16[8,14336]{1,0:T(8,128)(2,1)S(1)} %collective-permute-done.2), channel_id=1, source_target_pairs={{0,4},{1,3},{2,0},{3,7},{4,8},{5,1},{6,2},{7,11},{8,12},{9,5},{10,... | collective-permute-start | bytes 688136 | tf_op jit(solution)/shard_map/ppermute | solution.py:159
  22.6 7.1 %collective-permute-start.9 = (bf16[8,14336]{1,0:T(8,128)(2,1)S(1)}, bf16[8,14336]{1,0:T(8,128)(2,1)S(1)}, u32[]{:S(2)}, u32[]{:S(2)}) collective-permute-start(bf16[8,14336]{1,0:T(8,128)(2,1)S(1)} %collective-permute-done.3), channel_id=1, source_target_pairs={{0,2},{1,5},{2,6},{3,1},{4,0},{5,9},{6,10},{7,3},{8,4},{9,13},{10,... | collective-permute-start | bytes 688136 | tf_op jit(solution)/shard_map/ppermute | solution.py:159
  24.9 6.7 %collective-permute-start.7 = (bf16[24,14336]{1,0:T(8,128)(2,1)S(1)}, bf16[24,14336]{1,0:T(8,128)(2,1)S(1)}, u32[]{:S(2)}, u32[]{:S(2)}) collective-permute-start(bf16[24,14336]{1,0:T(8,128)(2,1)S(1)} %constant_dynamic-update-slice_fusion.3.refs_2_), channel_id=1, source_target_pairs={{0,1},{1,0},{2,3},{3,2},{4,5},{5,4},{6,7},{7,6},{8,9},{9,8},{10,11... | collective-permute-start | bytes 2064392 | tf_op jit(solution)/shard_map/ppermute | solution.py:159
  25.0 6.7 %collective-permute-start.4 = (bf16[24,14336]{1,0:T(8,128)(2,1)S(1)}, bf16[24,14336]{1,0:T(8,128)(2,1)S(1)}, u32[]{:S(2)}, u32[]{:S(2)}) collective-permute-start(bf16[24,14336]{1,0:T(8,128)(2,1)S(1)} %get-tuple-element.9.refs_0_), channel_id=1, source_target_pairs={{0,1},{1,0},{2,3},{3,2},{4,5},{5,4},{6,7},{7,6},{8,9},{9,8},{10,11... | collective-permute-start | bytes 2064392 | tf_op jit(solution)/shard_map/ppermute | solution.py:159
  29.7 1.9 %collective-permute-start.10 = (bf16[16,14336]{1,0:T(8,128)(2,1)S(1)}, bf16[16,14336]{1,0:T(8,128)(2,1)S(1)}, u32[]{:S(2)}, u32[]{:S(2)}) collective-permute-start(bf16[16,14336]{1,0:T(8,128)(2,1)S(1)} %constant_dynamic-update-slice_fusion.6.refs_4_), channel_id=1, source_target_pairs={{0,1},{1,0},{2,3},{3,2},{4,5},{5,4},{6,7},{7,6},{8,9},{9,8},{10,11... | collective-permute-start | bytes 1376264 | tf_op jit(solution)/shard_map/ppermute | solution.py:159

commit v10 on v8

--- a/solution.py
+++ b/solution.py
@@ -146,14 +146,13 @@
     return onward, backward
 
 
-GROUPS = ((0, 1, 2), (8, 9, 10), (3, 4, 7), (11, 12, 15), (5, 6), (13, 14))
-
-
-def ring_gather(tokens, device, devices):
+GROUPS = ((0, 1, 2), (8, 9, 10), (3, 4), (11, 12), (5, 6), (13, 14), (7,), (15,))
+
+
+def ring_gather(tokens, devices):
     onward, backward = ring_plan(devices)
     sibling = [device ^ 1 for device in range(devices)]
-    across = [device ^ 2 for device in range(devices)]
-    mirror = [(at, at ^ 12) for at in range(devices) if at // 4 in (0, 3)]
+    middle = tokens.shape[1] // 2
 
     def send(value, target):
         return lax.ppermute(value, "col", list(enumerate(target)))
@@ -161,25 +160,25 @@
     def after(value, *others):
         return lax.optimization_barrier((value, *others))[0]
 
-    ahead, back = [tokens], [tokens]
-    for _ in range(2):
-        ahead.append(send(ahead[-1], onward))
-        back.append(send(back[-1], backward))
-    far = lax.ppermute(tokens, "col", mirror)
-    chip, core = device // 2, device % 2
-    at_end = (chip < 2) | (chip >= devices // 2 - 2)
-    came_ahead = (((chip == 3) | (chip == 4)) == (core == 0)) & ~at_end
-    held = jnp.where(at_end, far, jnp.where(came_ahead, ahead[1], back[1]))
-    half = send(held, across)
-    ahead.append(send(after(ahead[2], back[2]), onward))
-    back.append(send(after(back[2], ahead[2]), backward))
-    groups = []
-    for group, others in (
-        ((tokens, ahead[1], back[1]), (ahead[2], back[2])), ((ahead[2], back[2], half), (ahead[2], back[2])), ((ahead[3], back[3]), ()),
-    ):
-        group = jnp.concatenate(group, axis=0)
-        groups += [group, send(after(group, *others) if others else group, sibling)]
-    return groups
+    def joined(*values_by_half):
+        return jnp.concatenate([jnp.concatenate(values, axis=1) for values in values_by_half], axis=0)
+
+    ahead, back = send(tokens, onward), send(tokens, backward)
+    near = jnp.concatenate([tokens, ahead, back], axis=0)
+    beside = send(near, sibling)
+    hops = []
+    for columns in (slice(0, middle), slice(middle, None)):
+        ahead_2, back_2 = send(ahead[:, columns], onward), send(back[:, columns], backward)
+        ahead_3, back_3 = send(ahead_2, onward), send(back_2, backward)
+        ahead_3 = ahead_3 if columns.start else after(ahead_3, beside)
+        ahead_4 = send(ahead_3, onward)
+        hops.append((ahead_2, back_2, ahead_3, back_3, ahead_4))
+    ahead_2, back_2, ahead_3, back_3, ahead_4 = zip(*hops)
+    two, three, four = joined(ahead_2, back_2), joined(ahead_3, back_3), joined(ahead_4)
+    return [
+        near, beside, two, send(after(two, beside), sibling), three, send(three, sibling),
+        four, send(four, sibling),
+    ]
 
 def slab_origin(devices, device, number):
     chips = devices // 2
@@ -283,7 +282,7 @@
 def ring_form(tokens, slab_lengths, tile_owner, devices, device, slots):
     slab, units = tokens.shape
     width = units // devices
-    groups = ring_gather(tokens, device, devices)
+    groups = ring_gather(tokens, devices)
     table = jnp.concatenate([slab_lengths, tile_owner])
     return pl.pallas_call(
         functools.partial(ring_kernel, devices, slots),

time: 44.4 us -> 44.8 us (level)
  starting transfers between devices: 16.5 us -> 14.6 us
  waiting for transfers between devices: 13.1 us -> 14.9 us
    ppermute x10 -> x16, waiting for transfers between devices: 8.17 us -> 14.9 us  [send(): return lax.ppermute(value, 'col', list(enumerate(target)))]
    ppermute x1 -> x0, starting transfers between devices: 5.94 us -> none  [ring_gather(): far = lax.ppermute(tokens, 'col', mirror)]
    ppermute x1 -> x0, waiting for transfers between devices: 4.97 us -> none  [ring_gather(): far = lax.ppermute(tokens, 'col', mirror)]
    ppermute x10 -> x16, starting transfers between devices: 10.5 us -> 14.6 us  [send(): return lax.ppermute(value, 'col', list(enumerate(target)))]
    pallas_call x1, Pallas kernels: 12.6 us -> 13 us  [ring_form(): pl.pallas_call(functools.partial(ring_kernel, devices, slots), out_shape=...]
    unnamed x5 -> x3, local copies, waits for them, and re-layouts: 1.03 us -> 1.04 us
  transfers between devices with their start and end apart: 11 -> 16, of which waited for: 5 -> 8; matrix products, arithmetic and copies ran while one was open for 4% -> 4% of each run, Pallas kernels for 0% -> 0%
where the time goes in v10:
time: 44.8 us; the launch traced here: 44.5 us
  waiting for transfers between devices  14.9 us (33%)
  starting transfers between devices  14.6 us (33%)
  Pallas kernels  13 us (29%)
  local copies, waits for them, and re-layouts  1.1 us (2%)
  other arithmetic  0.82 us (2%)
    ppermute x16, waiting for transfers between devices, send(): return lax.ppermute(value, 'col', list(enumerate(target)))  14.9 us
    ppermute x16, starting transfers between devices, send(): return lax.ppermute(value, 'col', list(enumerate(target)))  14.6 us
    pallas_call x1, Pallas kernels, ring_form(): pl.pallas_call(functools.partial(ring_kernel, devices, slots), out_shape=...  13 us
    unnamed x3, local copies, waits for them, and re-layouts  1.04 us
  transfers between devices with their start and end apart: 16, of which 8 were waited for; matrix products, arithmetic and copies ran while one was open for 4% of the time, Pallas kernels for 0%

profile of v10, /device:TPU:0, one launch (start us, length us, event | category | flops | bytes accessed | tf_op | source)
XLA Modules:
  0.0 44.5 jit_solution(13333304079023849075)
XLA Ops:
  0.0 3.0 %collective-permute-start = (bf16[8,14336]{1,0:T(8,128)(2,1)}, bf16[8,14336]{1,0:T(8,128)(2,1)S(1)}, u32[]{:S(2)}, u32[]{:S(2)}) collective-permute-start(bf16[8,14336]{1,0:T(8,128)(2,1)} %param.3), channel_id=1, source_target_pairs={{0,4},{1,3},{2,0},{3,7},{4,8},{5,1},{6,2},{7,11},{8,12},{9,5},{10,... | collective-permute-start | bytes 688136 | tf_op jit(solution)/shard_map/ppermute | solution.py:158
  3.0 0.0 collective-permute-start.1
  3.0 1.0 %constant_dynamic-update-slice_fusion.2 = bf16[24,14336]{1,0:T(8,128)(2,1)S(1)} fusion(bf16[8,14336]{1,0:T(8,128)(2,1)} %param.3), kind=kLoop, calls=%fused_computation.4 | loop fusion | bytes 458752
  4.0 5.0 %collective-permute-done = bf16[8,14336]{1,0:T(8,128)(2,1)S(1)} collective-permute-done((bf16[8,14336]{1,0:T(8,128)(2,1)}, bf16[8,14336]{1,0:T(8,128)(2,1)S(1)}, u32[]{:S(2)}, u32[]{:S(2)}) %collective-permute-start) | collective-permute-done | bytes 229408 | tf_op jit(solution)/shard_map/ppermute | solution.py:158
  9.1 1.6 %collective-permute-start.3 = (bf16[8,7168]{1,0:T(8,128)(2,1)S(1)}, bf16[8,7168]{1,0:T(8,128)(2,1)S(1)}, u32[]{:S(2)}, u32[]{:S(2)}) collective-permute-start(bf16[8,7168]{1,0:T(8,128)(2,1)S(1)} %get-tuple-element.9), channel_id=1, source_target_pairs={{0,4},{1,3},{2,0},{3,7},{4,8},{5,1},{6,2},{7,11},{8,12},{9,5},{10,... | collective-permute-start | bytes 344072 | tf_op jit(solution)/shard_map/ppermute | solution.py:158
  10.7 1.7 %collective-permute-start.4 = (bf16[8,7168]{1,0:T(8,128)(2,1)S(1)}, bf16[8,7168]{1,0:T(8,128)(2,1)S(1)}, u32[]{:S(2)}, u32[]{:S(2)}) collective-permute-start(bf16[8,7168]{1,0:T(8,128)(2,1)S(1)} %get-tuple-element.10), channel_id=1, source_target_pairs={{0,4},{1,3},{2,0},{3,7},{4,8},{5,1},{6,2},{7,11},{8,12},{9,5},{10,... | collective-permute-start | bytes 344072 | tf_op jit(solution)/shard_map/ppermute | solution.py:158
  12.4 0.0 collective-permute-done.1
  12.4 0.3 collective-permute-start.5
  12.8 0.9 %collective-permute-start.6 = (bf16[8,7168]{1,0:T(8,128)(2,1)S(1)}, bf16[8,7168]{1,0:T(8,128)(2,1)S(1)}, u32[]{:S(2)}, u32[]{:S(2)}) collective-permute-start(bf16[8,7168]{1,0:T(8,128)(2,1)S(1)} %get-tuple-element.12), channel_id=1, source_target_pairs={{0,2},{1,5},{2,6},{3,1},{4,0},{5,9},{6,10},{7,3},{8,4},{9,13},{10,... | collective-permute-start | bytes 344072 | tf_op jit(solution)/shard_map/ppermute | solution.py:158
  13.7 0.1 collective-permute-start.2
  13.8 1.6 %collective-permute-done.3 = bf16[8,7168]{1,0:T(8,128)(2,1)S(1)} collective-permute-done((bf16[8,7168]{1,0:T(8,128)(2,1)S(1)}, bf16[8,7168]{1,0:T(8,128)(2,1)S(1)}, u32[]{:S(2)}, u32[]{:S(2)}) %collective-permute-start.3) | collective-permute-done | bytes 114720 | tf_op jit(solution)/shard_map/ppermute | solution.py:158
  15.4 1.2 %collective-permute-start.8 = (bf16[8,7168]{1,0:T(8,128)(2,1)S(1)}, bf16[8,7168]{1,0:T(8,128)(2,1)S(1)}, u32[]{:S(2)}, u32[]{:S(2)}) collective-permute-start(bf16[8,7168]{1,0:T(8,128)(2,1)S(1)} %collective-permute-done.3), channel_id=1, source_target_pairs={{0,4},{1,3},{2,0},{3,7},{4,8},{5,1},{6,2},{7,11},{8,12},{9,5},{10,... | collective-permute-start | bytes 344072 | tf_op jit(solution)/shard_map/ppermute | solution.py:158
  16.6 1.0 %collective-permute-done.4 = bf16[8,7168]{1,0:T(8,128)(2,1)S(1)} collective-permute-done((bf16[8,7168]{1,0:T(8,128)(2,1)S(1)}, bf16[8,7168]{1,0:T(8,128)(2,1)S(1)}, u32[]{:S(2)}, u32[]{:S(2)}) %collective-permute-start.4) | collective-permute-done | bytes 114720 | tf_op jit(solution)/shard_map/ppermute | solution.py:158
  17.6 0.8 %collective-permute-start.9 = (bf16[8,7168]{1,0:T(8,128)(2,1)S(1)}, bf16[8,7168]{1,0:T(8,128)(2,1)S(1)}, u32[]{:S(2)}, u32[]{:S(2)}) collective-permute-start(bf16[8,7168]{1,0:T(8,128)(2,1)S(1)} %collective-permute-done.4), channel_id=1, source_target_pairs={{0,4},{1,3},{2,0},{3,7},{4,8},{5,1},{6,2},{7,11},{8,12},{9,5},{10,... | collective-permute-start | bytes 344072 | tf_op jit(solution)/shard_map/ppermute | solution.py:158
  18.4 0.0 collective-permute-done.5
  18.4 1.2 %collective-permute-start.10 = (bf16[8,7168]{1,0:T(8,128)(2,1)S(1)}, bf16[8,7168]{1,0:T(8,128)(2,1)S(1)}, u32[]{:S(2)}, u32[]{:S(2)}) collective-permute-start(bf16[8,7168]{1,0:T(8,128)(2,1)S(1)} %collective-permute-done.5), channel_id=1, source_target_pairs={{0,2},{1,5},{2,6},{3,1},{4,0},{5,9},{6,10},{7,3},{8,4},{9,13},{10,... | collective-permute-start | bytes 344072 | tf_op jit(solution)/shard_map/ppermute | solution.py:158
  19.7 0.4 collective-permute-done.6
  20.1 1.2 %collective-permute-start.11 = (bf16[8,7168]{1,0:T(8,128)(2,1)S(1)}, bf16[8,7168]{1,0:T(8,128)(2,1)S(1)}, u32[]{:S(2)}, u32[]{:S(2)}) collective-permute-start(bf16[8,7168]{1,0:T(8,128)(2,1)S(1)} %collective-permute-done.6), channel_id=1, source_target_pairs={{0,2},{1,5},{2,6},{3,1},{4,0},{5,9},{6,10},{7,3},{8,4},{9,13},{10,... | collective-permute-start | bytes 344072 | tf_op jit(solution)/shard_map/ppermute | solution.py:158
  21.3 2.4 %collective-permute-done.9 = bf16[8,7168]{1,0:T(8,128)(2,1)S(1)} collective-permute-done((bf16[8,7168]{1,0:T(8,128)(2,1)S(1)}, bf16[8,7168]{1,0:T(8,128)(2,1)S(1)}, u32[]{:S(2)}, u32[]{:S(2)}) %collective-permute-start.9) | collective-permute-done | bytes 114720 | tf_op jit(solution)/shard_map/ppermute | solution.py:158
  23.7 1.2 %collective-permute-start.14 = (bf16[8,7168]{1,0:T(8,128)(2,1)S(1)}, bf16[8,7168]{1,0:T(8,128)(2,1)S(1)}, u32[]{:S(2)}, u32[]{:S(2)}) collective-permute-start(bf16[8,7168]{1,0:T(8,128)(2,1)S(1)} %collective-permute-done.9), channel_id=1, source_target_pairs={{0,4},{1,3},{2,0},{3,7},{4,8},{5,1},{6,2},{7,11},{8,12},{9,5},{10,... | collective-permute-start | bytes 344072 | tf_op jit(solution)/shard_map/ppermute | solution.py:158
  24.9 0.0 collective-permute-done.8
  24.9 0.0 collective-permute-done.2.refs_1_
  24.9 0.6 %collective-permute-start.13 = (bf16[8,7168]{1,0:T(8,128)(2,1)S(1)}, bf16[8,7168]{1,0:T(8,128)(2,1)S(1)}, u32[]{:S(2)}, u32[]{:S(2)}) collective-permute-start(bf16[8,7168]{1,0:T(8,128)(2,1)S(1)} %collective-permute-done.8), channel_id=1, source_target_pairs={{0,4},{1,3},{2,0},{3,7},{4,8},{5,1},{6,2},{7,11},{8,12},{9,5},{10,... | collective-permute-start | bytes 344072 | tf_op jit(solution)/shard_map/ppermute | solution.py:158
  25.6 0.0 collective-permute-done.10
  25.6 0.7 %collective-permute-done.11 = bf16[8,7168]{1,0:T(8,128)(2,1)S(1)} collective-permute-done((bf16[8,7168]{1,0:T(8,128)(2,1)S(1)}, bf16[8,7168]{1,0:T(8,128)(2,1)S(1)}, u32[]{:S(2)}, u32[]{:S(2)}) %collective-permute-start.11) | collective-permute-done | bytes 114720 | tf_op jit(solution)/shard_map/ppermute | solution.py:158
  26.3 0.1 collective-permute-start.12
  26.3 0.5 %collective-permute-start.7 = (bf16[16,14336]{1,0:T(8,128)(2,1)S(1)}, bf16[16,14336]{1,0:T(8,128)(2,1)S(1)}, u32[]{:S(2)}, u32[]{:S(2)}) collective-permute-start(bf16[16,14336]{1,0:T(8,128)(2,1)S(1)} %maximum_maximum_fusion.refs_2_), channel_id=1, source_target_pairs={{0,1},{1,0},{2,3},{3,2},{4,5},{5,4},{6,7},{7,6},{8,9},{9,8},{10,11... | collective-permute-start | bytes 1376264 | tf_op jit(solution)/shard_map/ppermute | solution.py:158
  26.8 2.9 %collective-permute-done.13 = bf16[8,7168]{1,0:T(8,128)(2,1)S(1)} collective-permute-done((bf16[8,7168]{1,0:T(8,128)(2,1)S(1)}, bf16[8,7168]{1,0:T(8,128)(2,1)S(1)}, u32[]{:S(2)}, u32[]{:S(2)}) %collective-permute-start.13) | collective-permute-done | bytes 114720 | tf_op jit(solution)/shard_map/ppermute | solution.py:158
  29.7 0.0 collective-permute-done.14
  29.8 0.1 collective-permute-start.15
  29.9 0.8 %pad_add_fusion.table_ref = s32[152]{0:T(256)S(1)} fusion(s32[136]{0:T(256)} %param.5, s32[16]{0:T(128)} %param.4), kind=kLoop, calls=%fused_computation.7 | loop fusion | flops 152 | bytes 1216 | tf_op jit(solution)/shard_map/concatenate | solution.py:286
  30.6 0.8 %collective-permute-done.15.refs_7_ = bf16[8,14336]{1,0:T(8,128)(2,1)} collective-permute-done((bf16[8,14336]{1,0:T(8,128)(2,1)S(1)}, bf16[8,14336]{1,0:T(8,128)(2,1)}, u32[]{:S(2)}, u32[]{:S(2)}) %collective-permute-start.15) | collective-permute-done | bytes 229408 | tf_op jit(solution)/shard_map/ppermute | solution.py:158
  31.5 0.0 collective-permute-done.12.refs_5_
  31.5 0.0 collective-permute-done.7.refs_3_
  31.5 13.0 %shard_map.37 = f32[11,896,896]{2,1,0:T(8,128)} custom-call(s32[1]{0:T(128)} %bitcast.device_ref, s32[152]{0:T(256)S(1)} %pad_add_fusion.table_ref, bf16[24,14336]{1,0:T(8,128)(2,1)S(1)} %constant_dynamic-update-slice_fusion.refs_0_, bf16[24,14336]{1,0:T(8,128)(2,1)S(1)} %collective-permute-done.2.refs_1_, ...), custom_call_target="tpu_custom_call" | custom-call | flops 2260729856 | bytes 35323904 | tf_op jit(solution)/shard_map/pallas_call | solution.py:287
  (8 shorter events, 0.1 us)
Async XLA Ops:
  0.0 9.1 %collective-permute-start = (bf16[8,14336]{1,0:T(8,128)(2,1)}, bf16[8,14336]{1,0:T(8,128)(2,1)S(1)}, u32[]{:S(2)}, u32[]{:S(2)}) collective-permute-start(bf16[8,14336]{1,0:T(8,128)(2,1)} %param.3), channel_id=1, source_target_pairs={{0,4},{1,3},{2,0},{3,7},{4,8},{5,1},{6,2},{7,11},{8,12},{9,5},{10,... | collective-permute-start | bytes 688136 | tf_op jit(solution)/shard_map/ppermute | solution.py:158
  3.0 9.4 %collective-permute-start.1 = (bf16[8,14336]{1,0:T(8,128)(2,1)}, bf16[8,14336]{1,0:T(8,128)(2,1)S(1)}, u32[]{:S(2)}, u32[]{:S(2)}) collective-permute-start(bf16[8,14336]{1,0:T(8,128)(2,1)} %param.3), channel_id=1, source_target_pairs={{0,2},{1,5},{2,6},{3,1},{4,0},{5,9},{6,10},{7,3},{8,4},{9,13},{10,... | collective-permute-start | bytes 688136 | tf_op jit(solution)/shard_map/ppermute | solution.py:158
  9.1 6.4 %collective-permute-start.3 = (bf16[8,7168]{1,0:T(8,128)(2,1)S(1)}, bf16[8,7168]{1,0:T(8,128)(2,1)S(1)}, u32[]{:S(2)}, u32[]{:S(2)}) collective-permute-start(bf16[8,7168]{1,0:T(8,128)(2,1)S(1)} %get-tuple-element.9), channel_id=1, source_target_pairs={{0,4},{1,3},{2,0},{3,7},{4,8},{5,1},{6,2},{7,11},{8,12},{9,5},{10,... | collective-permute-start | bytes 344072 | tf_op jit(solution)/shard_map/ppermute | solution.py:158
  10.7 7.0 %collective-permute-start.4 = (bf16[8,7168]{1,0:T(8,128)(2,1)S(1)}, bf16[8,7168]{1,0:T(8,128)(2,1)S(1)}, u32[]{:S(2)}, u32[]{:S(2)}) collective-permute-start(bf16[8,7168]{1,0:T(8,128)(2,1)S(1)} %get-tuple-element.10), channel_id=1, source_target_pairs={{0,4},{1,3},{2,0},{3,7},{4,8},{5,1},{6,2},{7,11},{8,12},{9,5},{10,... | collective-permute-start | bytes 344072 | tf_op jit(solution)/shard_map/ppermute | solution.py:158
  12.4 6.0 %collective-permute-start.5 = (bf16[8,7168]{1,0:T(8,128)(2,1)S(1)}, bf16[8,7168]{1,0:T(8,128)(2,1)S(1)}, u32[]{:S(2)}, u32[]{:S(2)}) collective-permute-start(bf16[8,7168]{1,0:T(8,128)(2,1)S(1)} %get-tuple-element.11), channel_id=1, source_target_pairs={{0,2},{1,5},{2,6},{3,1},{4,0},{5,9},{6,10},{7,3},{8,4},{9,13},{10,... | collective-permute-start | bytes 344072 | tf_op jit(solution)/shard_map/ppermute | solution.py:158
  12.8 7.3 %collective-permute-start.6 = (bf16[8,7168]{1,0:T(8,128)(2,1)S(1)}, bf16[8,7168]{1,0:T(8,128)(2,1)S(1)}, u32[]{:S(2)}, u32[]{:S(2)}) collective-permute-start(bf16[8,7168]{1,0:T(8,128)(2,1)S(1)} %get-tuple-element.12), channel_id=1, source_target_pairs={{0,2},{1,5},{2,6},{3,1},{4,0},{5,9},{6,10},{7,3},{8,4},{9,13},{10,... | collective-permute-start | bytes 344072 | tf_op jit(solution)/shard_map/ppermute | solution.py:158
  13.7 11.2 %collective-permute-start.2 = (bf16[24,14336]{1,0:T(8,128)(2,1)S(1)}, bf16[24,14336]{1,0:T(8,128)(2,1)S(1)}, u32[]{:S(2)}, u32[]{:S(2)}) collective-permute-start(bf16[24,14336]{1,0:T(8,128)(2,1)S(1)} %constant_dynamic-update-slice_fusion.refs_0_), channel_id=1, source_target_pairs={{0,1},{1,0},{2,3},{3,2},{4,5},{5,4},{6,7},{7,6},{8,9},{9,8},{10,11... | collective-permute-start | bytes 2064392 | tf_op jit(solution)/shard_map/ppermute | solution.py:158
  15.4 9.5 %collective-permute-start.8 = (bf16[8,7168]{1,0:T(8,128)(2,1)S(1)}, bf16[8,7168]{1,0:T(8,128)(2,1)S(1)}, u32[]{:S(2)}, u32[]{:S(2)}) collective-permute-start(bf16[8,7168]{1,0:T(8,128)(2,1)S(1)} %collective-permute-done.3), channel_id=1, source_target_pairs={{0,4},{1,3},{2,0},{3,7},{4,8},{5,1},{6,2},{7,11},{8,12},{9,5},{10,... | collective-permute-start | bytes 344072 | tf_op jit(solution)/shard_map/ppermute | solution.py:158
  17.6 6.1 %collective-permute-start.9 = (bf16[8,7168]{1,0:T(8,128)(2,1)S(1)}, bf16[8,7168]{1,0:T(8,128)(2,1)S(1)}, u32[]{:S(2)}, u32[]{:S(2)}) collective-permute-start(bf16[8,7168]{1,0:T(8,128)(2,1)S(1)} %collective-permute-done.4), channel_id=1, source_target_pairs={{0,4},{1,3},{2,0},{3,7},{4,8},{5,1},{6,2},{7,11},{8,12},{9,5},{10,... | collective-permute-start | bytes 344072 | tf_op jit(solution)/shard_map/ppermute | solution.py:158
  18.4 7.1 %collective-permute-start.10 = (bf16[8,7168]{1,0:T(8,128)(2,1)S(1)}, bf16[8,7168]{1,0:T(8,128)(2,1)S(1)}, u32[]{:S(2)}, u32[]{:S(2)}) collective-permute-start(bf16[8,7168]{1,0:T(8,128)(2,1)S(1)} %collective-permute-done.5), channel_id=1, source_target_pairs={{0,2},{1,5},{2,6},{3,1},{4,0},{5,9},{6,10},{7,3},{8,4},{9,13},{10,... | collective-permute-start | bytes 344072 | tf_op jit(solution)/shard_map/ppermute | solution.py:158
  20.1 6.1 %collective-permute-start.11 = (bf16[8,7168]{1,0:T(8,128)(2,1)S(1)}, bf16[8,7168]{1,0:T(8,128)(2,1)S(1)}, u32[]{:S(2)}, u32[]{:S(2)}) collective-permute-start(bf16[8,7168]{1,0:T(8,128)(2,1)S(1)} %collective-permute-done.6), channel_id=1, source_target_pairs={{0,2},{1,5},{2,6},{3,1},{4,0},{5,9},{6,10},{7,3},{8,4},{9,13},{10,... | collective-permute-start | bytes 344072 | tf_op jit(solution)/shard_map/ppermute | solution.py:158
  23.7 6.1 %collective-permute-start.14 = (bf16[8,7168]{1,0:T(8,128)(2,1)S(1)}, bf16[8,7168]{1,0:T(8,128)(2,1)S(1)}, u32[]{:S(2)}, u32[]{:S(2)}) collective-permute-start(bf16[8,7168]{1,0:T(8,128)(2,1)S(1)} %collective-permute-done.9), channel_id=1, source_target_pairs={{0,4},{1,3},{2,0},{3,7},{4,8},{5,1},{6,2},{7,11},{8,12},{9,5},{10,... | collective-permute-start | bytes 344072 | tf_op jit(solution)/shard_map/ppermute | solution.py:158
  24.9 4.8 %collective-permute-start.13 = (bf16[8,7168]{1,0:T(8,128)(2,1)S(1)}, bf16[8,7168]{1,0:T(8,128)(2,1)S(1)}, u32[]{:S(2)}, u32[]{:S(2)}) collective-permute-start(bf16[8,7168]{1,0:T(8,128)(2,1)S(1)} %collective-permute-done.8), channel_id=1, source_target_pairs={{0,4},{1,3},{2,0},{3,7},{4,8},{5,1},{6,2},{7,11},{8,12},{9,5},{10,... | collective-permute-start | bytes 344072 | tf_op jit(solution)/shard_map/ppermute | solution.py:158
  26.3 5.2 %collective-permute-start.12 = (bf16[16,14336]{1,0:T(8,128)(2,1)S(1)}, bf16[16,14336]{1,0:T(8,128)(2,1)S(1)}, u32[]{:S(2)}, u32[]{:S(2)}) collective-permute-start(bf16[16,14336]{1,0:T(8,128)(2,1)S(1)} %maximum_maximum_fusion.1.refs_4_), channel_id=1, source_target_pairs={{0,1},{1,0},{2,3},{3,2},{4,5},{5,4},{6,7},{7,6},{8,9},{9,8},{10,11... | collective-permute-start | bytes 1376264 | tf_op jit(solution)/shard_map/ppermute | solution.py:158
  26.3 5.1 %collective-permute-start.7 = (bf16[16,14336]{1,0:T(8,128)(2,1)S(1)}, bf16[16,14336]{1,0:T(8,128)(2,1)S(1)}, u32[]{:S(2)}, u32[]{:S(2)}) collective-permute-start(bf16[16,14336]{1,0:T(8,128)(2,1)S(1)} %maximum_maximum_fusion.refs_2_), channel_id=1, source_target_pairs={{0,1},{1,0},{2,3},{3,2},{4,5},{5,4},{6,7},{7,6},{8,9},{9,8},{10,11... | collective-permute-start | bytes 1376264 | tf_op jit(solution)/shard_map/ppermute | solution.py:158
  29.8 1.7 %collective-permute-start.15 = (bf16[8,14336]{1,0:T(8,128)(2,1)S(1)}, bf16[8,14336]{1,0:T(8,128)(2,1)}, u32[]{:S(2)}, u32[]{:S(2)}) collective-permute-start(bf16[8,14336]{1,0:T(8,128)(2,1)S(1)} %constant_dynamic-update-slice_fusion.3.refs_6_), channel_id=1, source_target_pairs={{0,1},{1,0},{2,3},{3,2},{4,5},{5,4},{6,7},{7,6},{8,9},{9,8},{10,11... | collective-permute-start | bytes 688136 | tf_op jit(solution)/shard_map/ppermute | solution.py:158

commit v11 on v8

--- a/solution.py
+++ b/solution.py
@@ -152,31 +152,26 @@
 def ring_gather(tokens, device, devices):
     onward, backward = ring_plan(devices)
     sibling = [device ^ 1 for device in range(devices)]
-    across = [device ^ 2 for device in range(devices)]
-    mirror = [(at, at ^ 12) for at in range(devices) if at // 4 in (0, 3)]
+    over = [at ^ 12 if at // 4 in (0, 3) else at ^ 2 for at in range(devices)]
 
     def send(value, target):
         return lax.ppermute(value, "col", list(enumerate(target)))
 
     def after(value, *others):
         return lax.optimization_barrier((value, *others))[0]
+
+    chip, core = device // 2, device % 2
+    came_ahead = ((chip % 4 == 0) | (chip % 4 == 3)) == (core == 0)
 
     ahead, back = [tokens], [tokens]
     for _ in range(2):
         ahead.append(send(ahead[-1], onward))
         back.append(send(back[-1], backward))
-    far = lax.ppermute(tokens, "col", mirror)
-    chip, core = device // 2, device % 2
-    at_end = (chip < 2) | (chip >= devices // 2 - 2)
-    came_ahead = (((chip == 3) | (chip == 4)) == (core == 0)) & ~at_end
-    held = jnp.where(at_end, far, jnp.where(came_ahead, ahead[1], back[1]))
-    half = send(held, across)
+    half = send(jnp.where(came_ahead, ahead[1], back[1]), over)
     ahead.append(send(after(ahead[2], back[2]), onward))
     back.append(send(after(back[2], ahead[2]), backward))
     groups = []
-    for group, others in (
-        ((tokens, ahead[1], back[1]), (ahead[2], back[2])), ((ahead[2], back[2], half), (ahead[2], back[2])), ((ahead[3], back[3]), ()),
-    ):
+    for group, others in (((tokens, ahead[1], back[1]), ()), ((ahead[2], back[2], half), ()), ((ahead[3], back[3]), ())):
         group = jnp.concatenate(group, axis=0)
         groups += [group, send(after(group, *others) if others else group, sibling)]
     return groups

time: 44.4 us -> 43 us (0.968)
  starting transfers between devices: 16.5 us -> 12.1 us
  waiting for transfers between devices: 13.1 us -> 16 us
    ppermute x10, waiting for transfers between devices: 8.17 us -> 16 us  [send(): return lax.ppermute(value, 'col', list(enumerate(target)))]
    ppermute x1 -> x0, starting transfers between devices: 5.94 us -> none  [ring_gather(): far = lax.ppermute(tokens, 'col', mirror)]
    ppermute x1 -> x0, waiting for transfers between devices: 4.97 us -> none  [ring_gather(): far = lax.ppermute(tokens, 'col', mirror)]
    ppermute x10, starting transfers between devices: 10.5 us -> 12.1 us  [send(): return lax.ppermute(value, 'col', list(enumerate(target)))]
  transfers between devices with their start and end apart: 11 -> 10, of which waited for: 5 -> 7; matrix products, arithmetic and copies ran while one was open for 4% -> 5% of each run, Pallas kernels for 0% -> 0%
where the time goes in v11:
time: 43 us; the launch traced here: 42.7 us
  waiting for transfers between devices  16 us (37%)
  Pallas kernels  12.6 us (29%)
  starting transfers between devices  12.1 us (28%)
  local copies, waits for them, and re-layouts  1.12 us (3%)
  other arithmetic  0.82 us (2%)
    ppermute x10, waiting for transfers between devices, send(): return lax.ppermute(value, 'col', list(enumerate(target)))  16 us
    pallas_call x1, Pallas kernels, ring_form(): pl.pallas_call(functools.partial(ring_kernel, devices, slots), out_shape=...  12.6 us
    ppermute x10, starting transfers between devices, send(): return lax.ppermute(value, 'col', list(enumerate(target)))  12.1 us
    unnamed x5, local copies, waits for them, and re-layouts  1.08 us
  transfers between devices with their start and end apart: 10, of which 7 were waited for; matrix products, arithmetic and copies ran while one was open for 5% of the time, Pallas kernels for 0%

profile of v11, /device:TPU:0, one launch (start us, length us, event | category | flops | bytes accessed | tf_op | source)
XLA Modules:
  0.0 42.7 jit_solution(5980483728969899924)
XLA Ops:
  0.0 3.0 %collective-permute-start = (bf16[8,14336]{1,0:T(8,128)(2,1)}, bf16[8,14336]{1,0:T(8,128)(2,1)S(1)}, u32[]{:S(2)}, u32[]{:S(2)}) collective-permute-start(bf16[8,14336]{1,0:T(8,128)(2,1)} %param.3), channel_id=1, source_target_pairs={{0,4},{1,3},{2,0},{3,7},{4,8},{5,1},{6,2},{7,11},{8,12},{9,5},{10,... | collective-permute-start | bytes 688136 | tf_op jit(solution)/shard_map/ppermute | solution.py:158
  3.0 0.0 collective-permute-start.1
  3.0 1.0 %constant_dynamic-update-slice_fusion.2 = bf16[24,14336]{1,0:T(8,128)(2,1)S(1)} fusion(bf16[8,14336]{1,0:T(8,128)(2,1)} %param.3), kind=kLoop, calls=%fused_computation.3 | loop fusion | bytes 458752
  4.1 5.0 %collective-permute-done = bf16[8,14336]{1,0:T(8,128)(2,1)S(1)} collective-permute-done((bf16[8,14336]{1,0:T(8,128)(2,1)}, bf16[8,14336]{1,0:T(8,128)(2,1)S(1)}, u32[]{:S(2)}, u32[]{:S(2)}) %collective-permute-start) | collective-permute-done | bytes 229408 | tf_op jit(solution)/shard_map/ppermute | solution.py:158
  9.1 1.5 %collective-permute-start.3 = (bf16[8,14336]{1,0:T(8,128)(2,1)S(1)}, bf16[8,14336]{1,0:T(8,128)(2,1)S(1)}, u32[]{:S(2)}, u32[]{:S(2)}) collective-permute-start(bf16[8,14336]{1,0:T(8,128)(2,1)S(1)} %collective-permute-done), channel_id=1, source_target_pairs={{0,4},{1,3},{2,0},{3,7},{4,8},{5,1},{6,2},{7,11},{8,12},{9,5},{10,... | collective-permute-start | bytes 688136 | tf_op jit(solution)/shard_map/ppermute | solution.py:158
  10.6 0.0 collective-permute-done.1
  10.6 0.9 %collective-permute-start.4 = (bf16[8,14336]{1,0:T(8,128)(2,1)S(1)}, bf16[8,14336]{1,0:T(8,128)(2,1)S(1)}, u32[]{:S(2)}, u32[]{:S(2)}) collective-permute-start(bf16[8,14336]{1,0:T(8,128)(2,1)S(1)} %collective-permute-done.1), channel_id=1, source_target_pairs={{0,2},{1,5},{2,6},{3,1},{4,0},{5,9},{6,10},{7,3},{8,4},{9,13},{10,... | collective-permute-start | bytes 688136 | tf_op jit(solution)/shard_map/ppermute | solution.py:158
  11.5 0.1 broadcast_select_fusion
  11.6 3.4 %collective-permute-start.5 = (bf16[8,14336]{1,0:T(8,128)(2,1)S(1)}, bf16[8,14336]{1,0:T(8,128)(2,1)S(1)}, u32[]{:S(2)}, u32[]{:S(2)}) collective-permute-start(bf16[8,14336]{1,0:T(8,128)(2,1)S(1)} %get-tuple-element.9), channel_id=1, source_target_pairs={{0,12},{1,13},{2,14},{3,15},{4,6},{5,7},{6,4},{7,5},{8,10},{9,11},... | collective-permute-start | bytes 688136 | tf_op jit(solution)/shard_map/ppermute | solution.py:158
  15.0 0.0 collective-permute-start.2
  15.0 2.4 %collective-permute-done.3 = bf16[8,14336]{1,0:T(8,128)(2,1)S(1)} collective-permute-done((bf16[8,14336]{1,0:T(8,128)(2,1)S(1)}, bf16[8,14336]{1,0:T(8,128)(2,1)S(1)}, u32[]{:S(2)}, u32[]{:S(2)}) %collective-permute-start.3) | collective-permute-done | bytes 229408 | tf_op jit(solution)/shard_map/ppermute | solution.py:158
  17.3 1.7 %collective-permute-done.4 = bf16[8,14336]{1,0:T(8,128)(2,1)S(1)} collective-permute-done((bf16[8,14336]{1,0:T(8,128)(2,1)S(1)}, bf16[8,14336]{1,0:T(8,128)(2,1)S(1)}, u32[]{:S(2)}, u32[]{:S(2)}) %collective-permute-start.4) | collective-permute-done | bytes 229408 | tf_op jit(solution)/shard_map/ppermute | solution.py:158
  19.1 3.1 %collective-permute-start.7 = (bf16[8,14336]{1,0:T(8,128)(2,1)S(1)}, bf16[8,14336]{1,0:T(8,128)(2,1)S(1)}, u32[]{:S(2)}, u32[]{:S(2)}) collective-permute-start(bf16[8,14336]{1,0:T(8,128)(2,1)S(1)} %collective-permute-done.3), channel_id=1, source_target_pairs={{0,4},{1,3},{2,0},{3,7},{4,8},{5,1},{6,2},{7,11},{8,12},{9,5},{10,... | collective-permute-start | bytes 688136 | tf_op jit(solution)/shard_map/ppermute | solution.py:158
  22.2 0.0 collective-permute-start.8
  22.2 2.1 %collective-permute-done.5 = bf16[8,14336]{1,0:T(8,128)(2,1)S(1)} collective-permute-done((bf16[8,14336]{1,0:T(8,128)(2,1)S(1)}, bf16[8,14336]{1,0:T(8,128)(2,1)S(1)}, u32[]{:S(2)}, u32[]{:S(2)}) %collective-permute-start.5) | collective-permute-done | bytes 229408 | tf_op jit(solution)/shard_map/ppermute | solution.py:158
  24.4 0.1 collective-permute-start.6
  24.5 1.3 %collective-permute-done.7 = bf16[8,14336]{1,0:T(8,128)(2,1)S(1)} collective-permute-done((bf16[8,14336]{1,0:T(8,128)(2,1)S(1)}, bf16[8,14336]{1,0:T(8,128)(2,1)S(1)}, u32[]{:S(2)}, u32[]{:S(2)}) %collective-permute-start.7) | collective-permute-done | bytes 229408 | tf_op jit(solution)/shard_map/ppermute | solution.py:158
  25.7 2.5 %collective-permute-done.8 = bf16[8,14336]{1,0:T(8,128)(2,1)S(1)} collective-permute-done((bf16[8,14336]{1,0:T(8,128)(2,1)S(1)}, bf16[8,14336]{1,0:T(8,128)(2,1)S(1)}, u32[]{:S(2)}, u32[]{:S(2)}) %collective-permute-start.8) | collective-permute-done | bytes 229408 | tf_op jit(solution)/shard_map/ppermute | solution.py:158
  28.2 0.1 collective-permute-start.9
  28.3 0.8 %pad_add_fusion.table_ref = s32[152]{0:T(256)S(1)} fusion(s32[136]{0:T(256)} %param.5, s32[16]{0:T(128)} %param.4), kind=kLoop, calls=%fused_computation.9 | loop fusion | flops 152 | bytes 1216 | tf_op jit(solution)/shard_map/concatenate | solution.py:282
  29.1 0.0 collective-permute-done.2.refs_1_
  29.1 1.0 %collective-permute-done.9.refs_5_ = bf16[16,14336]{1,0:T(8,128)(2,1)S(1)} collective-permute-done((bf16[16,14336]{1,0:T(8,128)(2,1)S(1)}, bf16[16,14336]{1,0:T(8,128)(2,1)S(1)}, u32[]{:S(2)}, u32[]{:S(2)}) %collective-permute-start.9) | collective-permute-done | bytes 458784 | tf_op jit(solution)/shard_map/ppermute | solution.py:158
  30.1 0.0 collective-permute-done.6.refs_3_
  30.1 12.6 %shard_map.37 = f32[11,896,896]{2,1,0:T(8,128)} custom-call(s32[1]{0:T(128)} %bitcast.device_ref, s32[152]{0:T(256)S(1)} %pad_add_fusion.table_ref, bf16[24,14336]{1,0:T(8,128)(2,1)S(1)} %get-tuple-element.10.refs_0_, bf16[24,14336]{1,0:T(8,128)(2,1)S(1)} %collective-permute-done.2.refs_1_, ...), custom_call_target="tpu_custom_call" | custom-call | flops 2260729856 | bytes 35323904 | tf_op jit(solution)/shard_map/pallas_call | solution.py:283
  (6 shorter events, 0.1 us)
Async XLA Ops:
  0.0 9.1 %collective-permute-start = (bf16[8,14336]{1,0:T(8,128)(2,1)}, bf16[8,14336]{1,0:T(8,128)(2,1)S(1)}, u32[]{:S(2)}, u32[]{:S(2)}) collective-permute-start(bf16[8,14336]{1,0:T(8,128)(2,1)} %param.3), channel_id=1, source_target_pairs={{0,4},{1,3},{2,0},{3,7},{4,8},{5,1},{6,2},{7,11},{8,12},{9,5},{10,... | collective-permute-start | bytes 688136 | tf_op jit(solution)/shard_map/ppermute | solution.py:158
  3.0 7.6 %collective-permute-start.1 = (bf16[8,14336]{1,0:T(8,128)(2,1)}, bf16[8,14336]{1,0:T(8,128)(2,1)S(1)}, u32[]{:S(2)}, u32[]{:S(2)}) collective-permute-start(bf16[8,14336]{1,0:T(8,128)(2,1)} %param.3), channel_id=1, source_target_pairs={{0,2},{1,5},{2,6},{3,1},{4,0},{5,9},{6,10},{7,3},{8,4},{9,13},{10,... | collective-permute-start | bytes 688136 | tf_op jit(solution)/shard_map/ppermute | solution.py:158
  9.1 8.3 %collective-permute-start.3 = (bf16[8,14336]{1,0:T(8,128)(2,1)S(1)}, bf16[8,14336]{1,0:T(8,128)(2,1)S(1)}, u32[]{:S(2)}, u32[]{:S(2)}) collective-permute-start(bf16[8,14336]{1,0:T(8,128)(2,1)S(1)} %collective-permute-done), channel_id=1, source_target_pairs={{0,4},{1,3},{2,0},{3,7},{4,8},{5,1},{6,2},{7,11},{8,12},{9,5},{10,... | collective-permute-start | bytes 688136 | tf_op jit(solution)/shard_map/ppermute | solution.py:158
  10.6 8.5 %collective-permute-start.4 = (bf16[8,14336]{1,0:T(8,128)(2,1)S(1)}, bf16[8,14336]{1,0:T(8,128)(2,1)S(1)}, u32[]{:S(2)}, u32[]{:S(2)}) collective-permute-start(bf16[8,14336]{1,0:T(8,128)(2,1)S(1)} %collective-permute-done.1), channel_id=1, source_target_pairs={{0,2},{1,5},{2,6},{3,1},{4,0},{5,9},{6,10},{7,3},{8,4},{9,13},{10,... | collective-permute-start | bytes 688136 | tf_op jit(solution)/shard_map/ppermute | solution.py:158
  11.6 12.8 %collective-permute-start.5 = (bf16[8,14336]{1,0:T(8,128)(2,1)S(1)}, bf16[8,14336]{1,0:T(8,128)(2,1)S(1)}, u32[]{:S(2)}, u32[]{:S(2)}) collective-permute-start(bf16[8,14336]{1,0:T(8,128)(2,1)S(1)} %get-tuple-element.9), channel_id=1, source_target_pairs={{0,12},{1,13},{2,14},{3,15},{4,6},{5,7},{6,4},{7,5},{8,10},{9,11},... | collective-permute-start | bytes 688136 | tf_op jit(solution)/shard_map/ppermute | solution.py:158
  15.0 14.1 %collective-permute-start.2 = (bf16[24,14336]{1,0:T(8,128)(2,1)S(1)}, bf16[24,14336]{1,0:T(8,128)(2,1)S(1)}, u32[]{:S(2)}, u32[]{:S(2)}) collective-permute-start(bf16[24,14336]{1,0:T(8,128)(2,1)S(1)} %get-tuple-element.10.refs_0_), channel_id=1, source_target_pairs={{0,1},{1,0},{2,3},{3,2},{4,5},{5,4},{6,7},{7,6},{8,9},{9,8},{10,11... | collective-permute-start | bytes 2064392 | tf_op jit(solution)/shard_map/ppermute | solution.py:158
  19.1 6.7 %collective-permute-start.7 = (bf16[8,14336]{1,0:T(8,128)(2,1)S(1)}, bf16[8,14336]{1,0:T(8,128)(2,1)S(1)}, u32[]{:S(2)}, u32[]{:S(2)}) collective-permute-start(bf16[8,14336]{1,0:T(8,128)(2,1)S(1)} %collective-permute-done.3), channel_id=1, source_target_pairs={{0,4},{1,3},{2,0},{3,7},{4,8},{5,1},{6,2},{7,11},{8,12},{9,5},{10,... | collective-permute-start | bytes 688136 | tf_op jit(solution)/shard_map/ppermute | solution.py:158
  22.2 6.0 %collective-permute-start.8 = (bf16[8,14336]{1,0:T(8,128)(2,1)S(1)}, bf16[8,14336]{1,0:T(8,128)(2,1)S(1)}, u32[]{:S(2)}, u32[]{:S(2)}) collective-permute-start(bf16[8,14336]{1,0:T(8,128)(2,1)S(1)} %collective-permute-done.4), channel_id=1, source_target_pairs={{0,2},{1,5},{2,6},{3,1},{4,0},{5,9},{6,10},{7,3},{8,4},{9,13},{10,... | collective-permute-start | bytes 688136 | tf_op jit(solution)/shard_map/ppermute | solution.py:158
  24.4 5.7 %collective-permute-start.6 = (bf16[24,14336]{1,0:T(8,128)(2,1)S(1)}, bf16[24,14336]{1,0:T(8,128)(2,1)S(1)}, u32[]{:S(2)}, u32[]{:S(2)}) collective-permute-start(bf16[24,14336]{1,0:T(8,128)(2,1)S(1)} %constant_dynamic-update-slice_fusion.3.refs_2_), channel_id=1, source_target_pairs={{0,1},{1,0},{2,3},{3,2},{4,5},{5,4},{6,7},{7,6},{8,9},{9,8},{10,11... | collective-permute-start | bytes 2064392 | tf_op jit(solution)/shard_map/ppermute | solution.py:158
  28.2 1.9 %collective-permute-start.9 = (bf16[16,14336]{1,0:T(8,128)(2,1)S(1)}, bf16[16,14336]{1,0:T(8,128)(2,1)S(1)}, u32[]{:S(2)}, u32[]{:S(2)}) collective-permute-start(bf16[16,14336]{1,0:T(8,128)(2,1)S(1)} %constant_dynamic-update-slice_fusion.6.refs_4_), channel_id=1, source_target_pairs={{0,1},{1,0},{2,3},{3,2},{4,5},{5,4},{6,7},{7,6},{8,9},{9,8},{10,11... | collective-permute-start | bytes 1376264 | tf_op jit(solution)/shard_map/ppermute | solution.py:158

commit v12 on v11

--- a/solution.py
+++ b/solution.py
@@ -146,7 +146,11 @@
     return onward, backward
 
 
-GROUPS = ((0, 1, 2), (8, 9, 10), (3, 4, 7), (11, 12, 15), (5, 6), (13, 14))
+GROUPS = ((0, 1, 2), (8, 9, 10), (3, 4), (11, 12), (5, 6, 7), (13, 14, 15))
+
+
+def first_needed(devices, chip):
+    return (2 * chip - devices // 2 - devices // 8 + devices) % devices
 
 
 def ring_gather(tokens, device, devices):
@@ -161,20 +165,45 @@
         return lax.optimization_barrier((value, *others))[0]
 
     chip, core = device // 2, device % 2
+    chips = devices // 2
+    even = chip % 2 == 0
+    next_chip = jnp.where(even, jnp.where(chip == chips - 2, chips - 1, chip + 2), jnp.where(chip == 1, 0, chip - 2))
+    last_chip = jnp.where(even, jnp.where(chip == 0, 1, chip - 2), jnp.where(chip == chips - 1, chips - 2, chip + 2))
+    onward_chip = jnp.where(core == 0, next_chip, last_chip)
+    backward_chip = jnp.where(core == 0, last_chip, next_chip)
+    over_chip = jnp.where((chip < 2) | (chip >= chips - 2), chip ^ 6, chip ^ 1)
+    chip, core = device // 2, device % 2
+    chips = devices // 2
+    even = chip % 2 == 0
+    next_chip = jnp.where(even, jnp.where(chip == chips - 2, chips - 1, chip + 2), jnp.where(chip == 1, 0, chip - 2))
+    last_chip = jnp.where(even, jnp.where(chip == 0, 1, chip - 2), jnp.where(chip == chips - 1, chips - 2, chip + 2))
+    onward_chip = jnp.where(core == 0, next_chip, last_chip)
+    backward_chip = jnp.where(core == 0, last_chip, next_chip)
+    over_chip = jnp.where((chip < 2) | (chip >= chips - 2), chip ^ 6, chip ^ 1)
     came_ahead = ((chip % 4 == 0) | (chip % 4 == 3)) == (core == 0)
+    slab, units = tokens.shape
+    needed = devices // 2 + devices // 8 + 2
+
+    def window(value, chip):
+        blocks = value.reshape(slab, devices, units // devices)
+        blocks = jnp.concatenate([blocks, blocks], axis=1)
+        blocks = lax.dynamic_slice_in_dim(blocks, first_needed(devices, chip), needed, axis=1)
+        return blocks.reshape(slab, -1)
 
     ahead, back = [tokens], [tokens]
     for _ in range(2):
         ahead.append(send(ahead[-1], onward))
         back.append(send(back[-1], backward))
-    half = send(jnp.where(came_ahead, ahead[1], back[1]), over)
-    ahead.append(send(after(ahead[2], back[2]), onward))
-    back.append(send(after(back[2], ahead[2]), backward))
-    groups = []
-    for group, others in (((tokens, ahead[1], back[1]), ()), ((ahead[2], back[2], half), ()), ((ahead[3], back[3]), ())):
-        group = jnp.concatenate(group, axis=0)
-        groups += [group, send(after(group, *others) if others else group, sibling)]
-    return groups
+    half = send(window(jnp.where(came_ahead, ahead[1], back[1]), over_chip), over)
+    ahead.append(send(window(ahead[2], onward_chip), onward))
+    back.append(send(window(back[2], backward_chip), backward))
+    near = jnp.concatenate((tokens, ahead[1], back[1]), axis=0)
+    middle = jnp.concatenate((ahead[2], back[2]), axis=0)
+    last = jnp.concatenate((ahead[3], back[3], half), axis=0)
+    near_beside = send(near, sibling)
+    middle_beside = send(middle, sibling)
+    last_beside = send(after(last, middle_beside), sibling)
+    return [near, near_beside, middle, middle_beside, last, last_beside]
 
 def slab_origin(devices, device, number):
     chips = devices // 2
@@ -204,9 +233,14 @@
         return pltpu.make_async_copy(zeros, out_ref.at[slot], zero_sems.at[slot])
 
     def load_block(partner, masked):
-        columns = pl.ds(pl.multiple_of(partner * width, 128), width)
         parts = []
         for numbers, ref in zip(GROUPS, groups):
+            whole = ref.shape[1] == devices * width
+            place = partner if whole else (partner - first_needed(devices, device // 2) + devices) % devices
+            columns = pl.ds(pl.multiple_of(place * width, 128), width)
+            whole = ref.shape[1] == devices * width
+            place = partner if whole else (partner - first_needed(devices, device // 2) + devices) % devices
+            columns = pl.ds(pl.multiple_of(place * width, 128), width)
             group = ref[:, columns].astype(jnp.float32)
             for at, number in enumerate(numbers):
                 part = group[at * slab:(at + 1) * slab]

time: 43 us -> 41.1 us (0.956)
  waiting for transfers between devices: 16 us -> 14.4 us
  starting transfers between devices: 12.1 us -> 11.4 us
    ppermute x10, waiting for transfers between devices: 16 us -> 14.4 us  [send(): return lax.ppermute(value, 'col', list(enumerate(target)))]
    ppermute x10, starting transfers between devices: 12.1 us -> 11.4 us  [send(): return lax.ppermute(value, 'col', list(enumerate(target)))]
  transfers between devices with their start and end apart: 10 -> 10, of which waited for: 7 -> 5; matrix products, arithmetic and copies ran while one was open for 5% -> 5% of each run, Pallas kernels for 0% -> 0%
where the time goes in v12:
time: 41.1 us; the launch traced here: 40.9 us
  waiting for transfers between devices  14.4 us (35%)
  Pallas kernels  12.6 us (31%)
  starting transfers between devices  11.4 us (28%)
  local copies, waits for them, and re-layouts  1.11 us (3%)
  other arithmetic  1.11 us (3%)
    ppermute x10, waiting for transfers between devices, send(): return lax.ppermute(value, 'col', list(enumerate(target)))  14.4 us
    pallas_call x1, Pallas kernels, ring_form(): pl.pallas_call(functools.partial(ring_kernel, devices, slots), out_shape=...  12.6 us
    ppermute x10, starting transfers between devices, send(): return lax.ppermute(value, 'col', list(enumerate(target)))  11.4 us
    unnamed x5, local copies, waits for them, and re-layouts  1.08 us
  transfers between devices with their start and end apart: 10, of which 5 were waited for; matrix products, arithmetic and copies ran while one was open for 5% of the time, Pallas kernels for 0%

profile of v12, /device:TPU:0, one launch (start us, length us, event | category | flops | bytes accessed | tf_op | source)
XLA Modules:
  0.0 40.9 jit_solution(991245248137540358)
XLA Ops:
  0.0 3.0 %collective-permute-start = (bf16[8,14336]{1,0:T(8,128)(2,1)}, bf16[8,14336]{1,0:T(8,128)(2,1)S(1)}, u32[]{:S(2)}, u32[]{:S(2)}) collective-permute-start(bf16[8,14336]{1,0:T(8,128)(2,1)} %param.3), channel_id=1, source_target_pairs={{0,4},{1,3},{2,0},{3,7},{4,8},{5,1},{6,2},{7,11},{8,12},{9,5},{10,... | collective-permute-start | bytes 688136 | tf_op jit(solution)/shard_map/ppermute | solution.py:162
  3.0 0.0 collective-permute-start.1
  3.0 1.0 %constant_dynamic-update-slice_fusion.2 = bf16[24,14336]{1,0:T(8,128)(2,1)S(1)} fusion(bf16[8,14336]{1,0:T(8,128)(2,1)} %param.3), kind=kLoop, calls=%fused_computation.12 | loop fusion | bytes 458752
  4.2 4.9 %collective-permute-done = bf16[8,14336]{1,0:T(8,128)(2,1)S(1)} collective-permute-done((bf16[8,14336]{1,0:T(8,128)(2,1)}, bf16[8,14336]{1,0:T(8,128)(2,1)S(1)}, u32[]{:S(2)}, u32[]{:S(2)}) %collective-permute-start) | collective-permute-done | bytes 229408 | tf_op jit(solution)/shard_map/ppermute | solution.py:162
  9.1 1.5 %collective-permute-start.3 = (bf16[8,14336]{1,0:T(8,128)(2,1)S(1)}, bf16[8,14336]{1,0:T(8,128)(2,1)S(1)}, u32[]{:S(2)}, u32[]{:S(2)}) collective-permute-start(bf16[8,14336]{1,0:T(8,128)(2,1)S(1)} %collective-permute-done), channel_id=1, source_target_pairs={{0,4},{1,3},{2,0},{3,7},{4,8},{5,1},{6,2},{7,11},{8,12},{9,5},{10,... | collective-permute-start | bytes 688136 | tf_op jit(solution)/shard_map/ppermute | solution.py:162
  10.6 0.0 collective-permute-done.1
  10.6 0.9 %collective-permute-start.4 = (bf16[8,14336]{1,0:T(8,128)(2,1)S(1)}, bf16[8,14336]{1,0:T(8,128)(2,1)S(1)}, u32[]{:S(2)}, u32[]{:S(2)}) collective-permute-start(bf16[8,14336]{1,0:T(8,128)(2,1)S(1)} %collective-permute-done.1), channel_id=1, source_target_pairs={{0,2},{1,5},{2,6},{3,1},{4,0},{5,9},{6,10},{7,3},{8,4},{9,13},{10,... | collective-permute-start | bytes 688136 | tf_op jit(solution)/shard_map/ppermute | solution.py:162
  11.5 0.1 broadcast_select_fusion
  11.6 0.1 fusion
  11.7 3.4 %collective-permute-start.8 = (bf16[8,10752]{1,0:T(8,128)(2,1)S(1)}, bf16[8,10752]{1,0:T(8,128)(2,1)S(1)}, u32[]{:S(2)}, u32[]{:S(2)}) collective-permute-start(bf16[8,10752]{1,0:T(8,128)(2,1)S(1)} %bitcast.10), channel_id=1, source_target_pairs={{0,12},{1,13},{2,14},{3,15},{4,6},{5,7},{6,4},{7,5},{8,10},{9,11},... | collective-permute-start | bytes 516104 | tf_op jit(solution)/shard_map/ppermute | solution.py:162
  15.1 0.0 collective-permute-start.2
  15.1 2.3 %collective-permute-done.3 = bf16[8,14336]{1,0:T(8,128)(2,1)S(1)} collective-permute-done((bf16[8,14336]{1,0:T(8,128)(2,1)S(1)}, bf16[8,14336]{1,0:T(8,128)(2,1)S(1)}, u32[]{:S(2)}, u32[]{:S(2)}) %collective-permute-start.3) | collective-permute-done | bytes 229408 | tf_op jit(solution)/shard_map/ppermute | solution.py:162
  17.3 0.1 fusion.2
  17.4 2.4 %collective-permute-start.6 = (bf16[8,10752]{1,0:T(8,128)(2,1)S(1)}, bf16[8,10752]{1,0:T(8,128)(2,1)S(1)}, u32[]{:S(2)}, u32[]{:S(2)}) collective-permute-start(bf16[8,10752]{1,0:T(8,128)(2,1)S(1)} %bitcast.11), channel_id=1, source_target_pairs={{0,4},{1,3},{2,0},{3,7},{4,8},{5,1},{6,2},{7,11},{8,12},{9,5},{10,... | collective-permute-start | bytes 516104 | tf_op jit(solution)/shard_map/ppermute | solution.py:162
  19.8 0.0 collective-permute-done.4
  19.8 0.1 fusion.1
  19.9 0.1 collective-permute-start.7
  20.0 0.1 collective-permute-start.5
  20.1 3.4 %collective-permute-done.6 = bf16[8,10752]{1,0:T(8,128)(2,1)S(1)} collective-permute-done((bf16[8,10752]{1,0:T(8,128)(2,1)S(1)}, bf16[8,10752]{1,0:T(8,128)(2,1)S(1)}, u32[]{:S(2)}, u32[]{:S(2)}) %collective-permute-start.6) | collective-permute-done | bytes 172064 | tf_op jit(solution)/shard_map/ppermute | solution.py:162
  23.5 2.8 %collective-permute-done.7 = bf16[8,10752]{1,0:T(8,128)(2,1)S(1)} collective-permute-done((bf16[8,10752]{1,0:T(8,128)(2,1)S(1)}, bf16[8,10752]{1,0:T(8,128)(2,1)S(1)}, u32[]{:S(2)}, u32[]{:S(2)}) %collective-permute-start.7) | collective-permute-done | bytes 172064 | tf_op jit(solution)/shard_map/ppermute | solution.py:162
  26.3 0.0 collective-permute-done.8
  26.3 0.0 collective-permute-done.5.refs_3_
  26.3 0.1 collective-permute-start.9
  26.4 0.8 %pad_add_fusion.table_ref = s32[152]{0:T(256)S(1)} fusion(s32[136]{0:T(256)} %param.5, s32[16]{0:T(128)} %param.4), kind=kLoop, calls=%fused_computation.18 | loop fusion | flops 152 | bytes 1216 | tf_op jit(solution)/shard_map/concatenate | solution.py:316
  27.2 0.0 collective-permute-done.2.refs_1_
  27.2 1.1 %collective-permute-done.9.refs_5_ = bf16[24,10752]{1,0:T(8,128)(2,1)S(1)} collective-permute-done((bf16[24,10752]{1,0:T(8,128)(2,1)S(1)}, bf16[24,10752]{1,0:T(8,128)(2,1)S(1)}, u32[]{:S(2)}, u32[]{:S(2)}) %collective-permute-start.9) | collective-permute-done | bytes 516128 | tf_op jit(solution)/shard_map/ppermute | solution.py:162
  28.3 12.6 %shard_map.37 = f32[11,896,896]{2,1,0:T(8,128)} custom-call(s32[1]{0:T(128)} %bitcast.device_ref, s32[152]{0:T(256)S(1)} %pad_add_fusion.table_ref, bf16[24,14336]{1,0:T(8,128)(2,1)S(1)} %get-tuple-element.8.refs_0_, bf16[24,14336]{1,0:T(8,128)(2,1)S(1)} %collective-permute-done.2.refs_1_, bf16[16,14336]{1,0:T(8,128)(2,1)S(1)} %constant_dynamic-update-slice_fusion.3.refs_2_, ...), custom_call_target="tpu_custom_call" | custom-call | flops 2260729856 | bytes 35323904 | tf_op jit(solution)/shard_map/pallas_call | solution.py:317
  (6 shorter events, 0.1 us)
Async XLA Ops:
  0.0 9.1 %collective-permute-start = (bf16[8,14336]{1,0:T(8,128)(2,1)}, bf16[8,14336]{1,0:T(8,128)(2,1)S(1)}, u32[]{:S(2)}, u32[]{:S(2)}) collective-permute-start(bf16[8,14336]{1,0:T(8,128)(2,1)} %param.3), channel_id=1, source_target_pairs={{0,4},{1,3},{2,0},{3,7},{4,8},{5,1},{6,2},{7,11},{8,12},{9,5},{10,... | collective-permute-start | bytes 688136 | tf_op jit(solution)/shard_map/ppermute | solution.py:162
  3.0 7.6 %collective-permute-start.1 = (bf16[8,14336]{1,0:T(8,128)(2,1)}, bf16[8,14336]{1,0:T(8,128)(2,1)S(1)}, u32[]{:S(2)}, u32[]{:S(2)}) collective-permute-start(bf16[8,14336]{1,0:T(8,128)(2,1)} %param.3), channel_id=1, source_target_pairs={{0,2},{1,5},{2,6},{3,1},{4,0},{5,9},{6,10},{7,3},{8,4},{9,13},{10,... | collective-permute-start | bytes 688136 | tf_op jit(solution)/shard_map/ppermute | solution.py:162
  9.1 8.3 %collective-permute-start.3 = (bf16[8,14336]{1,0:T(8,128)(2,1)S(1)}, bf16[8,14336]{1,0:T(8,128)(2,1)S(1)}, u32[]{:S(2)}, u32[]{:S(2)}) collective-permute-start(bf16[8,14336]{1,0:T(8,128)(2,1)S(1)} %collective-permute-done), channel_id=1, source_target_pairs={{0,4},{1,3},{2,0},{3,7},{4,8},{5,1},{6,2},{7,11},{8,12},{9,5},{10,... | collective-permute-start | bytes 688136 | tf_op jit(solution)/shard_map/ppermute | solution.py:162
  10.6 9.2 %collective-permute-start.4 = (bf16[8,14336]{1,0:T(8,128)(2,1)S(1)}, bf16[8,14336]{1,0:T(8,128)(2,1)S(1)}, u32[]{:S(2)}, u32[]{:S(2)}) collective-permute-start(bf16[8,14336]{1,0:T(8,128)(2,1)S(1)} %collective-permute-done.1), channel_id=1, source_target_pairs={{0,2},{1,5},{2,6},{3,1},{4,0},{5,9},{6,10},{7,3},{8,4},{9,13},{10,... | collective-permute-start | bytes 688136 | tf_op jit(solution)/shard_map/ppermute | solution.py:162
  11.7 14.6 %collective-permute-start.8 = (bf16[8,10752]{1,0:T(8,128)(2,1)S(1)}, bf16[8,10752]{1,0:T(8,128)(2,1)S(1)}, u32[]{:S(2)}, u32[]{:S(2)}) collective-permute-start(bf16[8,10752]{1,0:T(8,128)(2,1)S(1)} %bitcast.10), channel_id=1, source_target_pairs={{0,12},{1,13},{2,14},{3,15},{4,6},{5,7},{6,4},{7,5},{8,10},{9,11},... | collective-permute-start | bytes 516104 | tf_op jit(solution)/shard_map/ppermute | solution.py:162
  15.1 12.1 %collective-permute-start.2 = (bf16[24,14336]{1,0:T(8,128)(2,1)S(1)}, bf16[24,14336]{1,0:T(8,128)(2,1)S(1)}, u32[]{:S(2)}, u32[]{:S(2)}) collective-permute-start(bf16[24,14336]{1,0:T(8,128)(2,1)S(1)} %get-tuple-element.8.refs_0_), channel_id=1, source_target_pairs={{0,1},{1,0},{2,3},{3,2},{4,5},{5,4},{6,7},{7,6},{8,9},{9,8},{10,11... | collective-permute-start | bytes 2064392 | tf_op jit(solution)/shard_map/ppermute | solution.py:162
  17.4 6.0 %collective-permute-start.6 = (bf16[8,10752]{1,0:T(8,128)(2,1)S(1)}, bf16[8,10752]{1,0:T(8,128)(2,1)S(1)}, u32[]{:S(2)}, u32[]{:S(2)}) collective-permute-start(bf16[8,10752]{1,0:T(8,128)(2,1)S(1)} %bitcast.11), channel_id=1, source_target_pairs={{0,4},{1,3},{2,0},{3,7},{4,8},{5,1},{6,2},{7,11},{8,12},{9,5},{10,... | collective-permute-start | bytes 516104 | tf_op jit(solution)/shard_map/ppermute | solution.py:162
  19.9 6.3 %collective-permute-start.7 = (bf16[8,10752]{1,0:T(8,128)(2,1)S(1)}, bf16[8,10752]{1,0:T(8,128)(2,1)S(1)}, u32[]{:S(2)}, u32[]{:S(2)}) collective-permute-start(bf16[8,10752]{1,0:T(8,128)(2,1)S(1)} %bitcast.12), channel_id=1, source_target_pairs={{0,2},{1,5},{2,6},{3,1},{4,0},{5,9},{6,10},{7,3},{8,4},{9,13},{10,... | collective-permute-start | bytes 516104 | tf_op jit(solution)/shard_map/ppermute | solution.py:162
  20.0 6.3 %collective-permute-start.5 = (bf16[16,14336]{1,0:T(8,128)(2,1)S(1)}, bf16[16,14336]{1,0:T(8,128)(2,1)S(1)}, u32[]{:S(2)}, u32[]{:S(2)}) collective-permute-start(bf16[16,14336]{1,0:T(8,128)(2,1)S(1)} %constant_dynamic-update-slice_fusion.3.refs_2_), channel_id=1, source_target_pairs={{0,1},{1,0},{2,3},{3,2},{4,5},{5,4},{6,7},{7,6},{8,9},{9,8},{10,11... | collective-permute-start | bytes 1376264 | tf_op jit(solution)/shard_map/ppermute | solution.py:162
  26.3 2.0 %collective-permute-start.9 = (bf16[24,10752]{1,0:T(8,128)(2,1)S(1)}, bf16[24,10752]{1,0:T(8,128)(2,1)S(1)}, u32[]{:S(2)}, u32[]{:S(2)}) collective-permute-start(bf16[24,10752]{1,0:T(8,128)(2,1)S(1)} %constant_dynamic-update-slice_fusion.5.refs_4_), channel_id=1, source_target_pairs={{0,1},{1,0},{2,3},{3,2},{4,5},{5,4},{6,7},{7,6},{8,9},{9,8},{10,11... | collective-permute-start | bytes 1548296 | tf_op jit(solution)/shard_map/ppermute | solution.py:162

commit v13 on v12

--- a/solution.py
+++ b/solution.py
@@ -133,6 +133,10 @@
     )(tile_owner, device.reshape(1), scale.reshape(1), x, mask)
 
 
+def together(*values):
+    return lax.optimization_barrier(values)
+
+
 def ring_plan(devices):
     chips = devices // 2
     order = list(range(0, chips, 2)) + list(range(1, chips, 2))[::-1]
@@ -153,6 +157,11 @@
     return (2 * chip - devices // 2 - devices // 8 + devices) % devices
 
 
+def near_and_far(devices):
+    needed = devices // 2 + devices // 8 + 2
+    return (needed - needed // 2, needed), (0, needed - needed // 2)
+
+
 def ring_gather(tokens, device, devices):
     onward, backward = ring_plan(devices)
     sibling = [device ^ 1 for device in range(devices)]
@@ -160,9 +169,6 @@
 
     def send(value, target):
         return lax.ppermute(value, "col", list(enumerate(target)))
-
-    def after(value, *others):
-        return lax.optimization_barrier((value, *others))[0]
 
     chip, core = device // 2, device % 2
     chips = devices // 2
@@ -182,28 +188,37 @@
     over_chip = jnp.where((chip < 2) | (chip >= chips - 2), chip ^ 6, chip ^ 1)
     came_ahead = ((chip % 4 == 0) | (chip % 4 == 3)) == (core == 0)
     slab, units = tokens.shape
-    needed = devices // 2 + devices // 8 + 2
-
-    def window(value, chip):
+
+    def window(value, chip, run):
+        start, stop = run
         blocks = value.reshape(slab, devices, units // devices)
         blocks = jnp.concatenate([blocks, blocks], axis=1)
-        blocks = lax.dynamic_slice_in_dim(blocks, first_needed(devices, chip), needed, axis=1)
+        start_block = first_needed(devices, chip) + start
+        blocks = lax.dynamic_slice_in_dim(blocks, start_block, stop - start, axis=1)
         return blocks.reshape(slab, -1)
 
     ahead, back = [tokens], [tokens]
     for _ in range(2):
         ahead.append(send(ahead[-1], onward))
         back.append(send(back[-1], backward))
-    half = send(window(jnp.where(came_ahead, ahead[1], back[1]), over_chip), over)
-    ahead.append(send(window(ahead[2], onward_chip), onward))
-    back.append(send(window(back[2], backward_chip), backward))
+    near_run, far_run = near_and_far(devices)
+    held = jnp.where(came_ahead, ahead[1], back[1])
+    half_near = send(window(held, over_chip, near_run), over)
     near = jnp.concatenate((tokens, ahead[1], back[1]), axis=0)
-    middle = jnp.concatenate((ahead[2], back[2]), axis=0)
-    last = jnp.concatenate((ahead[3], back[3], half), axis=0)
     near_beside = send(near, sibling)
+    ahead_2, back_2, near_beside = together(ahead[2], back[2], near_beside)
+    ahead_near = send(window(ahead_2, onward_chip, near_run), onward)
+    back_near = send(window(back_2, backward_chip, near_run), backward)
+    held, half_near = together(held, half_near)
+    half_far = send(window(held, over_chip, far_run), over)
+    ahead_far = send(window(ahead_2, onward_chip, far_run), onward)
+    back_far = send(window(back_2, backward_chip, far_run), backward)
+    middle = jnp.concatenate((ahead_2, back_2), axis=0)
     middle_beside = send(middle, sibling)
-    last_beside = send(after(last, middle_beside), sibling)
-    return [near, near_beside, middle, middle_beside, last, last_beside]
+    last_near = jnp.concatenate((ahead_near, back_near, half_near), axis=0)
+    last_far = (ahead_far, back_far, half_far)
+    return [near, near_beside, middle, middle_beside], (last_near, last_far), lambda value: send(value, sibling)
+
 
 def slab_origin(devices, device, number):
     chips = devices // 2
@@ -217,15 +232,29 @@
     return 2 * chip + core
 
 
-def ring_kernel(devices, slots, device_ref, table_ref, *refs):
-    groups = refs[:len(GROUPS)]
-    out_ref, pair, tiles, zeros, out_sems, zero_sems = refs[len(GROUPS):]
+def ring_kernel(devices, slots, spans, at, device_ref, table_ref, *refs):
+    (near_run, far_run), refs = near_and_far(devices), list(refs)
+    whole, near = refs[:4], refs[4:6]
+    in_near = spans[at][0] >= near_run[0]
+    far = None if in_near else refs[6:8]
+    refs = refs[6 if in_near else 8:]
+    if at:
+        refs = refs[1:]
+    out_ref, pair, tiles, zeros, out_sems, zero_sems = refs
     device = device_ref[0]
     slab, width = pair.shape[1] // devices, pair.shape[2]
+    first = first_needed(devices, device // 2)
+
+    def place_of(partner):
+        return lax.rem(partner - first + devices, devices)
 
     def owned(partner):
         return table_ref[devices + tile_number(devices, device, partner)] == device
 
+    def within(partner, span):
+        place = place_of(partner)
+        return (place >= span[0]) & (place < span[1])
+
     def put(buffer, slot):
         return pltpu.make_async_copy(tiles.at[buffer], out_ref.at[slot], out_sems.at[buffer])
 
@@ -233,28 +262,33 @@
         return pltpu.make_async_copy(zeros, out_ref.at[slot], zero_sems.at[slot])
 
     def load_block(partner, masked):
+        run, last = (near_run, near) if masked or in_near else (far_run, far)
         parts = []
-        for numbers, ref in zip(GROUPS, groups):
-            whole = ref.shape[1] == devices * width
-            place = partner if whole else (partner - first_needed(devices, device // 2) + devices) % devices
-            columns = pl.ds(pl.multiple_of(place * width, 128), width)
-            whole = ref.shape[1] == devices * width
-            place = partner if whole else (partner - first_needed(devices, device // 2) + devices) % devices
-            columns = pl.ds(pl.multiple_of(place * width, 128), width)
-            group = ref[:, columns].astype(jnp.float32)
-            for at, number in enumerate(numbers):
-                part = group[at * slab:(at + 1) * slab]
+        for numbers, ref in zip(GROUPS, (*whole, *last)):
+            place = partner if ref.shape[1] == devices * width else place_of(partner) - run[0]
+            group = ref[:, pl.ds(pl.multiple_of(place * width, 128), width)].astype(jnp.float32)
+            for row, number in enumerate(numbers):
+                part = group[row * slab:(row + 1) * slab]
                 if masked:
-                    row = lax.broadcasted_iota(jnp.int32, (slab, width), 0)
-                    part = jnp.where(row < table_ref[slab_origin(devices, device, number)], part, 0.0)
+                    line = lax.broadcasted_iota(jnp.int32, (slab, width), 0)
+                    part = jnp.where(line < table_ref[slab_origin(devices, device, number)], part, 0.0)
                 parts.append(part)
         pair[0 if masked else 1] = jnp.concatenate(parts, axis=0).astype(jnp.bfloat16)
 
-    count = lax.fori_loop(
-        0, devices, lambda partner, total: total + owned(partner).astype(jnp.int32), jnp.int32(0)
-    )
-
-    @pl.when(count < slots)
+    def add_owned(partner, counts):
+        mine = owned(partner).astype(jnp.int32)
+        spanned = [count + mine * within(partner, span).astype(jnp.int32) for count, span in zip(counts[1:], spans)]
+        return (counts[0] + mine, *spanned)
+
+    count, *in_span = lax.fori_loop(0, devices, add_owned, (jnp.int32(0),) * (1 + len(spans)))
+    clear_from, clear_to = count, count
+    for made, (start, stop) in zip(in_span[:at + 1], spans):
+        clear_from = clear_to
+        clear_to = jnp.minimum(clear_from + jnp.maximum(stop - start - made, 0), slots)
+    if at == len(spans) - 1:
+        clear_to = jnp.int32(slots)
+
+    @pl.when(clear_from < clear_to)
     def _():
         zeros[...] = jnp.zeros_like(zeros)
 
@@ -262,23 +296,25 @@
         clear(slot).start()
         return carry
 
-    lax.fori_loop(count, slots, start_clear, 0)
+    lax.fori_loop(clear_from, clear_to, start_clear, 0)
 
     load_block(device, True)
-    valid_count = lax.fori_loop(0, devices, lambda at, total: total + table_ref[at], jnp.int32(0))
+    valid_count = lax.fori_loop(0, devices, lambda row, total: total + table_ref[row], jnp.int32(0))
     scale = 1.0 / jnp.full((128, width), valid_count.astype(jnp.float32))
 
-    def visit(partner, slot):
+    def visit(partner, carry):
+        slot, made = carry
         mine = owned(partner)
-
-        @pl.when(mine)
+        now = mine & within(partner, spans[at])
+
+        @pl.when(now)
         def _():
-            buffer = lax.rem(slot, BUFFERS)
+            buffer = lax.rem(made, BUFFERS)
             load_block(partner, False)
 
-            @pl.when(slot >= BUFFERS)
+            @pl.when(made >= BUFFERS)
             def _():
-                put(buffer, slot - BUFFERS).wait()
+                put(buffer, slot).wait()
 
             left = (partner <= device).astype(jnp.int32)
             for row in range(0, width, 128):
@@ -292,48 +328,66 @@
                     tiles.at[buffer, strip], out_ref.at[slot, strip], out_sems.at[buffer]
                 ).start()
 
-        return slot + mine.astype(jnp.int32)
-
-    lax.fori_loop(0, devices, visit, jnp.int32(0))
-
-    def drain(slot, carry):
-        put(lax.rem(slot, BUFFERS), slot).wait()
-        return carry
-
-    lax.fori_loop(jnp.maximum(count - BUFFERS, 0), count, drain, 0)
+        return slot + mine.astype(jnp.int32), made + now.astype(jnp.int32)
+
+    _, made = lax.fori_loop(0, devices, visit, (jnp.int32(0), jnp.int32(0)))
+
+    def drain(number, carry):
+        put(lax.rem(number, BUFFERS), 0).wait()
+        return carry
+
+    lax.fori_loop(jnp.maximum(made - BUFFERS, 0), made, drain, 0)
 
     def end_clear(slot, carry):
         clear(slot).wait()
         return carry
 
-    lax.fori_loop(count, slots, end_clear, 0)
+    lax.fori_loop(clear_from, clear_to, end_clear, 0)
 
 
 def ring_form(tokens, slab_lengths, tile_owner, devices, device, slots):
     slab, units = tokens.shape
     width = units // devices
-    groups = ring_gather(tokens, device, devices)
+    near_run, far_run = near_and_far(devices)
+    early = near_run[0] + 2
+    spans = ((early, near_run[1]), (near_run[0], early), far_run)
+    whole, (near, far), beside = ring_gather(tokens, device, devices)
     table = jnp.concatenate([slab_lengths, tile_owner])
-    return pl.pallas_call(
-        functools.partial(ring_kernel, devices, slots),
-        out_shape=jax.ShapeDtypeStruct((slots, width, width), jnp.float32),
-        in_specs=[pl.BlockSpec(memory_space=pltpu.SMEM)] * 2
-        + [pl.BlockSpec(memory_space=pltpu.VMEM)] * len(groups),
-        out_specs=pl.BlockSpec(memory_space=pl.ANY),
-        scratch_shapes=[
-            pltpu.VMEM((2, slab * devices, width), jnp.bfloat16),
-            pltpu.VMEM((BUFFERS, width, width), jnp.float32),
-            pltpu.VMEM((width, width), jnp.float32),
-            pltpu.SemaphoreType.DMA((BUFFERS,)),
-            pltpu.SemaphoreType.DMA((slots,)),
-        ],
-        compiler_params=pltpu.CompilerParams(vmem_limit_bytes=32 * 1024 * 1024),
-        cost_estimate=pl.CostEstimate(
-            flops=2 * slots * slab * devices * width * width,
-            bytes_accessed=4 * slots * width * width,
-            transcendentals=0,
-        ),
-    )(device.reshape(1), table, *groups)
+
+    def make(at, groups, result):
+        given = [] if result is None else [result]
+        length = spans[at][1] - spans[at][0]
+        return pl.pallas_call(
+            functools.partial(ring_kernel, devices, slots, spans, at),
+            out_shape=jax.ShapeDtypeStruct((slots, width, width), jnp.float32),
+            in_specs=[pl.BlockSpec(memory_space=pltpu.SMEM)] * 2
+            + [pl.BlockSpec(memory_space=pltpu.VMEM)] * len(groups)
+            + [pl.BlockSpec(memory_space=pl.ANY)] * len(given),
+            out_specs=pl.BlockSpec(memory_space=pl.ANY),
+            input_output_aliases={2 + len(groups): 0} if given else {},
+            scratch_shapes=[
+                pltpu.VMEM((2, slab * devices, width), jnp.bfloat16),
+                pltpu.VMEM((BUFFERS, width, width), jnp.float32),
+                pltpu.VMEM((width, width), jnp.float32),
+                pltpu.SemaphoreType.DMA((BUFFERS,)),
+                pltpu.SemaphoreType.DMA((slots,)),
+            ],
+            compiler_params=pltpu.CompilerParams(vmem_limit_bytes=32 * 1024 * 1024),
+            cost_estimate=pl.CostEstimate(
+                flops=2 * length * slab * devices * width * width,
+                bytes_accessed=4 * length * width * width,
+                transcendentals=0,
+            ),
+        )(device.reshape(1), table, *groups, *given)
+
+    groups = whole + [near, beside(near)]
+    result = make(0, groups, None)
+    *far, result = together(*far, result)
+    far = jnp.concatenate(far, axis=0)
+    groups_far = groups + [far, beside(far)]
+    for at in range(1, len(spans)):
+        result = make(at, groups if spans[at][0] >= near_run[0] else groups_far, result)
+    return result
 
 
 def per_device(tokens, slab_lengths, tile_owner):

time: 41.1 us -> 50.5 us (1.23); the launches traced: 40.9 us -> 49.6 us
  Pallas kernels: 12.6 us -> 17.2 us
  starting transfers between devices: 11.4 us -> 14.2 us
  waiting for transfers between devices: 14.4 us -> 15.7 us
    pallas_call x1 -> x3, Pallas kernels: 12.6 us -> 17.2 us  [make(): pl.pallas_call(functools.partial(ring_kernel, devices, slots, spans, at),...]
    ppermute x10 -> x14, starting transfers between devices: 11.4 us -> 14.2 us  [send(): return lax.ppermute(value, 'col', list(enumerate(target)))]
    ppermute x10 -> x14, waiting for transfers between devices: 14.4 us -> 15.7 us  [send(): return lax.ppermute(value, 'col', list(enumerate(target)))]
    unnamed x5 -> x7, local copies, waits for them, and re-layouts: 1.08 us -> 1.08 us
  transfers between devices with their start and end apart: 10 -> 14, of which waited for: 5 -> 4; matrix products, arithmetic and copies ran while one was open for 5% -> 4% of each run, Pallas kernels for 0% -> 21%
where the time goes in v13:
time: 50.5 us; the launch traced here: 49.6 us
  Pallas kernels  17.2 us (34%)
  waiting for transfers between devices  15.7 us (31%)
  starting transfers between devices  14.2 us (28%)
  other arithmetic  1.14 us (2%)
  local copies, waits for them, and re-layouts  1.12 us (2%)
    pallas_call x3, Pallas kernels, make(): pl.pallas_call(functools.partial(ring_kernel, devices, slots, spans, at),...  17.2 us
    ppermute x14, waiting for transfers between devices, send(): return lax.ppermute(value, 'col', list(enumerate(target)))  15.7 us
    ppermute x14, starting transfers between devices, send(): return lax.ppermute(value, 'col', list(enumerate(target)))  14.2 us
    unnamed x7, local copies, waits for them, and re-layouts  1.08 us
  transfers between devices with their start and end apart: 14, of which 4 were waited for; matrix products, arithmetic and copies ran while one was open for 4% of the time, Pallas kernels for 21%

profile of v13, /device:TPU:0, one launch (start us, length us, event | category | flops | bytes accessed | tf_op | source)
XLA Modules:
  0.0 49.6 jit_solution(18438259258427674118)
XLA Ops:
  0.0 3.0 %collective-permute-start = (bf16[8,14336]{1,0:T(8,128)(2,1)}, bf16[8,14336]{1,0:T(8,128)(2,1)S(1)}, u32[]{:S(2)}, u32[]{:S(2)}) collective-permute-start(bf16[8,14336]{1,0:T(8,128)(2,1)} %param.3), channel_id=1, source_target_pairs={{0,4},{1,3},{2,0},{3,7},{4,8},{5,1},{6,2},{7,11},{8,12},{9,5},{10,... | collective-permute-start | bytes 688136 | tf_op jit(solution)/shard_map/ppermute | solution.py:171
  3.0 0.0 collective-permute-start.1
  3.0 1.0 %constant_dynamic-update-slice_fusion.2 = bf16[24,14336]{1,0:T(8,128)(2,1)S(1)} fusion(bf16[8,14336]{1,0:T(8,128)(2,1)} %param.3), kind=kLoop, calls=%fused_computation.21 | loop fusion | bytes 458752
  4.1 5.0 %collective-permute-done = bf16[8,14336]{1,0:T(8,128)(2,1)S(1)} collective-permute-done((bf16[8,14336]{1,0:T(8,128)(2,1)}, bf16[8,14336]{1,0:T(8,128)(2,1)S(1)}, u32[]{:S(2)}, u32[]{:S(2)}) %collective-permute-start) | collective-permute-done | bytes 229408 | tf_op jit(solution)/shard_map/ppermute | solution.py:171
  9.1 0.2 collective-permute-done.1
  9.3 0.1 broadcast_select_fusion
  9.3 0.2 collective-permute-start.4
  9.6 1.5 %collective-permute-start.2 = (bf16[8,14336]{1,0:T(8,128)(2,1)S(1)}, bf16[8,14336]{1,0:T(8,128)(2,1)S(1)}, u32[]{:S(2)}, u32[]{:S(2)}) collective-permute-start(bf16[8,14336]{1,0:T(8,128)(2,1)S(1)} %collective-permute-done), channel_id=1, source_target_pairs={{0,4},{1,3},{2,0},{3,7},{4,8},{5,1},{6,2},{7,11},{8,12},{9,5},{10,... | collective-permute-start | bytes 688136 | tf_op jit(solution)/shard_map/ppermute | solution.py:171
  11.0 0.8 %collective-permute-start.3 = (bf16[8,14336]{1,0:T(8,128)(2,1)S(1)}, bf16[8,14336]{1,0:T(8,128)(2,1)S(1)}, u32[]{:S(2)}, u32[]{:S(2)}) collective-permute-start(bf16[8,14336]{1,0:T(8,128)(2,1)S(1)} %collective-permute-done.1), channel_id=1, source_target_pairs={{0,2},{1,5},{2,6},{3,1},{4,0},{5,9},{6,10},{7,3},{8,4},{9,13},{10,... | collective-permute-start | bytes 688136 | tf_op jit(solution)/shard_map/ppermute | solution.py:171
  11.8 0.1 fusion.1
  11.8 3.3 %collective-permute-start.8 = (bf16[8,5376]{1,0:T(8,128)(2,1)S(1)}, bf16[8,5376]{1,0:T(8,128)(2,1)S(1)}, u32[]{:S(2)}, u32[]{:S(2)}) collective-permute-start(bf16[8,5376]{1,0:T(8,128)(2,1)S(1)} %bitcast.15), channel_id=1, source_target_pairs={{0,12},{1,13},{2,14},{3,15},{4,6},{5,7},{6,4},{7,5},{8,10},{9,11},... | collective-permute-start | bytes 258056 | tf_op jit(solution)/shard_map/ppermute | solution.py:171
  15.2 6.1 %collective-permute-done.8 = bf16[8,5376]{1,0:T(8,128)(2,1)S(1)} collective-permute-done((bf16[8,5376]{1,0:T(8,128)(2,1)S(1)}, bf16[8,5376]{1,0:T(8,128)(2,1)S(1)}, u32[]{:S(2)}, u32[]{:S(2)}) %collective-permute-start.8) | collective-permute-done | bytes 86048 | tf_op jit(solution)/shard_map/ppermute | solution.py:171
  21.3 0.0 collective-permute-done.2
  21.3 0.0 collective-permute-done.3
  21.3 0.0 collective-permute-done.4.refs_1_
  21.3 0.1 fusion.2
  21.4 2.8 %collective-permute-start.7 = (bf16[8,5376]{1,0:T(8,128)(2,1)S(1)}, bf16[8,5376]{1,0:T(8,128)(2,1)S(1)}, u32[]{:S(2)}, u32[]{:S(2)}) collective-permute-start(bf16[8,5376]{1,0:T(8,128)(2,1)S(1)} %bitcast.18), channel_id=1, source_target_pairs={{0,2},{1,5},{2,6},{3,1},{4,0},{5,9},{6,10},{7,3},{8,4},{9,13},{10,... | collective-permute-start | bytes 258056 | tf_op jit(solution)/shard_map/ppermute | solution.py:171
  24.2 0.1 fusion.4
  24.3 0.1 collective-permute-start.6
  24.4 0.1 collective-permute-start.5
  24.5 4.4 %collective-permute-done.6 = bf16[8,5376]{1,0:T(8,128)(2,1)S(1)} collective-permute-done((bf16[8,5376]{1,0:T(8,128)(2,1)S(1)}, bf16[8,5376]{1,0:T(8,128)(2,1)S(1)}, u32[]{:S(2)}, u32[]{:S(2)}) %collective-permute-start.6) | collective-permute-done | bytes 86048 | tf_op jit(solution)/shard_map/ppermute | solution.py:171
  28.9 0.0 collective-permute-done.7
  28.9 0.1 collective-permute-start.9
  29.0 0.1 fusion
  29.1 0.1 collective-permute-start.12
  29.1 1.0 %collective-permute-start.11 = (bf16[8,5376]{1,0:T(8,128)(2,1)S(1)}, bf16[8,5376]{1,0:T(8,128)(2,1)S(1)}, u32[]{:S(2)}, u32[]{:S(2)}) collective-permute-start(bf16[8,5376]{1,0:T(8,128)(2,1)S(1)} %bitcast.16), channel_id=1, source_target_pairs={{0,2},{1,5},{2,6},{3,1},{4,0},{5,9},{6,10},{7,3},{8,4},{9,13},{10,... | collective-permute-start | bytes 258056 | tf_op jit(solution)/shard_map/ppermute | solution.py:171
  30.1 1.1 %collective-permute-start.10 = (bf16[8,5376]{1,0:T(8,128)(2,1)S(1)}, bf16[8,5376]{1,0:T(8,128)(2,1)S(1)}, u32[]{:S(2)}, u32[]{:S(2)}) collective-permute-start(bf16[8,5376]{1,0:T(8,128)(2,1)S(1)} %bitcast.17), channel_id=1, source_target_pairs={{0,4},{1,3},{2,0},{3,7},{4,8},{5,1},{6,2},{7,11},{8,12},{9,5},{10,... | collective-permute-start | bytes 258056 | tf_op jit(solution)/shard_map/ppermute | solution.py:171
  31.2 0.8 %pad_add_fusion.table_ref = s32[152]{0:T(256)S(1)} fusion(s32[136]{0:T(256)} %param.5, s32[16]{0:T(128)} %param.4), kind=kLoop, calls=%fused_computation.30 | loop fusion | flops 152 | bytes 1216 | tf_op jit(solution)/shard_map/concatenate | solution.py:355
  32.0 0.0 collective-permute-done.9.refs_5_
  32.0 0.0 collective-permute-done.5.refs_3_
  32.0 5.8 %shard_map.37.refs_6_ = f32[11,896,896]{2,1,0:T(8,128)} custom-call(s32[1]{0:T(128)} %bitcast.device_ref, s32[152]{0:T(256)S(1)} %pad_add_fusion.table_ref, bf16[24,14336]{1,0:T(8,128)(2,1)S(1)} %get-tuple-element.28.refs_0_, bf16[24,14336]{1,0:T(8,128)(2,1)S(1)} %collective-permute-done.4.refs_1_, ...), custom_call_target="tpu_custom_call" | custom-call | flops 822083584 | bytes 12845056 | tf_op jit(solution)/shard_map/pallas_call | solution.py:360
  37.8 0.0 collective-permute-done.12
  37.8 0.0 collective-permute-done.11
  37.8 0.0 collective-permute-done.10
  37.9 0.3 collective-permute-start.13
  38.2 4.5 %shard_map.38.refs_8_ = f32[11,896,896]{2,1,0:T(8,128)} custom-call(s32[1]{0:T(128)} %bitcast.device_ref, s32[152]{0:T(256)S(1)} %pad_add_fusion.table_ref, bf16[24,14336]{1,0:T(8,128)(2,1)S(1)} %get-tuple-element.28.refs_0_, bf16[24,14336]{1,0:T(8,128)(2,1)S(1)} %collective-permute-done.4.refs_1_, ...), custom_call_target="tpu_custom_call", output_to_operand_aliasing={{}: (8, {})} | custom-call | flops 411041792 | bytes 6422528 | tf_op jit(solution)/shard_map/pallas_call | solution.py:360
  42.7 0.0 collective-permute-done.13.refs_7_
  42.7 6.9 %shard_map.39 = f32[11,896,896]{2,1,0:T(8,128)} custom-call(s32[1]{0:T(128)} %bitcast.device_ref, s32[152]{0:T(256)S(1)} %pad_add_fusion.table_ref, bf16[24,14336]{1,0:T(8,128)(2,1)S(1)} %get-tuple-element.28.refs_0_, bf16[24,14336]{1,0:T(8,128)(2,1)S(1)} %collective-permute-done.4.refs_1_, ...), custom_call_target="tpu_custom_call", output_to_operand_aliasing={{}: (10, {})} | custom-call | flops 1233125376 | bytes 19267584 | tf_op jit(solution)/shard_map/pallas_call | solution.py:360
  (9 shorter events, 0.1 us)
Async XLA Ops:
  0.0 9.1 %collective-permute-start = (bf16[8,14336]{1,0:T(8,128)(2,1)}, bf16[8,14336]{1,0:T(8,128)(2,1)S(1)}, u32[]{:S(2)}, u32[]{:S(2)}) collective-permute-start(bf16[8,14336]{1,0:T(8,128)(2,1)} %param.3), channel_id=1, source_target_pairs={{0,4},{1,3},{2,0},{3,7},{4,8},{5,1},{6,2},{7,11},{8,12},{9,5},{10,... | collective-permute-start | bytes 688136 | tf_op jit(solution)/shard_map/ppermute | solution.py:171
  3.0 6.2 %collective-permute-start.1 = (bf16[8,14336]{1,0:T(8,128)(2,1)}, bf16[8,14336]{1,0:T(8,128)(2,1)S(1)}, u32[]{:S(2)}, u32[]{:S(2)}) collective-permute-start(bf16[8,14336]{1,0:T(8,128)(2,1)} %param.3), channel_id=1, source_target_pairs={{0,2},{1,5},{2,6},{3,1},{4,0},{5,9},{6,10},{7,3},{8,4},{9,13},{10,... | collective-permute-start | bytes 688136 | tf_op jit(solution)/shard_map/ppermute | solution.py:171
  9.3 12.0 %collective-permute-start.4 = (bf16[24,14336]{1,0:T(8,128)(2,1)S(1)}, bf16[24,14336]{1,0:T(8,128)(2,1)S(1)}, u32[]{:S(2)}, u32[]{:S(2)}) collective-permute-start(bf16[24,14336]{1,0:T(8,128)(2,1)S(1)} %get-tuple-element.28.refs_0_), channel_id=1, source_target_pairs={{0,1},{1,0},{2,3},{3,2},{4,5},{5,4},{6,7},{7,6},{8,9},{9,8},{10,11... | collective-permute-start | bytes 2064392 | tf_op jit(solution)/shard_map/ppermute | solution.py:171
  9.6 11.7 %collective-permute-start.2 = (bf16[8,14336]{1,0:T(8,128)(2,1)S(1)}, bf16[8,14336]{1,0:T(8,128)(2,1)S(1)}, u32[]{:S(2)}, u32[]{:S(2)}) collective-permute-start(bf16[8,14336]{1,0:T(8,128)(2,1)S(1)} %collective-permute-done), channel_id=1, source_target_pairs={{0,4},{1,3},{2,0},{3,7},{4,8},{5,1},{6,2},{7,11},{8,12},{9,5},{10,... | collective-permute-start | bytes 688136 | tf_op jit(solution)/shard_map/ppermute | solution.py:171
  11.0 10.3 %collective-permute-start.3 = (bf16[8,14336]{1,0:T(8,128)(2,1)S(1)}, bf16[8,14336]{1,0:T(8,128)(2,1)S(1)}, u32[]{:S(2)}, u32[]{:S(2)}) collective-permute-start(bf16[8,14336]{1,0:T(8,128)(2,1)S(1)} %collective-permute-done.1), channel_id=1, source_target_pairs={{0,2},{1,5},{2,6},{3,1},{4,0},{5,9},{6,10},{7,3},{8,4},{9,13},{10,... | collective-permute-start | bytes 688136 | tf_op jit(solution)/shard_map/ppermute | solution.py:171
  11.8 9.4 %collective-permute-start.8 = (bf16[8,5376]{1,0:T(8,128)(2,1)S(1)}, bf16[8,5376]{1,0:T(8,128)(2,1)S(1)}, u32[]{:S(2)}, u32[]{:S(2)}) collective-permute-start(bf16[8,5376]{1,0:T(8,128)(2,1)S(1)} %bitcast.15), channel_id=1, source_target_pairs={{0,12},{1,13},{2,14},{3,15},{4,6},{5,7},{6,4},{7,5},{8,10},{9,11},... | collective-permute-start | bytes 258056 | tf_op jit(solution)/shard_map/ppermute | solution.py:171
  21.4 7.5 %collective-permute-start.7 = (bf16[8,5376]{1,0:T(8,128)(2,1)S(1)}, bf16[8,5376]{1,0:T(8,128)(2,1)S(1)}, u32[]{:S(2)}, u32[]{:S(2)}) collective-permute-start(bf16[8,5376]{1,0:T(8,128)(2,1)S(1)} %bitcast.18), channel_id=1, source_target_pairs={{0,2},{1,5},{2,6},{3,1},{4,0},{5,9},{6,10},{7,3},{8,4},{9,13},{10,... | collective-permute-start | bytes 258056 | tf_op jit(solution)/shard_map/ppermute | solution.py:171
  24.3 4.5 %collective-permute-start.6 = (bf16[8,5376]{1,0:T(8,128)(2,1)S(1)}, bf16[8,5376]{1,0:T(8,128)(2,1)S(1)}, u32[]{:S(2)}, u32[]{:S(2)}) collective-permute-start(bf16[8,5376]{1,0:T(8,128)(2,1)S(1)} %bitcast.20), channel_id=1, source_target_pairs={{0,4},{1,3},{2,0},{3,7},{4,8},{5,1},{6,2},{7,11},{8,12},{9,5},{10,... | collective-permute-start | bytes 258056 | tf_op jit(solution)/shard_map/ppermute | solution.py:171
  24.4 7.6 %collective-permute-start.5 = (bf16[16,14336]{1,0:T(8,128)(2,1)S(1)}, bf16[16,14336]{1,0:T(8,128)(2,1)S(1)}, u32[]{:S(2)}, u32[]{:S(2)}) collective-permute-start(bf16[16,14336]{1,0:T(8,128)(2,1)S(1)} %constant_dynamic-update-slice_fusion.3.refs_2_), channel_id=1, source_target_pairs={{0,1},{1,0},{2,3},{3,2},{4,5},{5,4},{6,7},{7,6},{8,9},{9,8},{10,11... | collective-permute-start | bytes 1376264 | tf_op jit(solution)/shard_map/ppermute | solution.py:171
  28.9 3.1 %collective-permute-start.9 = (bf16[24,5376]{1,0:T(8,128)(2,1)S(1)}, bf16[24,5376]{1,0:T(8,128)(2,1)S(1)}, u32[]{:S(2)}, u32[]{:S(2)}) collective-permute-start(bf16[24,5376]{1,0:T(8,128)(2,1)S(1)} %constant_dynamic-update-slice_fusion.5.refs_4_), channel_id=1, source_target_pairs={{0,1},{1,0},{2,3},{3,2},{4,5},{5,4},{6,7},{7,6},{8,9},{9,8},{10,11... | collective-permute-start | bytes 774152 | tf_op jit(solution)/shard_map/ppermute | solution.py:171
  29.1 8.8 %collective-permute-start.12 = (bf16[8,5376]{1,0:T(8,128)(2,1)S(1)}, bf16[8,5376]{1,0:T(8,128)(2,1)S(1)}, u32[]{:S(2)}, u32[]{:S(2)}) collective-permute-start(bf16[8,5376]{1,0:T(8,128)(2,1)S(1)} %bitcast.19), channel_id=1, source_target_pairs={{0,12},{1,13},{2,14},{3,15},{4,6},{5,7},{6,4},{7,5},{8,10},{9,11},... | collective-permute-start | bytes 258056 | tf_op jit(solution)/shard_map/ppermute | solution.py:171
  29.1 8.7 %collective-permute-start.11 = (bf16[8,5376]{1,0:T(8,128)(2,1)S(1)}, bf16[8,5376]{1,0:T(8,128)(2,1)S(1)}, u32[]{:S(2)}, u32[]{:S(2)}) collective-permute-start(bf16[8,5376]{1,0:T(8,128)(2,1)S(1)} %bitcast.16), channel_id=1, source_target_pairs={{0,2},{1,5},{2,6},{3,1},{4,0},{5,9},{6,10},{7,3},{8,4},{9,13},{10,... | collective-permute-start | bytes 258056 | tf_op jit(solution)/shard_map/ppermute | solution.py:171
  30.1 7.7 %collective-permute-start.10 = (bf16[8,5376]{1,0:T(8,128)(2,1)S(1)}, bf16[8,5376]{1,0:T(8,128)(2,1)S(1)}, u32[]{:S(2)}, u32[]{:S(2)}) collective-permute-start(bf16[8,5376]{1,0:T(8,128)(2,1)S(1)} %bitcast.17), channel_id=1, source_target_pairs={{0,4},{1,3},{2,0},{3,7},{4,8},{5,1},{6,2},{7,11},{8,12},{9,5},{10,... | collective-permute-start | bytes 258056 | tf_op jit(solution)/shard_map/ppermute | solution.py:171
  37.9 4.8 %collective-permute-start.13 = (bf16[24,5376]{1,0:T(8,128)(2,1)S(1)}, bf16[24,5376]{1,0:T(8,128)(2,1)S(1)}, u32[]{:S(2)}, u32[]{:S(2)}) collective-permute-start(bf16[24,5376]{1,0:T(8,128)(2,1)S(1)} %constant_dynamic-update-slice_fusion.8.refs_6_), channel_id=1, source_target_pairs={{0,1},{1,0},{2,3},{3,2},{4,5},{5,4},{6,7},{7,6},{8,9},{9,8},{10,11... | collective-permute-start | bytes 774152 | tf_op jit(solution)/shard_map/ppermute | solution.py:171

commit v14 on v12

--- a/solution.py
+++ b/solution.py
@@ -8,6 +8,7 @@
 from jax.sharding import PartitionSpec as P
 
 BUFFERS = 4
+STRIP = 256
 RING_DEVICES = 16
 
 
@@ -146,7 +147,7 @@
     return onward, backward
 
 
-GROUPS = ((0, 1, 2), (8, 9, 10), (3, 4), (11, 12), (5, 6, 7), (13, 14, 15))
+GROUPS = ((0, 1, 2), (8, 9, 10), (3, 4), (11, 12), (5, 7), (13, 15), (6,), (14,))
 
 
 def first_needed(devices, chip):
@@ -199,11 +200,11 @@
     back.append(send(window(back[2], backward_chip), backward))
     near = jnp.concatenate((tokens, ahead[1], back[1]), axis=0)
     middle = jnp.concatenate((ahead[2], back[2]), axis=0)
-    last = jnp.concatenate((ahead[3], back[3], half), axis=0)
+    last = jnp.concatenate((ahead[3], half), axis=0)
     near_beside = send(near, sibling)
     middle_beside = send(middle, sibling)
     last_beside = send(after(last, middle_beside), sibling)
-    return [near, near_beside, middle, middle_beside, last, last_beside]
+    return [near, near_beside, middle, middle_beside, last, last_beside, back[3], send(back[3], sibling)]
 
 def slab_origin(devices, device, number):
     chips = devices // 2
@@ -222,6 +223,7 @@
     out_ref, pair, tiles, zeros, out_sems, zero_sems = refs[len(GROUPS):]
     device = device_ref[0]
     slab, width = pair.shape[1] // devices, pair.shape[2]
+    first = first_needed(devices, device // 2)
 
     def owned(partner):
         return table_ref[devices + tile_number(devices, device, partner)] == device
@@ -235,13 +237,10 @@
     def load_block(partner, masked):
         parts = []
         for numbers, ref in zip(GROUPS, groups):
-            whole = ref.shape[1] == devices * width
-            place = partner if whole else (partner - first_needed(devices, device // 2) + devices) % devices
-            columns = pl.ds(pl.multiple_of(place * width, 128), width)
-            whole = ref.shape[1] == devices * width
-            place = partner if whole else (partner - first_needed(devices, device // 2) + devices) % devices
-            columns = pl.ds(pl.multiple_of(place * width, 128), width)
-            group = ref[:, columns].astype(jnp.float32)
+            place = partner
+            if ref.shape[1] < devices * width:
+                place = lax.rem(partner - first + devices, devices)
+            group = ref[:, pl.ds(pl.multiple_of(place * width, 128), width)].astype(jnp.float32)
             for at, number in enumerate(numbers):
                 part = group[at * slab:(at + 1) * slab]
                 if masked:
@@ -250,23 +249,11 @@
                 parts.append(part)
         pair[0 if masked else 1] = jnp.concatenate(parts, axis=0).astype(jnp.bfloat16)
 
-    count = lax.fori_loop(
-        0, devices, lambda partner, total: total + owned(partner).astype(jnp.int32), jnp.int32(0)
-    )
-
-    @pl.when(count < slots)
-    def _():
-        zeros[...] = jnp.zeros_like(zeros)
-
-    def start_clear(slot, carry):
-        clear(slot).start()
-        return carry
-
-    lax.fori_loop(count, slots, start_clear, 0)
-
     load_block(device, True)
-    valid_count = lax.fori_loop(0, devices, lambda at, total: total + table_ref[at], jnp.int32(0))
-    scale = 1.0 / jnp.full((128, width), valid_count.astype(jnp.float32))
+    valid_count = table_ref[0]
+    for at in range(1, devices):
+        valid_count = valid_count + table_ref[at]
+    scale = 1.0 / jnp.full((8, width), valid_count.astype(jnp.float32))
 
     def visit(partner, slot):
         mine = owned(partner)
@@ -281,20 +268,31 @@
                 put(buffer, slot - BUFFERS).wait()
 
             left = (partner <= device).astype(jnp.int32)
-            for row in range(0, width, 128):
-                strip = pl.ds(row, 128)
+            for row in range(0, width, STRIP):
+                rows = min(STRIP, width - row)
+                strip = pl.ds(row, rows)
                 product = lax.dot_general(
-                    pair[left, :, row:row + 128], pair[1 - left], (((0,), (0,)), ((), ())),
+                    pair[left, :, row:row + rows], pair[1 - left], (((0,), (0,)), ((), ())),
                     preferred_element_type=jnp.float32,
                 )
-                tiles[buffer, strip, :] = product * scale
+                tiles[buffer, strip, :] = product * scale[:1]
                 pltpu.make_async_copy(
                     tiles.at[buffer, strip], out_ref.at[slot, strip], out_sems.at[buffer]
                 ).start()
 
         return slot + mine.astype(jnp.int32)
 
-    lax.fori_loop(0, devices, visit, jnp.int32(0))
+    count = lax.fori_loop(0, devices, visit, jnp.int32(0))
+
+    @pl.when(count < slots)
+    def _():
+        zeros[...] = jnp.zeros_like(zeros)
+
+    def start_clear(slot, carry):
+        clear(slot).start()
+        return carry
+
+    lax.fori_loop(count, slots, start_clear, 0)
 
     def drain(slot, carry):
         put(lax.rem(slot, BUFFERS), slot).wait()

time: 41.1 us -> 40.5 us (0.985)
  waiting for transfers between devices: 14.4 us -> 13.8 us
    ppermute x10 -> x11, waiting for transfers between devices: 14.4 us -> 13.8 us  [send(): return lax.ppermute(value, 'col', list(enumerate(target)))]
    unnamed x5 -> x4, local copies, waits for them, and re-layouts: 1.08 us -> 1.06 us
    ppermute x10 -> x11, starting transfers between devices: 11.4 us -> 11.4 us  [send(): return lax.ppermute(value, 'col', list(enumerate(target)))]
  transfers between devices with their start and end apart: 10 -> 11, of which waited for: 5 -> 5; matrix products, arithmetic and copies ran while one was open for 5% -> 5% of each run, Pallas kernels for 0% -> 0%
where the time goes in v14:
time: 40.5 us; the launch traced here: 40.3 us
  waiting for transfers between devices  13.8 us (34%)
  Pallas kernels  12.6 us (31%)
  starting transfers between devices  11.4 us (28%)
  other arithmetic  1.11 us (3%)
  local copies, waits for them, and re-layouts  1.09 us (3%)
    ppermute x11, waiting for transfers between devices, send(): return lax.ppermute(value, 'col', list(enumerate(target)))  13.8 us
    pallas_call x1, Pallas kernels, ring_form(): pl.pallas_call(functools.partial(ring_kernel, devices, slots), out_shape=...  12.6 us
    ppermute x11, starting transfers between devices, send(): return lax.ppermute(value, 'col', list(enumerate(target)))  11.4 us
    unnamed x4, local copies, waits for them, and re-layouts  1.06 us
  transfers between devices with their start and end apart: 11, of which 5 were waited for; matrix products, arithmetic and copies ran while one was open for 5% of the time, Pallas kernels for 0%

profile of v14, /device:TPU:0, one launch (start us, length us, event | category | flops | bytes accessed | tf_op | source)
XLA Modules:
  0.0 40.3 jit_solution(6829515825520164952)
XLA Ops:
  0.0 3.0 %collective-permute-start = (bf16[8,14336]{1,0:T(8,128)(2,1)}, bf16[8,14336]{1,0:T(8,128)(2,1)S(1)}, u32[]{:S(2)}, u32[]{:S(2)}) collective-permute-start(bf16[8,14336]{1,0:T(8,128)(2,1)} %param.3), channel_id=1, source_target_pairs={{0,4},{1,3},{2,0},{3,7},{4,8},{5,1},{6,2},{7,11},{8,12},{9,5},{10,... | collective-permute-start | bytes 688136 | tf_op jit(solution)/shard_map/ppermute | solution.py:163
  3.0 0.0 collective-permute-start.1
  3.0 1.0 %constant_dynamic-update-slice_fusion.2 = bf16[24,14336]{1,0:T(8,128)(2,1)S(1)} fusion(bf16[8,14336]{1,0:T(8,128)(2,1)} %param.3), kind=kLoop, calls=%fused_computation.12 | loop fusion | bytes 458752
  4.2 4.9 %collective-permute-done = bf16[8,14336]{1,0:T(8,128)(2,1)S(1)} collective-permute-done((bf16[8,14336]{1,0:T(8,128)(2,1)}, bf16[8,14336]{1,0:T(8,128)(2,1)S(1)}, u32[]{:S(2)}, u32[]{:S(2)}) %collective-permute-start) | collective-permute-done | bytes 229408 | tf_op jit(solution)/shard_map/ppermute | solution.py:163
  9.1 1.5 %collective-permute-start.3 = (bf16[8,14336]{1,0:T(8,128)(2,1)S(1)}, bf16[8,14336]{1,0:T(8,128)(2,1)S(1)}, u32[]{:S(2)}, u32[]{:S(2)}) collective-permute-start(bf16[8,14336]{1,0:T(8,128)(2,1)S(1)} %collective-permute-done), channel_id=1, source_target_pairs={{0,4},{1,3},{2,0},{3,7},{4,8},{5,1},{6,2},{7,11},{8,12},{9,5},{10,... | collective-permute-start | bytes 688136 | tf_op jit(solution)/shard_map/ppermute | solution.py:163
  10.6 0.0 collective-permute-done.1
  10.6 0.9 %collective-permute-start.4 = (bf16[8,14336]{1,0:T(8,128)(2,1)S(1)}, bf16[8,14336]{1,0:T(8,128)(2,1)S(1)}, u32[]{:S(2)}, u32[]{:S(2)}) collective-permute-start(bf16[8,14336]{1,0:T(8,128)(2,1)S(1)} %collective-permute-done.1), channel_id=1, source_target_pairs={{0,2},{1,5},{2,6},{3,1},{4,0},{5,9},{6,10},{7,3},{8,4},{9,13},{10,... | collective-permute-start | bytes 688136 | tf_op jit(solution)/shard_map/ppermute | solution.py:163
  11.5 0.1 broadcast_select_fusion
  11.6 0.1 fusion.1
  11.7 3.4 %collective-permute-start.7 = (bf16[8,10752]{1,0:T(8,128)(2,1)S(1)}, bf16[8,10752]{1,0:T(8,128)(2,1)S(1)}, u32[]{:S(2)}, u32[]{:S(2)}) collective-permute-start(bf16[8,10752]{1,0:T(8,128)(2,1)S(1)} %bitcast.10), channel_id=1, source_target_pairs={{0,12},{1,13},{2,14},{3,15},{4,6},{5,7},{6,4},{7,5},{8,10},{9,11},... | collective-permute-start | bytes 516104 | tf_op jit(solution)/shard_map/ppermute | solution.py:163
  15.1 0.0 collective-permute-start.2
  15.1 2.3 %collective-permute-done.3 = bf16[8,14336]{1,0:T(8,128)(2,1)S(1)} collective-permute-done((bf16[8,14336]{1,0:T(8,128)(2,1)S(1)}, bf16[8,14336]{1,0:T(8,128)(2,1)S(1)}, u32[]{:S(2)}, u32[]{:S(2)}) %collective-permute-start.3) | collective-permute-done | bytes 229408 | tf_op jit(solution)/shard_map/ppermute | solution.py:163
  17.3 0.1 fusion.2
  17.4 2.4 %collective-permute-start.6 = (bf16[8,10752]{1,0:T(8,128)(2,1)S(1)}, bf16[8,10752]{1,0:T(8,128)(2,1)S(1)}, u32[]{:S(2)}, u32[]{:S(2)}) collective-permute-start(bf16[8,10752]{1,0:T(8,128)(2,1)S(1)} %bitcast.12), channel_id=1, source_target_pairs={{0,4},{1,3},{2,0},{3,7},{4,8},{5,1},{6,2},{7,11},{8,12},{9,5},{10,... | collective-permute-start | bytes 516104 | tf_op jit(solution)/shard_map/ppermute | solution.py:163
  19.8 0.0 collective-permute-done.4
  19.8 0.1 fusion
  19.9 0.1 collective-permute-start.9
  20.0 0.1 collective-permute-start.5
  20.1 3.4 %collective-permute-done.6 = bf16[8,10752]{1,0:T(8,128)(2,1)S(1)} collective-permute-done((bf16[8,10752]{1,0:T(8,128)(2,1)S(1)}, bf16[8,10752]{1,0:T(8,128)(2,1)S(1)}, u32[]{:S(2)}, u32[]{:S(2)}) %collective-permute-start.6) | collective-permute-done | bytes 172064 | tf_op jit(solution)/shard_map/ppermute | solution.py:163
  23.5 0.0 collective-permute-done.7
  23.5 0.0 collective-permute-done.5.refs_3_
  23.5 0.1 collective-permute-start.8
  23.6 2.7 %collective-permute-done.9.refs_6_ = bf16[8,10752]{1,0:T(8,128)(2,1)S(1)} collective-permute-done((bf16[8,10752]{1,0:T(8,128)(2,1)S(1)}, bf16[8,10752]{1,0:T(8,128)(2,1)S(1)}, u32[]{:S(2)}, u32[]{:S(2)}) %collective-permute-start.9) | collective-permute-done | bytes 172064 | tf_op jit(solution)/shard_map/ppermute | solution.py:163
  26.3 0.0 collective-permute-start.10
  26.3 0.8 %pad_add_fusion.table_ref = s32[152]{0:T(256)S(1)} fusion(s32[136]{0:T(256)} %param.5, s32[16]{0:T(128)} %param.4), kind=kLoop, calls=%fused_computation.17 | loop fusion | flops 152 | bytes 1216 | tf_op jit(solution)/shard_map/concatenate | solution.py:314
  27.0 0.6 %collective-permute-done.10.refs_7_ = bf16[8,10752]{1,0:T(8,128)(2,1)S(1)} collective-permute-done((bf16[8,10752]{1,0:T(8,128)(2,1)S(1)}, bf16[8,10752]{1,0:T(8,128)(2,1)S(1)}, u32[]{:S(2)}, u32[]{:S(2)}) %collective-permute-start.10) | collective-permute-done | bytes 172064 | tf_op jit(solution)/shard_map/ppermute | solution.py:163
  27.7 0.0 collective-permute-done.2.refs_1_
  27.7 0.0 collective-permute-done.8.refs_5_
  27.7 12.6 %shard_map.37 = f32[11,896,896]{2,1,0:T(8,128)} custom-call(s32[1]{0:T(128)} %bitcast.device_ref, s32[152]{0:T(256)S(1)} %pad_add_fusion.table_ref, bf16[24,14336]{1,0:T(8,128)(2,1)S(1)} %get-tuple-element.8.refs_0_, bf16[24,14336]{1,0:T(8,128)(2,1)S(1)} %collective-permute-done.2.refs_1_, bf16[16,14336]{1,0:T(8,128)(2,1)S(1)} %constant_dynamic-update-slice_fusion.3.refs_2_, ...), custom_call_target="tpu_custom_call" | custom-call | flops 2260729856 | bytes 35323904 | tf_op jit(solution)/shard_map/pallas_call | solution.py:315
  (5 shorter events, 0.1 us)
Async XLA Ops:
  0.0 9.1 %collective-permute-start = (bf16[8,14336]{1,0:T(8,128)(2,1)}, bf16[8,14336]{1,0:T(8,128)(2,1)S(1)}, u32[]{:S(2)}, u32[]{:S(2)}) collective-permute-start(bf16[8,14336]{1,0:T(8,128)(2,1)} %param.3), channel_id=1, source_target_pairs={{0,4},{1,3},{2,0},{3,7},{4,8},{5,1},{6,2},{7,11},{8,12},{9,5},{10,... | collective-permute-start | bytes 688136 | tf_op jit(solution)/shard_map/ppermute | solution.py:163
  3.0 7.6 %collective-permute-start.1 = (bf16[8,14336]{1,0:T(8,128)(2,1)}, bf16[8,14336]{1,0:T(8,128)(2,1)S(1)}, u32[]{:S(2)}, u32[]{:S(2)}) collective-permute-start(bf16[8,14336]{1,0:T(8,128)(2,1)} %param.3), channel_id=1, source_target_pairs={{0,2},{1,5},{2,6},{3,1},{4,0},{5,9},{6,10},{7,3},{8,4},{9,13},{10,... | collective-permute-start | bytes 688136 | tf_op jit(solution)/shard_map/ppermute | solution.py:163
  9.1 8.3 %collective-permute-start.3 = (bf16[8,14336]{1,0:T(8,128)(2,1)S(1)}, bf16[8,14336]{1,0:T(8,128)(2,1)S(1)}, u32[]{:S(2)}, u32[]{:S(2)}) collective-permute-start(bf16[8,14336]{1,0:T(8,128)(2,1)S(1)} %collective-permute-done), channel_id=1, source_target_pairs={{0,4},{1,3},{2,0},{3,7},{4,8},{5,1},{6,2},{7,11},{8,12},{9,5},{10,... | collective-permute-start | bytes 688136 | tf_op jit(solution)/shard_map/ppermute | solution.py:163
  10.6 9.2 %collective-permute-start.4 = (bf16[8,14336]{1,0:T(8,128)(2,1)S(1)}, bf16[8,14336]{1,0:T(8,128)(2,1)S(1)}, u32[]{:S(2)}, u32[]{:S(2)}) collective-permute-start(bf16[8,14336]{1,0:T(8,128)(2,1)S(1)} %collective-permute-done.1), channel_id=1, source_target_pairs={{0,2},{1,5},{2,6},{3,1},{4,0},{5,9},{6,10},{7,3},{8,4},{9,13},{10,... | collective-permute-start | bytes 688136 | tf_op jit(solution)/shard_map/ppermute | solution.py:163
  11.7 11.8 %collective-permute-start.7 = (bf16[8,10752]{1,0:T(8,128)(2,1)S(1)}, bf16[8,10752]{1,0:T(8,128)(2,1)S(1)}, u32[]{:S(2)}, u32[]{:S(2)}) collective-permute-start(bf16[8,10752]{1,0:T(8,128)(2,1)S(1)} %bitcast.10), channel_id=1, source_target_pairs={{0,12},{1,13},{2,14},{3,15},{4,6},{5,7},{6,4},{7,5},{8,10},{9,11},... | collective-permute-start | bytes 516104 | tf_op jit(solution)/shard_map/ppermute | solution.py:163
  15.1 12.6 %collective-permute-start.2 = (bf16[24,14336]{1,0:T(8,128)(2,1)S(1)}, bf16[24,14336]{1,0:T(8,128)(2,1)S(1)}, u32[]{:S(2)}, u32[]{:S(2)}) collective-permute-start(bf16[24,14336]{1,0:T(8,128)(2,1)S(1)} %get-tuple-element.8.refs_0_), channel_id=1, source_target_pairs={{0,1},{1,0},{2,3},{3,2},{4,5},{5,4},{6,7},{7,6},{8,9},{9,8},{10,11... | collective-permute-start | bytes 2064392 | tf_op jit(solution)/shard_map/ppermute | solution.py:163
  17.4 6.0 %collective-permute-start.6 = (bf16[8,10752]{1,0:T(8,128)(2,1)S(1)}, bf16[8,10752]{1,0:T(8,128)(2,1)S(1)}, u32[]{:S(2)}, u32[]{:S(2)}) collective-permute-start(bf16[8,10752]{1,0:T(8,128)(2,1)S(1)} %bitcast.12), channel_id=1, source_target_pairs={{0,4},{1,3},{2,0},{3,7},{4,8},{5,1},{6,2},{7,11},{8,12},{9,5},{10,... | collective-permute-start | bytes 516104 | tf_op jit(solution)/shard_map/ppermute | solution.py:163
  19.9 6.3 %collective-permute-start.9 = (bf16[8,10752]{1,0:T(8,128)(2,1)S(1)}, bf16[8,10752]{1,0:T(8,128)(2,1)S(1)}, u32[]{:S(2)}, u32[]{:S(2)}) collective-permute-start(bf16[8,10752]{1,0:T(8,128)(2,1)S(1)} %bitcast.11), channel_id=1, source_target_pairs={{0,2},{1,5},{2,6},{3,1},{4,0},{5,9},{6,10},{7,3},{8,4},{9,13},{10,... | collective-permute-start | bytes 516104 | tf_op jit(solution)/shard_map/ppermute | solution.py:163
  20.0 3.5 %collective-permute-start.5 = (bf16[16,14336]{1,0:T(8,128)(2,1)S(1)}, bf16[16,14336]{1,0:T(8,128)(2,1)S(1)}, u32[]{:S(2)}, u32[]{:S(2)}) collective-permute-start(bf16[16,14336]{1,0:T(8,128)(2,1)S(1)} %constant_dynamic-update-slice_fusion.3.refs_2_), channel_id=1, source_target_pairs={{0,1},{1,0},{2,3},{3,2},{4,5},{5,4},{6,7},{7,6},{8,9},{9,8},{10,11... | collective-permute-start | bytes 1376264 | tf_op jit(solution)/shard_map/ppermute | solution.py:163
  23.5 4.1 %collective-permute-start.8 = (bf16[16,10752]{1,0:T(8,128)(2,1)S(1)}, bf16[16,10752]{1,0:T(8,128)(2,1)S(1)}, u32[]{:S(2)}, u32[]{:S(2)}) collective-permute-start(bf16[16,10752]{1,0:T(8,128)(2,1)S(1)} %constant_dynamic-update-slice_fusion.5.refs_4_), channel_id=1, source_target_pairs={{0,1},{1,0},{2,3},{3,2},{4,5},{5,4},{6,7},{7,6},{8,9},{9,8},{10,11... | collective-permute-start | bytes 1032200 | tf_op jit(solution)/shard_map/ppermute | solution.py:163
  26.3 1.4 %collective-permute-start.10 = (bf16[8,10752]{1,0:T(8,128)(2,1)S(1)}, bf16[8,10752]{1,0:T(8,128)(2,1)S(1)}, u32[]{:S(2)}, u32[]{:S(2)}) collective-permute-start(bf16[8,10752]{1,0:T(8,128)(2,1)S(1)} %collective-permute-done.9.refs_6_), channel_id=1, source_target_pairs={{0,1},{1,0},{2,3},{3,2},{4,5},{5,4},{6,7},{7,6},{8,9},{9,8},{10,11... | collective-permute-start | bytes 516104 | tf_op jit(solution)/shard_map/ppermute | solution.py:163

commit v15 on v14

--- a/solution.py
+++ b/solution.py
@@ -147,7 +147,7 @@
     return onward, backward
 
 
-GROUPS = ((0, 1, 2), (8, 9, 10), (3, 4), (11, 12), (5, 7), (13, 15), (6,), (14,))
+GROUPS = ((0, 1, 2), (8, 9, 10), (3, 4), (11, 12), (7, 15), (5,), (13,), (6,), (14,))
 
 
 def first_needed(devices, chip):
@@ -195,16 +195,26 @@
     for _ in range(2):
         ahead.append(send(ahead[-1], onward))
         back.append(send(back[-1], backward))
-    half = send(window(jnp.where(came_ahead, ahead[1], back[1]), over_chip), over)
-    ahead.append(send(window(ahead[2], onward_chip), onward))
-    back.append(send(window(back[2], backward_chip), backward))
     near = jnp.concatenate((tokens, ahead[1], back[1]), axis=0)
+    near_beside = send(near, sibling)
+    ours = jnp.where(came_ahead, ahead[1], back[1])
+    theirs = jnp.where(came_ahead, near_beside[2 * slab:], near_beside[slab:2 * slab])
+    both = jnp.concatenate((window(ours, over_chip), window(theirs, over_chip)), axis=0)
+    arrived = lax.ppermute(both, "col", [(at, over[at]) for at in range(1, devices, 2)])
+    handed = lax.ppermute(arrived, "col", [(at, at - 1) for at in range(1, devices, 2)])
+    half = jnp.concatenate((
+        jnp.where(core == 1, arrived[:slab], handed[slab:]),
+        jnp.where(core == 1, arrived[slab:], handed[:slab]),
+    ), axis=0)
+    ahead.append(send(window(after(ahead[2], both), onward_chip), onward))
+    back.append(send(window(after(back[2], both), backward_chip), backward))
     middle = jnp.concatenate((ahead[2], back[2]), axis=0)
-    last = jnp.concatenate((ahead[3], half), axis=0)
-    near_beside = send(near, sibling)
     middle_beside = send(middle, sibling)
-    last_beside = send(after(last, middle_beside), sibling)
-    return [near, near_beside, middle, middle_beside, last, last_beside, back[3], send(back[3], sibling)]
+    return [
+        near, near_beside, middle, middle_beside, half,
+        ahead[3], send(ahead[3], sibling), back[3], send(back[3], sibling),
+    ]
+
 
 def slab_origin(devices, device, number):
     chips = devices // 2

time: 40.5 us -> 42.3 us (1.044); the launches traced: 40.3 us -> 41.6 us
  starting transfers between devices: 11.4 us -> 15.1 us
  waiting for transfers between devices: 13.8 us -> 11.4 us
    ppermute x11 -> x10, waiting for transfers between devices: 13.8 us -> 11.4 us  [send(): return lax.ppermute(value, 'col', list(enumerate(target)))]
    ppermute x0 -> x2, starting transfers between devices: none -> 1.96 us  [the longest x1 1.28 us: ring_gather(): lax.ppermute(arrived, 'col', [(at, at - 1) for at in range(1, devices, 2)])]
    ppermute x11 -> x10, starting transfers between devices: 11.4 us -> 13.1 us  [send(): return lax.ppermute(value, 'col', list(enumerate(target)))]
    unnamed x4 -> x3, local copies, waits for them, and re-layouts: 1.06 us -> 1.05 us
  transfers between devices with their start and end apart: 11 -> 12, of which waited for: 5 -> 8; matrix products, arithmetic and copies ran while one was open for 5% -> 6% of each run, Pallas kernels for 0% -> 0%
where the time goes in v15:
time: 42.3 us; the launch traced here: 41.6 us
  starting transfers between devices  15.1 us (36%)
  Pallas kernels  12.6 us (30%)
  waiting for transfers between devices  11.4 us (27%)
  other arithmetic  1.29 us (3%)
  local copies, waits for them, and re-layouts  1.07 us (3%)
    ppermute x10, starting transfers between devices, send(): return lax.ppermute(value, 'col', list(enumerate(target)))  13.1 us
    pallas_call x1, Pallas kernels, ring_form(): pl.pallas_call(functools.partial(ring_kernel, devices, slots), out_shape=...  12.6 us
    ppermute x10, waiting for transfers between devices, send(): return lax.ppermute(value, 'col', list(enumerate(target)))  11.4 us
    ppermute x1, starting transfers between devices, ring_gather(): lax.ppermute(arrived, 'col', [(at, at - 1) for at in range(1, devices, 2)])  1.28 us
    unnamed x3, local copies, waits for them, and re-layouts  1.05 us
  transfers between devices with their start and end apart: 12, of which 8 were waited for; matrix products, arithmetic and copies ran while one was open for 6% of the time, Pallas kernels for 0%

profile of v15, /device:TPU:0, one launch (start us, length us, event | category | flops | bytes accessed | tf_op | source)
XLA Modules:
  0.0 41.6 jit_solution(1759431788980789070)
XLA Ops:
  0.0 3.0 %collective-permute-start = (bf16[8,14336]{1,0:T(8,128)(2,1)}, bf16[8,14336]{1,0:T(8,128)(2,1)S(1)}, u32[]{:S(2)}, u32[]{:S(2)}) collective-permute-start(bf16[8,14336]{1,0:T(8,128)(2,1)} %param.3), channel_id=1, source_target_pairs={{0,4},{1,3},{2,0},{3,7},{4,8},{5,1},{6,2},{7,11},{8,12},{9,5},{10,... | collective-permute-start | bytes 688136 | tf_op jit(solution)/shard_map/ppermute | solution.py:163
  3.0 0.0 collective-permute-start.1
  3.0 1.0 %constant_dynamic-update-slice_fusion.2 = bf16[24,14336]{1,0:T(8,128)(2,1)S(1)} fusion(bf16[8,14336]{1,0:T(8,128)(2,1)} %param.3), kind=kLoop, calls=%fused_computation.20 | loop fusion | bytes 458752
  4.1 5.0 %collective-permute-done = bf16[8,14336]{1,0:T(8,128)(2,1)S(1)} collective-permute-done((bf16[8,14336]{1,0:T(8,128)(2,1)}, bf16[8,14336]{1,0:T(8,128)(2,1)S(1)}, u32[]{:S(2)}, u32[]{:S(2)}) %collective-permute-start) | collective-permute-done | bytes 229408 | tf_op jit(solution)/shard_map/ppermute | solution.py:163
  9.1 0.2 collective-permute-done.1
  9.3 0.1 broadcast_select_fusion
  9.3 0.2 collective-permute-start.2
  9.6 0.8 %pad_add_fusion.table_ref = s32[152]{0:T(256)S(1)} fusion(s32[136]{0:T(256)} %param.5, s32[16]{0:T(128)} %param.4), kind=kLoop, calls=%fused_computation.23 | loop fusion | flops 152 | bytes 1216 | tf_op jit(solution)/shard_map/concatenate | solution.py:324
  10.3 1.5 %collective-permute-start.3 = (bf16[8,14336]{1,0:T(8,128)(2,1)S(1)}, bf16[8,14336]{1,0:T(8,128)(2,1)S(1)}, u32[]{:S(2)}, u32[]{:S(2)}) collective-permute-start(bf16[8,14336]{1,0:T(8,128)(2,1)S(1)} %collective-permute-done), channel_id=1, source_target_pairs={{0,4},{1,3},{2,0},{3,7},{4,8},{5,1},{6,2},{7,11},{8,12},{9,5},{10,... | collective-permute-start | bytes 688136 | tf_op jit(solution)/shard_map/ppermute | solution.py:163
  11.9 0.7 %collective-permute-start.4 = (bf16[8,14336]{1,0:T(8,128)(2,1)S(1)}, bf16[8,14336]{1,0:T(8,128)(2,1)S(1)}, u32[]{:S(2)}, u32[]{:S(2)}) collective-permute-start(bf16[8,14336]{1,0:T(8,128)(2,1)S(1)} %collective-permute-done.1), channel_id=1, source_target_pairs={{0,2},{1,5},{2,6},{3,1},{4,0},{5,9},{6,10},{7,3},{8,4},{9,13},{10,... | collective-permute-start | bytes 688136 | tf_op jit(solution)/shard_map/ppermute | solution.py:163
  12.6 0.0 collective-permute-done.2.refs_1_
  12.6 0.2 fusion.2
  12.8 0.7 %collective-permute-start.6 = (bf16[16,10752]{1,0:T(8,128)(2,1)S(1)}, bf16[16,10752]{1,0:T(8,128)(2,1)S(1)}, u32[]{:S(2)}, u32[]{:S(2)}) collective-permute-start(bf16[16,10752]{1,0:T(8,128)(2,1)S(1)} %pad_maximum_fusion), channel_id=1, source_target_pairs={{1,13},{3,15},{5,7},{7,5},{9,11},{11,9},{13,1},{15,3},{17,29},{19,... | collective-permute-start | bytes 1032200 | tf_op jit(solution)/shard_map/ppermute | solution.py:203
  13.5 4.3 %collective-permute-done.3 = bf16[8,14336]{1,0:T(8,128)(2,1)S(1)} collective-permute-done((bf16[8,14336]{1,0:T(8,128)(2,1)S(1)}, bf16[8,14336]{1,0:T(8,128)(2,1)S(1)}, u32[]{:S(2)}, u32[]{:S(2)}) %collective-permute-start.3) | collective-permute-done | bytes 229408 | tf_op jit(solution)/shard_map/ppermute | solution.py:163
  17.8 0.3 collective-permute-done.4
  18.2 0.1 fusion.1
  18.3 2.2 %collective-permute-start.8 = (bf16[8,10752]{1,0:T(8,128)(2,1)S(1)}, bf16[8,10752]{1,0:T(8,128)(2,1)S(1)}, u32[]{:S(2)}, u32[]{:S(2)}) collective-permute-start(bf16[8,10752]{1,0:T(8,128)(2,1)S(1)} %bitcast.16), channel_id=1, source_target_pairs={{0,4},{1,3},{2,0},{3,7},{4,8},{5,1},{6,2},{7,11},{8,12},{9,5},{10,... | collective-permute-start | bytes 516104 | tf_op jit(solution)/shard_map/ppermute | solution.py:163
  20.5 0.1 fusion
  20.6 0.2 collective-permute-start.10
  20.7 0.0 collective-permute-done.6
  20.7 1.3 %collective-permute-start.7 = (bf16[16,10752]{1,0:T(8,128)(2,1)S(1)}, bf16[16,10752]{1,0:T(8,128)(2,1)S(1)}, u32[]{:S(2)}, u32[]{:S(2)}) collective-permute-start(bf16[16,10752]{1,0:T(8,128)(2,1)S(1)} %collective-permute-done.6), channel_id=1, source_target_pairs={{1,0},{3,2},{5,4},{7,6},{9,8},{11,10},{13,12},{15,14},{17,16},{19,... | collective-permute-start | bytes 1032200 | tf_op jit(solution)/shard_map/ppermute | solution.py:204
  22.0 3.2 %collective-permute-start.5 = (bf16[16,14336]{1,0:T(8,128)(2,1)S(1)}, bf16[16,14336]{1,0:T(8,128)(2,1)S(1)}, u32[]{:S(2)}, u32[]{:S(2)}) collective-permute-start(bf16[16,14336]{1,0:T(8,128)(2,1)S(1)} %constant_dynamic-update-slice_fusion.3.refs_2_), channel_id=1, source_target_pairs={{0,1},{1,0},{2,3},{3,2},{4,5},{5,4},{6,7},{7,6},{8,9},{9,8},{10,11... | collective-permute-start | bytes 1376264 | tf_op jit(solution)/shard_map/ppermute | solution.py:163
  25.2 0.1 collective-permute-done.8.refs_5_
  25.3 2.0 %collective-permute-start.9 = (bf16[8,10752]{1,0:T(8,128)(2,1)S(1)}, bf16[8,10752]{1,0:T(8,128)(2,1)S(1)}, u32[]{:S(2)}, u32[]{:S(2)}) collective-permute-start(bf16[8,10752]{1,0:T(8,128)(2,1)S(1)} %collective-permute-done.8.refs_5_), channel_id=1, source_target_pairs={{0,1},{1,0},{2,3},{3,2},{4,5},{5,4},{6,7},{7,6},{8,9},{9,8},{10,11... | collective-permute-start | bytes 516104 | tf_op jit(solution)/shard_map/ppermute | solution.py:163
  27.3 0.2 collective-permute-done.10.refs_7_
  27.6 0.0 collective-permute-start.11
  27.6 0.0 collective-permute-done.7
  27.6 0.0 collective-permute-done.5.refs_3_
  27.6 0.7 %collective-permute-done.9.refs_6_ = bf16[8,10752]{1,0:T(8,128)(2,1)S(1)} collective-permute-done((bf16[8,10752]{1,0:T(8,128)(2,1)S(1)}, bf16[8,10752]{1,0:T(8,128)(2,1)S(1)}, u32[]{:S(2)}, u32[]{:S(2)}) %collective-permute-start.9) | collective-permute-done | bytes 172064 | tf_op jit(solution)/shard_map/ppermute | solution.py:163
  28.4 0.6 %collective-permute-done.11.refs_8_ = bf16[8,10752]{1,0:T(8,128)(2,1)S(1)} collective-permute-done((bf16[8,10752]{1,0:T(8,128)(2,1)S(1)}, bf16[8,10752]{1,0:T(8,128)(2,1)S(1)}, u32[]{:S(2)}, u32[]{:S(2)}) %collective-permute-start.11) | collective-permute-done | bytes 172064 | tf_op jit(solution)/shard_map/ppermute | solution.py:163
  29.0 12.6 %shard_map.37 = f32[11,896,896]{2,1,0:T(8,128)} custom-call(s32[1]{0:T(128)} %bitcast.device_ref, s32[152]{0:T(256)S(1)} %pad_add_fusion.table_ref, bf16[24,14336]{1,0:T(8,128)(2,1)S(1)} %get-tuple-element.12.refs_0_, bf16[24,14336]{1,0:T(8,128)(2,1)S(1)} %collective-permute-done.2.refs_1_, ...), custom_call_target="tpu_custom_call" | custom-call | flops 2260729856 | bytes 35323904 | tf_op jit(solution)/shard_map/pallas_call | solution.py:325
  (7 shorter events, 0.2 us)
Async XLA Ops:
  0.0 9.1 %collective-permute-start = (bf16[8,14336]{1,0:T(8,128)(2,1)}, bf16[8,14336]{1,0:T(8,128)(2,1)S(1)}, u32[]{:S(2)}, u32[]{:S(2)}) collective-permute-start(bf16[8,14336]{1,0:T(8,128)(2,1)} %param.3), channel_id=1, source_target_pairs={{0,4},{1,3},{2,0},{3,7},{4,8},{5,1},{6,2},{7,11},{8,12},{9,5},{10,... | collective-permute-start | bytes 688136 | tf_op jit(solution)/shard_map/ppermute | solution.py:163
  3.0 6.2 %collective-permute-start.1 = (bf16[8,14336]{1,0:T(8,128)(2,1)}, bf16[8,14336]{1,0:T(8,128)(2,1)S(1)}, u32[]{:S(2)}, u32[]{:S(2)}) collective-permute-start(bf16[8,14336]{1,0:T(8,128)(2,1)} %param.3), channel_id=1, source_target_pairs={{0,2},{1,5},{2,6},{3,1},{4,0},{5,9},{6,10},{7,3},{8,4},{9,13},{10,... | collective-permute-start | bytes 688136 | tf_op jit(solution)/shard_map/ppermute | solution.py:163
  9.3 3.3 %collective-permute-start.2 = (bf16[24,14336]{1,0:T(8,128)(2,1)S(1)}, bf16[24,14336]{1,0:T(8,128)(2,1)S(1)}, u32[]{:S(2)}, u32[]{:S(2)}) collective-permute-start(bf16[24,14336]{1,0:T(8,128)(2,1)S(1)} %get-tuple-element.12.refs_0_), channel_id=1, source_target_pairs={{0,1},{1,0},{2,3},{3,2},{4,5},{5,4},{6,7},{7,6},{8,9},{9,8},{10,11... | collective-permute-start | bytes 2064392 | tf_op jit(solution)/shard_map/ppermute | solution.py:163
  10.3 7.5 %collective-permute-start.3 = (bf16[8,14336]{1,0:T(8,128)(2,1)S(1)}, bf16[8,14336]{1,0:T(8,128)(2,1)S(1)}, u32[]{:S(2)}, u32[]{:S(2)}) collective-permute-start(bf16[8,14336]{1,0:T(8,128)(2,1)S(1)} %collective-permute-done), channel_id=1, source_target_pairs={{0,4},{1,3},{2,0},{3,7},{4,8},{5,1},{6,2},{7,11},{8,12},{9,5},{10,... | collective-permute-start | bytes 688136 | tf_op jit(solution)/shard_map/ppermute | solution.py:163
  11.9 6.3 %collective-permute-start.4 = (bf16[8,14336]{1,0:T(8,128)(2,1)S(1)}, bf16[8,14336]{1,0:T(8,128)(2,1)S(1)}, u32[]{:S(2)}, u32[]{:S(2)}) collective-permute-start(bf16[8,14336]{1,0:T(8,128)(2,1)S(1)} %collective-permute-done.1), channel_id=1, source_target_pairs={{0,2},{1,5},{2,6},{3,1},{4,0},{5,9},{6,10},{7,3},{8,4},{9,13},{10,... | collective-permute-start | bytes 688136 | tf_op jit(solution)/shard_map/ppermute | solution.py:163
  12.8 7.9 %collective-permute-start.6 = (bf16[16,10752]{1,0:T(8,128)(2,1)S(1)}, bf16[16,10752]{1,0:T(8,128)(2,1)S(1)}, u32[]{:S(2)}, u32[]{:S(2)}) collective-permute-start(bf16[16,10752]{1,0:T(8,128)(2,1)S(1)} %pad_maximum_fusion), channel_id=1, source_target_pairs={{1,13},{3,15},{5,7},{7,5},{9,11},{11,9},{13,1},{15,3},{17,29},{19,... | collective-permute-start | bytes 1032200 | tf_op jit(solution)/shard_map/ppermute | solution.py:203
  18.3 7.1 %collective-permute-start.8 = (bf16[8,10752]{1,0:T(8,128)(2,1)S(1)}, bf16[8,10752]{1,0:T(8,128)(2,1)S(1)}, u32[]{:S(2)}, u32[]{:S(2)}) collective-permute-start(bf16[8,10752]{1,0:T(8,128)(2,1)S(1)} %bitcast.16), channel_id=1, source_target_pairs={{0,4},{1,3},{2,0},{3,7},{4,8},{5,1},{6,2},{7,11},{8,12},{9,5},{10,... | collective-permute-start | bytes 516104 | tf_op jit(solution)/shard_map/ppermute | solution.py:163
  20.6 7.0 %collective-permute-start.10 = (bf16[8,10752]{1,0:T(8,128)(2,1)S(1)}, bf16[8,10752]{1,0:T(8,128)(2,1)S(1)}, u32[]{:S(2)}, u32[]{:S(2)}) collective-permute-start(bf16[8,10752]{1,0:T(8,128)(2,1)S(1)} %bitcast.15), channel_id=1, source_target_pairs={{0,2},{1,5},{2,6},{3,1},{4,0},{5,9},{6,10},{7,3},{8,4},{9,13},{10,... | collective-permute-start | bytes 516104 | tf_op jit(solution)/shard_map/ppermute | solution.py:163
  20.7 6.8 %collective-permute-start.7 = (bf16[16,10752]{1,0:T(8,128)(2,1)S(1)}, bf16[16,10752]{1,0:T(8,128)(2,1)S(1)}, u32[]{:S(2)}, u32[]{:S(2)}) collective-permute-start(bf16[16,10752]{1,0:T(8,128)(2,1)S(1)} %collective-permute-done.6), channel_id=1, source_target_pairs={{1,0},{3,2},{5,4},{7,6},{9,8},{11,10},{13,12},{15,14},{17,16},{19,... | collective-permute-start | bytes 1032200 | tf_op jit(solution)/shard_map/ppermute | solution.py:204
  22.0 5.6 %collective-permute-start.5 = (bf16[16,14336]{1,0:T(8,128)(2,1)S(1)}, bf16[16,14336]{1,0:T(8,128)(2,1)S(1)}, u32[]{:S(2)}, u32[]{:S(2)}) collective-permute-start(bf16[16,14336]{1,0:T(8,128)(2,1)S(1)} %constant_dynamic-update-slice_fusion.3.refs_2_), channel_id=1, source_target_pairs={{0,1},{1,0},{2,3},{3,2},{4,5},{5,4},{6,7},{7,6},{8,9},{9,8},{10,11... | collective-permute-start | bytes 1376264 | tf_op jit(solution)/shard_map/ppermute | solution.py:163
  25.3 3.1 %collective-permute-start.9 = (bf16[8,10752]{1,0:T(8,128)(2,1)S(1)}, bf16[8,10752]{1,0:T(8,128)(2,1)S(1)}, u32[]{:S(2)}, u32[]{:S(2)}) collective-permute-start(bf16[8,10752]{1,0:T(8,128)(2,1)S(1)} %collective-permute-done.8.refs_5_), channel_id=1, source_target_pairs={{0,1},{1,0},{2,3},{3,2},{4,5},{5,4},{6,7},{7,6},{8,9},{9,8},{10,11... | collective-permute-start | bytes 516104 | tf_op jit(solution)/shard_map/ppermute | solution.py:163
  27.6 1.4 %collective-permute-start.11 = (bf16[8,10752]{1,0:T(8,128)(2,1)S(1)}, bf16[8,10752]{1,0:T(8,128)(2,1)S(1)}, u32[]{:S(2)}, u32[]{:S(2)}) collective-permute-start(bf16[8,10752]{1,0:T(8,128)(2,1)S(1)} %collective-permute-done.10.refs_7_), channel_id=1, source_target_pairs={{0,1},{1,0},{2,3},{3,2},{4,5},{5,4},{6,7},{7,6},{8,9},{9,8},{10,11... | collective-permute-start | bytes 516104 | tf_op jit(solution)/shard_map/ppermute | solution.py:163

commit v16 on v14

--- a/solution.py
+++ b/solution.py
@@ -147,7 +147,7 @@
     return onward, backward
 
 
-GROUPS = ((0, 1, 2), (8, 9, 10), (3, 4), (11, 12), (5, 7), (13, 15), (6,), (14,))
+GROUPS = ((0, 1, 2), (8, 9, 10), (3, 4), (11, 12), (5, 6), (13, 14), (7,), (15,))
 
 
 def first_needed(devices, chip):
@@ -195,16 +195,16 @@
     for _ in range(2):
         ahead.append(send(ahead[-1], onward))
         back.append(send(back[-1], backward))
-    half = send(window(jnp.where(came_ahead, ahead[1], back[1]), over_chip), over)
     ahead.append(send(window(ahead[2], onward_chip), onward))
     back.append(send(window(back[2], backward_chip), backward))
-    near = jnp.concatenate((tokens, ahead[1], back[1]), axis=0)
-    middle = jnp.concatenate((ahead[2], back[2]), axis=0)
-    last = jnp.concatenate((ahead[3], half), axis=0)
-    near_beside = send(near, sibling)
-    middle_beside = send(middle, sibling)
-    last_beside = send(after(last, middle_beside), sibling)
-    return [near, near_beside, middle, middle_beside, last, last_beside, back[3], send(back[3], sibling)]
+    held = after(jnp.where(came_ahead, ahead[1], back[1]), ahead[2], back[2])
+    half = send(window(held, over_chip), over)
+    groups = []
+    for group in ((tokens, ahead[1], back[1]), (ahead[2], back[2]), (ahead[3], back[3]), (half,)):
+        group = jnp.concatenate(group, axis=0)
+        groups += [group, send(group, sibling)]
+    return groups
+
 
 def slab_origin(devices, device, number):
     chips = devices // 2

time: 40.5 us -> 44.1 us (1.089)
  waiting for transfers between devices: 13.8 us -> 18.7 us
  starting transfers between devices: 11.4 us -> 10.1 us
    ppermute x11, waiting for transfers between devices: 13.8 us -> 18.7 us  [send(): return lax.ppermute(value, 'col', list(enumerate(target)))]
    ppermute x11, starting transfers between devices: 11.4 us -> 10.1 us  [send(): return lax.ppermute(value, 'col', list(enumerate(target)))]
  transfers between devices with their start and end apart: 11 -> 11, of which waited for: 5 -> 7; matrix products, arithmetic and copies ran while one was open for 5% -> 5% of each run, Pallas kernels for 0% -> 0%
where the time goes in v16:
time: 44.1 us; the launch traced here: 43.9 us
  waiting for transfers between devices  18.7 us (42%)
  Pallas kernels  12.6 us (29%)
  starting transfers between devices  10.1 us (23%)
  other arithmetic  1.11 us (3%)
  local copies, waits for them, and re-layouts  1.09 us (2%)
    ppermute x11, waiting for transfers between devices, send(): return lax.ppermute(value, 'col', list(enumerate(target)))  18.7 us
    pallas_call x1, Pallas kernels, ring_form(): pl.pallas_call(functools.partial(ring_kernel, devices, slots), out_shape=...  12.6 us
    ppermute x11, starting transfers between devices, send(): return lax.ppermute(value, 'col', list(enumerate(target)))  10.1 us
    unnamed x4, local copies, waits for them, and re-layouts  1.06 us
  transfers between devices with their start and end apart: 11, of which 7 were waited for; matrix products, arithmetic and copies ran while one was open for 5% of the time, Pallas kernels for 0%

profile of v16, /device:TPU:0, one launch (start us, length us, event | category | flops | bytes accessed | tf_op | source)
XLA Modules:
  0.0 43.9 jit_solution(11586099771145255413)
XLA Ops:
  0.0 3.0 %collective-permute-start = (bf16[8,14336]{1,0:T(8,128)(2,1)}, bf16[8,14336]{1,0:T(8,128)(2,1)S(1)}, u32[]{:S(2)}, u32[]{:S(2)}) collective-permute-start(bf16[8,14336]{1,0:T(8,128)(2,1)} %param.3), channel_id=1, source_target_pairs={{0,4},{1,3},{2,0},{3,7},{4,8},{5,1},{6,2},{7,11},{8,12},{9,5},{10,... | collective-permute-start | bytes 688136 | tf_op jit(solution)/shard_map/ppermute | solution.py:163
  3.0 0.0 collective-permute-start.1
  3.0 1.0 %constant_dynamic-update-slice_fusion.2 = bf16[24,14336]{1,0:T(8,128)(2,1)S(1)} fusion(bf16[8,14336]{1,0:T(8,128)(2,1)} %param.3), kind=kLoop, calls=%fused_computation.12 | loop fusion | bytes 458752
  4.2 4.9 %collective-permute-done = bf16[8,14336]{1,0:T(8,128)(2,1)S(1)} collective-permute-done((bf16[8,14336]{1,0:T(8,128)(2,1)}, bf16[8,14336]{1,0:T(8,128)(2,1)S(1)}, u32[]{:S(2)}, u32[]{:S(2)}) %collective-permute-start) | collective-permute-done | bytes 229408 | tf_op jit(solution)/shard_map/ppermute | solution.py:163
  9.1 1.5 %collective-permute-start.3 = (bf16[8,14336]{1,0:T(8,128)(2,1)S(1)}, bf16[8,14336]{1,0:T(8,128)(2,1)S(1)}, u32[]{:S(2)}, u32[]{:S(2)}) collective-permute-start(bf16[8,14336]{1,0:T(8,128)(2,1)S(1)} %collective-permute-done), channel_id=1, source_target_pairs={{0,4},{1,3},{2,0},{3,7},{4,8},{5,1},{6,2},{7,11},{8,12},{9,5},{10,... | collective-permute-start | bytes 688136 | tf_op jit(solution)/shard_map/ppermute | solution.py:163
  10.6 0.0 collective-permute-done.1
  10.6 0.9 %collective-permute-start.4 = (bf16[8,14336]{1,0:T(8,128)(2,1)S(1)}, bf16[8,14336]{1,0:T(8,128)(2,1)S(1)}, u32[]{:S(2)}, u32[]{:S(2)}) collective-permute-start(bf16[8,14336]{1,0:T(8,128)(2,1)S(1)} %collective-permute-done.1), channel_id=1, source_target_pairs={{0,2},{1,5},{2,6},{3,1},{4,0},{5,9},{6,10},{7,3},{8,4},{9,13},{10,... | collective-permute-start | bytes 688136 | tf_op jit(solution)/shard_map/ppermute | solution.py:163
  11.5 0.1 broadcast_select_fusion
  11.6 0.1 collective-permute-start.2
  11.6 5.7 %collective-permute-done.3 = bf16[8,14336]{1,0:T(8,128)(2,1)S(1)} collective-permute-done((bf16[8,14336]{1,0:T(8,128)(2,1)S(1)}, bf16[8,14336]{1,0:T(8,128)(2,1)S(1)}, u32[]{:S(2)}, u32[]{:S(2)}) %collective-permute-start.3) | collective-permute-done | bytes 229408 | tf_op jit(solution)/shard_map/ppermute | solution.py:163
  17.3 0.1 fusion.2
  17.4 0.1 collective-permute-start.6
  17.5 0.9 %collective-permute-done.4 = bf16[8,14336]{1,0:T(8,128)(2,1)S(1)} collective-permute-done((bf16[8,14336]{1,0:T(8,128)(2,1)S(1)}, bf16[8,14336]{1,0:T(8,128)(2,1)S(1)}, u32[]{:S(2)}, u32[]{:S(2)}) %collective-permute-start.4) | collective-permute-done | bytes 229408 | tf_op jit(solution)/shard_map/ppermute | solution.py:163
  18.4 0.1 fusion.1
  18.5 1.2 %collective-permute-start.7 = (bf16[8,10752]{1,0:T(8,128)(2,1)S(1)}, bf16[8,10752]{1,0:T(8,128)(2,1)S(1)}, u32[]{:S(2)}, u32[]{:S(2)}) collective-permute-start(bf16[8,10752]{1,0:T(8,128)(2,1)S(1)} %bitcast.11), channel_id=1, source_target_pairs={{0,2},{1,5},{2,6},{3,1},{4,0},{5,9},{6,10},{7,3},{8,4},{9,13},{10,... | collective-permute-start | bytes 516104 | tf_op jit(solution)/shard_map/ppermute | solution.py:163
  19.7 0.1 collective-permute-start.5
  19.8 0.1 fusion
  19.9 3.2 %collective-permute-start.9 = (bf16[8,10752]{1,0:T(8,128)(2,1)S(1)}, bf16[8,10752]{1,0:T(8,128)(2,1)S(1)}, u32[]{:S(2)}, u32[]{:S(2)}) collective-permute-start(bf16[8,10752]{1,0:T(8,128)(2,1)S(1)} %bitcast.12), channel_id=1, source_target_pairs={{0,12},{1,13},{2,14},{3,15},{4,6},{5,7},{6,4},{7,5},{8,10},{9,11},... | collective-permute-start | bytes 516104 | tf_op jit(solution)/shard_map/ppermute | solution.py:163
  23.1 0.3 collective-permute-done.6
  23.4 0.5 %collective-permute-done.7 = bf16[8,10752]{1,0:T(8,128)(2,1)S(1)} collective-permute-done((bf16[8,10752]{1,0:T(8,128)(2,1)S(1)}, bf16[8,10752]{1,0:T(8,128)(2,1)S(1)}, u32[]{:S(2)}, u32[]{:S(2)}) %collective-permute-start.7) | collective-permute-done | bytes 172064 | tf_op jit(solution)/shard_map/ppermute | solution.py:163
  23.9 0.1 collective-permute-start.8
  24.0 5.9 %collective-permute-done.9.refs_6_ = bf16[8,10752]{1,0:T(8,128)(2,1)S(1)} collective-permute-done((bf16[8,10752]{1,0:T(8,128)(2,1)S(1)}, bf16[8,10752]{1,0:T(8,128)(2,1)S(1)}, u32[]{:S(2)}, u32[]{:S(2)}) %collective-permute-start.9) | collective-permute-done | bytes 172064 | tf_op jit(solution)/shard_map/ppermute | solution.py:163
  29.9 0.0 collective-permute-start.10
  29.9 0.8 %pad_add_fusion.table_ref = s32[152]{0:T(256)S(1)} fusion(s32[136]{0:T(256)} %param.5, s32[16]{0:T(128)} %param.4), kind=kLoop, calls=%fused_computation.17 | loop fusion | flops 152 | bytes 1216 | tf_op jit(solution)/shard_map/concatenate | solution.py:314
  30.6 0.6 %collective-permute-done.10.refs_7_ = bf16[8,10752]{1,0:T(8,128)(2,1)S(1)} collective-permute-done((bf16[8,10752]{1,0:T(8,128)(2,1)S(1)}, bf16[8,10752]{1,0:T(8,128)(2,1)S(1)}, u32[]{:S(2)}, u32[]{:S(2)}) %collective-permute-start.10) | collective-permute-done | bytes 172064 | tf_op jit(solution)/shard_map/ppermute | solution.py:163
  31.3 0.0 collective-permute-done.5.refs_3_
  31.3 0.0 collective-permute-done.2.refs_1_
  31.3 0.0 collective-permute-done.8.refs_5_
  31.3 12.6 %shard_map.37 = f32[11,896,896]{2,1,0:T(8,128)} custom-call(s32[1]{0:T(128)} %bitcast.device_ref, s32[152]{0:T(256)S(1)} %pad_add_fusion.table_ref, bf16[24,14336]{1,0:T(8,128)(2,1)S(1)} %get-tuple-element.8.refs_0_, bf16[24,14336]{1,0:T(8,128)(2,1)S(1)} %collective-permute-done.2.refs_1_, bf16[16,14336]{1,0:T(8,128)(2,1)S(1)} %constant_dynamic-update-slice_fusion.3.refs_2_, ...), custom_call_target="tpu_custom_call" | custom-call | flops 2260729856 | bytes 35323904 | tf_op jit(solution)/shard_map/pallas_call | solution.py:315
  (5 shorter events, 0.1 us)
Async XLA Ops:
  0.0 9.1 %collective-permute-start = (bf16[8,14336]{1,0:T(8,128)(2,1)}, bf16[8,14336]{1,0:T(8,128)(2,1)S(1)}, u32[]{:S(2)}, u32[]{:S(2)}) collective-permute-start(bf16[8,14336]{1,0:T(8,128)(2,1)} %param.3), channel_id=1, source_target_pairs={{0,4},{1,3},{2,0},{3,7},{4,8},{5,1},{6,2},{7,11},{8,12},{9,5},{10,... | collective-permute-start | bytes 688136 | tf_op jit(solution)/shard_map/ppermute | solution.py:163
  3.0 7.6 %collective-permute-start.1 = (bf16[8,14336]{1,0:T(8,128)(2,1)}, bf16[8,14336]{1,0:T(8,128)(2,1)S(1)}, u32[]{:S(2)}, u32[]{:S(2)}) collective-permute-start(bf16[8,14336]{1,0:T(8,128)(2,1)} %param.3), channel_id=1, source_target_pairs={{0,2},{1,5},{2,6},{3,1},{4,0},{5,9},{6,10},{7,3},{8,4},{9,13},{10,... | collective-permute-start | bytes 688136 | tf_op jit(solution)/shard_map/ppermute | solution.py:163
  9.1 8.3 %collective-permute-start.3 = (bf16[8,14336]{1,0:T(8,128)(2,1)S(1)}, bf16[8,14336]{1,0:T(8,128)(2,1)S(1)}, u32[]{:S(2)}, u32[]{:S(2)}) collective-permute-start(bf16[8,14336]{1,0:T(8,128)(2,1)S(1)} %collective-permute-done), channel_id=1, source_target_pairs={{0,4},{1,3},{2,0},{3,7},{4,8},{5,1},{6,2},{7,11},{8,12},{9,5},{10,... | collective-permute-start | bytes 688136 | tf_op jit(solution)/shard_map/ppermute | solution.py:163
  10.6 7.8 %collective-permute-start.4 = (bf16[8,14336]{1,0:T(8,128)(2,1)S(1)}, bf16[8,14336]{1,0:T(8,128)(2,1)S(1)}, u32[]{:S(2)}, u32[]{:S(2)}) collective-permute-start(bf16[8,14336]{1,0:T(8,128)(2,1)S(1)} %collective-permute-done.1), channel_id=1, source_target_pairs={{0,2},{1,5},{2,6},{3,1},{4,0},{5,9},{6,10},{7,3},{8,4},{9,13},{10,... | collective-permute-start | bytes 688136 | tf_op jit(solution)/shard_map/ppermute | solution.py:163
  11.6 19.7 %collective-permute-start.2 = (bf16[24,14336]{1,0:T(8,128)(2,1)S(1)}, bf16[24,14336]{1,0:T(8,128)(2,1)S(1)}, u32[]{:S(2)}, u32[]{:S(2)}) collective-permute-start(bf16[24,14336]{1,0:T(8,128)(2,1)S(1)} %get-tuple-element.8.refs_0_), channel_id=1, source_target_pairs={{0,1},{1,0},{2,3},{3,2},{4,5},{5,4},{6,7},{7,6},{8,9},{9,8},{10,11... | collective-permute-start | bytes 2064392 | tf_op jit(solution)/shard_map/ppermute | solution.py:163
  17.4 5.9 %collective-permute-start.6 = (bf16[8,10752]{1,0:T(8,128)(2,1)S(1)}, bf16[8,10752]{1,0:T(8,128)(2,1)S(1)}, u32[]{:S(2)}, u32[]{:S(2)}) collective-permute-start(bf16[8,10752]{1,0:T(8,128)(2,1)S(1)} %bitcast.10), channel_id=1, source_target_pairs={{0,4},{1,3},{2,0},{3,7},{4,8},{5,1},{6,2},{7,11},{8,12},{9,5},{10,... | collective-permute-start | bytes 516104 | tf_op jit(solution)/shard_map/ppermute | solution.py:163
  18.5 5.5 %collective-permute-start.7 = (bf16[8,10752]{1,0:T(8,128)(2,1)S(1)}, bf16[8,10752]{1,0:T(8,128)(2,1)S(1)}, u32[]{:S(2)}, u32[]{:S(2)}) collective-permute-start(bf16[8,10752]{1,0:T(8,128)(2,1)S(1)} %bitcast.11), channel_id=1, source_target_pairs={{0,2},{1,5},{2,6},{3,1},{4,0},{5,9},{6,10},{7,3},{8,4},{9,13},{10,... | collective-permute-start | bytes 516104 | tf_op jit(solution)/shard_map/ppermute | solution.py:163
  19.7 11.6 %collective-permute-start.5 = (bf16[16,14336]{1,0:T(8,128)(2,1)S(1)}, bf16[16,14336]{1,0:T(8,128)(2,1)S(1)}, u32[]{:S(2)}, u32[]{:S(2)}) collective-permute-start(bf16[16,14336]{1,0:T(8,128)(2,1)S(1)} %constant_dynamic-update-slice_fusion.3.refs_2_), channel_id=1, source_target_pairs={{0,1},{1,0},{2,3},{3,2},{4,5},{5,4},{6,7},{7,6},{8,9},{9,8},{10,11... | collective-permute-start | bytes 1376264 | tf_op jit(solution)/shard_map/ppermute | solution.py:163
  19.9 10.0 %collective-permute-start.9 = (bf16[8,10752]{1,0:T(8,128)(2,1)S(1)}, bf16[8,10752]{1,0:T(8,128)(2,1)S(1)}, u32[]{:S(2)}, u32[]{:S(2)}) collective-permute-start(bf16[8,10752]{1,0:T(8,128)(2,1)S(1)} %bitcast.12), channel_id=1, source_target_pairs={{0,12},{1,13},{2,14},{3,15},{4,6},{5,7},{6,4},{7,5},{8,10},{9,11},... | collective-permute-start | bytes 516104 | tf_op jit(solution)/shard_map/ppermute | solution.py:163
  23.9 7.4 %collective-permute-start.8 = (bf16[16,10752]{1,0:T(8,128)(2,1)S(1)}, bf16[16,10752]{1,0:T(8,128)(2,1)S(1)}, u32[]{:S(2)}, u32[]{:S(2)}) collective-permute-start(bf16[16,10752]{1,0:T(8,128)(2,1)S(1)} %constant_dynamic-update-slice_fusion.5.refs_4_), channel_id=1, source_target_pairs={{0,1},{1,0},{2,3},{3,2},{4,5},{5,4},{6,7},{7,6},{8,9},{9,8},{10,11... | collective-permute-start | bytes 1032200 | tf_op jit(solution)/shard_map/ppermute | solution.py:163
  29.9 1.4 %collective-permute-start.10 = (bf16[8,10752]{1,0:T(8,128)(2,1)S(1)}, bf16[8,10752]{1,0:T(8,128)(2,1)S(1)}, u32[]{:S(2)}, u32[]{:S(2)}) collective-permute-start(bf16[8,10752]{1,0:T(8,128)(2,1)S(1)} %collective-permute-done.9.refs_6_), channel_id=1, source_target_pairs={{0,1},{1,0},{2,3},{3,2},{4,5},{5,4},{6,7},{7,6},{8,9},{9,8},{10,11... | collective-permute-start | bytes 516104 | tf_op jit(solution)/shard_map/ppermute | solution.py:163

commit v17 on v14

--- a/solution.py
+++ b/solution.py
@@ -202,9 +202,10 @@
     middle = jnp.concatenate((ahead[2], back[2]), axis=0)
     last = jnp.concatenate((ahead[3], half), axis=0)
     near_beside = send(near, sibling)
-    middle_beside = send(middle, sibling)
+    middle_beside = send(jnp.concatenate((window(ahead[2], chip), window(back[2], chip)), axis=0), sibling)
     last_beside = send(after(last, middle_beside), sibling)
     return [near, near_beside, middle, middle_beside, last, last_beside, back[3], send(back[3], sibling)]
+
 
 def slab_origin(devices, device, number):
     chips = devices // 2
@@ -218,10 +219,10 @@
     return 2 * chip + core
 
 
-def ring_kernel(devices, slots, device_ref, table_ref, *refs):
+def ring_kernel(devices, slots, table_ref, *refs):
     groups = refs[:len(GROUPS)]
     out_ref, pair, tiles, zeros, out_sems, zero_sems = refs[len(GROUPS):]
-    device = device_ref[0]
+    device = table_ref[table_ref.shape[0] - 1]
     slab, width = pair.shape[1] // devices, pair.shape[2]
     first = first_needed(devices, device // 2)
 
@@ -311,11 +312,11 @@
     slab, units = tokens.shape
     width = units // devices
     groups = ring_gather(tokens, device, devices)
-    table = jnp.concatenate([slab_lengths, tile_owner])
+    table = jnp.concatenate([slab_lengths, tile_owner, device.reshape(1)])
     return pl.pallas_call(
         functools.partial(ring_kernel, devices, slots),
         out_shape=jax.ShapeDtypeStruct((slots, width, width), jnp.float32),
-        in_specs=[pl.BlockSpec(memory_space=pltpu.SMEM)] * 2
+        in_specs=[pl.BlockSpec(memory_space=pltpu.SMEM)]
         + [pl.BlockSpec(memory_space=pltpu.VMEM)] * len(groups),
         out_specs=pl.BlockSpec(memory_space=pl.ANY),
         scratch_shapes=[
@@ -331,7 +332,7 @@
             bytes_accessed=4 * slots * width * width,
             transcendentals=0,
         ),
-    )(device.reshape(1), table, *groups)
+    )(table, *groups)
 
 
 def per_device(tokens, slab_lengths, tile_owner):

time: 40.5 us -> 41 us (1.012)
  the two profiles are of different devices: /device:TPU:0 before, /device:TPU:19 now
where the time goes in v17:
time: 41 us; the launch traced here: 40.8 us
  starting transfers between devices  16.2 us (40%)
  Pallas kernels  12.7 us (31%)
  waiting for transfers between devices  9.38 us (23%)
  other arithmetic  1.31 us (3%)
  local copies, waits for them, and re-layouts  1.03 us (3%)
    ppermute x11, starting transfers between devices, send(): return lax.ppermute(value, 'col', list(enumerate(target)))  16.2 us
    pallas_call x1, Pallas kernels, ring_form(): pl.pallas_call(functools.partial(ring_kernel, devices, slots), out_shape=...  12.7 us
    ppermute x11, waiting for transfers between devices, send(): return lax.ppermute(value, 'col', list(enumerate(target)))  9.38 us
    unnamed x3, local copies, waits for them, and re-layouts  1.01 us
  transfers between devices with their start and end apart: 11, of which 4 were waited for; matrix products, arithmetic and copies ran while one was open for 6% of the time, Pallas kernels for 0%

profile of v17, /device:TPU:19, one launch (start us, length us, event | category | flops | bytes accessed | tf_op | source)
XLA Modules:
  0.0 40.8 jit_solution(9410683622628022355)
XLA Ops:
  0.0 1.3 %collective-permute-start = (bf16[8,14336]{1,0:T(8,128)(2,1)}, bf16[8,14336]{1,0:T(8,128)(2,1)S(1)}, u32[]{:S(2)}, u32[]{:S(2)}) collective-permute-start(bf16[8,14336]{1,0:T(8,128)(2,1)} %param.3), channel_id=1, source_target_pairs={{0,4},{1,3},{2,0},{3,7},{4,8},{5,1},{6,2},{7,11},{8,12},{9,5},{10,... | collective-permute-start | bytes 688136 | tf_op jit(solution)/shard_map/ppermute | solution.py:163
  1.3 0.2 collective-permute-start.1
  1.5 1.0 %constant_dynamic-update-slice_fusion.2 = bf16[24,14336]{1,0:T(8,128)(2,1)S(1)} fusion(bf16[8,14336]{1,0:T(8,128)(2,1)} %param.3), kind=kLoop, calls=%fused_computation.20 | loop fusion | bytes 458752
  2.6 0.8 %pad_add_fusion.table_ref = s32[153]{0:T(256)S(1)} fusion(s32[1]{0:T(128)} %bitcast, s32[136]{0:T(256)} %param.5, s32[16]{0:T(128)} %param.4), kind=kLoop, calls=%fused_computation.23 | loop fusion | flops 306 | bytes 1224 | tf_op jit(solution)/shard_map/concatenate | solution.py:315
  3.4 2.8 %collective-permute-done = bf16[8,14336]{1,0:T(8,128)(2,1)S(1)} collective-permute-done((bf16[8,14336]{1,0:T(8,128)(2,1)}, bf16[8,14336]{1,0:T(8,128)(2,1)S(1)}, u32[]{:S(2)}, u32[]{:S(2)}) %collective-permute-start) | collective-permute-done | bytes 229408 | tf_op jit(solution)/shard_map/ppermute | solution.py:163
  6.2 1.3 %collective-permute-start.3 = (bf16[8,14336]{1,0:T(8,128)(2,1)S(1)}, bf16[8,14336]{1,0:T(8,128)(2,1)S(1)}, u32[]{:S(2)}, u32[]{:S(2)}) collective-permute-start(bf16[8,14336]{1,0:T(8,128)(2,1)S(1)} %collective-permute-done), channel_id=1, source_target_pairs={{0,4},{1,3},{2,0},{3,7},{4,8},{5,1},{6,2},{7,11},{8,12},{9,5},{10,... | collective-permute-start | bytes 688136 | tf_op jit(solution)/shard_map/ppermute | solution.py:163
  7.5 1.3 %collective-permute-done.1 = bf16[8,14336]{1,0:T(8,128)(2,1)S(1)} collective-permute-done((bf16[8,14336]{1,0:T(8,128)(2,1)}, bf16[8,14336]{1,0:T(8,128)(2,1)S(1)}, u32[]{:S(2)}, u32[]{:S(2)}) %collective-permute-start.1) | collective-permute-done | bytes 229408 | tf_op jit(solution)/shard_map/ppermute | solution.py:163
  8.8 0.2 collective-permute-start.4
  9.0 0.1 broadcast_select_fusion
  9.1 0.1 fusion
  9.2 0.1 collective-permute-start.7
  9.3 2.3 %collective-permute-start.2 = (bf16[24,14336]{1,0:T(8,128)(2,1)S(1)}, bf16[24,14336]{1,0:T(8,128)(2,1)S(1)}, u32[]{:S(2)}, u32[]{:S(2)}) collective-permute-start(bf16[24,14336]{1,0:T(8,128)(2,1)S(1)} %get-tuple-element.10.refs_0_), channel_id=1, source_target_pairs={{0,1},{1,0},{2,3},{3,2},{4,5},{5,4},{6,7},{7,6},{8,9},{9,8},{10,11... | collective-permute-start | bytes 2064392 | tf_op jit(solution)/shard_map/ppermute | solution.py:163
  11.6 0.0 collective-permute-done.3
  11.6 4.0 %collective-permute-done.4 = bf16[8,14336]{1,0:T(8,128)(2,1)S(1)} collective-permute-done((bf16[8,14336]{1,0:T(8,128)(2,1)S(1)}, bf16[8,14336]{1,0:T(8,128)(2,1)S(1)}, u32[]{:S(2)}, u32[]{:S(2)}) %collective-permute-start.4) | collective-permute-done | bytes 229408 | tf_op jit(solution)/shard_map/ppermute | solution.py:163
  15.6 0.3 fusion.1
  15.9 0.2 collective-permute-start.9
  16.2 1.3 %collective-permute-start.6 = (bf16[8,10752]{1,0:T(8,128)(2,1)S(1)}, bf16[8,10752]{1,0:T(8,128)(2,1)S(1)}, u32[]{:S(2)}, u32[]{:S(2)}) collective-permute-start(bf16[8,10752]{1,0:T(8,128)(2,1)S(1)} %bitcast.14), channel_id=1, source_target_pairs={{0,4},{1,3},{2,0},{3,7},{4,8},{5,1},{6,2},{7,11},{8,12},{9,5},{10,... | collective-permute-start | bytes 516104 | tf_op jit(solution)/shard_map/ppermute | solution.py:163
  17.5 4.4 %collective-permute-start.5 = (bf16[16,10752]{1,0:T(8,128)(2,1)S(1)}, bf16[16,10752]{1,0:T(8,128)(2,1)S(1)}, u32[]{:S(2)}, u32[]{:S(2)}) collective-permute-start(bf16[16,10752]{1,0:T(8,128)(2,1)S(1)} %pad_maximum_fusion.1), channel_id=1, source_target_pairs={{0,1},{1,0},{2,3},{3,2},{4,5},{5,4},{6,7},{7,6},{8,9},{9,8},{10,11... | collective-permute-start | bytes 1032200 | tf_op jit(solution)/shard_map/ppermute | solution.py:163
  21.8 0.0 collective-permute-done.9.refs_6_
  21.8 3.3 %collective-permute-start.10 = (bf16[8,10752]{1,0:T(8,128)(2,1)S(1)}, bf16[8,10752]{1,0:T(8,128)(2,1)S(1)}, u32[]{:S(2)}, u32[]{:S(2)}) collective-permute-start(bf16[8,10752]{1,0:T(8,128)(2,1)S(1)} %collective-permute-done.9.refs_6_), channel_id=1, source_target_pairs={{0,1},{1,0},{2,3},{3,2},{4,5},{5,4},{6,7},{7,6},{8,9},{9,8},{10,11... | collective-permute-start | bytes 516104 | tf_op jit(solution)/shard_map/ppermute | solution.py:163
  25.1 0.0 collective-permute-done.6
  25.1 0.0 collective-permute-done.7
  25.2 0.0 collective-permute-done.5.refs_3_
  25.2 1.7 %collective-permute-start.8 = (bf16[16,10752]{1,0:T(8,128)(2,1)S(1)}, bf16[16,10752]{1,0:T(8,128)(2,1)S(1)}, u32[]{:S(2)}, u32[]{:S(2)}) collective-permute-start(bf16[16,10752]{1,0:T(8,128)(2,1)S(1)} %constant_dynamic-update-slice_fusion.3.refs_4_), channel_id=1, source_target_pairs={{0,1},{1,0},{2,3},{3,2},{4,5},{5,4},{6,7},{7,6},{8,9},{9,8},{10,11... | collective-permute-start | bytes 1032200 | tf_op jit(solution)/shard_map/ppermute | solution.py:163
  26.9 0.0 collective-permute-done.10.refs_7_
  26.9 0.0 collective-permute-done.2.refs_1_
  26.9 1.2 %collective-permute-done.8.refs_5_ = bf16[16,10752]{1,0:T(8,128)(2,1)S(1)} collective-permute-done((bf16[16,10752]{1,0:T(8,128)(2,1)S(1)}, bf16[16,10752]{1,0:T(8,128)(2,1)S(1)}, u32[]{:S(2)}, u32[]{:S(2)}) %collective-permute-start.8) | collective-permute-done | bytes 344096 | tf_op jit(solution)/shard_map/ppermute | solution.py:163
  28.1 12.7 %shard_map.37 = f32[11,896,896]{2,1,0:T(8,128)} custom-call(s32[153]{0:T(256)S(1)} %pad_add_fusion.table_ref, bf16[24,14336]{1,0:T(8,128)(2,1)S(1)} %get-tuple-element.10.refs_0_, bf16[24,14336]{1,0:T(8,128)(2,1)S(1)} %collective-permute-done.2.refs_1_, bf16[16,14336]{1,0:T(8,128)(2,1)S(1)} %pad_maximum_fusion.refs_2_, ...), custom_call_target="tpu_custom_call" | custom-call | flops 2260729856 | bytes 35323904 | tf_op jit(solution)/shard_map/pallas_call | solution.py:316
  (5 shorter events, 0.1 us)
Async XLA Ops:
  0.0 6.2 %collective-permute-start = (bf16[8,14336]{1,0:T(8,128)(2,1)}, bf16[8,14336]{1,0:T(8,128)(2,1)S(1)}, u32[]{:S(2)}, u32[]{:S(2)}) collective-permute-start(bf16[8,14336]{1,0:T(8,128)(2,1)} %param.3), channel_id=1, source_target_pairs={{0,4},{1,3},{2,0},{3,7},{4,8},{5,1},{6,2},{7,11},{8,12},{9,5},{10,... | collective-permute-start | bytes 688136 | tf_op jit(solution)/shard_map/ppermute | solution.py:163
  1.3 7.5 %collective-permute-start.1 = (bf16[8,14336]{1,0:T(8,128)(2,1)}, bf16[8,14336]{1,0:T(8,128)(2,1)S(1)}, u32[]{:S(2)}, u32[]{:S(2)}) collective-permute-start(bf16[8,14336]{1,0:T(8,128)(2,1)} %param.3), channel_id=1, source_target_pairs={{0,2},{1,5},{2,6},{3,1},{4,0},{5,9},{6,10},{7,3},{8,4},{9,13},{10,... | collective-permute-start | bytes 688136 | tf_op jit(solution)/shard_map/ppermute | solution.py:163
  6.2 5.4 %collective-permute-start.3 = (bf16[8,14336]{1,0:T(8,128)(2,1)S(1)}, bf16[8,14336]{1,0:T(8,128)(2,1)S(1)}, u32[]{:S(2)}, u32[]{:S(2)}) collective-permute-start(bf16[8,14336]{1,0:T(8,128)(2,1)S(1)} %collective-permute-done), channel_id=1, source_target_pairs={{0,4},{1,3},{2,0},{3,7},{4,8},{5,1},{6,2},{7,11},{8,12},{9,5},{10,... | collective-permute-start | bytes 688136 | tf_op jit(solution)/shard_map/ppermute | solution.py:163
  8.8 6.8 %collective-permute-start.4 = (bf16[8,14336]{1,0:T(8,128)(2,1)S(1)}, bf16[8,14336]{1,0:T(8,128)(2,1)S(1)}, u32[]{:S(2)}, u32[]{:S(2)}) collective-permute-start(bf16[8,14336]{1,0:T(8,128)(2,1)S(1)} %collective-permute-done.1), channel_id=1, source_target_pairs={{0,2},{1,5},{2,6},{3,1},{4,0},{5,9},{6,10},{7,3},{8,4},{9,13},{10,... | collective-permute-start | bytes 688136 | tf_op jit(solution)/shard_map/ppermute | solution.py:163
  9.2 16.0 %collective-permute-start.7 = (bf16[8,10752]{1,0:T(8,128)(2,1)S(1)}, bf16[8,10752]{1,0:T(8,128)(2,1)S(1)}, u32[]{:S(2)}, u32[]{:S(2)}) collective-permute-start(bf16[8,10752]{1,0:T(8,128)(2,1)S(1)} %bitcast.16), channel_id=1, source_target_pairs={{0,12},{1,13},{2,14},{3,15},{4,6},{5,7},{6,4},{7,5},{8,10},{9,11},... | collective-permute-start | bytes 516104 | tf_op jit(solution)/shard_map/ppermute | solution.py:163
  9.3 17.7 %collective-permute-start.2 = (bf16[24,14336]{1,0:T(8,128)(2,1)S(1)}, bf16[24,14336]{1,0:T(8,128)(2,1)S(1)}, u32[]{:S(2)}, u32[]{:S(2)}) collective-permute-start(bf16[24,14336]{1,0:T(8,128)(2,1)S(1)} %get-tuple-element.10.refs_0_), channel_id=1, source_target_pairs={{0,1},{1,0},{2,3},{3,2},{4,5},{5,4},{6,7},{7,6},{8,9},{9,8},{10,11... | collective-permute-start | bytes 2064392 | tf_op jit(solution)/shard_map/ppermute | solution.py:163
  15.9 5.9 %collective-permute-start.9 = (bf16[8,10752]{1,0:T(8,128)(2,1)S(1)}, bf16[8,10752]{1,0:T(8,128)(2,1)S(1)}, u32[]{:S(2)}, u32[]{:S(2)}) collective-permute-start(bf16[8,10752]{1,0:T(8,128)(2,1)S(1)} %bitcast.15), channel_id=1, source_target_pairs={{0,2},{1,5},{2,6},{3,1},{4,0},{5,9},{6,10},{7,3},{8,4},{9,13},{10,... | collective-permute-start | bytes 516104 | tf_op jit(solution)/shard_map/ppermute | solution.py:163
  16.2 9.0 %collective-permute-start.6 = (bf16[8,10752]{1,0:T(8,128)(2,1)S(1)}, bf16[8,10752]{1,0:T(8,128)(2,1)S(1)}, u32[]{:S(2)}, u32[]{:S(2)}) collective-permute-start(bf16[8,10752]{1,0:T(8,128)(2,1)S(1)} %bitcast.14), channel_id=1, source_target_pairs={{0,4},{1,3},{2,0},{3,7},{4,8},{5,1},{6,2},{7,11},{8,12},{9,5},{10,... | collective-permute-start | bytes 516104 | tf_op jit(solution)/shard_map/ppermute | solution.py:163
  17.5 7.7 %collective-permute-start.5 = (bf16[16,10752]{1,0:T(8,128)(2,1)S(1)}, bf16[16,10752]{1,0:T(8,128)(2,1)S(1)}, u32[]{:S(2)}, u32[]{:S(2)}) collective-permute-start(bf16[16,10752]{1,0:T(8,128)(2,1)S(1)} %pad_maximum_fusion.1), channel_id=1, source_target_pairs={{0,1},{1,0},{2,3},{3,2},{4,5},{5,4},{6,7},{7,6},{8,9},{9,8},{10,11... | collective-permute-start | bytes 1032200 | tf_op jit(solution)/shard_map/ppermute | solution.py:163
  21.8 5.1 %collective-permute-start.10 = (bf16[8,10752]{1,0:T(8,128)(2,1)S(1)}, bf16[8,10752]{1,0:T(8,128)(2,1)S(1)}, u32[]{:S(2)}, u32[]{:S(2)}) collective-permute-start(bf16[8,10752]{1,0:T(8,128)(2,1)S(1)} %collective-permute-done.9.refs_6_), channel_id=1, source_target_pairs={{0,1},{1,0},{2,3},{3,2},{4,5},{5,4},{6,7},{7,6},{8,9},{9,8},{10,11... | collective-permute-start | bytes 516104 | tf_op jit(solution)/shard_map/ppermute | solution.py:163
  25.2 3.0 %collective-permute-start.8 = (bf16[16,10752]{1,0:T(8,128)(2,1)S(1)}, bf16[16,10752]{1,0:T(8,128)(2,1)S(1)}, u32[]{:S(2)}, u32[]{:S(2)}) collective-permute-start(bf16[16,10752]{1,0:T(8,128)(2,1)S(1)} %constant_dynamic-update-slice_fusion.3.refs_4_), channel_id=1, source_target_pairs={{0,1},{1,0},{2,3},{3,2},{4,5},{5,4},{6,7},{7,6},{8,9},{9,8},{10,11... | collective-permute-start | bytes 1032200 | tf_op jit(solution)/shard_map/ppermute | solution.py:163

commit v18 on v17

--- a/solution.py
+++ b/solution.py
@@ -196,13 +196,28 @@
         ahead.append(send(ahead[-1], onward))
         back.append(send(back[-1], backward))
     half = send(window(jnp.where(came_ahead, ahead[1], back[1]), over_chip), over)
-    ahead.append(send(window(ahead[2], onward_chip), onward))
-    back.append(send(window(back[2], backward_chip), backward))
+    middle_chips = range(2, chips - 2)
+    across = [(at, at ^ 2) for at in range(devices) if at // 2 in middle_chips]
+    neighbor = lax.ppermute(window(tokens, over_chip), "col", across)
+
+    def last_hop(value, target, chip):
+        far = [target[target[target[at]]] for at in range(devices)]
+        pairs = [
+            (at, to) for at, to in enumerate(target)
+            if not (to // 2 in middle_chips and far[to ^ 2] == to)
+        ]
+        return lax.ppermute(window(value, chip), "col", pairs)
+
+    is_middle = (chip >= 2) & (chip < chips - 2)
+    by_ahead = is_middle & (((chip == 2) | (chip == 5)) == (core == 0))
+    by_back = is_middle & (((chip == 3) | (chip == 4)) == (core == 0))
+    ahead.append(jnp.where(by_ahead, neighbor, last_hop(ahead[2], onward, onward_chip)))
+    back.append(jnp.where(by_back, neighbor, last_hop(back[2], backward, backward_chip)))
     near = jnp.concatenate((tokens, ahead[1], back[1]), axis=0)
     middle = jnp.concatenate((ahead[2], back[2]), axis=0)
     last = jnp.concatenate((ahead[3], half), axis=0)
     near_beside = send(near, sibling)
-    middle_beside = send(jnp.concatenate((window(ahead[2], chip), window(back[2], chip)), axis=0), sibling)
+    middle_beside = send(middle, sibling)
     last_beside = send(after(last, middle_beside), sibling)
     return [near, near_beside, middle, middle_beside, last, last_beside, back[3], send(back[3], sibling)]
 

time: 41 us -> 44.2 us (1.078)
  the two profiles are of different devices: /device:TPU:19 before, /device:TPU:11 now
where the time goes in v18:
time: 44.2 us; the launch traced here: 44 us
  starting transfers between devices  24.7 us (56%)
  Pallas kernels  12.5 us (28%)
  waiting for transfers between devices  3.29 us (7%)
  other arithmetic  2.22 us (5%)
  local copies, waits for them, and re-layouts  1.01 us (2%)
    ppermute x9, starting transfers between devices, send(): return lax.ppermute(value, 'col', list(enumerate(target)))  16.9 us
    pallas_call x1, Pallas kernels, ring_form(): pl.pallas_call(functools.partial(ring_kernel, devices, slots), out_shape=...  12.5 us
    ppermute x2, starting transfers between devices, last_hop(): return lax.ppermute(window(value, chip), 'col', pairs)  5.64 us
    ppermute x9, waiting for transfers between devices, send(): return lax.ppermute(value, 'col', list(enumerate(target)))  3.28 us
    ppermute x1, starting transfers between devices, ring_gather(): neighbor = lax.ppermute(window(tokens, over_chip), 'col', across)  2.14 us
    concatenate x4, other arithmetic, window(): blocks = jnp.concatenate([blocks, blocks], axis=1)  1.35 us
    unnamed x3, local copies, waits for them, and re-layouts  0.99 us
  transfers between devices with their start and end apart: 12, of which 3 were waited for; matrix products, arithmetic and copies ran while one was open for 7% of the time, Pallas kernels for 0%

profile of v18, /device:TPU:11, one launch (start us, length us, event | category | flops | bytes accessed | tf_op | source)
XLA Modules:
  0.0 44.0 jit_solution(16422892055302229027)
XLA Ops:
  0.0 0.2 collective-permute-start.1
  0.2 1.3 %collective-permute-start = (bf16[8,14336]{1,0:T(8,128)(2,1)}, bf16[8,14336]{1,0:T(8,128)(2,1)S(1)}, u32[]{:S(2)}, u32[]{:S(2)}) collective-permute-start(bf16[8,14336]{1,0:T(8,128)(2,1)} %param.3), channel_id=1, source_target_pairs={{0,4},{1,3},{2,0},{3,7},{4,8},{5,1},{6,2},{7,11},{8,12},{9,5},{10,... | collective-permute-start | bytes 688136 | tf_op jit(solution)/shard_map/ppermute | solution.py:163
  1.5 1.0 %fusion.3 = bf16[8,12,896]{2,0,1:T(8,128)(2,1)S(1)} fusion(s32[]{:T(128)S(6)} %select_n.100, bf16[8,16,896]{2,0,1:T(8,128)(2,1)} %bitcast.9), kind=kLoop, calls=%fused_computation.13 | loop fusion | flops 86016 | bytes 401412 | tf_op jit(solution)/shard_map/concatenate | solution.py:190
  2.5 2.1 %collective-permute-start.6 = (bf16[8,10752]{1,0:T(8,128)(2,1)S(1)}, bf16[8,10752]{1,0:T(8,128)(2,1)S(1)}, u32[]{:S(2)}, u32[]{:S(2)}) collective-permute-start(bf16[8,10752]{1,0:T(8,128)(2,1)S(1)} %bitcast.13), channel_id=1, source_target_pairs={{4,6},{5,7},{6,4},{7,5},{8,10},{9,11},{10,8},{11,9},{20,22},{21,23... | collective-permute-start | bytes 516104 | tf_op jit(solution)/shard_map/ppermute | solution.py:201
  4.7 1.0 %constant_dynamic-update-slice_fusion.2 = bf16[24,14336]{1,0:T(8,128)(2,1)S(1)} fusion(bf16[8,14336]{1,0:T(8,128)(2,1)} %param.3), kind=kLoop, calls=%fused_computation.18 | loop fusion | bytes 458752
  5.8 0.0 collective-permute-done.1
  5.8 0.1 collective-permute-start.4
  5.8 1.2 %collective-permute-done = bf16[8,14336]{1,0:T(8,128)(2,1)S(1)} collective-permute-done((bf16[8,14336]{1,0:T(8,128)(2,1)}, bf16[8,14336]{1,0:T(8,128)(2,1)S(1)}, u32[]{:S(2)}, u32[]{:S(2)}) %collective-permute-start) | collective-permute-done | bytes 229408 | tf_op jit(solution)/shard_map/ppermute | solution.py:163
  7.0 1.3 %collective-permute-start.3 = (bf16[8,14336]{1,0:T(8,128)(2,1)S(1)}, bf16[8,14336]{1,0:T(8,128)(2,1)S(1)}, u32[]{:S(2)}, u32[]{:S(2)}) collective-permute-start(bf16[8,14336]{1,0:T(8,128)(2,1)S(1)} %collective-permute-done), channel_id=1, source_target_pairs={{0,4},{1,3},{2,0},{3,7},{4,8},{5,1},{6,2},{7,11},{8,12},{9,5},{10,... | collective-permute-start | bytes 688136 | tf_op jit(solution)/shard_map/ppermute | solution.py:163
  8.4 0.1 broadcast_select_fusion
  8.4 0.1 fusion.1
  8.5 1.0 %collective-permute-start.8 = (bf16[8,10752]{1,0:T(8,128)(2,1)S(1)}, bf16[8,10752]{1,0:T(8,128)(2,1)S(1)}, u32[]{:S(2)}, u32[]{:S(2)}) collective-permute-start(bf16[8,10752]{1,0:T(8,128)(2,1)S(1)} %bitcast.14), channel_id=1, source_target_pairs={{0,12},{1,13},{2,14},{3,15},{4,6},{5,7},{6,4},{7,5},{8,10},{9,11},... | collective-permute-start | bytes 516104 | tf_op jit(solution)/shard_map/ppermute | solution.py:163
  9.5 2.5 %collective-permute-start.2 = (bf16[24,14336]{1,0:T(8,128)(2,1)S(1)}, bf16[24,14336]{1,0:T(8,128)(2,1)S(1)}, u32[]{:S(2)}, u32[]{:S(2)}) collective-permute-start(bf16[24,14336]{1,0:T(8,128)(2,1)S(1)} %get-tuple-element.8.refs_0_), channel_id=1, source_target_pairs={{0,1},{1,0},{2,3},{3,2},{4,5},{5,4},{6,7},{7,6},{8,9},{9,8},{10,11... | collective-permute-start | bytes 2064392 | tf_op jit(solution)/shard_map/ppermute | solution.py:163
  12.0 0.0 collective-permute-done.4
  12.0 0.1 fusion
  12.1 4.3 %collective-permute-start.10 = (bf16[8,10752]{1,0:T(8,128)(2,1)S(1)}, bf16[8,10752]{1,0:T(8,128)(2,1)S(1)}, u32[]{:S(2)}, u32[]{:S(2)}) collective-permute-start(bf16[8,10752]{1,0:T(8,128)(2,1)S(1)} %bitcast.15), channel_id=1, source_target_pairs={{0,2},{3,1},{4,0},{5,9},{6,10},{7,3},{8,4},{9,13},{10,14},{11,7},{... | collective-permute-start | bytes 516104 | tf_op jit(solution)/shard_map/ppermute | solution.py:209
  16.5 0.0 collective-permute-done.3
  16.5 0.1 fusion.2
  16.6 1.3 %collective-permute-start.7 = (bf16[8,10752]{1,0:T(8,128)(2,1)S(1)}, bf16[8,10752]{1,0:T(8,128)(2,1)S(1)}, u32[]{:S(2)}, u32[]{:S(2)}) collective-permute-start(bf16[8,10752]{1,0:T(8,128)(2,1)S(1)} %bitcast.16), channel_id=1, source_target_pairs={{1,3},{2,0},{4,8},{5,1},{6,2},{7,11},{8,12},{9,5},{10,6},{11,15},{... | collective-permute-start | bytes 516104 | tf_op jit(solution)/shard_map/ppermute | solution.py:209
  18.0 0.0 collective-permute-done.6
  18.0 6.5 %collective-permute-start.5 = (bf16[16,14336]{1,0:T(8,128)(2,1)S(1)}, bf16[16,14336]{1,0:T(8,128)(2,1)S(1)}, u32[]{:S(2)}, u32[]{:S(2)}) collective-permute-start(bf16[16,14336]{1,0:T(8,128)(2,1)S(1)} %constant_dynamic-update-slice_fusion.3.refs_2_), channel_id=1, source_target_pairs={{0,1},{1,0},{2,3},{3,2},{4,5},{5,4},{6,7},{7,6},{8,9},{9,8},{10,11... | collective-permute-start | bytes 1376264 | tf_op jit(solution)/shard_map/ppermute | solution.py:163
  24.5 0.0 collective-permute-done.10
  24.5 0.0 collective-permute-done.7
  24.6 0.0 collective-permute-done.8
  24.6 1.4 %collective-permute-done.5.refs_3_ = bf16[16,14336]{1,0:T(8,128)(2,1)S(1)} collective-permute-done((bf16[16,14336]{1,0:T(8,128)(2,1)S(1)}, bf16[16,14336]{1,0:T(8,128)(2,1)S(1)}, u32[]{:S(2)}, u32[]{:S(2)}) %collective-permute-start.5) | collective-permute-done | bytes 458784 | tf_op jit(solution)/shard_map/ppermute | solution.py:163
  26.0 4.0 %collective-permute-start.9 = (bf16[16,10752]{1,0:T(8,128)(2,1)S(1)}, bf16[16,10752]{1,0:T(8,128)(2,1)S(1)}, u32[]{:S(2)}, u32[]{:S(2)}) collective-permute-start(bf16[16,10752]{1,0:T(8,128)(2,1)S(1)} %pad_maximum_fusion.refs_4_), channel_id=1, source_target_pairs={{0,1},{1,0},{2,3},{3,2},{4,5},{5,4},{6,7},{7,6},{8,9},{9,8},{10,11... | collective-permute-start | bytes 1032200 | tf_op jit(solution)/shard_map/ppermute | solution.py:163
  29.9 0.1 collective-permute-start.11
  30.0 0.8 %pad_add_fusion.table_ref = s32[153]{0:T(256)S(1)} fusion(s32[1]{0:T(128)} %bitcast, s32[136]{0:T(256)} %param.5, s32[16]{0:T(128)} %param.4), kind=kLoop, calls=%fused_computation.21 | loop fusion | flops 306 | bytes 1224 | tf_op jit(solution)/shard_map/concatenate | solution.py:330
  30.8 0.7 %collective-permute-done.11.refs_7_ = bf16[8,10752]{1,0:T(8,128)(2,1)S(1)} collective-permute-done((bf16[8,10752]{1,0:T(8,128)(2,1)S(1)}, bf16[8,10752]{1,0:T(8,128)(2,1)S(1)}, u32[]{:S(2)}, u32[]{:S(2)}) %collective-permute-start.11) | collective-permute-done | bytes 172064 | tf_op jit(solution)/shard_map/ppermute | solution.py:163
  31.5 0.0 collective-permute-done.2.refs_1_
  31.5 0.0 collective-permute-done.9.refs_5_
  31.5 12.5 %shard_map.37 = f32[11,896,896]{2,1,0:T(8,128)} custom-call(s32[153]{0:T(256)S(1)} %pad_add_fusion.table_ref, bf16[24,14336]{1,0:T(8,128)(2,1)S(1)} %get-tuple-element.8.refs_0_, bf16[24,14336]{1,0:T(8,128)(2,1)S(1)} %collective-permute-done.2.refs_1_, bf16[16,14336]{1,0:T(8,128)(2,1)S(1)} %constant_dynamic-update-slice_fusion.3.refs_2_, ...), custom_call_target="tpu_custom_call" | custom-call | flops 2260729856 | bytes 35323904 | tf_op jit(solution)/shard_map/pallas_call | solution.py:331
  (5 shorter events, 0.1 us)
Async XLA Ops:
  0.0 5.8 %collective-permute-start.1 = (bf16[8,14336]{1,0:T(8,128)(2,1)}, bf16[8,14336]{1,0:T(8,128)(2,1)S(1)}, u32[]{:S(2)}, u32[]{:S(2)}) collective-permute-start(bf16[8,14336]{1,0:T(8,128)(2,1)} %param.3), channel_id=1, source_target_pairs={{0,2},{1,5},{2,6},{3,1},{4,0},{5,9},{6,10},{7,3},{8,4},{9,13},{10,... | collective-permute-start | bytes 688136 | tf_op jit(solution)/shard_map/ppermute | solution.py:163
  0.2 6.9 %collective-permute-start = (bf16[8,14336]{1,0:T(8,128)(2,1)}, bf16[8,14336]{1,0:T(8,128)(2,1)S(1)}, u32[]{:S(2)}, u32[]{:S(2)}) collective-permute-start(bf16[8,14336]{1,0:T(8,128)(2,1)} %param.3), channel_id=1, source_target_pairs={{0,4},{1,3},{2,0},{3,7},{4,8},{5,1},{6,2},{7,11},{8,12},{9,5},{10,... | collective-permute-start | bytes 688136 | tf_op jit(solution)/shard_map/ppermute | solution.py:163
  2.5 15.5 %collective-permute-start.6 = (bf16[8,10752]{1,0:T(8,128)(2,1)S(1)}, bf16[8,10752]{1,0:T(8,128)(2,1)S(1)}, u32[]{:S(2)}, u32[]{:S(2)}) collective-permute-start(bf16[8,10752]{1,0:T(8,128)(2,1)S(1)} %bitcast.13), channel_id=1, source_target_pairs={{4,6},{5,7},{6,4},{7,5},{8,10},{9,11},{10,8},{11,9},{20,22},{21,23... | collective-permute-start | bytes 516104 | tf_op jit(solution)/shard_map/ppermute | solution.py:201
  5.8 6.3 %collective-permute-start.4 = (bf16[8,14336]{1,0:T(8,128)(2,1)S(1)}, bf16[8,14336]{1,0:T(8,128)(2,1)S(1)}, u32[]{:S(2)}, u32[]{:S(2)}) collective-permute-start(bf16[8,14336]{1,0:T(8,128)(2,1)S(1)} %collective-permute-done.1), channel_id=1, source_target_pairs={{0,2},{1,5},{2,6},{3,1},{4,0},{5,9},{6,10},{7,3},{8,4},{9,13},{10,... | collective-permute-start | bytes 688136 | tf_op jit(solution)/shard_map/ppermute | solution.py:163
  7.0 9.4 %collective-permute-start.3 = (bf16[8,14336]{1,0:T(8,128)(2,1)S(1)}, bf16[8,14336]{1,0:T(8,128)(2,1)S(1)}, u32[]{:S(2)}, u32[]{:S(2)}) collective-permute-start(bf16[8,14336]{1,0:T(8,128)(2,1)S(1)} %collective-permute-done), channel_id=1, source_target_pairs={{0,4},{1,3},{2,0},{3,7},{4,8},{5,1},{6,2},{7,11},{8,12},{9,5},{10,... | collective-permute-start | bytes 688136 | tf_op jit(solution)/shard_map/ppermute | solution.py:163
  8.5 16.0 %collective-permute-start.8 = (bf16[8,10752]{1,0:T(8,128)(2,1)S(1)}, bf16[8,10752]{1,0:T(8,128)(2,1)S(1)}, u32[]{:S(2)}, u32[]{:S(2)}) collective-permute-start(bf16[8,10752]{1,0:T(8,128)(2,1)S(1)} %bitcast.14), channel_id=1, source_target_pairs={{0,12},{1,13},{2,14},{3,15},{4,6},{5,7},{6,4},{7,5},{8,10},{9,11},... | collective-permute-start | bytes 516104 | tf_op jit(solution)/shard_map/ppermute | solution.py:163
  9.5 22.0 %collective-permute-start.2 = (bf16[24,14336]{1,0:T(8,128)(2,1)S(1)}, bf16[24,14336]{1,0:T(8,128)(2,1)S(1)}, u32[]{:S(2)}, u32[]{:S(2)}) collective-permute-start(bf16[24,14336]{1,0:T(8,128)(2,1)S(1)} %get-tuple-element.8.refs_0_), channel_id=1, source_target_pairs={{0,1},{1,0},{2,3},{3,2},{4,5},{5,4},{6,7},{7,6},{8,9},{9,8},{10,11... | collective-permute-start | bytes 2064392 | tf_op jit(solution)/shard_map/ppermute | solution.py:163
  12.1 12.4 %collective-permute-start.10 = (bf16[8,10752]{1,0:T(8,128)(2,1)S(1)}, bf16[8,10752]{1,0:T(8,128)(2,1)S(1)}, u32[]{:S(2)}, u32[]{:S(2)}) collective-permute-start(bf16[8,10752]{1,0:T(8,128)(2,1)S(1)} %bitcast.15), channel_id=1, source_target_pairs={{0,2},{3,1},{4,0},{5,9},{6,10},{7,3},{8,4},{9,13},{10,14},{11,7},{... | collective-permute-start | bytes 516104 | tf_op jit(solution)/shard_map/ppermute | solution.py:209
  16.6 7.9 %collective-permute-start.7 = (bf16[8,10752]{1,0:T(8,128)(2,1)S(1)}, bf16[8,10752]{1,0:T(8,128)(2,1)S(1)}, u32[]{:S(2)}, u32[]{:S(2)}) collective-permute-start(bf16[8,10752]{1,0:T(8,128)(2,1)S(1)} %bitcast.16), channel_id=1, source_target_pairs={{1,3},{2,0},{4,8},{5,1},{6,2},{7,11},{8,12},{9,5},{10,6},{11,15},{... | collective-permute-start | bytes 516104 | tf_op jit(solution)/shard_map/ppermute | solution.py:209
  18.0 8.0 %collective-permute-start.5 = (bf16[16,14336]{1,0:T(8,128)(2,1)S(1)}, bf16[16,14336]{1,0:T(8,128)(2,1)S(1)}, u32[]{:S(2)}, u32[]{:S(2)}) collective-permute-start(bf16[16,14336]{1,0:T(8,128)(2,1)S(1)} %constant_dynamic-update-slice_fusion.3.refs_2_), channel_id=1, source_target_pairs={{0,1},{1,0},{2,3},{3,2},{4,5},{5,4},{6,7},{7,6},{8,9},{9,8},{10,11... | collective-permute-start | bytes 1376264 | tf_op jit(solution)/shard_map/ppermute | solution.py:163
  26.0 5.5 %collective-permute-start.9 = (bf16[16,10752]{1,0:T(8,128)(2,1)S(1)}, bf16[16,10752]{1,0:T(8,128)(2,1)S(1)}, u32[]{:S(2)}, u32[]{:S(2)}) collective-permute-start(bf16[16,10752]{1,0:T(8,128)(2,1)S(1)} %pad_maximum_fusion.refs_4_), channel_id=1, source_target_pairs={{0,1},{1,0},{2,3},{3,2},{4,5},{5,4},{6,7},{7,6},{8,9},{9,8},{10,11... | collective-permute-start | bytes 1032200 | tf_op jit(solution)/shard_map/ppermute | solution.py:163
  29.9 1.5 %collective-permute-start.11 = (bf16[8,10752]{1,0:T(8,128)(2,1)S(1)}, bf16[8,10752]{1,0:T(8,128)(2,1)S(1)}, u32[]{:S(2)}, u32[]{:S(2)}) collective-permute-start(bf16[8,10752]{1,0:T(8,128)(2,1)S(1)} %get-tuple-element.9.refs_6_), channel_id=1, source_target_pairs={{0,1},{1,0},{2,3},{3,2},{4,5},{5,4},{6,7},{7,6},{8,9},{9,8},{10,11... | collective-permute-start | bytes 516104 | tf_op jit(solution)/shard_map/ppermute | solution.py:163

commit v19 on v17

--- a/solution.py
+++ b/solution.py
@@ -147,7 +147,7 @@
     return onward, backward
 
 
-GROUPS = ((0, 1, 2), (8, 9, 10), (3, 4), (11, 12), (5, 7), (13, 15), (6,), (14,))
+GROUPS = ((0, 1, 2), (8, 9, 10), (3, 4), (11, 12), (6,), (14,), (7,), (15,), (5,), (13,))
 
 
 def first_needed(devices, chip):
@@ -200,11 +200,12 @@
     back.append(send(window(back[2], backward_chip), backward))
     near = jnp.concatenate((tokens, ahead[1], back[1]), axis=0)
     middle = jnp.concatenate((ahead[2], back[2]), axis=0)
-    last = jnp.concatenate((ahead[3], half), axis=0)
     near_beside = send(near, sibling)
     middle_beside = send(jnp.concatenate((window(ahead[2], chip), window(back[2], chip)), axis=0), sibling)
-    last_beside = send(after(last, middle_beside), sibling)
-    return [near, near_beside, middle, middle_beside, last, last_beside, back[3], send(back[3], sibling)]
+    groups = [near, near_beside, middle, middle_beside]
+    for value in (back[3], half, ahead[3]):
+        groups += [value, send(after(value, back[3]) if value is half else value, sibling)]
+    return groups
 
 
 def slab_origin(devices, device, number):

time: 41 us -> 40.6 us (level)
    ppermute x11 -> x12, waiting for transfers between devices: 9.38 us -> 9.15 us  [send(): return lax.ppermute(value, 'col', list(enumerate(target)))]
    ppermute x11 -> x12, starting transfers between devices: 16.2 us -> 16.1 us  [send(): return lax.ppermute(value, 'col', list(enumerate(target)))]
    unnamed x3 -> x2, local copies, waits for them, and re-layouts: 1.01 us -> 1 us
  transfers between devices with their start and end apart: 11 -> 12, of which waited for: 4 -> 4; matrix products, arithmetic and copies ran while one was open for 6% -> 6% of each run, Pallas kernels for 0% -> 0%
where the time goes in v19:
time: 40.6 us; the launch traced here: 40.5 us
  starting transfers between devices  16.1 us (40%)
  Pallas kernels  12.7 us (31%)
  waiting for transfers between devices  9.15 us (23%)
  other arithmetic  1.31 us (3%)
  local copies, waits for them, and re-layouts  1 us (2%)
    ppermute x12, starting transfers between devices, send(): return lax.ppermute(value, 'col', list(enumerate(target)))  16.1 us
    pallas_call x1, Pallas kernels, ring_form(): pl.pallas_call(functools.partial(ring_kernel, devices, slots), out_shape=...  12.7 us
    ppermute x12, waiting for transfers between devices, send(): return lax.ppermute(value, 'col', list(enumerate(target)))  9.15 us
    unnamed x2, local copies, waits for them, and re-layouts  1 us
  transfers between devices with their start and end apart: 12, of which 4 were waited for; matrix products, arithmetic and copies ran while one was open for 6% of the time, Pallas kernels for 0%

profile of v19, /device:TPU:19, one launch (start us, length us, event | category | flops | bytes accessed | tf_op | source)
XLA Modules:
  0.0 40.5 jit_solution(3292424851854266661)
XLA Ops:
  0.0 1.3 %collective-permute-start = (bf16[8,14336]{1,0:T(8,128)(2,1)}, bf16[8,14336]{1,0:T(8,128)(2,1)S(1)}, u32[]{:S(2)}, u32[]{:S(2)}) collective-permute-start(bf16[8,14336]{1,0:T(8,128)(2,1)} %param.3), channel_id=1, source_target_pairs={{0,4},{1,3},{2,0},{3,7},{4,8},{5,1},{6,2},{7,11},{8,12},{9,5},{10,... | collective-permute-start | bytes 688136 | tf_op jit(solution)/shard_map/ppermute | solution.py:163
  1.3 0.2 collective-permute-start.1
  1.5 1.0 %constant_dynamic-update-slice_fusion.2 = bf16[24,14336]{1,0:T(8,128)(2,1)S(1)} fusion(bf16[8,14336]{1,0:T(8,128)(2,1)} %param.3), kind=kLoop, calls=%fused_computation.20 | loop fusion | bytes 458752
  2.6 0.8 %pad_add_fusion.table_ref = s32[153]{0:T(256)S(1)} fusion(s32[1]{0:T(128)} %bitcast, s32[136]{0:T(256)} %param.5, s32[16]{0:T(128)} %param.4), kind=kLoop, calls=%fused_computation.21 | loop fusion | flops 306 | bytes 1224 | tf_op jit(solution)/shard_map/concatenate | solution.py:316
  3.4 2.8 %collective-permute-done = bf16[8,14336]{1,0:T(8,128)(2,1)S(1)} collective-permute-done((bf16[8,14336]{1,0:T(8,128)(2,1)}, bf16[8,14336]{1,0:T(8,128)(2,1)S(1)}, u32[]{:S(2)}, u32[]{:S(2)}) %collective-permute-start) | collective-permute-done | bytes 229408 | tf_op jit(solution)/shard_map/ppermute | solution.py:163
  6.2 1.3 %collective-permute-start.3 = (bf16[8,14336]{1,0:T(8,128)(2,1)S(1)}, bf16[8,14336]{1,0:T(8,128)(2,1)S(1)}, u32[]{:S(2)}, u32[]{:S(2)}) collective-permute-start(bf16[8,14336]{1,0:T(8,128)(2,1)S(1)} %collective-permute-done), channel_id=1, source_target_pairs={{0,4},{1,3},{2,0},{3,7},{4,8},{5,1},{6,2},{7,11},{8,12},{9,5},{10,... | collective-permute-start | bytes 688136 | tf_op jit(solution)/shard_map/ppermute | solution.py:163
  7.5 1.3 %collective-permute-done.1 = bf16[8,14336]{1,0:T(8,128)(2,1)S(1)} collective-permute-done((bf16[8,14336]{1,0:T(8,128)(2,1)}, bf16[8,14336]{1,0:T(8,128)(2,1)S(1)}, u32[]{:S(2)}, u32[]{:S(2)}) %collective-permute-start.1) | collective-permute-done | bytes 229408 | tf_op jit(solution)/shard_map/ppermute | solution.py:163
  8.8 0.2 collective-permute-start.4
  9.0 0.1 broadcast_select_fusion
  9.1 0.1 fusion
  9.2 0.1 collective-permute-start.8
  9.3 2.3 %collective-permute-start.2 = (bf16[24,14336]{1,0:T(8,128)(2,1)S(1)}, bf16[24,14336]{1,0:T(8,128)(2,1)S(1)}, u32[]{:S(2)}, u32[]{:S(2)}) collective-permute-start(bf16[24,14336]{1,0:T(8,128)(2,1)S(1)} %get-tuple-element.10.refs_0_), channel_id=1, source_target_pairs={{0,1},{1,0},{2,3},{3,2},{4,5},{5,4},{6,7},{7,6},{8,9},{9,8},{10,11... | collective-permute-start | bytes 2064392 | tf_op jit(solution)/shard_map/ppermute | solution.py:163
  11.6 0.0 collective-permute-done.3
  11.6 4.0 %collective-permute-done.4 = bf16[8,14336]{1,0:T(8,128)(2,1)S(1)} collective-permute-done((bf16[8,14336]{1,0:T(8,128)(2,1)S(1)}, bf16[8,14336]{1,0:T(8,128)(2,1)S(1)}, u32[]{:S(2)}, u32[]{:S(2)}) %collective-permute-start.4) | collective-permute-done | bytes 229408 | tf_op jit(solution)/shard_map/ppermute | solution.py:163
  15.6 0.3 fusion.1
  15.9 0.2 collective-permute-start.6
  16.2 1.3 %collective-permute-start.10 = (bf16[8,10752]{1,0:T(8,128)(2,1)S(1)}, bf16[8,10752]{1,0:T(8,128)(2,1)S(1)}, u32[]{:S(2)}, u32[]{:S(2)}) collective-permute-start(bf16[8,10752]{1,0:T(8,128)(2,1)S(1)} %bitcast.14), channel_id=1, source_target_pairs={{0,4},{1,3},{2,0},{3,7},{4,8},{5,1},{6,2},{7,11},{8,12},{9,5},{10,... | collective-permute-start | bytes 516104 | tf_op jit(solution)/shard_map/ppermute | solution.py:163
  17.5 4.4 %collective-permute-start.5 = (bf16[16,10752]{1,0:T(8,128)(2,1)S(1)}, bf16[16,10752]{1,0:T(8,128)(2,1)S(1)}, u32[]{:S(2)}, u32[]{:S(2)}) collective-permute-start(bf16[16,10752]{1,0:T(8,128)(2,1)S(1)} %pad_maximum_fusion.1), channel_id=1, source_target_pairs={{0,1},{1,0},{2,3},{3,2},{4,5},{5,4},{6,7},{7,6},{8,9},{9,8},{10,11... | collective-permute-start | bytes 1032200 | tf_op jit(solution)/shard_map/ppermute | solution.py:163
  21.8 0.0 collective-permute-done.8.refs_6_
  21.8 0.0 collective-permute-done.6.refs_4_
  21.8 3.3 %collective-permute-start.9 = (bf16[8,10752]{1,0:T(8,128)(2,1)S(1)}, bf16[8,10752]{1,0:T(8,128)(2,1)S(1)}, u32[]{:S(2)}, u32[]{:S(2)}) collective-permute-start(bf16[8,10752]{1,0:T(8,128)(2,1)S(1)} %collective-permute-done.8.refs_6_), channel_id=1, source_target_pairs={{0,1},{1,0},{2,3},{3,2},{4,5},{5,4},{6,7},{7,6},{8,9},{9,8},{10,11... | collective-permute-start | bytes 516104 | tf_op jit(solution)/shard_map/ppermute | solution.py:163
  25.1 0.0 collective-permute-start.7
  25.1 0.0 collective-permute-done.10.refs_8_
  25.1 1.6 %collective-permute-start.11 = (bf16[8,10752]{1,0:T(8,128)(2,1)S(1)}, bf16[8,10752]{1,0:T(8,128)(2,1)S(1)}, u32[]{:S(2)}, u32[]{:S(2)}) collective-permute-start(bf16[8,10752]{1,0:T(8,128)(2,1)S(1)} %collective-permute-done.10.refs_8_), channel_id=1, source_target_pairs={{0,1},{1,0},{2,3},{3,2},{4,5},{5,4},{6,7},{7,6},{8,9},{9,8},{10,11... | collective-permute-start | bytes 516104 | tf_op jit(solution)/shard_map/ppermute | solution.py:163
  26.8 0.0 collective-permute-done.7.refs_5_
  26.8 1.0 %collective-permute-done.11.refs_9_ = bf16[8,10752]{1,0:T(8,128)(2,1)S(1)} collective-permute-done((bf16[8,10752]{1,0:T(8,128)(2,1)S(1)}, bf16[8,10752]{1,0:T(8,128)(2,1)S(1)}, u32[]{:S(2)}, u32[]{:S(2)}) %collective-permute-start.11) | collective-permute-done | bytes 172064 | tf_op jit(solution)/shard_map/ppermute | solution.py:163
  27.8 0.0 collective-permute-done.9.refs_7_
  27.8 0.0 collective-permute-done.5.refs_3_
  27.8 0.0 collective-permute-done.2.refs_1_
  27.8 12.7 %shard_map.37 = f32[11,896,896]{2,1,0:T(8,128)} custom-call(s32[153]{0:T(256)S(1)} %pad_add_fusion.table_ref, bf16[24,14336]{1,0:T(8,128)(2,1)S(1)} %get-tuple-element.10.refs_0_, bf16[24,14336]{1,0:T(8,128)(2,1)S(1)} %collective-permute-done.2.refs_1_, bf16[16,14336]{1,0:T(8,128)(2,1)S(1)} %pad_maximum_fusion.refs_2_, ...), custom_call_target="tpu_custom_call" | custom-call | flops 2260729856 | bytes 35323904 | tf_op jit(solution)/shard_map/pallas_call | solution.py:317
  (3 shorter events, 0.1 us)
Async XLA Ops:
  0.0 6.2 %collective-permute-start = (bf16[8,14336]{1,0:T(8,128)(2,1)}, bf16[8,14336]{1,0:T(8,128)(2,1)S(1)}, u32[]{:S(2)}, u32[]{:S(2)}) collective-permute-start(bf16[8,14336]{1,0:T(8,128)(2,1)} %param.3), channel_id=1, source_target_pairs={{0,4},{1,3},{2,0},{3,7},{4,8},{5,1},{6,2},{7,11},{8,12},{9,5},{10,... | collective-permute-start | bytes 688136 | tf_op jit(solution)/shard_map/ppermute | solution.py:163
  1.3 7.5 %collective-permute-start.1 = (bf16[8,14336]{1,0:T(8,128)(2,1)}, bf16[8,14336]{1,0:T(8,128)(2,1)S(1)}, u32[]{:S(2)}, u32[]{:S(2)}) collective-permute-start(bf16[8,14336]{1,0:T(8,128)(2,1)} %param.3), channel_id=1, source_target_pairs={{0,2},{1,5},{2,6},{3,1},{4,0},{5,9},{6,10},{7,3},{8,4},{9,13},{10,... | collective-permute-start | bytes 688136 | tf_op jit(solution)/shard_map/ppermute | solution.py:163
  6.2 5.4 %collective-permute-start.3 = (bf16[8,14336]{1,0:T(8,128)(2,1)S(1)}, bf16[8,14336]{1,0:T(8,128)(2,1)S(1)}, u32[]{:S(2)}, u32[]{:S(2)}) collective-permute-start(bf16[8,14336]{1,0:T(8,128)(2,1)S(1)} %collective-permute-done), channel_id=1, source_target_pairs={{0,4},{1,3},{2,0},{3,7},{4,8},{5,1},{6,2},{7,11},{8,12},{9,5},{10,... | collective-permute-start | bytes 688136 | tf_op jit(solution)/shard_map/ppermute | solution.py:163
  8.8 6.8 %collective-permute-start.4 = (bf16[8,14336]{1,0:T(8,128)(2,1)S(1)}, bf16[8,14336]{1,0:T(8,128)(2,1)S(1)}, u32[]{:S(2)}, u32[]{:S(2)}) collective-permute-start(bf16[8,14336]{1,0:T(8,128)(2,1)S(1)} %collective-permute-done.1), channel_id=1, source_target_pairs={{0,2},{1,5},{2,6},{3,1},{4,0},{5,9},{6,10},{7,3},{8,4},{9,13},{10,... | collective-permute-start | bytes 688136 | tf_op jit(solution)/shard_map/ppermute | solution.py:163
  9.2 12.7 %collective-permute-start.8 = (bf16[8,10752]{1,0:T(8,128)(2,1)S(1)}, bf16[8,10752]{1,0:T(8,128)(2,1)S(1)}, u32[]{:S(2)}, u32[]{:S(2)}) collective-permute-start(bf16[8,10752]{1,0:T(8,128)(2,1)S(1)} %bitcast.16), channel_id=1, source_target_pairs={{0,12},{1,13},{2,14},{3,15},{4,6},{5,7},{6,4},{7,5},{8,10},{9,11},... | collective-permute-start | bytes 516104 | tf_op jit(solution)/shard_map/ppermute | solution.py:163
  9.3 18.5 %collective-permute-start.2 = (bf16[24,14336]{1,0:T(8,128)(2,1)S(1)}, bf16[24,14336]{1,0:T(8,128)(2,1)S(1)}, u32[]{:S(2)}, u32[]{:S(2)}) collective-permute-start(bf16[24,14336]{1,0:T(8,128)(2,1)S(1)} %get-tuple-element.10.refs_0_), channel_id=1, source_target_pairs={{0,1},{1,0},{2,3},{3,2},{4,5},{5,4},{6,7},{7,6},{8,9},{9,8},{10,11... | collective-permute-start | bytes 2064392 | tf_op jit(solution)/shard_map/ppermute | solution.py:163
  15.9 5.9 %collective-permute-start.6 = (bf16[8,10752]{1,0:T(8,128)(2,1)S(1)}, bf16[8,10752]{1,0:T(8,128)(2,1)S(1)}, u32[]{:S(2)}, u32[]{:S(2)}) collective-permute-start(bf16[8,10752]{1,0:T(8,128)(2,1)S(1)} %bitcast.15), channel_id=1, source_target_pairs={{0,2},{1,5},{2,6},{3,1},{4,0},{5,9},{6,10},{7,3},{8,4},{9,13},{10,... | collective-permute-start | bytes 516104 | tf_op jit(solution)/shard_map/ppermute | solution.py:163
  16.2 9.0 %collective-permute-start.10 = (bf16[8,10752]{1,0:T(8,128)(2,1)S(1)}, bf16[8,10752]{1,0:T(8,128)(2,1)S(1)}, u32[]{:S(2)}, u32[]{:S(2)}) collective-permute-start(bf16[8,10752]{1,0:T(8,128)(2,1)S(1)} %bitcast.14), channel_id=1, source_target_pairs={{0,4},{1,3},{2,0},{3,7},{4,8},{5,1},{6,2},{7,11},{8,12},{9,5},{10,... | collective-permute-start | bytes 516104 | tf_op jit(solution)/shard_map/ppermute | solution.py:163
  17.5 10.3 %collective-permute-start.5 = (bf16[16,10752]{1,0:T(8,128)(2,1)S(1)}, bf16[16,10752]{1,0:T(8,128)(2,1)S(1)}, u32[]{:S(2)}, u32[]{:S(2)}) collective-permute-start(bf16[16,10752]{1,0:T(8,128)(2,1)S(1)} %pad_maximum_fusion.1), channel_id=1, source_target_pairs={{0,1},{1,0},{2,3},{3,2},{4,5},{5,4},{6,7},{7,6},{8,9},{9,8},{10,11... | collective-permute-start | bytes 1032200 | tf_op jit(solution)/shard_map/ppermute | solution.py:163
  21.8 5.9 %collective-permute-start.9 = (bf16[8,10752]{1,0:T(8,128)(2,1)S(1)}, bf16[8,10752]{1,0:T(8,128)(2,1)S(1)}, u32[]{:S(2)}, u32[]{:S(2)}) collective-permute-start(bf16[8,10752]{1,0:T(8,128)(2,1)S(1)} %collective-permute-done.8.refs_6_), channel_id=1, source_target_pairs={{0,1},{1,0},{2,3},{3,2},{4,5},{5,4},{6,7},{7,6},{8,9},{9,8},{10,11... | collective-permute-start | bytes 516104 | tf_op jit(solution)/shard_map/ppermute | solution.py:163
  25.1 1.6 %collective-permute-start.7 = (bf16[8,10752]{1,0:T(8,128)(2,1)S(1)}, bf16[8,10752]{1,0:T(8,128)(2,1)S(1)}, u32[]{:S(2)}, u32[]{:S(2)}) collective-permute-start(bf16[8,10752]{1,0:T(8,128)(2,1)S(1)} %collective-permute-done.6.refs_4_), channel_id=1, source_target_pairs={{0,1},{1,0},{2,3},{3,2},{4,5},{5,4},{6,7},{7,6},{8,9},{9,8},{10,11... | collective-permute-start | bytes 516104 | tf_op jit(solution)/shard_map/ppermute | solution.py:163
  25.1 2.6 %collective-permute-start.11 = (bf16[8,10752]{1,0:T(8,128)(2,1)S(1)}, bf16[8,10752]{1,0:T(8,128)(2,1)S(1)}, u32[]{:S(2)}, u32[]{:S(2)}) collective-permute-start(bf16[8,10752]{1,0:T(8,128)(2,1)S(1)} %collective-permute-done.10.refs_8_), channel_id=1, source_target_pairs={{0,1},{1,0},{2,3},{3,2},{4,5},{5,4},{6,7},{7,6},{8,9},{9,8},{10,11... | collective-permute-start | bytes 516104 | tf_op jit(solution)/shard_map/ppermute | solution.py:163

commit v20 on v14

--- a/solution.py
+++ b/solution.py
@@ -141,8 +141,7 @@
     onward = []
     for device in range(devices):
         chip, core = divmod(device, 2)
-        step = 1 if core == 0 else -1
-        onward.append(order[(place[chip] + step) % chips] * 2 + core)
+        onward.append(order[(place[chip] + 1) % chips] * 2 + core)
     backward = [onward.index(device) for device in range(devices)]
     return onward, backward
 
@@ -165,23 +164,17 @@
     def after(value, *others):
         return lax.optimization_barrier((value, *others))[0]
 
-    chip, core = device // 2, device % 2
-    chips = devices // 2
+    chip, chips = device // 2, devices // 2
     even = chip % 2 == 0
     next_chip = jnp.where(even, jnp.where(chip == chips - 2, chips - 1, chip + 2), jnp.where(chip == 1, 0, chip - 2))
     last_chip = jnp.where(even, jnp.where(chip == 0, 1, chip - 2), jnp.where(chip == chips - 1, chips - 2, chip + 2))
-    onward_chip = jnp.where(core == 0, next_chip, last_chip)
-    backward_chip = jnp.where(core == 0, last_chip, next_chip)
     over_chip = jnp.where((chip < 2) | (chip >= chips - 2), chip ^ 6, chip ^ 1)
-    chip, core = device // 2, device % 2
-    chips = devices // 2
+    chip, chips = device // 2, devices // 2
     even = chip % 2 == 0
     next_chip = jnp.where(even, jnp.where(chip == chips - 2, chips - 1, chip + 2), jnp.where(chip == 1, 0, chip - 2))
     last_chip = jnp.where(even, jnp.where(chip == 0, 1, chip - 2), jnp.where(chip == chips - 1, chips - 2, chip + 2))
-    onward_chip = jnp.where(core == 0, next_chip, last_chip)
-    backward_chip = jnp.where(core == 0, last_chip, next_chip)
     over_chip = jnp.where((chip < 2) | (chip >= chips - 2), chip ^ 6, chip ^ 1)
-    came_ahead = ((chip % 4 == 0) | (chip % 4 == 3)) == (core == 0)
+    came_ahead = (chip % 4 == 0) | (chip % 4 == 3)
     slab, units = tokens.shape
     needed = devices // 2 + devices // 8 + 2
 
@@ -196,8 +189,8 @@
         ahead.append(send(ahead[-1], onward))
         back.append(send(back[-1], backward))
     half = send(window(jnp.where(came_ahead, ahead[1], back[1]), over_chip), over)
-    ahead.append(send(window(ahead[2], onward_chip), onward))
-    back.append(send(window(back[2], backward_chip), backward))
+    ahead.append(send(window(ahead[2], next_chip), onward))
+    back.append(send(window(back[2], last_chip), backward))
     near = jnp.concatenate((tokens, ahead[1], back[1]), axis=0)
     middle = jnp.concatenate((ahead[2], back[2]), axis=0)
     last = jnp.concatenate((ahead[3], half), axis=0)
@@ -213,7 +206,7 @@
     chip, core = device // 2, device % 2
     core = 1 - core if flip else core
     place = jnp.where(chip % 2 == 0, chip // 2, chips - 1 - chip // 2)
-    place = (place - (1 - 2 * core) * hops + chips) % chips
+    place = (place - hops + chips) % chips
     chip = jnp.where(2 * place < chips, 2 * place, 2 * (chips - 1 - place) + 1)
     return 2 * chip + core
 

time: 40.5 us -> 39.9 us (0.985)
  waiting for transfers between devices: 13.8 us -> 13 us
    ppermute x11, waiting for transfers between devices: 13.8 us -> 13 us  [send(): return lax.ppermute(value, 'col', list(enumerate(target)))]
  transfers between devices with their start and end apart: 11 -> 11, of which waited for: 5 -> 6; matrix products, arithmetic and copies ran while one was open for 5% -> 6% of each run, Pallas kernels for 0% -> 0%
where the time goes in v20:
time: 39.9 us; the launch traced here: 39.8 us
  waiting for transfers between devices  13 us (33%)
  Pallas kernels  12.6 us (32%)
  starting transfers between devices  11.7 us (29%)
  other arithmetic  1.11 us (3%)
  local copies, waits for them, and re-layouts  1.09 us (3%)
    ppermute x11, waiting for transfers between devices, send(): return lax.ppermute(value, 'col', list(enumerate(target)))  13 us
    pallas_call x1, Pallas kernels, ring_form(): pl.pallas_call(functools.partial(ring_kernel, devices, slots), out_shape=...  12.6 us
    ppermute x11, starting transfers between devices, send(): return lax.ppermute(value, 'col', list(enumerate(target)))  11.7 us
    unnamed x4, local copies, waits for them, and re-layouts  1.06 us
  transfers between devices with their start and end apart: 11, of which 6 were waited for; matrix products, arithmetic and copies ran while one was open for 6% of the time, Pallas kernels for 0%

profile of v20, /device:TPU:0, one launch (start us, length us, event | category | flops | bytes accessed | tf_op | source)
XLA Modules:
  0.0 39.8 jit_solution(12841601296563839485)
XLA Ops:
  0.0 3.0 %collective-permute-start = (bf16[8,14336]{1,0:T(8,128)(2,1)}, bf16[8,14336]{1,0:T(8,128)(2,1)S(1)}, u32[]{:S(2)}, u32[]{:S(2)}) collective-permute-start(bf16[8,14336]{1,0:T(8,128)(2,1)} %param.3), channel_id=1, source_target_pairs={{0,4},{1,5},{2,0},{3,1},{4,8},{5,9},{6,2},{7,3},{8,12},{9,13},{10,... | collective-permute-start | bytes 688136 | tf_op jit(solution)/shard_map/ppermute | solution.py:162
  3.0 0.0 collective-permute-start.1
  3.0 1.0 %constant_dynamic-update-slice_fusion.2 = bf16[24,14336]{1,0:T(8,128)(2,1)S(1)} fusion(bf16[8,14336]{1,0:T(8,128)(2,1)} %param.3), kind=kLoop, calls=%fused_computation.12 | loop fusion | bytes 458752
  4.2 4.6 %collective-permute-done = bf16[8,14336]{1,0:T(8,128)(2,1)S(1)} collective-permute-done((bf16[8,14336]{1,0:T(8,128)(2,1)}, bf16[8,14336]{1,0:T(8,128)(2,1)S(1)}, u32[]{:S(2)}, u32[]{:S(2)}) %collective-permute-start) | collective-permute-done | bytes 229408 | tf_op jit(solution)/shard_map/ppermute | solution.py:162
  8.8 1.8 %collective-permute-start.3 = (bf16[8,14336]{1,0:T(8,128)(2,1)S(1)}, bf16[8,14336]{1,0:T(8,128)(2,1)S(1)}, u32[]{:S(2)}, u32[]{:S(2)}) collective-permute-start(bf16[8,14336]{1,0:T(8,128)(2,1)S(1)} %collective-permute-done), channel_id=1, source_target_pairs={{0,4},{1,5},{2,0},{3,1},{4,8},{5,9},{6,2},{7,3},{8,12},{9,13},{10,... | collective-permute-start | bytes 688136 | tf_op jit(solution)/shard_map/ppermute | solution.py:162
  10.6 0.0 collective-permute-done.1
  10.6 0.2 collective-permute-start.4
  10.8 0.1 broadcast_select_fusion
  10.9 0.1 fusion.1
  11.0 3.9 %collective-permute-start.7 = (bf16[8,10752]{1,0:T(8,128)(2,1)S(1)}, bf16[8,10752]{1,0:T(8,128)(2,1)S(1)}, u32[]{:S(2)}, u32[]{:S(2)}) collective-permute-start(bf16[8,10752]{1,0:T(8,128)(2,1)S(1)} %bitcast.10), channel_id=1, source_target_pairs={{0,12},{1,13},{2,14},{3,15},{4,6},{5,7},{6,4},{7,5},{8,10},{9,11},... | collective-permute-start | bytes 516104 | tf_op jit(solution)/shard_map/ppermute | solution.py:162
  14.9 0.0 collective-permute-start.2
  14.9 0.8 %collective-permute-done.3 = bf16[8,14336]{1,0:T(8,128)(2,1)S(1)} collective-permute-done((bf16[8,14336]{1,0:T(8,128)(2,1)S(1)}, bf16[8,14336]{1,0:T(8,128)(2,1)S(1)}, u32[]{:S(2)}, u32[]{:S(2)}) %collective-permute-start.3) | collective-permute-done | bytes 229408 | tf_op jit(solution)/shard_map/ppermute | solution.py:162
  15.7 0.1 fusion.2
  15.8 2.5 %collective-permute-start.6 = (bf16[8,10752]{1,0:T(8,128)(2,1)S(1)}, bf16[8,10752]{1,0:T(8,128)(2,1)S(1)}, u32[]{:S(2)}, u32[]{:S(2)}) collective-permute-start(bf16[8,10752]{1,0:T(8,128)(2,1)S(1)} %bitcast.12), channel_id=1, source_target_pairs={{0,4},{1,5},{2,0},{3,1},{4,8},{5,9},{6,2},{7,3},{8,12},{9,13},{10,... | collective-permute-start | bytes 516104 | tf_op jit(solution)/shard_map/ppermute | solution.py:162
  18.3 0.0 collective-permute-done.4
  18.3 0.1 fusion
  18.4 0.1 collective-permute-start.9
  18.5 0.1 collective-permute-start.5
  18.6 3.4 %collective-permute-done.6 = bf16[8,10752]{1,0:T(8,128)(2,1)S(1)} collective-permute-done((bf16[8,10752]{1,0:T(8,128)(2,1)S(1)}, bf16[8,10752]{1,0:T(8,128)(2,1)S(1)}, u32[]{:S(2)}, u32[]{:S(2)}) %collective-permute-start.6) | collective-permute-done | bytes 172064 | tf_op jit(solution)/shard_map/ppermute | solution.py:162
  22.0 2.4 %collective-permute-done.7 = bf16[8,10752]{1,0:T(8,128)(2,1)S(1)} collective-permute-done((bf16[8,10752]{1,0:T(8,128)(2,1)S(1)}, bf16[8,10752]{1,0:T(8,128)(2,1)S(1)}, u32[]{:S(2)}, u32[]{:S(2)}) %collective-permute-start.7) | collective-permute-done | bytes 172064 | tf_op jit(solution)/shard_map/ppermute | solution.py:162
  24.5 0.0 collective-permute-done.5.refs_3_
  24.5 0.1 collective-permute-start.8
  24.5 1.2 %collective-permute-done.9.refs_6_ = bf16[8,10752]{1,0:T(8,128)(2,1)S(1)} collective-permute-done((bf16[8,10752]{1,0:T(8,128)(2,1)S(1)}, bf16[8,10752]{1,0:T(8,128)(2,1)S(1)}, u32[]{:S(2)}, u32[]{:S(2)}) %collective-permute-start.9) | collective-permute-done | bytes 172064 | tf_op jit(solution)/shard_map/ppermute | solution.py:162
  25.8 0.0 collective-permute-start.10
  25.8 0.8 %pad_add_fusion.table_ref = s32[152]{0:T(256)S(1)} fusion(s32[136]{0:T(256)} %param.5, s32[16]{0:T(128)} %param.4), kind=kLoop, calls=%fused_computation.17 | loop fusion | flops 152 | bytes 1216 | tf_op jit(solution)/shard_map/concatenate | solution.py:307
  26.5 0.6 %collective-permute-done.10.refs_7_ = bf16[8,10752]{1,0:T(8,128)(2,1)S(1)} collective-permute-done((bf16[8,10752]{1,0:T(8,128)(2,1)S(1)}, bf16[8,10752]{1,0:T(8,128)(2,1)S(1)}, u32[]{:S(2)}, u32[]{:S(2)}) %collective-permute-start.10) | collective-permute-done | bytes 172064 | tf_op jit(solution)/shard_map/ppermute | solution.py:162
  27.2 0.0 collective-permute-done.2.refs_1_
  27.2 0.0 collective-permute-done.8.refs_5_
  27.2 12.6 %shard_map.37 = f32[11,896,896]{2,1,0:T(8,128)} custom-call(s32[1]{0:T(128)} %bitcast.device_ref, s32[152]{0:T(256)S(1)} %pad_add_fusion.table_ref, bf16[24,14336]{1,0:T(8,128)(2,1)S(1)} %get-tuple-element.8.refs_0_, bf16[24,14336]{1,0:T(8,128)(2,1)S(1)} %collective-permute-done.2.refs_1_, bf16[16,14336]{1,0:T(8,128)(2,1)S(1)} %constant_dynamic-update-slice_fusion.3.refs_2_, ...), custom_call_target="tpu_custom_call" | custom-call | flops 2260729856 | bytes 35323904 | tf_op jit(solution)/shard_map/pallas_call | solution.py:308
  (5 shorter events, 0.1 us)
Async XLA Ops:
  0.0 8.7 %collective-permute-start = (bf16[8,14336]{1,0:T(8,128)(2,1)}, bf16[8,14336]{1,0:T(8,128)(2,1)S(1)}, u32[]{:S(2)}, u32[]{:S(2)}) collective-permute-start(bf16[8,14336]{1,0:T(8,128)(2,1)} %param.3), channel_id=1, source_target_pairs={{0,4},{1,5},{2,0},{3,1},{4,8},{5,9},{6,2},{7,3},{8,12},{9,13},{10,... | collective-permute-start | bytes 688136 | tf_op jit(solution)/shard_map/ppermute | solution.py:162
  3.0 7.6 %collective-permute-start.1 = (bf16[8,14336]{1,0:T(8,128)(2,1)}, bf16[8,14336]{1,0:T(8,128)(2,1)S(1)}, u32[]{:S(2)}, u32[]{:S(2)}) collective-permute-start(bf16[8,14336]{1,0:T(8,128)(2,1)} %param.3), channel_id=1, source_target_pairs={{0,2},{1,3},{2,6},{3,7},{4,0},{5,1},{6,10},{7,11},{8,4},{9,5},{10,... | collective-permute-start | bytes 688136 | tf_op jit(solution)/shard_map/ppermute | solution.py:162
  8.8 6.9 %collective-permute-start.3 = (bf16[8,14336]{1,0:T(8,128)(2,1)S(1)}, bf16[8,14336]{1,0:T(8,128)(2,1)S(1)}, u32[]{:S(2)}, u32[]{:S(2)}) collective-permute-start(bf16[8,14336]{1,0:T(8,128)(2,1)S(1)} %collective-permute-done), channel_id=1, source_target_pairs={{0,4},{1,5},{2,0},{3,1},{4,8},{5,9},{6,2},{7,3},{8,12},{9,13},{10,... | collective-permute-start | bytes 688136 | tf_op jit(solution)/shard_map/ppermute | solution.py:162
  10.6 7.7 %collective-permute-start.4 = (bf16[8,14336]{1,0:T(8,128)(2,1)S(1)}, bf16[8,14336]{1,0:T(8,128)(2,1)S(1)}, u32[]{:S(2)}, u32[]{:S(2)}) collective-permute-start(bf16[8,14336]{1,0:T(8,128)(2,1)S(1)} %collective-permute-done.1), channel_id=1, source_target_pairs={{0,2},{1,3},{2,6},{3,7},{4,0},{5,1},{6,10},{7,11},{8,4},{9,5},{10,... | collective-permute-start | bytes 688136 | tf_op jit(solution)/shard_map/ppermute | solution.py:162
  11.0 13.5 %collective-permute-start.7 = (bf16[8,10752]{1,0:T(8,128)(2,1)S(1)}, bf16[8,10752]{1,0:T(8,128)(2,1)S(1)}, u32[]{:S(2)}, u32[]{:S(2)}) collective-permute-start(bf16[8,10752]{1,0:T(8,128)(2,1)S(1)} %bitcast.10), channel_id=1, source_target_pairs={{0,12},{1,13},{2,14},{3,15},{4,6},{5,7},{6,4},{7,5},{8,10},{9,11},... | collective-permute-start | bytes 516104 | tf_op jit(solution)/shard_map/ppermute | solution.py:162
  14.9 12.3 %collective-permute-start.2 = (bf16[24,14336]{1,0:T(8,128)(2,1)S(1)}, bf16[24,14336]{1,0:T(8,128)(2,1)S(1)}, u32[]{:S(2)}, u32[]{:S(2)}) collective-permute-start(bf16[24,14336]{1,0:T(8,128)(2,1)S(1)} %get-tuple-element.8.refs_0_), channel_id=1, source_target_pairs={{0,1},{1,0},{2,3},{3,2},{4,5},{5,4},{6,7},{7,6},{8,9},{9,8},{10,11... | collective-permute-start | bytes 2064392 | tf_op jit(solution)/shard_map/ppermute | solution.py:162
  15.8 6.2 %collective-permute-start.6 = (bf16[8,10752]{1,0:T(8,128)(2,1)S(1)}, bf16[8,10752]{1,0:T(8,128)(2,1)S(1)}, u32[]{:S(2)}, u32[]{:S(2)}) collective-permute-start(bf16[8,10752]{1,0:T(8,128)(2,1)S(1)} %bitcast.12), channel_id=1, source_target_pairs={{0,4},{1,5},{2,0},{3,1},{4,8},{5,9},{6,2},{7,3},{8,12},{9,13},{10,... | collective-permute-start | bytes 516104 | tf_op jit(solution)/shard_map/ppermute | solution.py:162
  18.4 7.4 %collective-permute-start.9 = (bf16[8,10752]{1,0:T(8,128)(2,1)S(1)}, bf16[8,10752]{1,0:T(8,128)(2,1)S(1)}, u32[]{:S(2)}, u32[]{:S(2)}) collective-permute-start(bf16[8,10752]{1,0:T(8,128)(2,1)S(1)} %bitcast.11), channel_id=1, source_target_pairs={{0,2},{1,3},{2,6},{3,7},{4,0},{5,1},{6,10},{7,11},{8,4},{9,5},{10,... | collective-permute-start | bytes 516104 | tf_op jit(solution)/shard_map/ppermute | solution.py:162
  18.5 5.9 %collective-permute-start.5 = (bf16[16,14336]{1,0:T(8,128)(2,1)S(1)}, bf16[16,14336]{1,0:T(8,128)(2,1)S(1)}, u32[]{:S(2)}, u32[]{:S(2)}) collective-permute-start(bf16[16,14336]{1,0:T(8,128)(2,1)S(1)} %constant_dynamic-update-slice_fusion.3.refs_2_), channel_id=1, source_target_pairs={{0,1},{1,0},{2,3},{3,2},{4,5},{5,4},{6,7},{7,6},{8,9},{9,8},{10,11... | collective-permute-start | bytes 1376264 | tf_op jit(solution)/shard_map/ppermute | solution.py:162
  24.5 2.7 %collective-permute-start.8 = (bf16[16,10752]{1,0:T(8,128)(2,1)S(1)}, bf16[16,10752]{1,0:T(8,128)(2,1)S(1)}, u32[]{:S(2)}, u32[]{:S(2)}) collective-permute-start(bf16[16,10752]{1,0:T(8,128)(2,1)S(1)} %constant_dynamic-update-slice_fusion.5.refs_4_), channel_id=1, source_target_pairs={{0,1},{1,0},{2,3},{3,2},{4,5},{5,4},{6,7},{7,6},{8,9},{9,8},{10,11... | collective-permute-start | bytes 1032200 | tf_op jit(solution)/shard_map/ppermute | solution.py:162
  25.8 1.4 %collective-permute-start.10 = (bf16[8,10752]{1,0:T(8,128)(2,1)S(1)}, bf16[8,10752]{1,0:T(8,128)(2,1)S(1)}, u32[]{:S(2)}, u32[]{:S(2)}) collective-permute-start(bf16[8,10752]{1,0:T(8,128)(2,1)S(1)} %collective-permute-done.9.refs_6_), channel_id=1, source_target_pairs={{0,1},{1,0},{2,3},{3,2},{4,5},{5,4},{6,7},{7,6},{8,9},{9,8},{10,11... | collective-permute-start | bytes 516104 | tf_op jit(solution)/shard_map/ppermute | solution.py:162

commit v21 on v20

--- a/solution.py
+++ b/solution.py
@@ -146,7 +146,7 @@
     return onward, backward
 
 
-GROUPS = ((0, 1, 2), (8, 9, 10), (3, 4), (11, 12), (5, 7), (13, 15), (6,), (14,))
+GROUPS = ((0, 1, 2), (8, 9, 10), (3, 4), (11, 12), (6,), (14,), (7,), (15,), (5,), (13,))
 
 
 def first_needed(devices, chip):
@@ -193,11 +193,13 @@
     back.append(send(window(back[2], last_chip), backward))
     near = jnp.concatenate((tokens, ahead[1], back[1]), axis=0)
     middle = jnp.concatenate((ahead[2], back[2]), axis=0)
-    last = jnp.concatenate((ahead[3], half), axis=0)
     near_beside = send(near, sibling)
-    middle_beside = send(middle, sibling)
-    last_beside = send(after(last, middle_beside), sibling)
-    return [near, near_beside, middle, middle_beside, last, last_beside, back[3], send(back[3], sibling)]
+    middle_beside = send(jnp.concatenate((window(ahead[2], chip), window(back[2], chip)), axis=0), sibling)
+    groups = [near, near_beside, middle, middle_beside]
+    for value in (back[3], half, ahead[3]):
+        groups += [value, send(after(value, back[3]) if value is half else value, sibling)]
+    return groups
+
 
 def slab_origin(devices, device, number):
     chips = devices // 2
@@ -211,10 +213,10 @@
     return 2 * chip + core
 
 
-def ring_kernel(devices, slots, device_ref, table_ref, *refs):
+def ring_kernel(devices, slots, table_ref, *refs):
     groups = refs[:len(GROUPS)]
     out_ref, pair, tiles, zeros, out_sems, zero_sems = refs[len(GROUPS):]
-    device = device_ref[0]
+    device = table_ref[table_ref.shape[0] - 1]
     slab, width = pair.shape[1] // devices, pair.shape[2]
     first = first_needed(devices, device // 2)
 
@@ -304,11 +306,11 @@
     slab, units = tokens.shape
     width = units // devices
     groups = ring_gather(tokens, device, devices)
-    table = jnp.concatenate([slab_lengths, tile_owner])
+    table = jnp.concatenate([slab_lengths, tile_owner, device.reshape(1)])
     return pl.pallas_call(
         functools.partial(ring_kernel, devices, slots),
         out_shape=jax.ShapeDtypeStruct((slots, width, width), jnp.float32),
-        in_specs=[pl.BlockSpec(memory_space=pltpu.SMEM)] * 2
+        in_specs=[pl.BlockSpec(memory_space=pltpu.SMEM)]
         + [pl.BlockSpec(memory_space=pltpu.VMEM)] * len(groups),
         out_specs=pl.BlockSpec(memory_space=pl.ANY),
         scratch_shapes=[
@@ -324,7 +326,7 @@
             bytes_accessed=4 * slots * width * width,
             transcendentals=0,
         ),
-    )(device.reshape(1), table, *groups)
+    )(table, *groups)
 
 
 def per_device(tokens, slab_lengths, tile_owner):

time: 39.9 us -> 40 us (level)
  starting transfers between devices: 11.7 us -> 12.7 us
  waiting for transfers between devices: 13 us -> 12 us
    ppermute x11 -> x12, waiting for transfers between devices: 13 us -> 12 us  [send(): return lax.ppermute(value, 'col', list(enumerate(target)))]
    ppermute x11 -> x12, starting transfers between devices: 11.7 us -> 12.7 us  [send(): return lax.ppermute(value, 'col', list(enumerate(target)))]
    concatenate x1 -> x3, other arithmetic: 0.76 us -> 0.81 us  [the longest x1 0.76 us: ring_form(): table = jnp.concatenate([slab_lengths, tile_owner, device.reshape(1)])]
    unnamed x4 -> x2, local copies, waits for them, and re-layouts: 1.06 us -> 1.03 us
  transfers between devices with their start and end apart: 11 -> 12, of which waited for: 6 -> 7; matrix products, arithmetic and copies ran while one was open for 6% -> 6% of each run, Pallas kernels for 0% -> 0%
where the time goes in v21:
time: 40 us; the launch traced here: 39.8 us
  starting transfers between devices  12.7 us (32%)
  Pallas kernels  12.6 us (32%)
  waiting for transfers between devices  12 us (30%)
  other arithmetic  1.32 us (3%)
  local copies, waits for them, and re-layouts  1.03 us (3%)
    ppermute x12, starting transfers between devices, send(): return lax.ppermute(value, 'col', list(enumerate(target)))  12.7 us
    pallas_call x1, Pallas kernels, ring_form(): pl.pallas_call(functools.partial(ring_kernel, devices, slots), out_shape=...  12.6 us
    ppermute x12, waiting for transfers between devices, send(): return lax.ppermute(value, 'col', list(enumerate(target)))  12 us
    unnamed x2, local copies, waits for them, and re-layouts  1.03 us
  transfers between devices with their start and end apart: 12, of which 7 were waited for; matrix products, arithmetic and copies ran while one was open for 6% of the time, Pallas kernels for 0%

profile of v21, /device:TPU:0, one launch (start us, length us, event | category | flops | bytes accessed | tf_op | source)
XLA Modules:
  0.0 39.8 jit_solution(13963961798705334893)
XLA Ops:
  0.0 3.0 %collective-permute-start = (bf16[8,14336]{1,0:T(8,128)(2,1)}, bf16[8,14336]{1,0:T(8,128)(2,1)S(1)}, u32[]{:S(2)}, u32[]{:S(2)}) collective-permute-start(bf16[8,14336]{1,0:T(8,128)(2,1)} %param.3), channel_id=1, source_target_pairs={{0,4},{1,5},{2,0},{3,1},{4,8},{5,9},{6,2},{7,3},{8,12},{9,13},{10,... | collective-permute-start | bytes 688136 | tf_op jit(solution)/shard_map/ppermute | solution.py:162
  3.0 0.0 collective-permute-start.1
  3.0 1.0 %constant_dynamic-update-slice_fusion.2 = bf16[24,14336]{1,0:T(8,128)(2,1)S(1)} fusion(bf16[8,14336]{1,0:T(8,128)(2,1)} %param.3), kind=kLoop, calls=%fused_computation.20 | loop fusion | bytes 458752
  4.2 0.8 %pad_add_fusion.table_ref = s32[153]{0:T(256)S(1)} fusion(s32[1]{0:T(128)} %bitcast, s32[136]{0:T(256)} %param.5, s32[16]{0:T(128)} %param.4), kind=kLoop, calls=%fused_computation.21 | loop fusion | flops 306 | bytes 1224 | tf_op jit(solution)/shard_map/concatenate | solution.py:309
  5.0 3.8 %collective-permute-done = bf16[8,14336]{1,0:T(8,128)(2,1)S(1)} collective-permute-done((bf16[8,14336]{1,0:T(8,128)(2,1)}, bf16[8,14336]{1,0:T(8,128)(2,1)S(1)}, u32[]{:S(2)}, u32[]{:S(2)}) %collective-permute-start) | collective-permute-done | bytes 229408 | tf_op jit(solution)/shard_map/ppermute | solution.py:162
  8.8 1.8 %collective-permute-start.3 = (bf16[8,14336]{1,0:T(8,128)(2,1)S(1)}, bf16[8,14336]{1,0:T(8,128)(2,1)S(1)}, u32[]{:S(2)}, u32[]{:S(2)}) collective-permute-start(bf16[8,14336]{1,0:T(8,128)(2,1)S(1)} %collective-permute-done), channel_id=1, source_target_pairs={{0,4},{1,5},{2,0},{3,1},{4,8},{5,9},{6,2},{7,3},{8,12},{9,13},{10,... | collective-permute-start | bytes 688136 | tf_op jit(solution)/shard_map/ppermute | solution.py:162
  10.6 0.0 collective-permute-done.1
  10.6 0.2 collective-permute-start.4
  10.8 0.1 broadcast_select_fusion
  10.9 0.1 fusion
  11.0 3.9 %collective-permute-start.8 = (bf16[8,10752]{1,0:T(8,128)(2,1)S(1)}, bf16[8,10752]{1,0:T(8,128)(2,1)S(1)}, u32[]{:S(2)}, u32[]{:S(2)}) collective-permute-start(bf16[8,10752]{1,0:T(8,128)(2,1)S(1)} %bitcast.16), channel_id=1, source_target_pairs={{0,12},{1,13},{2,14},{3,15},{4,6},{5,7},{6,4},{7,5},{8,10},{9,11},... | collective-permute-start | bytes 516104 | tf_op jit(solution)/shard_map/ppermute | solution.py:162
  14.9 0.0 collective-permute-start.2
  14.9 0.8 %collective-permute-done.3 = bf16[8,14336]{1,0:T(8,128)(2,1)S(1)} collective-permute-done((bf16[8,14336]{1,0:T(8,128)(2,1)S(1)}, bf16[8,14336]{1,0:T(8,128)(2,1)S(1)}, u32[]{:S(2)}, u32[]{:S(2)}) %collective-permute-start.3) | collective-permute-done | bytes 229408 | tf_op jit(solution)/shard_map/ppermute | solution.py:162
  15.7 1.4 %collective-permute-done.4 = bf16[8,14336]{1,0:T(8,128)(2,1)S(1)} collective-permute-done((bf16[8,14336]{1,0:T(8,128)(2,1)S(1)}, bf16[8,14336]{1,0:T(8,128)(2,1)S(1)}, u32[]{:S(2)}, u32[]{:S(2)}) %collective-permute-start.4) | collective-permute-done | bytes 229408 | tf_op jit(solution)/shard_map/ppermute | solution.py:162
  17.1 0.3 fusion.1
  17.4 0.5 %collective-permute-start.6 = (bf16[8,10752]{1,0:T(8,128)(2,1)S(1)}, bf16[8,10752]{1,0:T(8,128)(2,1)S(1)}, u32[]{:S(2)}, u32[]{:S(2)}) collective-permute-start(bf16[8,10752]{1,0:T(8,128)(2,1)S(1)} %bitcast.15), channel_id=1, source_target_pairs={{0,2},{1,3},{2,6},{3,7},{4,0},{5,1},{6,10},{7,11},{8,4},{9,5},{10,... | collective-permute-start | bytes 516104 | tf_op jit(solution)/shard_map/ppermute | solution.py:162
  17.9 2.7 %collective-permute-start.10 = (bf16[8,10752]{1,0:T(8,128)(2,1)S(1)}, bf16[8,10752]{1,0:T(8,128)(2,1)S(1)}, u32[]{:S(2)}, u32[]{:S(2)}) collective-permute-start(bf16[8,10752]{1,0:T(8,128)(2,1)S(1)} %bitcast.14), channel_id=1, source_target_pairs={{0,4},{1,5},{2,0},{3,1},{4,8},{5,9},{6,2},{7,3},{8,12},{9,13},{10,... | collective-permute-start | bytes 516104 | tf_op jit(solution)/shard_map/ppermute | solution.py:162
  20.6 0.1 collective-permute-start.5
  20.7 3.8 %collective-permute-done.8.refs_6_ = bf16[8,10752]{1,0:T(8,128)(2,1)S(1)} collective-permute-done((bf16[8,10752]{1,0:T(8,128)(2,1)S(1)}, bf16[8,10752]{1,0:T(8,128)(2,1)S(1)}, u32[]{:S(2)}, u32[]{:S(2)}) %collective-permute-start.8) | collective-permute-done | bytes 172064 | tf_op jit(solution)/shard_map/ppermute | solution.py:162
  24.5 0.8 %collective-permute-done.6.refs_4_ = bf16[8,10752]{1,0:T(8,128)(2,1)S(1)} collective-permute-done((bf16[8,10752]{1,0:T(8,128)(2,1)S(1)}, bf16[8,10752]{1,0:T(8,128)(2,1)S(1)}, u32[]{:S(2)}, u32[]{:S(2)}) %collective-permute-start.6) | collective-permute-done | bytes 172064 | tf_op jit(solution)/shard_map/ppermute | solution.py:162
  25.3 0.0 collective-permute-start.9
  25.3 0.5 %collective-permute-start.7 = (bf16[8,10752]{1,0:T(8,128)(2,1)S(1)}, bf16[8,10752]{1,0:T(8,128)(2,1)S(1)}, u32[]{:S(2)}, u32[]{:S(2)}) collective-permute-start(bf16[8,10752]{1,0:T(8,128)(2,1)S(1)} %collective-permute-done.6.refs_4_), channel_id=1, source_target_pairs={{0,1},{1,0},{2,3},{3,2},{4,5},{5,4},{6,7},{7,6},{8,9},{9,8},{10,11... | collective-permute-start | bytes 516104 | tf_op jit(solution)/shard_map/ppermute | solution.py:162
  25.8 0.0 collective-permute-done.10.refs_8_
  25.8 0.0 collective-permute-start.11
  25.9 1.1 %collective-permute-done.7.refs_5_ = bf16[8,10752]{1,0:T(8,128)(2,1)S(1)} collective-permute-done((bf16[8,10752]{1,0:T(8,128)(2,1)S(1)}, bf16[8,10752]{1,0:T(8,128)(2,1)S(1)}, u32[]{:S(2)}, u32[]{:S(2)}) %collective-permute-start.7) | collective-permute-done | bytes 172064 | tf_op jit(solution)/shard_map/ppermute | solution.py:162
  27.0 0.3 collective-permute-done.11.refs_9_
  27.2 0.0 collective-permute-done.9.refs_7_
  27.2 0.0 collective-permute-done.5.refs_3_
  27.2 0.0 collective-permute-done.2.refs_1_
  27.2 12.6 %shard_map.37 = f32[11,896,896]{2,1,0:T(8,128)} custom-call(s32[153]{0:T(256)S(1)} %pad_add_fusion.table_ref, bf16[24,14336]{1,0:T(8,128)(2,1)S(1)} %get-tuple-element.10.refs_0_, bf16[24,14336]{1,0:T(8,128)(2,1)S(1)} %collective-permute-done.2.refs_1_, bf16[16,14336]{1,0:T(8,128)(2,1)S(1)} %pad_maximum_fusion.refs_2_, ...), custom_call_target="tpu_custom_call" | custom-call | flops 2260729856 | bytes 35323904 | tf_op jit(solution)/shard_map/pallas_call | solution.py:310
  (3 shorter events, 0.1 us)
Async XLA Ops:
  0.0 8.7 %collective-permute-start = (bf16[8,14336]{1,0:T(8,128)(2,1)}, bf16[8,14336]{1,0:T(8,128)(2,1)S(1)}, u32[]{:S(2)}, u32[]{:S(2)}) collective-permute-start(bf16[8,14336]{1,0:T(8,128)(2,1)} %param.3), channel_id=1, source_target_pairs={{0,4},{1,5},{2,0},{3,1},{4,8},{5,9},{6,2},{7,3},{8,12},{9,13},{10,... | collective-permute-start | bytes 688136 | tf_op jit(solution)/shard_map/ppermute | solution.py:162
  3.0 7.6 %collective-permute-start.1 = (bf16[8,14336]{1,0:T(8,128)(2,1)}, bf16[8,14336]{1,0:T(8,128)(2,1)S(1)}, u32[]{:S(2)}, u32[]{:S(2)}) collective-permute-start(bf16[8,14336]{1,0:T(8,128)(2,1)} %param.3), channel_id=1, source_target_pairs={{0,2},{1,3},{2,6},{3,7},{4,0},{5,1},{6,10},{7,11},{8,4},{9,5},{10,... | collective-permute-start | bytes 688136 | tf_op jit(solution)/shard_map/ppermute | solution.py:162
  8.8 6.9 %collective-permute-start.3 = (bf16[8,14336]{1,0:T(8,128)(2,1)S(1)}, bf16[8,14336]{1,0:T(8,128)(2,1)S(1)}, u32[]{:S(2)}, u32[]{:S(2)}) collective-permute-start(bf16[8,14336]{1,0:T(8,128)(2,1)S(1)} %collective-permute-done), channel_id=1, source_target_pairs={{0,4},{1,5},{2,0},{3,1},{4,8},{5,9},{6,2},{7,3},{8,12},{9,13},{10,... | collective-permute-start | bytes 688136 | tf_op jit(solution)/shard_map/ppermute | solution.py:162
  10.6 6.5 %collective-permute-start.4 = (bf16[8,14336]{1,0:T(8,128)(2,1)S(1)}, bf16[8,14336]{1,0:T(8,128)(2,1)S(1)}, u32[]{:S(2)}, u32[]{:S(2)}) collective-permute-start(bf16[8,14336]{1,0:T(8,128)(2,1)S(1)} %collective-permute-done.1), channel_id=1, source_target_pairs={{0,2},{1,3},{2,6},{3,7},{4,0},{5,1},{6,10},{7,11},{8,4},{9,5},{10,... | collective-permute-start | bytes 688136 | tf_op jit(solution)/shard_map/ppermute | solution.py:162
  11.0 13.5 %collective-permute-start.8 = (bf16[8,10752]{1,0:T(8,128)(2,1)S(1)}, bf16[8,10752]{1,0:T(8,128)(2,1)S(1)}, u32[]{:S(2)}, u32[]{:S(2)}) collective-permute-start(bf16[8,10752]{1,0:T(8,128)(2,1)S(1)} %bitcast.16), channel_id=1, source_target_pairs={{0,12},{1,13},{2,14},{3,15},{4,6},{5,7},{6,4},{7,5},{8,10},{9,11},... | collective-permute-start | bytes 516104 | tf_op jit(solution)/shard_map/ppermute | solution.py:162
  14.9 12.3 %collective-permute-start.2 = (bf16[24,14336]{1,0:T(8,128)(2,1)S(1)}, bf16[24,14336]{1,0:T(8,128)(2,1)S(1)}, u32[]{:S(2)}, u32[]{:S(2)}) collective-permute-start(bf16[24,14336]{1,0:T(8,128)(2,1)S(1)} %get-tuple-element.10.refs_0_), channel_id=1, source_target_pairs={{0,1},{1,0},{2,3},{3,2},{4,5},{5,4},{6,7},{7,6},{8,9},{9,8},{10,11... | collective-permute-start | bytes 2064392 | tf_op jit(solution)/shard_map/ppermute | solution.py:162
  17.4 7.9 %collective-permute-start.6 = (bf16[8,10752]{1,0:T(8,128)(2,1)S(1)}, bf16[8,10752]{1,0:T(8,128)(2,1)S(1)}, u32[]{:S(2)}, u32[]{:S(2)}) collective-permute-start(bf16[8,10752]{1,0:T(8,128)(2,1)S(1)} %bitcast.15), channel_id=1, source_target_pairs={{0,2},{1,3},{2,6},{3,7},{4,0},{5,1},{6,10},{7,11},{8,4},{9,5},{10,... | collective-permute-start | bytes 516104 | tf_op jit(solution)/shard_map/ppermute | solution.py:162
  17.9 7.9 %collective-permute-start.10 = (bf16[8,10752]{1,0:T(8,128)(2,1)S(1)}, bf16[8,10752]{1,0:T(8,128)(2,1)S(1)}, u32[]{:S(2)}, u32[]{:S(2)}) collective-permute-start(bf16[8,10752]{1,0:T(8,128)(2,1)S(1)} %bitcast.14), channel_id=1, source_target_pairs={{0,4},{1,5},{2,0},{3,1},{4,8},{5,9},{6,2},{7,3},{8,12},{9,13},{10,... | collective-permute-start | bytes 516104 | tf_op jit(solution)/shard_map/ppermute | solution.py:162
  20.6 6.6 %collective-permute-start.5 = (bf16[16,10752]{1,0:T(8,128)(2,1)S(1)}, bf16[16,10752]{1,0:T(8,128)(2,1)S(1)}, u32[]{:S(2)}, u32[]{:S(2)}) collective-permute-start(bf16[16,10752]{1,0:T(8,128)(2,1)S(1)} %pad_maximum_fusion.1), channel_id=1, source_target_pairs={{0,1},{1,0},{2,3},{3,2},{4,5},{5,4},{6,7},{7,6},{8,9},{9,8},{10,11... | collective-permute-start | bytes 1032200 | tf_op jit(solution)/shard_map/ppermute | solution.py:162
  25.3 1.9 %collective-permute-start.9 = (bf16[8,10752]{1,0:T(8,128)(2,1)S(1)}, bf16[8,10752]{1,0:T(8,128)(2,1)S(1)}, u32[]{:S(2)}, u32[]{:S(2)}) collective-permute-start(bf16[8,10752]{1,0:T(8,128)(2,1)S(1)} %collective-permute-done.8.refs_6_), channel_id=1, source_target_pairs={{0,1},{1,0},{2,3},{3,2},{4,5},{5,4},{6,7},{7,6},{8,9},{9,8},{10,11... | collective-permute-start | bytes 516104 | tf_op jit(solution)/shard_map/ppermute | solution.py:162
  25.3 1.6 %collective-permute-start.7 = (bf16[8,10752]{1,0:T(8,128)(2,1)S(1)}, bf16[8,10752]{1,0:T(8,128)(2,1)S(1)}, u32[]{:S(2)}, u32[]{:S(2)}) collective-permute-start(bf16[8,10752]{1,0:T(8,128)(2,1)S(1)} %collective-permute-done.6.refs_4_), channel_id=1, source_target_pairs={{0,1},{1,0},{2,3},{3,2},{4,5},{5,4},{6,7},{7,6},{8,9},{9,8},{10,11... | collective-permute-start | bytes 516104 | tf_op jit(solution)/shard_map/ppermute | solution.py:162
  25.8 1.4 %collective-permute-start.11 = (bf16[8,10752]{1,0:T(8,128)(2,1)S(1)}, bf16[8,10752]{1,0:T(8,128)(2,1)S(1)}, u32[]{:S(2)}, u32[]{:S(2)}) collective-permute-start(bf16[8,10752]{1,0:T(8,128)(2,1)S(1)} %collective-permute-done.10.refs_8_), channel_id=1, source_target_pairs={{0,1},{1,0},{2,3},{3,2},{4,5},{5,4},{6,7},{7,6},{8,9},{9,8},{10,11... | collective-permute-start | bytes 516104 | tf_op jit(solution)/shard_map/ppermute | solution.py:162

commit v22 on v20

--- a/solution.py
+++ b/solution.py
@@ -141,7 +141,7 @@
     onward = []
     for device in range(devices):
         chip, core = divmod(device, 2)
-        onward.append(order[(place[chip] + 1) % chips] * 2 + core)
+        onward.append(order[(place[chip] - 1) % chips] * 2 + core)
     backward = [onward.index(device) for device in range(devices)]
     return onward, backward
 
@@ -174,7 +174,7 @@
     next_chip = jnp.where(even, jnp.where(chip == chips - 2, chips - 1, chip + 2), jnp.where(chip == 1, 0, chip - 2))
     last_chip = jnp.where(even, jnp.where(chip == 0, 1, chip - 2), jnp.where(chip == chips - 1, chips - 2, chip + 2))
     over_chip = jnp.where((chip < 2) | (chip >= chips - 2), chip ^ 6, chip ^ 1)
-    came_ahead = (chip % 4 == 0) | (chip % 4 == 3)
+    came_ahead = (chip % 4 == 1) | (chip % 4 == 2)
     slab, units = tokens.shape
     needed = devices // 2 + devices // 8 + 2
 
@@ -189,8 +189,8 @@
         ahead.append(send(ahead[-1], onward))
         back.append(send(back[-1], backward))
     half = send(window(jnp.where(came_ahead, ahead[1], back[1]), over_chip), over)
-    ahead.append(send(window(ahead[2], next_chip), onward))
-    back.append(send(window(back[2], last_chip), backward))
+    ahead.append(send(window(ahead[2], last_chip), onward))
+    back.append(send(window(back[2], next_chip), backward))
     near = jnp.concatenate((tokens, ahead[1], back[1]), axis=0)
     middle = jnp.concatenate((ahead[2], back[2]), axis=0)
     last = jnp.concatenate((ahead[3], half), axis=0)
@@ -206,7 +206,7 @@
     chip, core = device // 2, device % 2
     core = 1 - core if flip else core
     place = jnp.where(chip % 2 == 0, chip // 2, chips - 1 - chip // 2)
-    place = (place - hops + chips) % chips
+    place = (place + hops + chips) % chips
     chip = jnp.where(2 * place < chips, 2 * place, 2 * (chips - 1 - place) + 1)
     return 2 * chip + core
 

time: 39.9 us -> 39 us (0.977)
  waiting for transfers between devices: 13 us -> 11.4 us
  starting transfers between devices: 11.7 us -> 12.4 us
    ppermute x11, waiting for transfers between devices: 13 us -> 11.4 us  [send(): return lax.ppermute(value, 'col', list(enumerate(target)))]
    ppermute x11, starting transfers between devices: 11.7 us -> 12.4 us  [send(): return lax.ppermute(value, 'col', list(enumerate(target)))]
  transfers between devices with their start and end apart: 11 -> 11, of which waited for: 6 -> 4; matrix products, arithmetic and copies ran while one was open for 6% -> 6% of each run, Pallas kernels for 0% -> 0%
where the time goes in v22:
time: 39 us; the launch traced here: 38.8 us
  Pallas kernels  12.6 us (32%)
  starting transfers between devices  12.4 us (32%)
  waiting for transfers between devices  11.4 us (29%)
  other arithmetic  1.11 us (3%)
  local copies, waits for them, and re-layouts  1.06 us (3%)
    pallas_call x1, Pallas kernels, ring_form(): pl.pallas_call(functools.partial(ring_kernel, devices, slots), out_shape=...  12.6 us
    ppermute x11, starting transfers between devices, send(): return lax.ppermute(value, 'col', list(enumerate(target)))  12.4 us
    ppermute x11, waiting for transfers between devices, send(): return lax.ppermute(value, 'col', list(enumerate(target)))  11.4 us
    unnamed x4, local copies, waits for them, and re-layouts  1.03 us
  transfers between devices with their start and end apart: 11, of which 4 were waited for; matrix products, arithmetic and copies ran while one was open for 6% of the time, Pallas kernels for 0%

profile of v22, /device:TPU:0, one launch (start us, length us, event | category | flops | bytes accessed | tf_op | source)
XLA Modules:
  0.0 38.8 jit_solution(71609756495934312)
XLA Ops:
  0.0 2.9 %collective-permute-start = (bf16[8,14336]{1,0:T(8,128)(2,1)}, bf16[8,14336]{1,0:T(8,128)(2,1)S(1)}, u32[]{:S(2)}, u32[]{:S(2)}) collective-permute-start(bf16[8,14336]{1,0:T(8,128)(2,1)} %param.3), channel_id=1, source_target_pairs={{0,2},{1,3},{2,6},{3,7},{4,0},{5,1},{6,10},{7,11},{8,4},{9,5},{10,... | collective-permute-start | bytes 688136 | tf_op jit(solution)/shard_map/ppermute | solution.py:162
  2.9 0.1 collective-permute-start.1
  3.0 1.0 %constant_dynamic-update-slice_fusion.2 = bf16[24,14336]{1,0:T(8,128)(2,1)S(1)} fusion(bf16[8,14336]{1,0:T(8,128)(2,1)} %param.3), kind=kLoop, calls=%fused_computation.12 | loop fusion | bytes 458752
  4.2 4.7 %collective-permute-done = bf16[8,14336]{1,0:T(8,128)(2,1)S(1)} collective-permute-done((bf16[8,14336]{1,0:T(8,128)(2,1)}, bf16[8,14336]{1,0:T(8,128)(2,1)S(1)}, u32[]{:S(2)}, u32[]{:S(2)}) %collective-permute-start) | collective-permute-done | bytes 229408 | tf_op jit(solution)/shard_map/ppermute | solution.py:162
  8.8 1.7 %collective-permute-start.3 = (bf16[8,14336]{1,0:T(8,128)(2,1)S(1)}, bf16[8,14336]{1,0:T(8,128)(2,1)S(1)}, u32[]{:S(2)}, u32[]{:S(2)}) collective-permute-start(bf16[8,14336]{1,0:T(8,128)(2,1)S(1)} %collective-permute-done), channel_id=1, source_target_pairs={{0,2},{1,3},{2,6},{3,7},{4,0},{5,1},{6,10},{7,11},{8,4},{9,5},{10,... | collective-permute-start | bytes 688136 | tf_op jit(solution)/shard_map/ppermute | solution.py:162
  10.5 0.0 collective-permute-done.1
  10.5 0.4 collective-permute-start.4
  10.9 0.1 broadcast_select_fusion
  11.0 0.1 fusion.1
  11.1 3.8 %collective-permute-start.7 = (bf16[8,10752]{1,0:T(8,128)(2,1)S(1)}, bf16[8,10752]{1,0:T(8,128)(2,1)S(1)}, u32[]{:S(2)}, u32[]{:S(2)}) collective-permute-start(bf16[8,10752]{1,0:T(8,128)(2,1)S(1)} %bitcast.10), channel_id=1, source_target_pairs={{0,12},{1,13},{2,14},{3,15},{4,6},{5,7},{6,4},{7,5},{8,10},{9,11},... | collective-permute-start | bytes 516104 | tf_op jit(solution)/shard_map/ppermute | solution.py:162
  14.9 0.0 collective-permute-start.2
  14.9 0.9 %collective-permute-done.3 = bf16[8,14336]{1,0:T(8,128)(2,1)S(1)} collective-permute-done((bf16[8,14336]{1,0:T(8,128)(2,1)S(1)}, bf16[8,14336]{1,0:T(8,128)(2,1)S(1)}, u32[]{:S(2)}, u32[]{:S(2)}) %collective-permute-start.3) | collective-permute-done | bytes 229408 | tf_op jit(solution)/shard_map/ppermute | solution.py:162
  15.8 0.1 fusion.2
  15.9 1.4 %collective-permute-start.6 = (bf16[8,10752]{1,0:T(8,128)(2,1)S(1)}, bf16[8,10752]{1,0:T(8,128)(2,1)S(1)}, u32[]{:S(2)}, u32[]{:S(2)}) collective-permute-start(bf16[8,10752]{1,0:T(8,128)(2,1)S(1)} %bitcast.12), channel_id=1, source_target_pairs={{0,2},{1,3},{2,6},{3,7},{4,0},{5,1},{6,10},{7,11},{8,4},{9,5},{10,... | collective-permute-start | bytes 516104 | tf_op jit(solution)/shard_map/ppermute | solution.py:162
  17.3 0.0 collective-permute-done.4
  17.3 0.1 fusion
  17.4 1.5 %collective-permute-start.9 = (bf16[8,10752]{1,0:T(8,128)(2,1)S(1)}, bf16[8,10752]{1,0:T(8,128)(2,1)S(1)}, u32[]{:S(2)}, u32[]{:S(2)}) collective-permute-start(bf16[8,10752]{1,0:T(8,128)(2,1)S(1)} %bitcast.11), channel_id=1, source_target_pairs={{0,4},{1,5},{2,0},{3,1},{4,8},{5,9},{6,2},{7,3},{8,12},{9,13},{10,... | collective-permute-start | bytes 516104 | tf_op jit(solution)/shard_map/ppermute | solution.py:162
  19.0 0.1 collective-permute-start.5
  19.1 5.1 %collective-permute-done.6 = bf16[8,10752]{1,0:T(8,128)(2,1)S(1)} collective-permute-done((bf16[8,10752]{1,0:T(8,128)(2,1)S(1)}, bf16[8,10752]{1,0:T(8,128)(2,1)S(1)}, u32[]{:S(2)}, u32[]{:S(2)}) %collective-permute-start.6) | collective-permute-done | bytes 172064 | tf_op jit(solution)/shard_map/ppermute | solution.py:162
  24.2 0.0 collective-permute-done.7
  24.2 0.0 collective-permute-done.5.refs_3_
  24.2 0.1 collective-permute-start.8
  24.3 0.0 collective-permute-done.9.refs_6_
  24.3 0.5 %collective-permute-start.10 = (bf16[8,10752]{1,0:T(8,128)(2,1)S(1)}, bf16[8,10752]{1,0:T(8,128)(2,1)S(1)}, u32[]{:S(2)}, u32[]{:S(2)}) collective-permute-start(bf16[8,10752]{1,0:T(8,128)(2,1)S(1)} %collective-permute-done.9.refs_6_), channel_id=1, source_target_pairs={{0,1},{1,0},{2,3},{3,2},{4,5},{5,4},{6,7},{7,6},{8,9},{9,8},{10,11... | collective-permute-start | bytes 516104 | tf_op jit(solution)/shard_map/ppermute | solution.py:162
  24.8 0.8 %pad_add_fusion.table_ref = s32[152]{0:T(256)S(1)} fusion(s32[136]{0:T(256)} %param.5, s32[16]{0:T(128)} %param.4), kind=kLoop, calls=%fused_computation.17 | loop fusion | flops 152 | bytes 1216 | tf_op jit(solution)/shard_map/concatenate | solution.py:307
  25.6 0.6 %collective-permute-done.10.refs_7_ = bf16[8,10752]{1,0:T(8,128)(2,1)S(1)} collective-permute-done((bf16[8,10752]{1,0:T(8,128)(2,1)S(1)}, bf16[8,10752]{1,0:T(8,128)(2,1)S(1)}, u32[]{:S(2)}, u32[]{:S(2)}) %collective-permute-start.10) | collective-permute-done | bytes 172064 | tf_op jit(solution)/shard_map/ppermute | solution.py:162
  26.2 0.0 collective-permute-done.2.refs_1_
  26.2 0.0 collective-permute-done.8.refs_5_
  26.2 12.6 %shard_map.37 = f32[11,896,896]{2,1,0:T(8,128)} custom-call(s32[1]{0:T(128)} %bitcast.device_ref, s32[152]{0:T(256)S(1)} %pad_add_fusion.table_ref, bf16[24,14336]{1,0:T(8,128)(2,1)S(1)} %get-tuple-element.8.refs_0_, bf16[24,14336]{1,0:T(8,128)(2,1)S(1)} %collective-permute-done.2.refs_1_, bf16[16,14336]{1,0:T(8,128)(2,1)S(1)} %constant_dynamic-update-slice_fusion.3.refs_2_, ...), custom_call_target="tpu_custom_call" | custom-call | flops 2260729856 | bytes 35323904 | tf_op jit(solution)/shard_map/pallas_call | solution.py:308
  (5 shorter events, 0.1 us)
Async XLA Ops:
  0.0 8.8 %collective-permute-start = (bf16[8,14336]{1,0:T(8,128)(2,1)}, bf16[8,14336]{1,0:T(8,128)(2,1)S(1)}, u32[]{:S(2)}, u32[]{:S(2)}) collective-permute-start(bf16[8,14336]{1,0:T(8,128)(2,1)} %param.3), channel_id=1, source_target_pairs={{0,2},{1,3},{2,6},{3,7},{4,0},{5,1},{6,10},{7,11},{8,4},{9,5},{10,... | collective-permute-start | bytes 688136 | tf_op jit(solution)/shard_map/ppermute | solution.py:162
  2.9 7.6 %collective-permute-start.1 = (bf16[8,14336]{1,0:T(8,128)(2,1)}, bf16[8,14336]{1,0:T(8,128)(2,1)S(1)}, u32[]{:S(2)}, u32[]{:S(2)}) collective-permute-start(bf16[8,14336]{1,0:T(8,128)(2,1)} %param.3), channel_id=1, source_target_pairs={{0,4},{1,5},{2,0},{3,1},{4,8},{5,9},{6,2},{7,3},{8,12},{9,13},{10,... | collective-permute-start | bytes 688136 | tf_op jit(solution)/shard_map/ppermute | solution.py:162
  8.8 7.0 %collective-permute-start.3 = (bf16[8,14336]{1,0:T(8,128)(2,1)S(1)}, bf16[8,14336]{1,0:T(8,128)(2,1)S(1)}, u32[]{:S(2)}, u32[]{:S(2)}) collective-permute-start(bf16[8,14336]{1,0:T(8,128)(2,1)S(1)} %collective-permute-done), channel_id=1, source_target_pairs={{0,2},{1,3},{2,6},{3,7},{4,0},{5,1},{6,10},{7,11},{8,4},{9,5},{10,... | collective-permute-start | bytes 688136 | tf_op jit(solution)/shard_map/ppermute | solution.py:162
  10.5 6.8 %collective-permute-start.4 = (bf16[8,14336]{1,0:T(8,128)(2,1)S(1)}, bf16[8,14336]{1,0:T(8,128)(2,1)S(1)}, u32[]{:S(2)}, u32[]{:S(2)}) collective-permute-start(bf16[8,14336]{1,0:T(8,128)(2,1)S(1)} %collective-permute-done.1), channel_id=1, source_target_pairs={{0,4},{1,5},{2,0},{3,1},{4,8},{5,9},{6,2},{7,3},{8,12},{9,13},{10,... | collective-permute-start | bytes 688136 | tf_op jit(solution)/shard_map/ppermute | solution.py:162
  11.1 13.1 %collective-permute-start.7 = (bf16[8,10752]{1,0:T(8,128)(2,1)S(1)}, bf16[8,10752]{1,0:T(8,128)(2,1)S(1)}, u32[]{:S(2)}, u32[]{:S(2)}) collective-permute-start(bf16[8,10752]{1,0:T(8,128)(2,1)S(1)} %bitcast.10), channel_id=1, source_target_pairs={{0,12},{1,13},{2,14},{3,15},{4,6},{5,7},{6,4},{7,5},{8,10},{9,11},... | collective-permute-start | bytes 516104 | tf_op jit(solution)/shard_map/ppermute | solution.py:162
  14.9 11.3 %collective-permute-start.2 = (bf16[24,14336]{1,0:T(8,128)(2,1)S(1)}, bf16[24,14336]{1,0:T(8,128)(2,1)S(1)}, u32[]{:S(2)}, u32[]{:S(2)}) collective-permute-start(bf16[24,14336]{1,0:T(8,128)(2,1)S(1)} %get-tuple-element.8.refs_0_), channel_id=1, source_target_pairs={{0,1},{1,0},{2,3},{3,2},{4,5},{5,4},{6,7},{7,6},{8,9},{9,8},{10,11... | collective-permute-start | bytes 2064392 | tf_op jit(solution)/shard_map/ppermute | solution.py:162
  15.9 8.3 %collective-permute-start.6 = (bf16[8,10752]{1,0:T(8,128)(2,1)S(1)}, bf16[8,10752]{1,0:T(8,128)(2,1)S(1)}, u32[]{:S(2)}, u32[]{:S(2)}) collective-permute-start(bf16[8,10752]{1,0:T(8,128)(2,1)S(1)} %bitcast.12), channel_id=1, source_target_pairs={{0,2},{1,3},{2,6},{3,7},{4,0},{5,1},{6,10},{7,11},{8,4},{9,5},{10,... | collective-permute-start | bytes 516104 | tf_op jit(solution)/shard_map/ppermute | solution.py:162
  17.4 6.9 %collective-permute-start.9 = (bf16[8,10752]{1,0:T(8,128)(2,1)S(1)}, bf16[8,10752]{1,0:T(8,128)(2,1)S(1)}, u32[]{:S(2)}, u32[]{:S(2)}) collective-permute-start(bf16[8,10752]{1,0:T(8,128)(2,1)S(1)} %bitcast.11), channel_id=1, source_target_pairs={{0,4},{1,5},{2,0},{3,1},{4,8},{5,9},{6,2},{7,3},{8,12},{9,13},{10,... | collective-permute-start | bytes 516104 | tf_op jit(solution)/shard_map/ppermute | solution.py:162
  19.0 5.2 %collective-permute-start.5 = (bf16[16,14336]{1,0:T(8,128)(2,1)S(1)}, bf16[16,14336]{1,0:T(8,128)(2,1)S(1)}, u32[]{:S(2)}, u32[]{:S(2)}) collective-permute-start(bf16[16,14336]{1,0:T(8,128)(2,1)S(1)} %constant_dynamic-update-slice_fusion.3.refs_2_), channel_id=1, source_target_pairs={{0,1},{1,0},{2,3},{3,2},{4,5},{5,4},{6,7},{7,6},{8,9},{9,8},{10,11... | collective-permute-start | bytes 1376264 | tf_op jit(solution)/shard_map/ppermute | solution.py:162
  24.2 2.0 %collective-permute-start.8 = (bf16[16,10752]{1,0:T(8,128)(2,1)S(1)}, bf16[16,10752]{1,0:T(8,128)(2,1)S(1)}, u32[]{:S(2)}, u32[]{:S(2)}) collective-permute-start(bf16[16,10752]{1,0:T(8,128)(2,1)S(1)} %constant_dynamic-update-slice_fusion.5.refs_4_), channel_id=1, source_target_pairs={{0,1},{1,0},{2,3},{3,2},{4,5},{5,4},{6,7},{7,6},{8,9},{9,8},{10,11... | collective-permute-start | bytes 1032200 | tf_op jit(solution)/shard_map/ppermute | solution.py:162
  24.3 1.9 %collective-permute-start.10 = (bf16[8,10752]{1,0:T(8,128)(2,1)S(1)}, bf16[8,10752]{1,0:T(8,128)(2,1)S(1)}, u32[]{:S(2)}, u32[]{:S(2)}) collective-permute-start(bf16[8,10752]{1,0:T(8,128)(2,1)S(1)} %collective-permute-done.9.refs_6_), channel_id=1, source_target_pairs={{0,1},{1,0},{2,3},{3,2},{4,5},{5,4},{6,7},{7,6},{8,9},{9,8},{10,11... | collective-permute-start | bytes 516104 | tf_op jit(solution)/shard_map/ppermute | solution.py:162

commit v23 on v22

--- a/solution.py
+++ b/solution.py
@@ -195,8 +195,9 @@
     middle = jnp.concatenate((ahead[2], back[2]), axis=0)
     last = jnp.concatenate((ahead[3], half), axis=0)
     near_beside = send(near, sibling)
-    middle_beside = send(middle, sibling)
-    last_beside = send(after(last, middle_beside), sibling)
+    needed = [window(after(value, ahead[2], back[2]), chip) for value in (ahead[2], back[2])]
+    middle_beside = send(jnp.concatenate(needed, axis=0), sibling)
+    last_beside = send(last, sibling)
     return [near, near_beside, middle, middle_beside, last, last_beside, back[3], send(back[3], sibling)]
 
 def slab_origin(devices, device, number):

time: 39 us -> 38.9 us (level)
    unnamed x4 -> x3, local copies, waits for them, and re-layouts: 1.03 us -> 1.01 us
where the time goes in v23:
time: 38.9 us; the launch traced here: 38.7 us
  Pallas kernels  12.5 us (32%)
  starting transfers between devices  12.4 us (32%)
  waiting for transfers between devices  11.2 us (29%)
  other arithmetic  1.32 us (3%)
  local copies, waits for them, and re-layouts  1.03 us (3%)
    pallas_call x1, Pallas kernels, ring_form(): pl.pallas_call(functools.partial(ring_kernel, devices, slots), out_shape=...  12.5 us
    ppermute x11, starting transfers between devices, send(): return lax.ppermute(value, 'col', list(enumerate(target)))  12.4 us
    ppermute x11, waiting for transfers between devices, send(): return lax.ppermute(value, 'col', list(enumerate(target)))  11.2 us
    unnamed x3, local copies, waits for them, and re-layouts  1.01 us
  transfers between devices with their start and end apart: 11, of which 4 were waited for; matrix products, arithmetic and copies ran while one was open for 6% of the time, Pallas kernels for 0%

profile of v23, /device:TPU:0, one launch (start us, length us, event | category | flops | bytes accessed | tf_op | source)
XLA Modules:
  0.0 38.7 jit_solution(840547655832169737)
XLA Ops:
  0.0 2.9 %collective-permute-start = (bf16[8,14336]{1,0:T(8,128)(2,1)}, bf16[8,14336]{1,0:T(8,128)(2,1)S(1)}, u32[]{:S(2)}, u32[]{:S(2)}) collective-permute-start(bf16[8,14336]{1,0:T(8,128)(2,1)} %param.3), channel_id=1, source_target_pairs={{0,2},{1,3},{2,6},{3,7},{4,0},{5,1},{6,10},{7,11},{8,4},{9,5},{10,... | collective-permute-start | bytes 688136 | tf_op jit(solution)/shard_map/ppermute | solution.py:162
  2.9 0.1 collective-permute-start.1
  3.0 1.0 %constant_dynamic-update-slice_fusion.2 = bf16[24,14336]{1,0:T(8,128)(2,1)S(1)} fusion(bf16[8,14336]{1,0:T(8,128)(2,1)} %param.3), kind=kLoop, calls=%fused_computation.20 | loop fusion | bytes 458752
  4.2 0.8 %pad_add_fusion.table_ref = s32[152]{0:T(256)S(1)} fusion(s32[136]{0:T(256)} %param.5, s32[16]{0:T(128)} %param.4), kind=kLoop, calls=%fused_computation.23 | loop fusion | flops 152 | bytes 1216 | tf_op jit(solution)/shard_map/concatenate | solution.py:308
  4.9 3.9 %collective-permute-done = bf16[8,14336]{1,0:T(8,128)(2,1)S(1)} collective-permute-done((bf16[8,14336]{1,0:T(8,128)(2,1)}, bf16[8,14336]{1,0:T(8,128)(2,1)S(1)}, u32[]{:S(2)}, u32[]{:S(2)}) %collective-permute-start) | collective-permute-done | bytes 229408 | tf_op jit(solution)/shard_map/ppermute | solution.py:162
  8.8 1.7 %collective-permute-start.3 = (bf16[8,14336]{1,0:T(8,128)(2,1)S(1)}, bf16[8,14336]{1,0:T(8,128)(2,1)S(1)}, u32[]{:S(2)}, u32[]{:S(2)}) collective-permute-start(bf16[8,14336]{1,0:T(8,128)(2,1)S(1)} %collective-permute-done), channel_id=1, source_target_pairs={{0,2},{1,3},{2,6},{3,7},{4,0},{5,1},{6,10},{7,11},{8,4},{9,5},{10,... | collective-permute-start | bytes 688136 | tf_op jit(solution)/shard_map/ppermute | solution.py:162
  10.5 0.0 collective-permute-done.1
  10.5 0.4 collective-permute-start.4
  10.9 0.1 broadcast_select_fusion
  11.0 0.1 fusion.1
  11.1 3.8 %collective-permute-start.7 = (bf16[8,10752]{1,0:T(8,128)(2,1)S(1)}, bf16[8,10752]{1,0:T(8,128)(2,1)S(1)}, u32[]{:S(2)}, u32[]{:S(2)}) collective-permute-start(bf16[8,10752]{1,0:T(8,128)(2,1)S(1)} %bitcast.18), channel_id=1, source_target_pairs={{0,12},{1,13},{2,14},{3,15},{4,6},{5,7},{6,4},{7,5},{8,10},{9,11},... | collective-permute-start | bytes 516104 | tf_op jit(solution)/shard_map/ppermute | solution.py:162
  14.9 0.0 collective-permute-start.2
  14.9 0.9 %collective-permute-done.3 = bf16[8,14336]{1,0:T(8,128)(2,1)S(1)} collective-permute-done((bf16[8,14336]{1,0:T(8,128)(2,1)S(1)}, bf16[8,14336]{1,0:T(8,128)(2,1)S(1)}, u32[]{:S(2)}, u32[]{:S(2)}) %collective-permute-start.3) | collective-permute-done | bytes 229408 | tf_op jit(solution)/shard_map/ppermute | solution.py:162
  15.8 0.1 fusion.2
  15.9 1.4 %collective-permute-start.6 = (bf16[8,10752]{1,0:T(8,128)(2,1)S(1)}, bf16[8,10752]{1,0:T(8,128)(2,1)S(1)}, u32[]{:S(2)}, u32[]{:S(2)}) collective-permute-start(bf16[8,10752]{1,0:T(8,128)(2,1)S(1)} %bitcast.20), channel_id=1, source_target_pairs={{0,2},{1,3},{2,6},{3,7},{4,0},{5,1},{6,10},{7,11},{8,4},{9,5},{10,... | collective-permute-start | bytes 516104 | tf_op jit(solution)/shard_map/ppermute | solution.py:162
  17.3 0.0 collective-permute-done.4
  17.3 0.1 fusion
  17.4 1.5 %collective-permute-start.9 = (bf16[8,10752]{1,0:T(8,128)(2,1)S(1)}, bf16[8,10752]{1,0:T(8,128)(2,1)S(1)}, u32[]{:S(2)}, u32[]{:S(2)}) collective-permute-start(bf16[8,10752]{1,0:T(8,128)(2,1)S(1)} %bitcast.19), channel_id=1, source_target_pairs={{0,4},{1,5},{2,0},{3,1},{4,8},{5,9},{6,2},{7,3},{8,12},{9,13},{10,... | collective-permute-start | bytes 516104 | tf_op jit(solution)/shard_map/ppermute | solution.py:162
  18.9 0.2 fusion.3
  19.1 0.1 collective-permute-start.5
  19.2 5.0 %collective-permute-done.6 = bf16[8,10752]{1,0:T(8,128)(2,1)S(1)} collective-permute-done((bf16[8,10752]{1,0:T(8,128)(2,1)S(1)}, bf16[8,10752]{1,0:T(8,128)(2,1)S(1)}, u32[]{:S(2)}, u32[]{:S(2)}) %collective-permute-start.6) | collective-permute-done | bytes 172064 | tf_op jit(solution)/shard_map/ppermute | solution.py:162
  24.2 0.0 collective-permute-done.7
  24.2 0.1 collective-permute-start.8
  24.3 0.0 collective-permute-done.9.refs_6_
  24.3 0.5 %collective-permute-start.10 = (bf16[8,10752]{1,0:T(8,128)(2,1)S(1)}, bf16[8,10752]{1,0:T(8,128)(2,1)S(1)}, u32[]{:S(2)}, u32[]{:S(2)}) collective-permute-start(bf16[8,10752]{1,0:T(8,128)(2,1)S(1)} %collective-permute-done.9.refs_6_), channel_id=1, source_target_pairs={{0,1},{1,0},{2,3},{3,2},{4,5},{5,4},{6,7},{7,6},{8,9},{9,8},{10,11... | collective-permute-start | bytes 516104 | tf_op jit(solution)/shard_map/ppermute | solution.py:162
  24.8 1.4 %collective-permute-done.10.refs_7_ = bf16[8,10752]{1,0:T(8,128)(2,1)S(1)} collective-permute-done((bf16[8,10752]{1,0:T(8,128)(2,1)S(1)}, bf16[8,10752]{1,0:T(8,128)(2,1)S(1)}, u32[]{:S(2)}, u32[]{:S(2)}) %collective-permute-start.10) | collective-permute-done | bytes 172064 | tf_op jit(solution)/shard_map/ppermute | solution.py:162
  26.2 0.0 collective-permute-done.5.refs_3_
  26.2 0.0 collective-permute-done.2.refs_1_
  26.2 0.0 collective-permute-done.8.refs_5_
  26.2 12.5 %shard_map.37 = f32[11,896,896]{2,1,0:T(8,128)} custom-call(s32[1]{0:T(128)} %bitcast.device_ref, s32[152]{0:T(256)S(1)} %pad_add_fusion.table_ref, bf16[24,14336]{1,0:T(8,128)(2,1)S(1)} %get-tuple-element.10.refs_0_, bf16[24,14336]{1,0:T(8,128)(2,1)S(1)} %collective-permute-done.2.refs_1_, bf16[16,14336]{1,0:T(8,128)(2,1)S(1)} %pad_maximum_fusion.refs_2_, ...), custom_call_target="tpu_custom_call" | custom-call | flops 2260729856 | bytes 35323904 | tf_op jit(solution)/shard_map/pallas_call | solution.py:309
  (5 shorter events, 0.1 us)
Async XLA Ops:
  0.0 8.8 %collective-permute-start = (bf16[8,14336]{1,0:T(8,128)(2,1)}, bf16[8,14336]{1,0:T(8,128)(2,1)S(1)}, u32[]{:S(2)}, u32[]{:S(2)}) collective-permute-start(bf16[8,14336]{1,0:T(8,128)(2,1)} %param.3), channel_id=1, source_target_pairs={{0,2},{1,3},{2,6},{3,7},{4,0},{5,1},{6,10},{7,11},{8,4},{9,5},{10,... | collective-permute-start | bytes 688136 | tf_op jit(solution)/shard_map/ppermute | solution.py:162
  2.9 7.6 %collective-permute-start.1 = (bf16[8,14336]{1,0:T(8,128)(2,1)}, bf16[8,14336]{1,0:T(8,128)(2,1)S(1)}, u32[]{:S(2)}, u32[]{:S(2)}) collective-permute-start(bf16[8,14336]{1,0:T(8,128)(2,1)} %param.3), channel_id=1, source_target_pairs={{0,4},{1,5},{2,0},{3,1},{4,8},{5,9},{6,2},{7,3},{8,12},{9,13},{10,... | collective-permute-start | bytes 688136 | tf_op jit(solution)/shard_map/ppermute | solution.py:162
  8.8 7.0 %collective-permute-start.3 = (bf16[8,14336]{1,0:T(8,128)(2,1)S(1)}, bf16[8,14336]{1,0:T(8,128)(2,1)S(1)}, u32[]{:S(2)}, u32[]{:S(2)}) collective-permute-start(bf16[8,14336]{1,0:T(8,128)(2,1)S(1)} %collective-permute-done), channel_id=1, source_target_pairs={{0,2},{1,3},{2,6},{3,7},{4,0},{5,1},{6,10},{7,11},{8,4},{9,5},{10,... | collective-permute-start | bytes 688136 | tf_op jit(solution)/shard_map/ppermute | solution.py:162
  10.5 6.8 %collective-permute-start.4 = (bf16[8,14336]{1,0:T(8,128)(2,1)S(1)}, bf16[8,14336]{1,0:T(8,128)(2,1)S(1)}, u32[]{:S(2)}, u32[]{:S(2)}) collective-permute-start(bf16[8,14336]{1,0:T(8,128)(2,1)S(1)} %collective-permute-done.1), channel_id=1, source_target_pairs={{0,4},{1,5},{2,0},{3,1},{4,8},{5,9},{6,2},{7,3},{8,12},{9,13},{10,... | collective-permute-start | bytes 688136 | tf_op jit(solution)/shard_map/ppermute | solution.py:162
  11.1 13.1 %collective-permute-start.7 = (bf16[8,10752]{1,0:T(8,128)(2,1)S(1)}, bf16[8,10752]{1,0:T(8,128)(2,1)S(1)}, u32[]{:S(2)}, u32[]{:S(2)}) collective-permute-start(bf16[8,10752]{1,0:T(8,128)(2,1)S(1)} %bitcast.18), channel_id=1, source_target_pairs={{0,12},{1,13},{2,14},{3,15},{4,6},{5,7},{6,4},{7,5},{8,10},{9,11},... | collective-permute-start | bytes 516104 | tf_op jit(solution)/shard_map/ppermute | solution.py:162
  14.9 11.3 %collective-permute-start.2 = (bf16[24,14336]{1,0:T(8,128)(2,1)S(1)}, bf16[24,14336]{1,0:T(8,128)(2,1)S(1)}, u32[]{:S(2)}, u32[]{:S(2)}) collective-permute-start(bf16[24,14336]{1,0:T(8,128)(2,1)S(1)} %get-tuple-element.10.refs_0_), channel_id=1, source_target_pairs={{0,1},{1,0},{2,3},{3,2},{4,5},{5,4},{6,7},{7,6},{8,9},{9,8},{10,11... | collective-permute-start | bytes 2064392 | tf_op jit(solution)/shard_map/ppermute | solution.py:162
  15.9 8.3 %collective-permute-start.6 = (bf16[8,10752]{1,0:T(8,128)(2,1)S(1)}, bf16[8,10752]{1,0:T(8,128)(2,1)S(1)}, u32[]{:S(2)}, u32[]{:S(2)}) collective-permute-start(bf16[8,10752]{1,0:T(8,128)(2,1)S(1)} %bitcast.20), channel_id=1, source_target_pairs={{0,2},{1,3},{2,6},{3,7},{4,0},{5,1},{6,10},{7,11},{8,4},{9,5},{10,... | collective-permute-start | bytes 516104 | tf_op jit(solution)/shard_map/ppermute | solution.py:162
  17.4 6.9 %collective-permute-start.9 = (bf16[8,10752]{1,0:T(8,128)(2,1)S(1)}, bf16[8,10752]{1,0:T(8,128)(2,1)S(1)}, u32[]{:S(2)}, u32[]{:S(2)}) collective-permute-start(bf16[8,10752]{1,0:T(8,128)(2,1)S(1)} %bitcast.19), channel_id=1, source_target_pairs={{0,4},{1,5},{2,0},{3,1},{4,8},{5,9},{6,2},{7,3},{8,12},{9,13},{10,... | collective-permute-start | bytes 516104 | tf_op jit(solution)/shard_map/ppermute | solution.py:162
  19.1 7.1 %collective-permute-start.5 = (bf16[16,10752]{1,0:T(8,128)(2,1)S(1)}, bf16[16,10752]{1,0:T(8,128)(2,1)S(1)}, u32[]{:S(2)}, u32[]{:S(2)}) collective-permute-start(bf16[16,10752]{1,0:T(8,128)(2,1)S(1)} %pad_maximum_fusion.1), channel_id=1, source_target_pairs={{0,1},{1,0},{2,3},{3,2},{4,5},{5,4},{6,7},{7,6},{8,9},{9,8},{10,11... | collective-permute-start | bytes 1032200 | tf_op jit(solution)/shard_map/ppermute | solution.py:162
  24.2 2.0 %collective-permute-start.8 = (bf16[16,10752]{1,0:T(8,128)(2,1)S(1)}, bf16[16,10752]{1,0:T(8,128)(2,1)S(1)}, u32[]{:S(2)}, u32[]{:S(2)}) collective-permute-start(bf16[16,10752]{1,0:T(8,128)(2,1)S(1)} %constant_dynamic-update-slice_fusion.3.refs_4_), channel_id=1, source_target_pairs={{0,1},{1,0},{2,3},{3,2},{4,5},{5,4},{6,7},{7,6},{8,9},{9,8},{10,11... | collective-permute-start | bytes 1032200 | tf_op jit(solution)/shard_map/ppermute | solution.py:162
  24.3 1.9 %collective-permute-start.10 = (bf16[8,10752]{1,0:T(8,128)(2,1)S(1)}, bf16[8,10752]{1,0:T(8,128)(2,1)S(1)}, u32[]{:S(2)}, u32[]{:S(2)}) collective-permute-start(bf16[8,10752]{1,0:T(8,128)(2,1)S(1)} %collective-permute-done.9.refs_6_), channel_id=1, source_target_pairs={{0,1},{1,0},{2,3},{3,2},{4,5},{5,4},{6,7},{7,6},{8,9},{9,8},{10,11... | collective-permute-start | bytes 516104 | tf_op jit(solution)/shard_map/ppermute | solution.py:162

commit v24 on v23

--- a/solution.py
+++ b/solution.py
@@ -8,7 +8,7 @@
 from jax.sharding import PartitionSpec as P
 
 BUFFERS = 4
-STRIP = 256
+STRIP = 128
 RING_DEVICES = 16
 
 
@@ -212,10 +212,10 @@
     return 2 * chip + core
 
 
-def ring_kernel(devices, slots, device_ref, table_ref, *refs):
+def ring_kernel(devices, slots, table_ref, *refs):
     groups = refs[:len(GROUPS)]
     out_ref, pair, tiles, zeros, out_sems, zero_sems = refs[len(GROUPS):]
-    device = device_ref[0]
+    device = table_ref[table_ref.shape[0] - 1]
     slab, width = pair.shape[1] // devices, pair.shape[2]
     first = first_needed(devices, device // 2)
 
@@ -305,11 +305,11 @@
     slab, units = tokens.shape
     width = units // devices
     groups = ring_gather(tokens, device, devices)
-    table = jnp.concatenate([slab_lengths, tile_owner])
+    table = jnp.concatenate([slab_lengths, tile_owner, device.reshape(1)])
     return pl.pallas_call(
         functools.partial(ring_kernel, devices, slots),
         out_shape=jax.ShapeDtypeStruct((slots, width, width), jnp.float32),
-        in_specs=[pl.BlockSpec(memory_space=pltpu.SMEM)] * 2
+        in_specs=[pl.BlockSpec(memory_space=pltpu.SMEM)]
         + [pl.BlockSpec(memory_space=pltpu.VMEM)] * len(groups),
         out_specs=pl.BlockSpec(memory_space=pl.ANY),
         scratch_shapes=[
@@ -325,7 +325,7 @@
             bytes_accessed=4 * slots * width * width,
             transcendentals=0,
         ),
-    )(device.reshape(1), table, *groups)
+    )(table, *groups)
 
 
 def per_device(tokens, slab_lengths, tile_owner):

time: 38.9 us -> 38.9 us (level)
  no operation moved by 1% of the time
where the time goes in v24:
time: 38.9 us; the launch traced here: 38.7 us
  Pallas kernels  12.5 us (32%)
  starting transfers between devices  12.4 us (32%)
  waiting for transfers between devices  11.2 us (29%)
  other arithmetic  1.32 us (3%)
  local copies, waits for them, and re-layouts  1.03 us (3%)
    pallas_call x1, Pallas kernels, ring_form(): pl.pallas_call(functools.partial(ring_kernel, devices, slots), out_shape=...  12.5 us
    ppermute x11, starting transfers between devices, send(): return lax.ppermute(value, 'col', list(enumerate(target)))  12.4 us
    ppermute x11, waiting for transfers between devices, send(): return lax.ppermute(value, 'col', list(enumerate(target)))  11.2 us
    unnamed x3, local copies, waits for them, and re-layouts  1.01 us
  transfers between devices with their start and end apart: 11, of which 4 were waited for; matrix products, arithmetic and copies ran while one was open for 6% of the time, Pallas kernels for 0%

profile of v24, /device:TPU:0, one launch (start us, length us, event | category | flops | bytes accessed | tf_op | source)
XLA Modules:
  0.0 38.7 jit_solution(8126919250732421498)
XLA Ops:
  0.0 2.9 %collective-permute-start = (bf16[8,14336]{1,0:T(8,128)(2,1)}, bf16[8,14336]{1,0:T(8,128)(2,1)S(1)}, u32[]{:S(2)}, u32[]{:S(2)}) collective-permute-start(bf16[8,14336]{1,0:T(8,128)(2,1)} %param.3), channel_id=1, source_target_pairs={{0,2},{1,3},{2,6},{3,7},{4,0},{5,1},{6,10},{7,11},{8,4},{9,5},{10,... | collective-permute-start | bytes 688136 | tf_op jit(solution)/shard_map/ppermute | solution.py:162
  2.9 0.1 collective-permute-start.1
  3.0 1.0 %constant_dynamic-update-slice_fusion.2 = bf16[24,14336]{1,0:T(8,128)(2,1)S(1)} fusion(bf16[8,14336]{1,0:T(8,128)(2,1)} %param.3), kind=kLoop, calls=%fused_computation.20 | loop fusion | bytes 458752
  4.2 0.8 %pad_add_fusion.table_ref = s32[153]{0:T(256)S(1)} fusion(s32[1]{0:T(128)} %bitcast, s32[136]{0:T(256)} %param.5, s32[16]{0:T(128)} %param.4), kind=kLoop, calls=%fused_computation.23 | loop fusion | flops 306 | bytes 1224 | tf_op jit(solution)/shard_map/concatenate | solution.py:308
  4.9 3.9 %collective-permute-done = bf16[8,14336]{1,0:T(8,128)(2,1)S(1)} collective-permute-done((bf16[8,14336]{1,0:T(8,128)(2,1)}, bf16[8,14336]{1,0:T(8,128)(2,1)S(1)}, u32[]{:S(2)}, u32[]{:S(2)}) %collective-permute-start) | collective-permute-done | bytes 229408 | tf_op jit(solution)/shard_map/ppermute | solution.py:162
  8.8 1.7 %collective-permute-start.3 = (bf16[8,14336]{1,0:T(8,128)(2,1)S(1)}, bf16[8,14336]{1,0:T(8,128)(2,1)S(1)}, u32[]{:S(2)}, u32[]{:S(2)}) collective-permute-start(bf16[8,14336]{1,0:T(8,128)(2,1)S(1)} %collective-permute-done), channel_id=1, source_target_pairs={{0,2},{1,3},{2,6},{3,7},{4,0},{5,1},{6,10},{7,11},{8,4},{9,5},{10,... | collective-permute-start | bytes 688136 | tf_op jit(solution)/shard_map/ppermute | solution.py:162
  10.5 0.0 collective-permute-done.1
  10.5 0.4 collective-permute-start.4
  10.9 0.1 broadcast_select_fusion
  11.0 0.1 fusion.1
  11.1 3.8 %collective-permute-start.7 = (bf16[8,10752]{1,0:T(8,128)(2,1)S(1)}, bf16[8,10752]{1,0:T(8,128)(2,1)S(1)}, u32[]{:S(2)}, u32[]{:S(2)}) collective-permute-start(bf16[8,10752]{1,0:T(8,128)(2,1)S(1)} %bitcast.18), channel_id=1, source_target_pairs={{0,12},{1,13},{2,14},{3,15},{4,6},{5,7},{6,4},{7,5},{8,10},{9,11},... | collective-permute-start | bytes 516104 | tf_op jit(solution)/shard_map/ppermute | solution.py:162
  14.9 0.0 collective-permute-start.2
  14.9 0.9 %collective-permute-done.3 = bf16[8,14336]{1,0:T(8,128)(2,1)S(1)} collective-permute-done((bf16[8,14336]{1,0:T(8,128)(2,1)S(1)}, bf16[8,14336]{1,0:T(8,128)(2,1)S(1)}, u32[]{:S(2)}, u32[]{:S(2)}) %collective-permute-start.3) | collective-permute-done | bytes 229408 | tf_op jit(solution)/shard_map/ppermute | solution.py:162
  15.8 0.1 fusion.2
  15.9 1.4 %collective-permute-start.6 = (bf16[8,10752]{1,0:T(8,128)(2,1)S(1)}, bf16[8,10752]{1,0:T(8,128)(2,1)S(1)}, u32[]{:S(2)}, u32[]{:S(2)}) collective-permute-start(bf16[8,10752]{1,0:T(8,128)(2,1)S(1)} %bitcast.20), channel_id=1, source_target_pairs={{0,2},{1,3},{2,6},{3,7},{4,0},{5,1},{6,10},{7,11},{8,4},{9,5},{10,... | collective-permute-start | bytes 516104 | tf_op jit(solution)/shard_map/ppermute | solution.py:162
  17.3 0.0 collective-permute-done.4
  17.3 0.1 fusion
  17.4 1.5 %collective-permute-start.9 = (bf16[8,10752]{1,0:T(8,128)(2,1)S(1)}, bf16[8,10752]{1,0:T(8,128)(2,1)S(1)}, u32[]{:S(2)}, u32[]{:S(2)}) collective-permute-start(bf16[8,10752]{1,0:T(8,128)(2,1)S(1)} %bitcast.19), channel_id=1, source_target_pairs={{0,4},{1,5},{2,0},{3,1},{4,8},{5,9},{6,2},{7,3},{8,12},{9,13},{10,... | collective-permute-start | bytes 516104 | tf_op jit(solution)/shard_map/ppermute | solution.py:162
  18.9 0.2 fusion.3
  19.1 0.1 collective-permute-start.5
  19.2 5.0 %collective-permute-done.6 = bf16[8,10752]{1,0:T(8,128)(2,1)S(1)} collective-permute-done((bf16[8,10752]{1,0:T(8,128)(2,1)S(1)}, bf16[8,10752]{1,0:T(8,128)(2,1)S(1)}, u32[]{:S(2)}, u32[]{:S(2)}) %collective-permute-start.6) | collective-permute-done | bytes 172064 | tf_op jit(solution)/shard_map/ppermute | solution.py:162
  24.2 0.0 collective-permute-done.7
  24.2 0.1 collective-permute-start.8
  24.3 0.0 collective-permute-done.9.refs_6_
  24.3 0.5 %collective-permute-start.10 = (bf16[8,10752]{1,0:T(8,128)(2,1)S(1)}, bf16[8,10752]{1,0:T(8,128)(2,1)S(1)}, u32[]{:S(2)}, u32[]{:S(2)}) collective-permute-start(bf16[8,10752]{1,0:T(8,128)(2,1)S(1)} %collective-permute-done.9.refs_6_), channel_id=1, source_target_pairs={{0,1},{1,0},{2,3},{3,2},{4,5},{5,4},{6,7},{7,6},{8,9},{9,8},{10,11... | collective-permute-start | bytes 516104 | tf_op jit(solution)/shard_map/ppermute | solution.py:162
  24.8 1.4 %collective-permute-done.10.refs_7_ = bf16[8,10752]{1,0:T(8,128)(2,1)S(1)} collective-permute-done((bf16[8,10752]{1,0:T(8,128)(2,1)S(1)}, bf16[8,10752]{1,0:T(8,128)(2,1)S(1)}, u32[]{:S(2)}, u32[]{:S(2)}) %collective-permute-start.10) | collective-permute-done | bytes 172064 | tf_op jit(solution)/shard_map/ppermute | solution.py:162
  26.2 0.0 collective-permute-done.5.refs_3_
  26.2 0.0 collective-permute-done.2.refs_1_
  26.2 0.0 collective-permute-done.8.refs_5_
  26.2 12.5 %shard_map.37 = f32[11,896,896]{2,1,0:T(8,128)} custom-call(s32[153]{0:T(256)S(1)} %pad_add_fusion.table_ref, bf16[24,14336]{1,0:T(8,128)(2,1)S(1)} %get-tuple-element.10.refs_0_, bf16[24,14336]{1,0:T(8,128)(2,1)S(1)} %collective-permute-done.2.refs_1_, bf16[16,14336]{1,0:T(8,128)(2,1)S(1)} %pad_maximum_fusion.refs_2_, ...), custom_call_target="tpu_custom_call" | custom-call | flops 2260729856 | bytes 35323904 | tf_op jit(solution)/shard_map/pallas_call | solution.py:309
  (5 shorter events, 0.1 us)
Async XLA Ops:
  0.0 8.8 %collective-permute-start = (bf16[8,14336]{1,0:T(8,128)(2,1)}, bf16[8,14336]{1,0:T(8,128)(2,1)S(1)}, u32[]{:S(2)}, u32[]{:S(2)}) collective-permute-start(bf16[8,14336]{1,0:T(8,128)(2,1)} %param.3), channel_id=1, source_target_pairs={{0,2},{1,3},{2,6},{3,7},{4,0},{5,1},{6,10},{7,11},{8,4},{9,5},{10,... | collective-permute-start | bytes 688136 | tf_op jit(solution)/shard_map/ppermute | solution.py:162
  2.9 7.6 %collective-permute-start.1 = (bf16[8,14336]{1,0:T(8,128)(2,1)}, bf16[8,14336]{1,0:T(8,128)(2,1)S(1)}, u32[]{:S(2)}, u32[]{:S(2)}) collective-permute-start(bf16[8,14336]{1,0:T(8,128)(2,1)} %param.3), channel_id=1, source_target_pairs={{0,4},{1,5},{2,0},{3,1},{4,8},{5,9},{6,2},{7,3},{8,12},{9,13},{10,... | collective-permute-start | bytes 688136 | tf_op jit(solution)/shard_map/ppermute | solution.py:162
  8.8 7.0 %collective-permute-start.3 = (bf16[8,14336]{1,0:T(8,128)(2,1)S(1)}, bf16[8,14336]{1,0:T(8,128)(2,1)S(1)}, u32[]{:S(2)}, u32[]{:S(2)}) collective-permute-start(bf16[8,14336]{1,0:T(8,128)(2,1)S(1)} %collective-permute-done), channel_id=1, source_target_pairs={{0,2},{1,3},{2,6},{3,7},{4,0},{5,1},{6,10},{7,11},{8,4},{9,5},{10,... | collective-permute-start | bytes 688136 | tf_op jit(solution)/shard_map/ppermute | solution.py:162
  10.5 6.8 %collective-permute-start.4 = (bf16[8,14336]{1,0:T(8,128)(2,1)S(1)}, bf16[8,14336]{1,0:T(8,128)(2,1)S(1)}, u32[]{:S(2)}, u32[]{:S(2)}) collective-permute-start(bf16[8,14336]{1,0:T(8,128)(2,1)S(1)} %collective-permute-done.1), channel_id=1, source_target_pairs={{0,4},{1,5},{2,0},{3,1},{4,8},{5,9},{6,2},{7,3},{8,12},{9,13},{10,... | collective-permute-start | bytes 688136 | tf_op jit(solution)/shard_map/ppermute | solution.py:162
  11.1 13.1 %collective-permute-start.7 = (bf16[8,10752]{1,0:T(8,128)(2,1)S(1)}, bf16[8,10752]{1,0:T(8,128)(2,1)S(1)}, u32[]{:S(2)}, u32[]{:S(2)}) collective-permute-start(bf16[8,10752]{1,0:T(8,128)(2,1)S(1)} %bitcast.18), channel_id=1, source_target_pairs={{0,12},{1,13},{2,14},{3,15},{4,6},{5,7},{6,4},{7,5},{8,10},{9,11},... | collective-permute-start | bytes 516104 | tf_op jit(solution)/shard_map/ppermute | solution.py:162
  14.9 11.3 %collective-permute-start.2 = (bf16[24,14336]{1,0:T(8,128)(2,1)S(1)}, bf16[24,14336]{1,0:T(8,128)(2,1)S(1)}, u32[]{:S(2)}, u32[]{:S(2)}) collective-permute-start(bf16[24,14336]{1,0:T(8,128)(2,1)S(1)} %get-tuple-element.10.refs_0_), channel_id=1, source_target_pairs={{0,1},{1,0},{2,3},{3,2},{4,5},{5,4},{6,7},{7,6},{8,9},{9,8},{10,11... | collective-permute-start | bytes 2064392 | tf_op jit(solution)/shard_map/ppermute | solution.py:162
  15.9 8.3 %collective-permute-start.6 = (bf16[8,10752]{1,0:T(8,128)(2,1)S(1)}, bf16[8,10752]{1,0:T(8,128)(2,1)S(1)}, u32[]{:S(2)}, u32[]{:S(2)}) collective-permute-start(bf16[8,10752]{1,0:T(8,128)(2,1)S(1)} %bitcast.20), channel_id=1, source_target_pairs={{0,2},{1,3},{2,6},{3,7},{4,0},{5,1},{6,10},{7,11},{8,4},{9,5},{10,... | collective-permute-start | bytes 516104 | tf_op jit(solution)/shard_map/ppermute | solution.py:162
  17.4 6.9 %collective-permute-start.9 = (bf16[8,10752]{1,0:T(8,128)(2,1)S(1)}, bf16[8,10752]{1,0:T(8,128)(2,1)S(1)}, u32[]{:S(2)}, u32[]{:S(2)}) collective-permute-start(bf16[8,10752]{1,0:T(8,128)(2,1)S(1)} %bitcast.19), channel_id=1, source_target_pairs={{0,4},{1,5},{2,0},{3,1},{4,8},{5,9},{6,2},{7,3},{8,12},{9,13},{10,... | collective-permute-start | bytes 516104 | tf_op jit(solution)/shard_map/ppermute | solution.py:162
  19.1 7.1 %collective-permute-start.5 = (bf16[16,10752]{1,0:T(8,128)(2,1)S(1)}, bf16[16,10752]{1,0:T(8,128)(2,1)S(1)}, u32[]{:S(2)}, u32[]{:S(2)}) collective-permute-start(bf16[16,10752]{1,0:T(8,128)(2,1)S(1)} %pad_maximum_fusion.1), channel_id=1, source_target_pairs={{0,1},{1,0},{2,3},{3,2},{4,5},{5,4},{6,7},{7,6},{8,9},{9,8},{10,11... | collective-permute-start | bytes 1032200 | tf_op jit(solution)/shard_map/ppermute | solution.py:162
  24.2 2.0 %collective-permute-start.8 = (bf16[16,10752]{1,0:T(8,128)(2,1)S(1)}, bf16[16,10752]{1,0:T(8,128)(2,1)S(1)}, u32[]{:S(2)}, u32[]{:S(2)}) collective-permute-start(bf16[16,10752]{1,0:T(8,128)(2,1)S(1)} %constant_dynamic-update-slice_fusion.3.refs_4_), channel_id=1, source_target_pairs={{0,1},{1,0},{2,3},{3,2},{4,5},{5,4},{6,7},{7,6},{8,9},{9,8},{10,11... | collective-permute-start | bytes 1032200 | tf_op jit(solution)/shard_map/ppermute | solution.py:162
  24.3 1.9 %collective-permute-start.10 = (bf16[8,10752]{1,0:T(8,128)(2,1)S(1)}, bf16[8,10752]{1,0:T(8,128)(2,1)S(1)}, u32[]{:S(2)}, u32[]{:S(2)}) collective-permute-start(bf16[8,10752]{1,0:T(8,128)(2,1)S(1)} %collective-permute-done.9.refs_6_), channel_id=1, source_target_pairs={{0,1},{1,0},{2,3},{3,2},{4,5},{5,4},{6,7},{7,6},{8,9},{9,8},{10,11... | collective-permute-start | bytes 516104 | tf_op jit(solution)/shard_map/ppermute | solution.py:162

commit v25 on v24

--- a/solution.py
+++ b/solution.py
@@ -194,7 +194,7 @@
     near = jnp.concatenate((tokens, ahead[1], back[1]), axis=0)
     middle = jnp.concatenate((ahead[2], back[2]), axis=0)
     last = jnp.concatenate((ahead[3], half), axis=0)
-    near_beside = send(near, sibling)
+    near_beside = send(after(near, ahead[2], back[2]), sibling)
     needed = [window(after(value, ahead[2], back[2]), chip) for value in (ahead[2], back[2])]
     middle_beside = send(jnp.concatenate(needed, axis=0), sibling)
     last_beside = send(last, sibling)

time: 38.9 us -> 38.8 us (level); the launches traced: 38.7 us -> 38 us
  waiting for transfers between devices: 11.2 us -> 9.94 us
  starting transfers between devices: 12.4 us -> 12.9 us
    ppermute x11, waiting for transfers between devices: 11.2 us -> 9.94 us  [send(): return lax.ppermute(value, 'col', list(enumerate(target)))]
    ppermute x11, starting transfers between devices: 12.4 us -> 12.9 us  [send(): return lax.ppermute(value, 'col', list(enumerate(target)))]
where the time goes in v25:
time: 38.8 us; the launch traced here: 38 us
  starting transfers between devices  12.9 us (33%)
  Pallas kernels  12.5 us (32%)
  waiting for transfers between devices  9.94 us (26%)
  other arithmetic  1.32 us (3%)
  local copies, waits for them, and re-layouts  1.03 us (3%)
    ppermute x11, starting transfers between devices, send(): return lax.ppermute(value, 'col', list(enumerate(target)))  12.9 us
    pallas_call x1, Pallas kernels, ring_form(): pl.pallas_call(functools.partial(ring_kernel, devices, slots), out_shape=...  12.5 us
    ppermute x11, waiting for transfers between devices, send(): return lax.ppermute(value, 'col', list(enumerate(target)))  9.94 us
    unnamed x3, local copies, waits for them, and re-layouts  1.01 us
  transfers between devices with their start and end apart: 11, of which 4 were waited for; matrix products, arithmetic and copies ran while one was open for 6% of the time, Pallas kernels for 0%

profile of v25, /device:TPU:0, one launch (start us, length us, event | category | flops | bytes accessed | tf_op | source)
XLA Modules:
  0.0 38.0 jit_solution(17494077624062084864)
XLA Ops:
  0.0 2.9 %collective-permute-start = (bf16[8,14336]{1,0:T(8,128)(2,1)}, bf16[8,14336]{1,0:T(8,128)(2,1)S(1)}, u32[]{:S(2)}, u32[]{:S(2)}) collective-permute-start(bf16[8,14336]{1,0:T(8,128)(2,1)} %param.3), channel_id=1, source_target_pairs={{0,2},{1,3},{2,6},{3,7},{4,0},{5,1},{6,10},{7,11},{8,4},{9,5},{10,... | collective-permute-start | bytes 688136 | tf_op jit(solution)/shard_map/ppermute | solution.py:162
  2.9 0.1 collective-permute-start.1
  3.0 1.0 %constant_dynamic-update-slice_fusion.2 = bf16[24,14336]{1,0:T(8,128)(2,1)S(1)} fusion(bf16[8,14336]{1,0:T(8,128)(2,1)} %param.3), kind=kLoop, calls=%fused_computation.20 | loop fusion | bytes 458752
  4.2 0.8 %pad_add_fusion.table_ref = s32[153]{0:T(256)S(1)} fusion(s32[1]{0:T(128)} %bitcast, s32[136]{0:T(256)} %param.5, s32[16]{0:T(128)} %param.4), kind=kLoop, calls=%fused_computation.23 | loop fusion | flops 306 | bytes 1224 | tf_op jit(solution)/shard_map/concatenate | solution.py:308
  4.9 3.9 %collective-permute-done = bf16[8,14336]{1,0:T(8,128)(2,1)S(1)} collective-permute-done((bf16[8,14336]{1,0:T(8,128)(2,1)}, bf16[8,14336]{1,0:T(8,128)(2,1)S(1)}, u32[]{:S(2)}, u32[]{:S(2)}) %collective-permute-start) | collective-permute-done | bytes 229408 | tf_op jit(solution)/shard_map/ppermute | solution.py:162
  8.8 1.7 %collective-permute-start.2 = (bf16[8,14336]{1,0:T(8,128)(2,1)S(1)}, bf16[8,14336]{1,0:T(8,128)(2,1)S(1)}, u32[]{:S(2)}, u32[]{:S(2)}) collective-permute-start(bf16[8,14336]{1,0:T(8,128)(2,1)S(1)} %collective-permute-done), channel_id=1, source_target_pairs={{0,2},{1,3},{2,6},{3,7},{4,0},{5,1},{6,10},{7,11},{8,4},{9,5},{10,... | collective-permute-start | bytes 688136 | tf_op jit(solution)/shard_map/ppermute | solution.py:162
  10.5 0.0 collective-permute-done.1
  10.5 0.4 collective-permute-start.3
  10.9 0.1 broadcast_select_fusion
  11.0 0.1 fusion.1
  11.1 3.8 %collective-permute-start.7 = (bf16[8,10752]{1,0:T(8,128)(2,1)S(1)}, bf16[8,10752]{1,0:T(8,128)(2,1)S(1)}, u32[]{:S(2)}, u32[]{:S(2)}) collective-permute-start(bf16[8,10752]{1,0:T(8,128)(2,1)S(1)} %bitcast.18), channel_id=1, source_target_pairs={{0,12},{1,13},{2,14},{3,15},{4,6},{5,7},{6,4},{7,5},{8,10},{9,11},... | collective-permute-start | bytes 516104 | tf_op jit(solution)/shard_map/ppermute | solution.py:162
  14.9 0.9 %collective-permute-done.2 = bf16[8,14336]{1,0:T(8,128)(2,1)S(1)} collective-permute-done((bf16[8,14336]{1,0:T(8,128)(2,1)S(1)}, bf16[8,14336]{1,0:T(8,128)(2,1)S(1)}, u32[]{:S(2)}, u32[]{:S(2)}) %collective-permute-start.2) | collective-permute-done | bytes 229408 | tf_op jit(solution)/shard_map/ppermute | solution.py:162
  15.8 0.1 fusion.2
  15.9 1.4 %collective-permute-start.6 = (bf16[8,10752]{1,0:T(8,128)(2,1)S(1)}, bf16[8,10752]{1,0:T(8,128)(2,1)S(1)}, u32[]{:S(2)}, u32[]{:S(2)}) collective-permute-start(bf16[8,10752]{1,0:T(8,128)(2,1)S(1)} %bitcast.20), channel_id=1, source_target_pairs={{0,2},{1,3},{2,6},{3,7},{4,0},{5,1},{6,10},{7,11},{8,4},{9,5},{10,... | collective-permute-start | bytes 516104 | tf_op jit(solution)/shard_map/ppermute | solution.py:162
  17.3 0.0 collective-permute-done.3
  17.3 0.1 fusion
  17.4 1.5 %collective-permute-start.9 = (bf16[8,10752]{1,0:T(8,128)(2,1)S(1)}, bf16[8,10752]{1,0:T(8,128)(2,1)S(1)}, u32[]{:S(2)}, u32[]{:S(2)}) collective-permute-start(bf16[8,10752]{1,0:T(8,128)(2,1)S(1)} %bitcast.19), channel_id=1, source_target_pairs={{0,4},{1,5},{2,0},{3,1},{4,8},{5,9},{6,2},{7,3},{8,12},{9,13},{10,... | collective-permute-start | bytes 516104 | tf_op jit(solution)/shard_map/ppermute | solution.py:162
  18.9 0.2 fusion.3
  19.1 0.1 collective-permute-start.5
  19.2 0.5 %collective-permute-start.4 = (bf16[24,14336]{1,0:T(8,128)(2,1)S(1)}, bf16[24,14336]{1,0:T(8,128)(2,1)S(1)}, u32[]{:S(2)}, u32[]{:S(2)}) collective-permute-start(bf16[24,14336]{1,0:T(8,128)(2,1)S(1)} %get-tuple-element.8.refs_0_), channel_id=1, source_target_pairs={{0,1},{1,0},{2,3},{3,2},{4,5},{5,4},{6,7},{7,6},{8,9},{9,8},{10,11... | collective-permute-start | bytes 2064392 | tf_op jit(solution)/shard_map/ppermute | solution.py:162
  19.7 3.8 %collective-permute-done.6 = bf16[8,10752]{1,0:T(8,128)(2,1)S(1)} collective-permute-done((bf16[8,10752]{1,0:T(8,128)(2,1)S(1)}, bf16[8,10752]{1,0:T(8,128)(2,1)S(1)}, u32[]{:S(2)}, u32[]{:S(2)}) %collective-permute-start.6) | collective-permute-done | bytes 172064 | tf_op jit(solution)/shard_map/ppermute | solution.py:162
  23.5 0.0 collective-permute-done.7
  23.5 0.1 collective-permute-start.8
  23.6 0.0 collective-permute-done.9.refs_6_
  23.6 0.5 %collective-permute-start.10 = (bf16[8,10752]{1,0:T(8,128)(2,1)S(1)}, bf16[8,10752]{1,0:T(8,128)(2,1)S(1)}, u32[]{:S(2)}, u32[]{:S(2)}) collective-permute-start(bf16[8,10752]{1,0:T(8,128)(2,1)S(1)} %collective-permute-done.9.refs_6_), channel_id=1, source_target_pairs={{0,1},{1,0},{2,3},{3,2},{4,5},{5,4},{6,7},{7,6},{8,9},{9,8},{10,11... | collective-permute-start | bytes 516104 | tf_op jit(solution)/shard_map/ppermute | solution.py:162
  24.1 1.4 %collective-permute-done.10.refs_7_ = bf16[8,10752]{1,0:T(8,128)(2,1)S(1)} collective-permute-done((bf16[8,10752]{1,0:T(8,128)(2,1)S(1)}, bf16[8,10752]{1,0:T(8,128)(2,1)S(1)}, u32[]{:S(2)}, u32[]{:S(2)}) %collective-permute-start.10) | collective-permute-done | bytes 172064 | tf_op jit(solution)/shard_map/ppermute | solution.py:162
  25.5 0.0 collective-permute-done.5.refs_3_
  25.5 0.0 collective-permute-done.8.refs_5_
  25.5 0.0 collective-permute-done.4.refs_1_
  25.5 12.5 %shard_map.37 = f32[11,896,896]{2,1,0:T(8,128)} custom-call(s32[153]{0:T(256)S(1)} %pad_add_fusion.table_ref, bf16[24,14336]{1,0:T(8,128)(2,1)S(1)} %get-tuple-element.8.refs_0_, bf16[24,14336]{1,0:T(8,128)(2,1)S(1)} %collective-permute-done.4.refs_1_, bf16[16,14336]{1,0:T(8,128)(2,1)S(1)} %pad_maximum_fusion.refs_2_, ...), custom_call_target="tpu_custom_call" | custom-call | flops 2260729856 | bytes 35323904 | tf_op jit(solution)/shard_map/pallas_call | solution.py:309
  (5 shorter events, 0.1 us)
Async XLA Ops:
  0.0 8.8 %collective-permute-start = (bf16[8,14336]{1,0:T(8,128)(2,1)}, bf16[8,14336]{1,0:T(8,128)(2,1)S(1)}, u32[]{:S(2)}, u32[]{:S(2)}) collective-permute-start(bf16[8,14336]{1,0:T(8,128)(2,1)} %param.3), channel_id=1, source_target_pairs={{0,2},{1,3},{2,6},{3,7},{4,0},{5,1},{6,10},{7,11},{8,4},{9,5},{10,... | collective-permute-start | bytes 688136 | tf_op jit(solution)/shard_map/ppermute | solution.py:162
  2.9 7.6 %collective-permute-start.1 = (bf16[8,14336]{1,0:T(8,128)(2,1)}, bf16[8,14336]{1,0:T(8,128)(2,1)S(1)}, u32[]{:S(2)}, u32[]{:S(2)}) collective-permute-start(bf16[8,14336]{1,0:T(8,128)(2,1)} %param.3), channel_id=1, source_target_pairs={{0,4},{1,5},{2,0},{3,1},{4,8},{5,9},{6,2},{7,3},{8,12},{9,13},{10,... | collective-permute-start | bytes 688136 | tf_op jit(solution)/shard_map/ppermute | solution.py:162
  8.8 7.0 %collective-permute-start.2 = (bf16[8,14336]{1,0:T(8,128)(2,1)S(1)}, bf16[8,14336]{1,0:T(8,128)(2,1)S(1)}, u32[]{:S(2)}, u32[]{:S(2)}) collective-permute-start(bf16[8,14336]{1,0:T(8,128)(2,1)S(1)} %collective-permute-done), channel_id=1, source_target_pairs={{0,2},{1,3},{2,6},{3,7},{4,0},{5,1},{6,10},{7,11},{8,4},{9,5},{10,... | collective-permute-start | bytes 688136 | tf_op jit(solution)/shard_map/ppermute | solution.py:162
  10.5 6.8 %collective-permute-start.3 = (bf16[8,14336]{1,0:T(8,128)(2,1)S(1)}, bf16[8,14336]{1,0:T(8,128)(2,1)S(1)}, u32[]{:S(2)}, u32[]{:S(2)}) collective-permute-start(bf16[8,14336]{1,0:T(8,128)(2,1)S(1)} %collective-permute-done.1), channel_id=1, source_target_pairs={{0,4},{1,5},{2,0},{3,1},{4,8},{5,9},{6,2},{7,3},{8,12},{9,13},{10,... | collective-permute-start | bytes 688136 | tf_op jit(solution)/shard_map/ppermute | solution.py:162
  11.1 12.4 %collective-permute-start.7 = (bf16[8,10752]{1,0:T(8,128)(2,1)S(1)}, bf16[8,10752]{1,0:T(8,128)(2,1)S(1)}, u32[]{:S(2)}, u32[]{:S(2)}) collective-permute-start(bf16[8,10752]{1,0:T(8,128)(2,1)S(1)} %bitcast.18), channel_id=1, source_target_pairs={{0,12},{1,13},{2,14},{3,15},{4,6},{5,7},{6,4},{7,5},{8,10},{9,11},... | collective-permute-start | bytes 516104 | tf_op jit(solution)/shard_map/ppermute | solution.py:162
  15.9 7.5 %collective-permute-start.6 = (bf16[8,10752]{1,0:T(8,128)(2,1)S(1)}, bf16[8,10752]{1,0:T(8,128)(2,1)S(1)}, u32[]{:S(2)}, u32[]{:S(2)}) collective-permute-start(bf16[8,10752]{1,0:T(8,128)(2,1)S(1)} %bitcast.20), channel_id=1, source_target_pairs={{0,2},{1,3},{2,6},{3,7},{4,0},{5,1},{6,10},{7,11},{8,4},{9,5},{10,... | collective-permute-start | bytes 516104 | tf_op jit(solution)/shard_map/ppermute | solution.py:162
  17.4 6.2 %collective-permute-start.9 = (bf16[8,10752]{1,0:T(8,128)(2,1)S(1)}, bf16[8,10752]{1,0:T(8,128)(2,1)S(1)}, u32[]{:S(2)}, u32[]{:S(2)}) collective-permute-start(bf16[8,10752]{1,0:T(8,128)(2,1)S(1)} %bitcast.19), channel_id=1, source_target_pairs={{0,4},{1,5},{2,0},{3,1},{4,8},{5,9},{6,2},{7,3},{8,12},{9,13},{10,... | collective-permute-start | bytes 516104 | tf_op jit(solution)/shard_map/ppermute | solution.py:162
  19.1 6.3 %collective-permute-start.5 = (bf16[16,10752]{1,0:T(8,128)(2,1)S(1)}, bf16[16,10752]{1,0:T(8,128)(2,1)S(1)}, u32[]{:S(2)}, u32[]{:S(2)}) collective-permute-start(bf16[16,10752]{1,0:T(8,128)(2,1)S(1)} %pad_maximum_fusion.1), channel_id=1, source_target_pairs={{0,1},{1,0},{2,3},{3,2},{4,5},{5,4},{6,7},{7,6},{8,9},{9,8},{10,11... | collective-permute-start | bytes 1032200 | tf_op jit(solution)/shard_map/ppermute | solution.py:162
  19.2 6.3 %collective-permute-start.4 = (bf16[24,14336]{1,0:T(8,128)(2,1)S(1)}, bf16[24,14336]{1,0:T(8,128)(2,1)S(1)}, u32[]{:S(2)}, u32[]{:S(2)}) collective-permute-start(bf16[24,14336]{1,0:T(8,128)(2,1)S(1)} %get-tuple-element.8.refs_0_), channel_id=1, source_target_pairs={{0,1},{1,0},{2,3},{3,2},{4,5},{5,4},{6,7},{7,6},{8,9},{9,8},{10,11... | collective-permute-start | bytes 2064392 | tf_op jit(solution)/shard_map/ppermute | solution.py:162
  23.5 2.0 %collective-permute-start.8 = (bf16[16,10752]{1,0:T(8,128)(2,1)S(1)}, bf16[16,10752]{1,0:T(8,128)(2,1)S(1)}, u32[]{:S(2)}, u32[]{:S(2)}) collective-permute-start(bf16[16,10752]{1,0:T(8,128)(2,1)S(1)} %constant_dynamic-update-slice_fusion.3.refs_4_), channel_id=1, source_target_pairs={{0,1},{1,0},{2,3},{3,2},{4,5},{5,4},{6,7},{7,6},{8,9},{9,8},{10,11... | collective-permute-start | bytes 1032200 | tf_op jit(solution)/shard_map/ppermute | solution.py:162
  23.6 1.9 %collective-permute-start.10 = (bf16[8,10752]{1,0:T(8,128)(2,1)S(1)}, bf16[8,10752]{1,0:T(8,128)(2,1)S(1)}, u32[]{:S(2)}, u32[]{:S(2)}) collective-permute-start(bf16[8,10752]{1,0:T(8,128)(2,1)S(1)} %collective-permute-done.9.refs_6_), channel_id=1, source_target_pairs={{0,1},{1,0},{2,3},{3,2},{4,5},{5,4},{6,7},{7,6},{8,9},{9,8},{10,11... | collective-permute-start | bytes 516104 | tf_op jit(solution)/shard_map/ppermute | solution.py:162

commit v26 on v25

--- a/solution.py
+++ b/solution.py
@@ -194,9 +194,11 @@
     near = jnp.concatenate((tokens, ahead[1], back[1]), axis=0)
     middle = jnp.concatenate((ahead[2], back[2]), axis=0)
     last = jnp.concatenate((ahead[3], half), axis=0)
-    near_beside = send(after(near, ahead[2], back[2]), sibling)
-    needed = [window(after(value, ahead[2], back[2]), chip) for value in (ahead[2], back[2])]
-    middle_beside = send(jnp.concatenate(needed, axis=0), sibling)
+    near_rows = after(near, ahead[2], back[2])
+    near_cut = [window(near_rows[at:at + slab], chip) for at in range(0, 3 * slab, slab)]
+    near_beside = send(jnp.concatenate(near_cut, axis=0), sibling)
+    middle_cut = [window(after(value, ahead[2], back[2]), chip) for value in (ahead[2], back[2])]
+    middle_beside = send(jnp.concatenate(middle_cut, axis=0), sibling)
     last_beside = send(last, sibling)
     return [near, near_beside, middle, middle_beside, last, last_beside, back[3], send(back[3], sibling)]
 

time: 38.8 us -> 38.7 us (level)
  waiting for transfers between devices: 9.94 us -> 9.5 us
    ppermute x11, waiting for transfers between devices: 9.94 us -> 9.5 us  [send(): return lax.ppermute(value, 'col', list(enumerate(target)))]
  transfers between devices with their start and end apart: 11 -> 11, of which waited for: 4 -> 4; matrix products, arithmetic and copies ran while one was open for 6% -> 7% of each run, Pallas kernels for 0% -> 0%
where the time goes in v26:
time: 38.7 us; the launch traced here: 38 us
  starting transfers between devices  13 us (34%)
  Pallas kernels  12.5 us (32%)
  waiting for transfers between devices  9.5 us (25%)
  other arithmetic  1.63 us (4%)
  local copies, waits for them, and re-layouts  1.08 us (3%)
    ppermute x11, starting transfers between devices, send(): return lax.ppermute(value, 'col', list(enumerate(target)))  13 us
    pallas_call x1, Pallas kernels, ring_form(): pl.pallas_call(functools.partial(ring_kernel, devices, slots), out_shape=...  12.5 us
    ppermute x11, waiting for transfers between devices, send(): return lax.ppermute(value, 'col', list(enumerate(target)))  9.5 us
    unnamed x3, local copies, waits for them, and re-layouts  1.01 us
  transfers between devices with their start and end apart: 11, of which 4 were waited for; matrix products, arithmetic and copies ran while one was open for 7% of the time, Pallas kernels for 0%

profile of v26, /device:TPU:0, one launch (start us, length us, event | category | flops | bytes accessed | tf_op | source)
XLA Modules:
  0.0 38.0 jit_solution(8121224304965283573)
XLA Ops:
  0.0 2.9 %collective-permute-start = (bf16[8,14336]{1,0:T(8,128)(2,1)}, bf16[8,14336]{1,0:T(8,128)(2,1)S(1)}, u32[]{:S(2)}, u32[]{:S(2)}) collective-permute-start(bf16[8,14336]{1,0:T(8,128)(2,1)} %param.3), channel_id=1, source_target_pairs={{0,2},{1,3},{2,6},{3,7},{4,0},{5,1},{6,10},{7,11},{8,4},{9,5},{10,... | collective-permute-start | bytes 688136 | tf_op jit(solution)/shard_map/ppermute | solution.py:162
  2.9 0.1 collective-permute-start.1
  3.0 1.0 %constant_dynamic-update-slice_fusion.2 = bf16[24,14336]{1,0:T(8,128)(2,1)S(1)} fusion(bf16[8,14336]{1,0:T(8,128)(2,1)} %param.3), kind=kLoop, calls=%fused_computation.30 | loop fusion | bytes 458752
  4.2 0.8 %pad_add_fusion.table_ref = s32[153]{0:T(256)S(1)} fusion(s32[1]{0:T(128)} %bitcast, s32[136]{0:T(256)} %param.5, s32[16]{0:T(128)} %param.4), kind=kLoop, calls=%fused_computation.33 | loop fusion | flops 306 | bytes 1224 | tf_op jit(solution)/shard_map/concatenate | solution.py:310
  4.9 3.9 %collective-permute-done = bf16[8,14336]{1,0:T(8,128)(2,1)S(1)} collective-permute-done((bf16[8,14336]{1,0:T(8,128)(2,1)}, bf16[8,14336]{1,0:T(8,128)(2,1)S(1)}, u32[]{:S(2)}, u32[]{:S(2)}) %collective-permute-start) | collective-permute-done | bytes 229408 | tf_op jit(solution)/shard_map/ppermute | solution.py:162
  8.8 1.7 %collective-permute-start.2 = (bf16[8,14336]{1,0:T(8,128)(2,1)S(1)}, bf16[8,14336]{1,0:T(8,128)(2,1)S(1)}, u32[]{:S(2)}, u32[]{:S(2)}) collective-permute-start(bf16[8,14336]{1,0:T(8,128)(2,1)S(1)} %collective-permute-done), channel_id=1, source_target_pairs={{0,2},{1,3},{2,6},{3,7},{4,0},{5,1},{6,10},{7,11},{8,4},{9,5},{10,... | collective-permute-start | bytes 688136 | tf_op jit(solution)/shard_map/ppermute | solution.py:162
  10.5 0.0 collective-permute-done.1
  10.5 0.4 collective-permute-start.3
  10.9 0.1 broadcast_select_fusion
  11.0 0.1 fusion.1
  11.1 3.8 %collective-permute-start.7 = (bf16[8,10752]{1,0:T(8,128)(2,1)S(1)}, bf16[8,10752]{1,0:T(8,128)(2,1)S(1)}, u32[]{:S(2)}, u32[]{:S(2)}) collective-permute-start(bf16[8,10752]{1,0:T(8,128)(2,1)S(1)} %bitcast.30), channel_id=1, source_target_pairs={{0,12},{1,13},{2,14},{3,15},{4,6},{5,7},{6,4},{7,5},{8,10},{9,11},... | collective-permute-start | bytes 516104 | tf_op jit(solution)/shard_map/ppermute | solution.py:162
  14.9 0.9 %collective-permute-done.2 = bf16[8,14336]{1,0:T(8,128)(2,1)S(1)} collective-permute-done((bf16[8,14336]{1,0:T(8,128)(2,1)S(1)}, bf16[8,14336]{1,0:T(8,128)(2,1)S(1)}, u32[]{:S(2)}, u32[]{:S(2)}) %collective-permute-start.2) | collective-permute-done | bytes 229408 | tf_op jit(solution)/shard_map/ppermute | solution.py:162
  15.8 0.1 fusion.2
  15.9 1.4 %collective-permute-start.6 = (bf16[8,10752]{1,0:T(8,128)(2,1)S(1)}, bf16[8,10752]{1,0:T(8,128)(2,1)S(1)}, u32[]{:S(2)}, u32[]{:S(2)}) collective-permute-start(bf16[8,10752]{1,0:T(8,128)(2,1)S(1)} %bitcast.32), channel_id=1, source_target_pairs={{0,2},{1,3},{2,6},{3,7},{4,0},{5,1},{6,10},{7,11},{8,4},{9,5},{10,... | collective-permute-start | bytes 516104 | tf_op jit(solution)/shard_map/ppermute | solution.py:162
  17.3 0.0 collective-permute-done.3
  17.3 0.1 fusion
  17.4 1.5 %collective-permute-start.9 = (bf16[8,10752]{1,0:T(8,128)(2,1)S(1)}, bf16[8,10752]{1,0:T(8,128)(2,1)S(1)}, u32[]{:S(2)}, u32[]{:S(2)}) collective-permute-start(bf16[8,10752]{1,0:T(8,128)(2,1)S(1)} %bitcast.31), channel_id=1, source_target_pairs={{0,4},{1,5},{2,0},{3,1},{4,8},{5,9},{6,2},{7,3},{8,12},{9,13},{10,... | collective-permute-start | bytes 516104 | tf_op jit(solution)/shard_map/ppermute | solution.py:162
  18.9 0.2 fusion.3
  19.1 0.1 collective-permute-start.5
  19.3 0.1 fusion.7
  19.4 0.2 fusion.5
  19.6 0.6 %collective-permute-start.4 = (bf16[24,10752]{1,0:T(8,128)(2,1)S(1)}, bf16[24,10752]{1,0:T(8,128)(2,1)S(1)}, u32[]{:S(2)}, u32[]{:S(2)}) collective-permute-start(bf16[24,10752]{1,0:T(8,128)(2,1)S(1)} %pad_maximum_fusion), channel_id=1, source_target_pairs={{0,1},{1,0},{2,3},{3,2},{4,5},{5,4},{6,7},{7,6},{8,9},{9,8},{10,11... | collective-permute-start | bytes 1548296 | tf_op jit(solution)/shard_map/ppermute | solution.py:162
  20.1 3.3 %collective-permute-done.6 = bf16[8,10752]{1,0:T(8,128)(2,1)S(1)} collective-permute-done((bf16[8,10752]{1,0:T(8,128)(2,1)S(1)}, bf16[8,10752]{1,0:T(8,128)(2,1)S(1)}, u32[]{:S(2)}, u32[]{:S(2)}) %collective-permute-start.6) | collective-permute-done | bytes 172064 | tf_op jit(solution)/shard_map/ppermute | solution.py:162
  23.5 0.0 collective-permute-done.7
  23.5 0.1 collective-permute-start.8
  23.6 0.0 collective-permute-done.9.refs_6_
  23.6 0.5 %collective-permute-start.10 = (bf16[8,10752]{1,0:T(8,128)(2,1)S(1)}, bf16[8,10752]{1,0:T(8,128)(2,1)S(1)}, u32[]{:S(2)}, u32[]{:S(2)}) collective-permute-start(bf16[8,10752]{1,0:T(8,128)(2,1)S(1)} %collective-permute-done.9.refs_6_), channel_id=1, source_target_pairs={{0,1},{1,0},{2,3},{3,2},{4,5},{5,4},{6,7},{7,6},{8,9},{9,8},{10,11... | collective-permute-start | bytes 516104 | tf_op jit(solution)/shard_map/ppermute | solution.py:162
  24.1 1.4 %collective-permute-done.10.refs_7_ = bf16[8,10752]{1,0:T(8,128)(2,1)S(1)} collective-permute-done((bf16[8,10752]{1,0:T(8,128)(2,1)S(1)}, bf16[8,10752]{1,0:T(8,128)(2,1)S(1)}, u32[]{:S(2)}, u32[]{:S(2)}) %collective-permute-start.10) | collective-permute-done | bytes 172064 | tf_op jit(solution)/shard_map/ppermute | solution.py:162
  25.5 0.0 collective-permute-done.5.refs_3_
  25.5 0.0 collective-permute-done.8.refs_5_
  25.5 0.0 collective-permute-done.4.refs_1_
  25.5 12.5 %shard_map.37 = f32[11,896,896]{2,1,0:T(8,128)} custom-call(s32[153]{0:T(256)S(1)} %pad_add_fusion.table_ref, bf16[24,14336]{1,0:T(8,128)(2,1)S(1)} %get-tuple-element.8.refs_0_, bf16[24,10752]{1,0:T(8,128)(2,1)S(1)} %collective-permute-done.4.refs_1_, bf16[16,14336]{1,0:T(8,128)(2,1)S(1)} %pad_maximum_fusion.1.refs_2_, ...), custom_call_target="tpu_custom_call" | custom-call | flops 2260729856 | bytes 35323904 | tf_op jit(solution)/shard_map/pallas_call | solution.py:311
  (7 shorter events, 0.2 us)
Async XLA Ops:
  0.0 8.8 %collective-permute-start = (bf16[8,14336]{1,0:T(8,128)(2,1)}, bf16[8,14336]{1,0:T(8,128)(2,1)S(1)}, u32[]{:S(2)}, u32[]{:S(2)}) collective-permute-start(bf16[8,14336]{1,0:T(8,128)(2,1)} %param.3), channel_id=1, source_target_pairs={{0,2},{1,3},{2,6},{3,7},{4,0},{5,1},{6,10},{7,11},{8,4},{9,5},{10,... | collective-permute-start | bytes 688136 | tf_op jit(solution)/shard_map/ppermute | solution.py:162
  2.9 7.6 %collective-permute-start.1 = (bf16[8,14336]{1,0:T(8,128)(2,1)}, bf16[8,14336]{1,0:T(8,128)(2,1)S(1)}, u32[]{:S(2)}, u32[]{:S(2)}) collective-permute-start(bf16[8,14336]{1,0:T(8,128)(2,1)} %param.3), channel_id=1, source_target_pairs={{0,4},{1,5},{2,0},{3,1},{4,8},{5,9},{6,2},{7,3},{8,12},{9,13},{10,... | collective-permute-start | bytes 688136 | tf_op jit(solution)/shard_map/ppermute | solution.py:162
  8.8 7.0 %collective-permute-start.2 = (bf16[8,14336]{1,0:T(8,128)(2,1)S(1)}, bf16[8,14336]{1,0:T(8,128)(2,1)S(1)}, u32[]{:S(2)}, u32[]{:S(2)}) collective-permute-start(bf16[8,14336]{1,0:T(8,128)(2,1)S(1)} %collective-permute-done), channel_id=1, source_target_pairs={{0,2},{1,3},{2,6},{3,7},{4,0},{5,1},{6,10},{7,11},{8,4},{9,5},{10,... | collective-permute-start | bytes 688136 | tf_op jit(solution)/shard_map/ppermute | solution.py:162
  10.5 6.8 %collective-permute-start.3 = (bf16[8,14336]{1,0:T(8,128)(2,1)S(1)}, bf16[8,14336]{1,0:T(8,128)(2,1)S(1)}, u32[]{:S(2)}, u32[]{:S(2)}) collective-permute-start(bf16[8,14336]{1,0:T(8,128)(2,1)S(1)} %collective-permute-done.1), channel_id=1, source_target_pairs={{0,4},{1,5},{2,0},{3,1},{4,8},{5,9},{6,2},{7,3},{8,12},{9,13},{10,... | collective-permute-start | bytes 688136 | tf_op jit(solution)/shard_map/ppermute | solution.py:162
  11.1 12.4 %collective-permute-start.7 = (bf16[8,10752]{1,0:T(8,128)(2,1)S(1)}, bf16[8,10752]{1,0:T(8,128)(2,1)S(1)}, u32[]{:S(2)}, u32[]{:S(2)}) collective-permute-start(bf16[8,10752]{1,0:T(8,128)(2,1)S(1)} %bitcast.30), channel_id=1, source_target_pairs={{0,12},{1,13},{2,14},{3,15},{4,6},{5,7},{6,4},{7,5},{8,10},{9,11},... | collective-permute-start | bytes 516104 | tf_op jit(solution)/shard_map/ppermute | solution.py:162
  15.9 7.5 %collective-permute-start.6 = (bf16[8,10752]{1,0:T(8,128)(2,1)S(1)}, bf16[8,10752]{1,0:T(8,128)(2,1)S(1)}, u32[]{:S(2)}, u32[]{:S(2)}) collective-permute-start(bf16[8,10752]{1,0:T(8,128)(2,1)S(1)} %bitcast.32), channel_id=1, source_target_pairs={{0,2},{1,3},{2,6},{3,7},{4,0},{5,1},{6,10},{7,11},{8,4},{9,5},{10,... | collective-permute-start | bytes 516104 | tf_op jit(solution)/shard_map/ppermute | solution.py:162
  17.4 6.2 %collective-permute-start.9 = (bf16[8,10752]{1,0:T(8,128)(2,1)S(1)}, bf16[8,10752]{1,0:T(8,128)(2,1)S(1)}, u32[]{:S(2)}, u32[]{:S(2)}) collective-permute-start(bf16[8,10752]{1,0:T(8,128)(2,1)S(1)} %bitcast.31), channel_id=1, source_target_pairs={{0,4},{1,5},{2,0},{3,1},{4,8},{5,9},{6,2},{7,3},{8,12},{9,13},{10,... | collective-permute-start | bytes 516104 | tf_op jit(solution)/shard_map/ppermute | solution.py:162
  19.1 6.3 %collective-permute-start.5 = (bf16[16,10752]{1,0:T(8,128)(2,1)S(1)}, bf16[16,10752]{1,0:T(8,128)(2,1)S(1)}, u32[]{:S(2)}, u32[]{:S(2)}) collective-permute-start(bf16[16,10752]{1,0:T(8,128)(2,1)S(1)} %pad_maximum_fusion.2), channel_id=1, source_target_pairs={{0,1},{1,0},{2,3},{3,2},{4,5},{5,4},{6,7},{7,6},{8,9},{9,8},{10,11... | collective-permute-start | bytes 1032200 | tf_op jit(solution)/shard_map/ppermute | solution.py:162
  19.6 5.9 %collective-permute-start.4 = (bf16[24,10752]{1,0:T(8,128)(2,1)S(1)}, bf16[24,10752]{1,0:T(8,128)(2,1)S(1)}, u32[]{:S(2)}, u32[]{:S(2)}) collective-permute-start(bf16[24,10752]{1,0:T(8,128)(2,1)S(1)} %pad_maximum_fusion), channel_id=1, source_target_pairs={{0,1},{1,0},{2,3},{3,2},{4,5},{5,4},{6,7},{7,6},{8,9},{9,8},{10,11... | collective-permute-start | bytes 1548296 | tf_op jit(solution)/shard_map/ppermute | solution.py:162
  23.5 2.0 %collective-permute-start.8 = (bf16[16,10752]{1,0:T(8,128)(2,1)S(1)}, bf16[16,10752]{1,0:T(8,128)(2,1)S(1)}, u32[]{:S(2)}, u32[]{:S(2)}) collective-permute-start(bf16[16,10752]{1,0:T(8,128)(2,1)S(1)} %constant_dynamic-update-slice_fusion.3.refs_4_), channel_id=1, source_target_pairs={{0,1},{1,0},{2,3},{3,2},{4,5},{5,4},{6,7},{7,6},{8,9},{9,8},{10,11... | collective-permute-start | bytes 1032200 | tf_op jit(solution)/shard_map/ppermute | solution.py:162
  23.6 1.9 %collective-permute-start.10 = (bf16[8,10752]{1,0:T(8,128)(2,1)S(1)}, bf16[8,10752]{1,0:T(8,128)(2,1)S(1)}, u32[]{:S(2)}, u32[]{:S(2)}) collective-permute-start(bf16[8,10752]{1,0:T(8,128)(2,1)S(1)} %collective-permute-done.9.refs_6_), channel_id=1, source_target_pairs={{0,1},{1,0},{2,3},{3,2},{4,5},{5,4},{6,7},{7,6},{8,9},{9,8},{10,11... | collective-permute-start | bytes 516104 | tf_op jit(solution)/shard_map/ppermute | solution.py:162

commit v27 on v25

--- a/solution.py
+++ b/solution.py
@@ -146,7 +146,7 @@
     return onward, backward
 
 
-GROUPS = ((0, 1, 2), (8, 9, 10), (3, 4), (11, 12), (5, 7), (13, 15), (6,), (14,))
+GROUPS = ((0, 1, 2), (3, 4), (8, 9, 10, 11, 12), (5, 7), (13, 15), (6,), (14,))
 
 
 def first_needed(devices, chip):
@@ -194,11 +194,11 @@
     near = jnp.concatenate((tokens, ahead[1], back[1]), axis=0)
     middle = jnp.concatenate((ahead[2], back[2]), axis=0)
     last = jnp.concatenate((ahead[3], half), axis=0)
-    near_beside = send(after(near, ahead[2], back[2]), sibling)
-    needed = [window(after(value, ahead[2], back[2]), chip) for value in (ahead[2], back[2])]
-    middle_beside = send(jnp.concatenate(needed, axis=0), sibling)
+    rows = [after(near, ahead[2], back[2])[at:at + slab] for at in range(0, 3 * slab, slab)]
+    rows += [after(value, ahead[2], back[2]) for value in (ahead[2], back[2])]
+    early_beside = send(jnp.concatenate([window(value, chip) for value in rows], axis=0), sibling)
     last_beside = send(last, sibling)
-    return [near, near_beside, middle, middle_beside, last, last_beside, back[3], send(back[3], sibling)]
+    return [near, middle, early_beside, last, last_beside, back[3], send(back[3], sibling)]
 
 def slab_origin(devices, device, number):
     chips = devices // 2

time: 38.8 us -> 38.7 us (level)
  starting transfers between devices: 12.9 us -> 12.4 us
    ppermute x11 -> x10, starting transfers between devices: 12.9 us -> 12.4 us  [send(): return lax.ppermute(value, 'col', list(enumerate(target)))]
    ppermute x11 -> x10, waiting for transfers between devices: 9.94 us -> 10 us  [send(): return lax.ppermute(value, 'col', list(enumerate(target)))]
    unnamed x3 -> x7, local copies, waits for them, and re-layouts: 1.01 us -> 1.07 us
  transfers between devices with their start and end apart: 11 -> 10, of which waited for: 4 -> 4; matrix products, arithmetic and copies ran while one was open for 6% -> 7% of each run, Pallas kernels for 0% -> 0%
where the time goes in v27:
time: 38.7 us; the launch traced here: 38 us
  Pallas kernels  12.5 us (32%)
  starting transfers between devices  12.4 us (32%)
  waiting for transfers between devices  10 us (26%)
  other arithmetic  1.58 us (4%)
  local copies, waits for them, and re-layouts  1.14 us (3%)
    pallas_call x1, Pallas kernels, ring_form(): pl.pallas_call(functools.partial(ring_kernel, devices, slots), out_shape=...  12.5 us
    ppermute x10, starting transfers between devices, send(): return lax.ppermute(value, 'col', list(enumerate(target)))  12.4 us
    ppermute x10, waiting for transfers between devices, send(): return lax.ppermute(value, 'col', list(enumerate(target)))  10 us
    unnamed x7, local copies, waits for them, and re-layouts  1.07 us
  transfers between devices with their start and end apart: 10, of which 4 were waited for; matrix products, arithmetic and copies ran while one was open for 7% of the time, Pallas kernels for 0%

profile of v27, /device:TPU:0, one launch (start us, length us, event | category | flops | bytes accessed | tf_op | source)
XLA Modules:
  0.0 38.0 jit_solution(13154602517181045170)
XLA Ops:
  0.0 2.9 %collective-permute-start = (bf16[8,14336]{1,0:T(8,128)(2,1)}, bf16[8,14336]{1,0:T(8,128)(2,1)S(1)}, u32[]{:S(2)}, u32[]{:S(2)}) collective-permute-start(bf16[8,14336]{1,0:T(8,128)(2,1)} %param.3), channel_id=1, source_target_pairs={{0,2},{1,3},{2,6},{3,7},{4,0},{5,1},{6,10},{7,11},{8,4},{9,5},{10,... | collective-permute-start | bytes 688136 | tf_op jit(solution)/shard_map/ppermute | solution.py:162
  2.9 0.1 collective-permute-start.1
  3.0 1.0 %constant_dynamic-update-slice_fusion.2 = bf16[24,14336]{1,0:T(8,128)(2,1)S(1)} fusion(bf16[8,14336]{1,0:T(8,128)(2,1)} %param.3), kind=kLoop, calls=%fused_computation.28 | loop fusion | bytes 458752
  4.2 0.8 %pad_add_fusion.table_ref = s32[153]{0:T(256)S(1)} fusion(s32[1]{0:T(128)} %bitcast, s32[136]{0:T(256)} %param.5, s32[16]{0:T(128)} %param.4), kind=kLoop, calls=%fused_computation.36 | loop fusion | flops 306 | bytes 1224 | tf_op jit(solution)/shard_map/concatenate | solution.py:308
  4.9 3.9 %collective-permute-done = bf16[8,14336]{1,0:T(8,128)(2,1)S(1)} collective-permute-done((bf16[8,14336]{1,0:T(8,128)(2,1)}, bf16[8,14336]{1,0:T(8,128)(2,1)S(1)}, u32[]{:S(2)}, u32[]{:S(2)}) %collective-permute-start) | collective-permute-done | bytes 229408 | tf_op jit(solution)/shard_map/ppermute | solution.py:162
  8.8 1.7 %collective-permute-start.2 = (bf16[8,14336]{1,0:T(8,128)(2,1)S(1)}, bf16[8,14336]{1,0:T(8,128)(2,1)S(1)}, u32[]{:S(2)}, u32[]{:S(2)}) collective-permute-start(bf16[8,14336]{1,0:T(8,128)(2,1)S(1)} %collective-permute-done), channel_id=1, source_target_pairs={{0,2},{1,3},{2,6},{3,7},{4,0},{5,1},{6,10},{7,11},{8,4},{9,5},{10,... | collective-permute-start | bytes 688136 | tf_op jit(solution)/shard_map/ppermute | solution.py:162
  10.5 0.0 collective-permute-done.1
  10.5 0.4 collective-permute-start.3
  10.9 0.1 broadcast_select_fusion
  11.0 0.1 fusion.1
  11.1 3.8 %collective-permute-start.6 = (bf16[8,10752]{1,0:T(8,128)(2,1)S(1)}, bf16[8,10752]{1,0:T(8,128)(2,1)S(1)}, u32[]{:S(2)}, u32[]{:S(2)}) collective-permute-start(bf16[8,10752]{1,0:T(8,128)(2,1)S(1)} %bitcast.30), channel_id=1, source_target_pairs={{0,12},{1,13},{2,14},{3,15},{4,6},{5,7},{6,4},{7,5},{8,10},{9,11},... | collective-permute-start | bytes 516104 | tf_op jit(solution)/shard_map/ppermute | solution.py:162
  14.9 0.9 %collective-permute-done.2 = bf16[8,14336]{1,0:T(8,128)(2,1)S(1)} collective-permute-done((bf16[8,14336]{1,0:T(8,128)(2,1)S(1)}, bf16[8,14336]{1,0:T(8,128)(2,1)S(1)}, u32[]{:S(2)}, u32[]{:S(2)}) %collective-permute-start.2) | collective-permute-done | bytes 229408 | tf_op jit(solution)/shard_map/ppermute | solution.py:162
  15.8 0.1 fusion.2
  15.9 1.4 %collective-permute-start.5 = (bf16[8,10752]{1,0:T(8,128)(2,1)S(1)}, bf16[8,10752]{1,0:T(8,128)(2,1)S(1)}, u32[]{:S(2)}, u32[]{:S(2)}) collective-permute-start(bf16[8,10752]{1,0:T(8,128)(2,1)S(1)} %bitcast.32), channel_id=1, source_target_pairs={{0,2},{1,3},{2,6},{3,7},{4,0},{5,1},{6,10},{7,11},{8,4},{9,5},{10,... | collective-permute-start | bytes 516104 | tf_op jit(solution)/shard_map/ppermute | solution.py:162
  17.3 0.0 collective-permute-done.3
  17.3 0.1 fusion
  17.4 1.5 %collective-permute-start.8 = (bf16[8,10752]{1,0:T(8,128)(2,1)S(1)}, bf16[8,10752]{1,0:T(8,128)(2,1)S(1)}, u32[]{:S(2)}, u32[]{:S(2)}) collective-permute-start(bf16[8,10752]{1,0:T(8,128)(2,1)S(1)} %bitcast.31), channel_id=1, source_target_pairs={{0,4},{1,5},{2,0},{3,1},{4,8},{5,9},{6,2},{7,3},{8,12},{9,13},{10,... | collective-permute-start | bytes 516104 | tf_op jit(solution)/shard_map/ppermute | solution.py:162
  19.0 0.1 fusion.7
  19.1 0.2 fusion.3
  19.3 0.2 fusion.5
  19.6 0.1 collective-permute-start.4
  19.6 3.8 %collective-permute-done.5 = bf16[8,10752]{1,0:T(8,128)(2,1)S(1)} collective-permute-done((bf16[8,10752]{1,0:T(8,128)(2,1)S(1)}, bf16[8,10752]{1,0:T(8,128)(2,1)S(1)}, u32[]{:S(2)}, u32[]{:S(2)}) %collective-permute-start.5) | collective-permute-done | bytes 172064 | tf_op jit(solution)/shard_map/ppermute | solution.py:162
  23.5 0.0 collective-permute-done.6
  23.5 0.1 collective-permute-start.7
  23.6 0.0 collective-permute-done.8.refs_5_
  23.6 0.5 %collective-permute-start.9 = (bf16[8,10752]{1,0:T(8,128)(2,1)S(1)}, bf16[8,10752]{1,0:T(8,128)(2,1)S(1)}, u32[]{:S(2)}, u32[]{:S(2)}) collective-permute-start(bf16[8,10752]{1,0:T(8,128)(2,1)S(1)} %collective-permute-done.8.refs_5_), channel_id=1, source_target_pairs={{0,1},{1,0},{2,3},{3,2},{4,5},{5,4},{6,7},{7,6},{8,9},{9,8},{10,11... | collective-permute-start | bytes 516104 | tf_op jit(solution)/shard_map/ppermute | solution.py:162
  24.1 1.4 %collective-permute-done.9.refs_6_ = bf16[8,10752]{1,0:T(8,128)(2,1)S(1)} collective-permute-done((bf16[8,10752]{1,0:T(8,128)(2,1)S(1)}, bf16[8,10752]{1,0:T(8,128)(2,1)S(1)}, u32[]{:S(2)}, u32[]{:S(2)}) %collective-permute-start.9) | collective-permute-done | bytes 172064 | tf_op jit(solution)/shard_map/ppermute | solution.py:162
  25.5 0.0 collective-permute-done.7.refs_4_
  25.5 0.0 collective-permute-done.4.refs_2_
  25.5 12.5 %shard_map.37 = f32[11,896,896]{2,1,0:T(8,128)} custom-call(s32[153]{0:T(256)S(1)} %pad_add_fusion.table_ref, bf16[24,14336]{1,0:T(8,128)(2,1)S(1)} %get-tuple-element.8.refs_0_, bf16[16,14336]{1,0:T(8,128)(2,1)S(1)} %pad_maximum_fusion.refs_1_, bf16[40,10752]{1,0:T(8,128)(2,1)S(1)} %collective-permute-done.4.refs_2_, ...), custom_call_target="tpu_custom_call" | custom-call | flops 2260729856 | bytes 35323904 | tf_op jit(solution)/shard_map/pallas_call | solution.py:309
  (10 shorter events, 0.2 us)
Async XLA Ops:
  0.0 8.8 %collective-permute-start = (bf16[8,14336]{1,0:T(8,128)(2,1)}, bf16[8,14336]{1,0:T(8,128)(2,1)S(1)}, u32[]{:S(2)}, u32[]{:S(2)}) collective-permute-start(bf16[8,14336]{1,0:T(8,128)(2,1)} %param.3), channel_id=1, source_target_pairs={{0,2},{1,3},{2,6},{3,7},{4,0},{5,1},{6,10},{7,11},{8,4},{9,5},{10,... | collective-permute-start | bytes 688136 | tf_op jit(solution)/shard_map/ppermute | solution.py:162
  2.9 7.6 %collective-permute-start.1 = (bf16[8,14336]{1,0:T(8,128)(2,1)}, bf16[8,14336]{1,0:T(8,128)(2,1)S(1)}, u32[]{:S(2)}, u32[]{:S(2)}) collective-permute-start(bf16[8,14336]{1,0:T(8,128)(2,1)} %param.3), channel_id=1, source_target_pairs={{0,4},{1,5},{2,0},{3,1},{4,8},{5,9},{6,2},{7,3},{8,12},{9,13},{10,... | collective-permute-start | bytes 688136 | tf_op jit(solution)/shard_map/ppermute | solution.py:162
  8.8 7.0 %collective-permute-start.2 = (bf16[8,14336]{1,0:T(8,128)(2,1)S(1)}, bf16[8,14336]{1,0:T(8,128)(2,1)S(1)}, u32[]{:S(2)}, u32[]{:S(2)}) collective-permute-start(bf16[8,14336]{1,0:T(8,128)(2,1)S(1)} %collective-permute-done), channel_id=1, source_target_pairs={{0,2},{1,3},{2,6},{3,7},{4,0},{5,1},{6,10},{7,11},{8,4},{9,5},{10,... | collective-permute-start | bytes 688136 | tf_op jit(solution)/shard_map/ppermute | solution.py:162
  10.5 6.8 %collective-permute-start.3 = (bf16[8,14336]{1,0:T(8,128)(2,1)S(1)}, bf16[8,14336]{1,0:T(8,128)(2,1)S(1)}, u32[]{:S(2)}, u32[]{:S(2)}) collective-permute-start(bf16[8,14336]{1,0:T(8,128)(2,1)S(1)} %collective-permute-done.1), channel_id=1, source_target_pairs={{0,4},{1,5},{2,0},{3,1},{4,8},{5,9},{6,2},{7,3},{8,12},{9,13},{10,... | collective-permute-start | bytes 688136 | tf_op jit(solution)/shard_map/ppermute | solution.py:162
  11.1 12.4 %collective-permute-start.6 = (bf16[8,10752]{1,0:T(8,128)(2,1)S(1)}, bf16[8,10752]{1,0:T(8,128)(2,1)S(1)}, u32[]{:S(2)}, u32[]{:S(2)}) collective-permute-start(bf16[8,10752]{1,0:T(8,128)(2,1)S(1)} %bitcast.30), channel_id=1, source_target_pairs={{0,12},{1,13},{2,14},{3,15},{4,6},{5,7},{6,4},{7,5},{8,10},{9,11},... | collective-permute-start | bytes 516104 | tf_op jit(solution)/shard_map/ppermute | solution.py:162
  15.9 7.5 %collective-permute-start.5 = (bf16[8,10752]{1,0:T(8,128)(2,1)S(1)}, bf16[8,10752]{1,0:T(8,128)(2,1)S(1)}, u32[]{:S(2)}, u32[]{:S(2)}) collective-permute-start(bf16[8,10752]{1,0:T(8,128)(2,1)S(1)} %bitcast.32), channel_id=1, source_target_pairs={{0,2},{1,3},{2,6},{3,7},{4,0},{5,1},{6,10},{7,11},{8,4},{9,5},{10,... | collective-permute-start | bytes 516104 | tf_op jit(solution)/shard_map/ppermute | solution.py:162
  17.4 6.2 %collective-permute-start.8 = (bf16[8,10752]{1,0:T(8,128)(2,1)S(1)}, bf16[8,10752]{1,0:T(8,128)(2,1)S(1)}, u32[]{:S(2)}, u32[]{:S(2)}) collective-permute-start(bf16[8,10752]{1,0:T(8,128)(2,1)S(1)} %bitcast.31), channel_id=1, source_target_pairs={{0,4},{1,5},{2,0},{3,1},{4,8},{5,9},{6,2},{7,3},{8,12},{9,13},{10,... | collective-permute-start | bytes 516104 | tf_op jit(solution)/shard_map/ppermute | solution.py:162
  19.6 5.9 %collective-permute-start.4 = (bf16[40,10752]{1,0:T(8,128)(2,1)S(1)}, bf16[40,10752]{1,0:T(8,128)(2,1)S(1)}, u32[]{:S(2)}, u32[]{:S(2)}) collective-permute-start(bf16[40,10752]{1,0:T(8,128)(2,1)S(1)} %constant_dynamic-update-slice_fusion.3), channel_id=1, source_target_pairs={{0,1},{1,0},{2,3},{3,2},{4,5},{5,4},{6,7},{7,6},{8,9},{9,8},{10,11... | collective-permute-start | bytes 2580488 | tf_op jit(solution)/shard_map/ppermute | solution.py:162
  23.5 2.0 %collective-permute-start.7 = (bf16[16,10752]{1,0:T(8,128)(2,1)S(1)}, bf16[16,10752]{1,0:T(8,128)(2,1)S(1)}, u32[]{:S(2)}, u32[]{:S(2)}) collective-permute-start(bf16[16,10752]{1,0:T(8,128)(2,1)S(1)} %constant_dynamic-update-slice_fusion.8.refs_3_), channel_id=1, source_target_pairs={{0,1},{1,0},{2,3},{3,2},{4,5},{5,4},{6,7},{7,6},{8,9},{9,8},{10,11... | collective-permute-start | bytes 1032200 | tf_op jit(solution)/shard_map/ppermute | solution.py:162
  23.6 1.9 %collective-permute-start.9 = (bf16[8,10752]{1,0:T(8,128)(2,1)S(1)}, bf16[8,10752]{1,0:T(8,128)(2,1)S(1)}, u32[]{:S(2)}, u32[]{:S(2)}) collective-permute-start(bf16[8,10752]{1,0:T(8,128)(2,1)S(1)} %collective-permute-done.8.refs_5_), channel_id=1, source_target_pairs={{0,1},{1,0},{2,3},{3,2},{4,5},{5,4},{6,7},{7,6},{8,9},{9,8},{10,11... | collective-permute-start | bytes 516104 | tf_op jit(solution)/shard_map/ppermute | solution.py:162

commit v28 on v25

--- a/solution.py
+++ b/solution.py
@@ -7,7 +7,7 @@
 from jax.experimental.pallas import tpu as pltpu
 from jax.sharding import PartitionSpec as P
 
-BUFFERS = 4
+BUFFERS = 6
 STRIP = 128
 RING_DEVICES = 16
 

time: 38.8 us -> 38.8 us (level)
  no operation moved by 1% of the time
where the time goes in v28:
time: 38.8 us; the launch traced here: 38 us
  starting transfers between devices  12.9 us (33%)
  Pallas kernels  12.6 us (32%)
  waiting for transfers between devices  9.94 us (26%)
  other arithmetic  1.32 us (3%)
  local copies, waits for them, and re-layouts  1.03 us (3%)
    ppermute x11, starting transfers between devices, send(): return lax.ppermute(value, 'col', list(enumerate(target)))  12.9 us
    pallas_call x1, Pallas kernels, ring_form(): pl.pallas_call(functools.partial(ring_kernel, devices, slots), out_shape=...  12.6 us
    ppermute x11, waiting for transfers between devices, send(): return lax.ppermute(value, 'col', list(enumerate(target)))  9.94 us
    unnamed x3, local copies, waits for them, and re-layouts  1.01 us
  transfers between devices with their start and end apart: 11, of which 4 were waited for; matrix products, arithmetic and copies ran while one was open for 6% of the time, Pallas kernels for 0%

profile of v28, /device:TPU:0, one launch (start us, length us, event | category | flops | bytes accessed | tf_op | source)
XLA Modules:
  0.0 38.0 jit_solution(4095119317613198234)
XLA Ops:
  0.0 2.9 %collective-permute-start = (bf16[8,14336]{1,0:T(8,128)(2,1)}, bf16[8,14336]{1,0:T(8,128)(2,1)S(1)}, u32[]{:S(2)}, u32[]{:S(2)}) collective-permute-start(bf16[8,14336]{1,0:T(8,128)(2,1)} %param.3), channel_id=1, source_target_pairs={{0,2},{1,3},{2,6},{3,7},{4,0},{5,1},{6,10},{7,11},{8,4},{9,5},{10,... | collective-permute-start | bytes 688136 | tf_op jit(solution)/shard_map/ppermute | solution.py:162
  2.9 0.1 collective-permute-start.1
  3.0 1.0 %constant_dynamic-update-slice_fusion.2 = bf16[24,14336]{1,0:T(8,128)(2,1)S(1)} fusion(bf16[8,14336]{1,0:T(8,128)(2,1)} %param.3), kind=kLoop, calls=%fused_computation.20 | loop fusion | bytes 458752
  4.2 0.8 %pad_add_fusion.table_ref = s32[153]{0:T(256)S(1)} fusion(s32[1]{0:T(128)} %bitcast, s32[136]{0:T(256)} %param.5, s32[16]{0:T(128)} %param.4), kind=kLoop, calls=%fused_computation.23 | loop fusion | flops 306 | bytes 1224 | tf_op jit(solution)/shard_map/concatenate | solution.py:308
  4.9 3.9 %collective-permute-done = bf16[8,14336]{1,0:T(8,128)(2,1)S(1)} collective-permute-done((bf16[8,14336]{1,0:T(8,128)(2,1)}, bf16[8,14336]{1,0:T(8,128)(2,1)S(1)}, u32[]{:S(2)}, u32[]{:S(2)}) %collective-permute-start) | collective-permute-done | bytes 229408 | tf_op jit(solution)/shard_map/ppermute | solution.py:162
  8.8 1.7 %collective-permute-start.2 = (bf16[8,14336]{1,0:T(8,128)(2,1)S(1)}, bf16[8,14336]{1,0:T(8,128)(2,1)S(1)}, u32[]{:S(2)}, u32[]{:S(2)}) collective-permute-start(bf16[8,14336]{1,0:T(8,128)(2,1)S(1)} %collective-permute-done), channel_id=1, source_target_pairs={{0,2},{1,3},{2,6},{3,7},{4,0},{5,1},{6,10},{7,11},{8,4},{9,5},{10,... | collective-permute-start | bytes 688136 | tf_op jit(solution)/shard_map/ppermute | solution.py:162
  10.5 0.0 collective-permute-done.1
  10.5 0.4 collective-permute-start.3
  10.9 0.1 broadcast_select_fusion
  11.0 0.1 fusion.1
  11.1 3.8 %collective-permute-start.7 = (bf16[8,10752]{1,0:T(8,128)(2,1)S(1)}, bf16[8,10752]{1,0:T(8,128)(2,1)S(1)}, u32[]{:S(2)}, u32[]{:S(2)}) collective-permute-start(bf16[8,10752]{1,0:T(8,128)(2,1)S(1)} %bitcast.18), channel_id=1, source_target_pairs={{0,12},{1,13},{2,14},{3,15},{4,6},{5,7},{6,4},{7,5},{8,10},{9,11},... | collective-permute-start | bytes 516104 | tf_op jit(solution)/shard_map/ppermute | solution.py:162
  14.9 0.9 %collective-permute-done.2 = bf16[8,14336]{1,0:T(8,128)(2,1)S(1)} collective-permute-done((bf16[8,14336]{1,0:T(8,128)(2,1)S(1)}, bf16[8,14336]{1,0:T(8,128)(2,1)S(1)}, u32[]{:S(2)}, u32[]{:S(2)}) %collective-permute-start.2) | collective-permute-done | bytes 229408 | tf_op jit(solution)/shard_map/ppermute | solution.py:162
  15.8 0.1 fusion.2
  15.9 1.4 %collective-permute-start.6 = (bf16[8,10752]{1,0:T(8,128)(2,1)S(1)}, bf16[8,10752]{1,0:T(8,128)(2,1)S(1)}, u32[]{:S(2)}, u32[]{:S(2)}) collective-permute-start(bf16[8,10752]{1,0:T(8,128)(2,1)S(1)} %bitcast.20), channel_id=1, source_target_pairs={{0,2},{1,3},{2,6},{3,7},{4,0},{5,1},{6,10},{7,11},{8,4},{9,5},{10,... | collective-permute-start | bytes 516104 | tf_op jit(solution)/shard_map/ppermute | solution.py:162
  17.3 0.0 collective-permute-done.3
  17.3 0.1 fusion
  17.4 1.5 %collective-permute-start.9 = (bf16[8,10752]{1,0:T(8,128)(2,1)S(1)}, bf16[8,10752]{1,0:T(8,128)(2,1)S(1)}, u32[]{:S(2)}, u32[]{:S(2)}) collective-permute-start(bf16[8,10752]{1,0:T(8,128)(2,1)S(1)} %bitcast.19), channel_id=1, source_target_pairs={{0,4},{1,5},{2,0},{3,1},{4,8},{5,9},{6,2},{7,3},{8,12},{9,13},{10,... | collective-permute-start | bytes 516104 | tf_op jit(solution)/shard_map/ppermute | solution.py:162
  18.9 0.2 fusion.3
  19.1 0.1 collective-permute-start.5
  19.2 0.5 %collective-permute-start.4 = (bf16[24,14336]{1,0:T(8,128)(2,1)S(1)}, bf16[24,14336]{1,0:T(8,128)(2,1)S(1)}, u32[]{:S(2)}, u32[]{:S(2)}) collective-permute-start(bf16[24,14336]{1,0:T(8,128)(2,1)S(1)} %get-tuple-element.8.refs_0_), channel_id=1, source_target_pairs={{0,1},{1,0},{2,3},{3,2},{4,5},{5,4},{6,7},{7,6},{8,9},{9,8},{10,11... | collective-permute-start | bytes 2064392 | tf_op jit(solution)/shard_map/ppermute | solution.py:162
  19.7 3.8 %collective-permute-done.6 = bf16[8,10752]{1,0:T(8,128)(2,1)S(1)} collective-permute-done((bf16[8,10752]{1,0:T(8,128)(2,1)S(1)}, bf16[8,10752]{1,0:T(8,128)(2,1)S(1)}, u32[]{:S(2)}, u32[]{:S(2)}) %collective-permute-start.6) | collective-permute-done | bytes 172064 | tf_op jit(solution)/shard_map/ppermute | solution.py:162
  23.5 0.0 collective-permute-done.7
  23.5 0.1 collective-permute-start.8
  23.6 0.0 collective-permute-done.9.refs_6_
  23.6 0.5 %collective-permute-start.10 = (bf16[8,10752]{1,0:T(8,128)(2,1)S(1)}, bf16[8,10752]{1,0:T(8,128)(2,1)S(1)}, u32[]{:S(2)}, u32[]{:S(2)}) collective-permute-start(bf16[8,10752]{1,0:T(8,128)(2,1)S(1)} %collective-permute-done.9.refs_6_), channel_id=1, source_target_pairs={{0,1},{1,0},{2,3},{3,2},{4,5},{5,4},{6,7},{7,6},{8,9},{9,8},{10,11... | collective-permute-start | bytes 516104 | tf_op jit(solution)/shard_map/ppermute | solution.py:162
  24.1 1.4 %collective-permute-done.10.refs_7_ = bf16[8,10752]{1,0:T(8,128)(2,1)S(1)} collective-permute-done((bf16[8,10752]{1,0:T(8,128)(2,1)S(1)}, bf16[8,10752]{1,0:T(8,128)(2,1)S(1)}, u32[]{:S(2)}, u32[]{:S(2)}) %collective-permute-start.10) | collective-permute-done | bytes 172064 | tf_op jit(solution)/shard_map/ppermute | solution.py:162
  25.5 0.0 collective-permute-done.5.refs_3_
  25.5 0.0 collective-permute-done.8.refs_5_
  25.5 0.0 collective-permute-done.4.refs_1_
  25.5 12.6 %shard_map.37 = f32[11,896,896]{2,1,0:T(8,128)} custom-call(s32[153]{0:T(256)S(1)} %pad_add_fusion.table_ref, bf16[24,14336]{1,0:T(8,128)(2,1)S(1)} %get-tuple-element.8.refs_0_, bf16[24,14336]{1,0:T(8,128)(2,1)S(1)} %collective-permute-done.4.refs_1_, bf16[16,14336]{1,0:T(8,128)(2,1)S(1)} %pad_maximum_fusion.refs_2_, ...), custom_call_target="tpu_custom_call" | custom-call | flops 2260729856 | bytes 35323904 | tf_op jit(solution)/shard_map/pallas_call | solution.py:309
  (5 shorter events, 0.1 us)
Async XLA Ops:
  0.0 8.8 %collective-permute-start = (bf16[8,14336]{1,0:T(8,128)(2,1)}, bf16[8,14336]{1,0:T(8,128)(2,1)S(1)}, u32[]{:S(2)}, u32[]{:S(2)}) collective-permute-start(bf16[8,14336]{1,0:T(8,128)(2,1)} %param.3), channel_id=1, source_target_pairs={{0,2},{1,3},{2,6},{3,7},{4,0},{5,1},{6,10},{7,11},{8,4},{9,5},{10,... | collective-permute-start | bytes 688136 | tf_op jit(solution)/shard_map/ppermute | solution.py:162
  2.9 7.6 %collective-permute-start.1 = (bf16[8,14336]{1,0:T(8,128)(2,1)}, bf16[8,14336]{1,0:T(8,128)(2,1)S(1)}, u32[]{:S(2)}, u32[]{:S(2)}) collective-permute-start(bf16[8,14336]{1,0:T(8,128)(2,1)} %param.3), channel_id=1, source_target_pairs={{0,4},{1,5},{2,0},{3,1},{4,8},{5,9},{6,2},{7,3},{8,12},{9,13},{10,... | collective-permute-start | bytes 688136 | tf_op jit(solution)/shard_map/ppermute | solution.py:162
  8.8 7.0 %collective-permute-start.2 = (bf16[8,14336]{1,0:T(8,128)(2,1)S(1)}, bf16[8,14336]{1,0:T(8,128)(2,1)S(1)}, u32[]{:S(2)}, u32[]{:S(2)}) collective-permute-start(bf16[8,14336]{1,0:T(8,128)(2,1)S(1)} %collective-permute-done), channel_id=1, source_target_pairs={{0,2},{1,3},{2,6},{3,7},{4,0},{5,1},{6,10},{7,11},{8,4},{9,5},{10,... | collective-permute-start | bytes 688136 | tf_op jit(solution)/shard_map/ppermute | solution.py:162
  10.5 6.8 %collective-permute-start.3 = (bf16[8,14336]{1,0:T(8,128)(2,1)S(1)}, bf16[8,14336]{1,0:T(8,128)(2,1)S(1)}, u32[]{:S(2)}, u32[]{:S(2)}) collective-permute-start(bf16[8,14336]{1,0:T(8,128)(2,1)S(1)} %collective-permute-done.1), channel_id=1, source_target_pairs={{0,4},{1,5},{2,0},{3,1},{4,8},{5,9},{6,2},{7,3},{8,12},{9,13},{10,... | collective-permute-start | bytes 688136 | tf_op jit(solution)/shard_map/ppermute | solution.py:162
  11.1 12.4 %collective-permute-start.7 = (bf16[8,10752]{1,0:T(8,128)(2,1)S(1)}, bf16[8,10752]{1,0:T(8,128)(2,1)S(1)}, u32[]{:S(2)}, u32[]{:S(2)}) collective-permute-start(bf16[8,10752]{1,0:T(8,128)(2,1)S(1)} %bitcast.18), channel_id=1, source_target_pairs={{0,12},{1,13},{2,14},{3,15},{4,6},{5,7},{6,4},{7,5},{8,10},{9,11},... | collective-permute-start | bytes 516104 | tf_op jit(solution)/shard_map/ppermute | solution.py:162
  15.9 7.5 %collective-permute-start.6 = (bf16[8,10752]{1,0:T(8,128)(2,1)S(1)}, bf16[8,10752]{1,0:T(8,128)(2,1)S(1)}, u32[]{:S(2)}, u32[]{:S(2)}) collective-permute-start(bf16[8,10752]{1,0:T(8,128)(2,1)S(1)} %bitcast.20), channel_id=1, source_target_pairs={{0,2},{1,3},{2,6},{3,7},{4,0},{5,1},{6,10},{7,11},{8,4},{9,5},{10,... | collective-permute-start | bytes 516104 | tf_op jit(solution)/shard_map/ppermute | solution.py:162
  17.4 6.2 %collective-permute-start.9 = (bf16[8,10752]{1,0:T(8,128)(2,1)S(1)}, bf16[8,10752]{1,0:T(8,128)(2,1)S(1)}, u32[]{:S(2)}, u32[]{:S(2)}) collective-permute-start(bf16[8,10752]{1,0:T(8,128)(2,1)S(1)} %bitcast.19), channel_id=1, source_target_pairs={{0,4},{1,5},{2,0},{3,1},{4,8},{5,9},{6,2},{7,3},{8,12},{9,13},{10,... | collective-permute-start | bytes 516104 | tf_op jit(solution)/shard_map/ppermute | solution.py:162
  19.1 6.3 %collective-permute-start.5 = (bf16[16,10752]{1,0:T(8,128)(2,1)S(1)}, bf16[16,10752]{1,0:T(8,128)(2,1)S(1)}, u32[]{:S(2)}, u32[]{:S(2)}) collective-permute-start(bf16[16,10752]{1,0:T(8,128)(2,1)S(1)} %pad_maximum_fusion.1), channel_id=1, source_target_pairs={{0,1},{1,0},{2,3},{3,2},{4,5},{5,4},{6,7},{7,6},{8,9},{9,8},{10,11... | collective-permute-start | bytes 1032200 | tf_op jit(solution)/shard_map/ppermute | solution.py:162
  19.2 6.3 %collective-permute-start.4 = (bf16[24,14336]{1,0:T(8,128)(2,1)S(1)}, bf16[24,14336]{1,0:T(8,128)(2,1)S(1)}, u32[]{:S(2)}, u32[]{:S(2)}) collective-permute-start(bf16[24,14336]{1,0:T(8,128)(2,1)S(1)} %get-tuple-element.8.refs_0_), channel_id=1, source_target_pairs={{0,1},{1,0},{2,3},{3,2},{4,5},{5,4},{6,7},{7,6},{8,9},{9,8},{10,11... | collective-permute-start | bytes 2064392 | tf_op jit(solution)/shard_map/ppermute | solution.py:162
  23.5 2.0 %collective-permute-start.8 = (bf16[16,10752]{1,0:T(8,128)(2,1)S(1)}, bf16[16,10752]{1,0:T(8,128)(2,1)S(1)}, u32[]{:S(2)}, u32[]{:S(2)}) collective-permute-start(bf16[16,10752]{1,0:T(8,128)(2,1)S(1)} %constant_dynamic-update-slice_fusion.3.refs_4_), channel_id=1, source_target_pairs={{0,1},{1,0},{2,3},{3,2},{4,5},{5,4},{6,7},{7,6},{8,9},{9,8},{10,11... | collective-permute-start | bytes 1032200 | tf_op jit(solution)/shard_map/ppermute | solution.py:162
  23.6 1.9 %collective-permute-start.10 = (bf16[8,10752]{1,0:T(8,128)(2,1)S(1)}, bf16[8,10752]{1,0:T(8,128)(2,1)S(1)}, u32[]{:S(2)}, u32[]{:S(2)}) collective-permute-start(bf16[8,10752]{1,0:T(8,128)(2,1)S(1)} %collective-permute-done.9.refs_6_), channel_id=1, source_target_pairs={{0,1},{1,0},{2,3},{3,2},{4,5},{5,4},{6,7},{7,6},{8,9},{9,8},{10,11... | collective-permute-start | bytes 516104 | tf_op jit(solution)/shard_map/ppermute | solution.py:162
